TPU v7x, 32 devices: a whole 2x2x4 slice. The times are simulated.
32 devices in a mesh: ctx: 16 (over z, y, x), tp: 2 (over core).
Axes of the slice: x: 2, y: 2, z: 4, core: 2. Of those that a mesh axis runs over, the one named last changes fastest.
Arguments:
- queries: bfloat16 [4096, 1536], P('ctx', 'tp'), may hold values from -8 to 8
- key_vectors: bfloat16 [4096, 1536], P('ctx', 'tp'), may hold values from -8 to 8
- value_vectors: bfloat16 [4096, 1536], P('ctx', 'tp'), may hold values from -6 to 6
- out_weight: bfloat16 [1536, 3072], P('tp'), may hold values from -0.15625 to 0.15625
- out_grad: bfloat16 [4096, 3072], P('ctx', 'tp'), may hold values from -6 to 6
- block_segment: int32 [32], replicated, may hold values from 0 to 5, as said below
Outputs:
- attention_out: bfloat16 [4096, 3072], P('ctx', 'tp')
- grad_queries: bfloat16 [4096, 1536], P('ctx', 'tp')
- grad_keys: bfloat16 [4096, 1536], P('ctx', 'tp')
- grad_values: bfloat16 [4096, 1536], P('ctx', 'tp')
- grad_weight: float32 [1536, 3072], P('tp')
Inputs may be any that keep to these rules, and one draw needn't show every extreme that they name: `block_segment`: blocks 0 to 3 hold 0; the other blocks form five runs of consecutive blocks, one run for each of 1 to 5, run lengths within one of each other, in an order that varies from draw to draw.
All inputs are finite; a program needn't handle non-finite values.
Results may differ from a plain program's by a relative error of at most 0.02.
Values may be sent and summed in bfloat16 or wider, within the bound.
No kernel may reach another device: no remote copies, remote signals or barrier semaphores. Data moves between devices by JAX's collectives and lax.ppermute only.
A program may use at most 128 MiB of HBM per device.

v0:
```python
import jax
import jax.numpy as jnp
from jax import lax
from jax.sharding import PartitionSpec as P

HEAD = 128
BLK = 128


neg_big = -1e30
target_id = 5
key_span = 512


def permitted_mask(query_seg, key_seg):
    query_col = query_seg[:, None]
    key_row = key_seg[None, :]
    return (query_col == 0) | (query_col == target_id) | (key_row == 0) | (query_col == key_row)


def head_scores(query_heads, key_block, permitted, score_scale):
    scores = (
        jnp.einsum("qhd,khd->hqk", query_heads, key_block, preferred_element_type=jnp.float32)
        * score_scale
    )
    return jnp.where(permitted[None], scores, neg_big)


def score_gradients(
    query_heads, key_block, value_block, grad_heads, permitted, log_total, row_delta, score_scale
):
    scores = head_scores(query_heads, key_block, permitted, score_scale)
    prob_rows = jnp.where(permitted[None], jnp.exp(scores - log_total[:, :, None]), 0.0)
    prob_grads = jnp.einsum(
        "qhd,khd->hqk", grad_heads, value_block, preferred_element_type=jnp.float32
    )
    return (prob_rows, (prob_rows * (prob_grads - row_delta[:, :, None])).astype(jnp.bfloat16))


def per_device(queries, key_vectors, value_vectors, out_weight, out_grad, block_segment):
    local_rows, local_width = queries.shape
    heads_here = local_width // HEAD
    score_scale = HEAD ** (-0.5)
    key_all, value_all = (
        lax.all_gather(key_vectors, "ctx", axis=0, tiled=True),
        lax.all_gather(value_vectors, "ctx", axis=0, tiled=True),
    )
    all_rows = key_all.shape[0]
    seg_rows = jnp.repeat(block_segment, BLK, total_repeat_length=all_rows)
    first_row = lax.axis_index("ctx") * local_rows
    query_seg = lax.dynamic_slice_in_dim(seg_rows, first_row, local_rows)
    query_heads = queries.reshape(local_rows, heads_here, HEAD)
    block_count = all_rows // key_span
    key_blocks = key_all.reshape(block_count, key_span, heads_here, HEAD)
    value_blocks = value_all.reshape(block_count, key_span, heads_here, HEAD)
    seg_blocks = seg_rows.reshape(block_count, key_span)

    def stats_step(totals, block_ops):
        row_top, row_mass = totals
        key_block, block_seg = block_ops
        permitted = permitted_mask(query_seg, block_seg)
        scores = head_scores(query_heads, key_block, permitted, score_scale)
        new_top = jnp.maximum(row_top, jnp.max(scores, axis=2))
        shifted = jnp.where(permitted[None], jnp.exp(scores - new_top[:, :, None]), 0.0)
        return ((new_top, row_mass * jnp.exp(row_top - new_top) + jnp.sum(shifted, axis=2)), None)

    start_top = jnp.full((heads_here, local_rows), neg_big, jnp.float32)
    start_mass = jnp.zeros((heads_here, local_rows), jnp.float32)
    (row_top, row_mass), _ = lax.scan(stats_step, (start_top, start_mass), (key_blocks, seg_blocks))
    log_total = row_top + jnp.log(row_mass)

    def value_step(values_acc, block_ops):
        key_block, value_block, block_seg = block_ops
        permitted = permitted_mask(query_seg, block_seg)
        scores = head_scores(query_heads, key_block, permitted, score_scale)
        weights = jnp.where(permitted[None], jnp.exp(scores - log_total[:, :, None]), 0.0).astype(
            jnp.bfloat16
        )
        return (
            values_acc
            + jnp.einsum("hqk,khd->qhd", weights, value_block, preferred_element_type=jnp.float32),
            None,
        )

    zero_heads = jnp.zeros((local_rows, heads_here, HEAD), jnp.float32)
    values_acc, _ = lax.scan(value_step, zero_heads, (key_blocks, value_blocks, seg_blocks))
    attention = values_acc.reshape(local_rows, local_width).astype(jnp.bfloat16)
    projected = jnp.dot(attention, out_weight, preferred_element_type=jnp.float32)
    attention_out = lax.psum_scatter(
        projected.astype(jnp.bfloat16), "tp", scatter_dimension=1, tiled=True
    )
    full_grad = lax.all_gather(out_grad, "tp", axis=1, tiled=True)
    grad_attn = lax.dot_general(
        full_grad, out_weight, (((1,), (1,)), ((), ())), preferred_element_type=jnp.float32
    ).astype(jnp.bfloat16)
    weight_term = lax.dot_general(
        attention, full_grad, (((0,), (0,)), ((), ())), preferred_element_type=jnp.float32
    )
    grad_weight = lax.psum(weight_term.astype(jnp.bfloat16), "ctx").astype(jnp.float32)
    grad_heads = grad_attn.reshape(local_rows, heads_here, HEAD)
    attn_heads = attention.reshape(local_rows, heads_here, HEAD)
    row_delta = jnp.sum(grad_heads.astype(jnp.float32) * attn_heads.astype(jnp.float32), axis=2).T

    def back_step(query_acc, block_ops):
        key_block, value_block, block_seg = block_ops
        permitted = permitted_mask(query_seg, block_seg)
        prob_rows, score_grads = score_gradients(
            query_heads,
            key_block,
            value_block,
            grad_heads,
            permitted,
            log_total,
            row_delta,
            score_scale,
        )
        new_acc = query_acc + jnp.einsum(
            "hqk,khd->qhd", score_grads, key_block, preferred_element_type=jnp.float32
        )
        key_part = (
            score_scale
            * jnp.einsum(
                "hqk,qhd->khd", score_grads, query_heads, preferred_element_type=jnp.float32
            )
        ).astype(jnp.bfloat16)
        value_part = jnp.einsum(
            "hqk,qhd->khd",
            prob_rows.astype(jnp.bfloat16),
            grad_heads,
            preferred_element_type=jnp.float32,
        ).astype(jnp.bfloat16)
        return (new_acc, (key_part, value_part))

    query_acc, (key_parts, value_parts) = lax.scan(
        back_step, zero_heads, (key_blocks, value_blocks, seg_blocks)
    )
    summed_keys, summed_values = (
        lax.psum_scatter(
            key_parts.reshape(all_rows, local_width).astype(jnp.bfloat16),
            "ctx",
            scatter_dimension=0,
            tiled=True,
        ).astype(jnp.float32),
        lax.psum_scatter(
            value_parts.reshape(all_rows, local_width).astype(jnp.bfloat16),
            "ctx",
            scatter_dimension=0,
            tiled=True,
        ).astype(jnp.float32),
    )
    grad_keys = summed_keys.astype(jnp.bfloat16)
    grad_values = summed_values.astype(jnp.bfloat16)
    grad_queries = (score_scale * query_acc).reshape(local_rows, local_width).astype(jnp.bfloat16)
    return (attention_out, grad_queries, grad_keys, grad_values, grad_weight)


def solution(mesh):
    in_specs = (P("ctx", "tp"), P("ctx", "tp"), P("ctx", "tp"), P("tp", None), P("ctx", "tp"), P())
    out_specs = (P("ctx", "tp"), P("ctx", "tp"), P("ctx", "tp"), P("ctx", "tp"), P("tp", None))
    return jax.shard_map(
        per_device, mesh=mesh, in_specs=in_specs, out_specs=out_specs, check_vma=False
    )
```

profile of v0, /device:TPU:13, one launch (start us, length us, event | category | flops | bytes accessed | tf_op | source)
XLA Modules:
  0.0 868.9 jit_solution(7104052309001396771)
XLA Ops:
  19.0 15.6 %select_select_fusion = s32[4096]{0:T(1024)S(1)} fusion(pred[4096]{0:T(1024)(128)(4,1)S(1)} %get-tuple-element.333, pred[4096]{0:T(1024)(128)(4,1)S(1)} %get-tuple-element.332, pred[4096]{0:T(1024)(128)(4,1)S(1)} %get-tuple-element.331, pred[4096]{0:T(1024)(128)(4,1)S(1)} %get-tuple-element.330, pred[4096]{0:T(1024)(128)(4,1)S(1)} %get-tuple-element.329, ...), kind=kLoop, calls=%fused_computation.113 | loop fusion | flops 102400 | bytes 135268 | tf_op jit(solution)/shard_map/jit(_take)/gather | solution.py:49
  41.3 75.7 %all-gather.6.cloned.1.call-done = bf16[4096,768]{1,0:T(8,128)(2,1)} async-done(((bf16[256,768]{1,0:T(8,128)(2,1)}), bf16[4096,768]{1,0:T(8,128)(2,1)}) %all-gather.6.cloned.1.call-update) | async-done | bytes 6291472 | tf_op jit(solution)/shard_map/all_gather | solution.py:45
  117.0 8.6 copy.24
  125.7 9.7 %copy.46 = bf16[96,8,8,512]{3,2,1,0:T(8,128)(2,1)} copy(bf16[96,8,8,512]{3,1,2,0:T(8,128)(2,1)} %bitcast.245) | data formatting | bytes 12582912
  135.4 9.1 %copy.26 = bf16[8,512,6,128]{3,1,2,0:T(8,128)(2,1)} copy(bf16[8,512,6,128]{1,0,3,2:T(8,128)(2,1)} %bitcast.239) | data formatting | bytes 12582912
  144.5 9.7 %copy.29 = bf16[8,512,6,128]{3,2,1,0:T(8,128)(2,1)} copy(bf16[8,512,6,128]{1,0,3,2:T(8,128)(2,1)} %bitcast.240) | data formatting | bytes 12582912
  154.2 58.1 %all-gather.4.cloned.1.call-done = bf16[4096,768]{1,0:T(8,128)(2,1)} async-done(((bf16[256,768]{1,0:T(8,128)(2,1)}), bf16[4096,768]{1,0:T(8,128)(2,1)}) %all-gather.4.cloned.1.call-update) | async-done | bytes 6291472 | tf_op jit(solution)/shard_map/all_gather | solution.py:46
  212.3 8.9 %copy.23 = bf16[4096,768]{0,1:T(8,128)(2,1)} copy(bf16[4096,768]{1,0:T(8,128)(2,1)} %all-gather.4.cloned.1.call-done) | data formatting | bytes 12582912 | tf_op jit(solution)/shard_map/all_gather | solution.py:46
  221.2 7.0 copy.45
  230.8 5.0 copy.28
  235.8 9.1 %copy.34 = bf16[8,512,6,128]{3,1,2,0:T(8,128)(2,1)} copy(bf16[8,512,6,128]{1,0,3,2:T(8,128)(2,1)} %bitcast.242) | data formatting | bytes 12582912
  244.9 55.6 %while.40 = (s32[]{:T(128)}, f32[6,256]{1,0:T(8,128)S(1)}, f32[6,256]{1,0:T(8,128)}, s32[256]{0:T(256)}, s32[8,512]{1,0:T(8,128)}, /*index=5*/bf16[8,512,6,128]{...) while((s32[]{:T(128)}, f32[6,256]{1,0:T(8,128)S(1)}, f32[6,256]{1,0:T(8,128)}, ...), condition=%wide.region_3.4_spmd.clone, body=%wide.region_0.3_spmd.clone.sunk | while | flops 208020224 | bytes 8528064 | solution.py:69
  301.2 60.0 %while.41 = (s32[]{:T(128)}, f32[256,6,128]{0,2,1:T(8,128)}, bf16[8,512,6,128]{1,3,2,0:T(8,128)(2,1)}, s32[256]{0:T(256)}, s32[8,512]{1,0:T(8,128)}, /*index=5*/...) while((s32[]{:T(128)}, f32[256,6,128]{0,2,1:T(8,128)}, ...), condition=%wide.region_5.6_spmd.clone, body=%wide.region_4.5_spmd.clone.sunk | while | flops 407373056 | bytes 5521527 | solution.py:86
  362.5 5.0 convolution_convert_fusion
  368.7 89.3 %while.42 = (s32[]{:T(128)}, f32[256,6,128]{0,2,1:T(8,128)S(1)}, bf16[8,512,6,128]{3,1,2,0:T(8,128)(2,1)}, bf16[8,512,6,128]{3,1,2,0:T(8,128)(2,1)}, bf16[8,512,...) while((s32[]{:T(128)}, f32[256,6,128]{0,2,1:T(8,128)S(1)}, ...), condition=%wide.region_9.10_spmd.clone, body=%wide.region_8.9_spmd.clone.sunk | while | flops 1018037504 | bytes 21657748 | solution.py:134
  458.1 9.1 %copy.36 = bf16[8,512,6,128]{1,0,3,2:T(8,128)(2,1)} copy(bf16[8,512,6,128]{3,1,2,0:T(8,128)(2,1)} %get-tuple-element.165) | data formatting | bytes 12582912 | tf_op jit(solution)/shard_map/while | solution.py:134
  467.1 9.6 %copy.47 = bf16[96,8,8,512]{3,1,2,0:T(8,128)(2,1)} copy(bf16[96,8,8,512]{3,2,1,0:T(8,128)(2,1)} %bitcast.247) | data formatting | bytes 12582912
  476.8 9.4 %copy.37 = bf16[8,512,6,128]{1,0,3,2:T(8,128)(2,1)} copy(bf16[8,512,6,128]{3,1,2,0:T(8,128)(2,1)} %get-tuple-element.166) | data formatting | bytes 12582912 | tf_op jit(solution)/shard_map/while | solution.py:134
  486.2 9.6 %copy.48 = bf16[96,8,8,512]{3,1,2,0:T(8,128)(2,1)} copy(bf16[96,8,8,512]{3,2,1,0:T(8,128)(2,1)} %bitcast.248) | data formatting | bytes 12582912
  501.9 43.9 %all-reduce.2.cloned.1.call-done = bf16[768,3072]{1,0:T(8,128)(2,1)} async-done(((bf16[768,3072]{1,0:T(8,128)(2,1)}), bf16[768,3072]{1,0:T(8,128)(2,1)}) %all-reduce.2.cloned.1.call-update) | async-done | bytes 4718608 | tf_op jit(solution)/shard_map/psum | solution.py:99
  545.8 7.4 convert_element_type.65
  553.1 142.7 %reduce-scatter.6.cloned.1.call-done = bf16[256,768]{0,1:T(8,128)(2,1)} async-done(((bf16[4096,768]{0,1:T(8,128)(2,1)}), bf16[256,768]{0,1:T(8,128)(2,1)}) %reduce-scatter.6.cloned.1.call-update) | async-done | bytes 393232 | tf_op jit(solution)/shard_map/reduce_scatter | solution.py:138
  697.8 149.8 %reduce-scatter.8.cloned.1.call-done = bf16[256,768]{0,1:T(8,128)(2,1)} async-done(((bf16[4096,768]{0,1:T(8,128)(2,1)}), bf16[256,768]{0,1:T(8,128)(2,1)}) %reduce-scatter.8.cloned.1.call-update) | async-done | bytes 393232 | tf_op jit(solution)/shard_map/reduce_scatter | solution.py:144
  849.5 12.1 %reduce-scatter.4.cloned.1.call-done = bf16[256,1536]{1,0:T(8,128)(2,1)} async-done(((bf16[256,3072]{1,0:T(8,128)(2,1)}), bf16[256,1536]{1,0:T(8,128)(2,1)}) %reduce-scatter.4.cloned.1.call-update) | async-done | bytes 786448 | tf_op jit(solution)/shard_map/reduce_scatter | solution.py:89
  (276 shorter events, 237.9 us)
Async XLA Ops:
  7.2 28.1 %copy-start.9 = (s32[8,4]{0,1:T(4,128)S(1)}, s32[8,4]{0,1:T(4,128)}, u32[]{:S(2)}) copy-start(s32[8,4]{0,1:T(4,128)} %constant.156.clone.1) | copy-start | bytes 388
  7.2 28.1 %copy-start.10 = (s32[8,4]{0,1:T(4,128)S(1)}, s32[8,4]{0,1:T(4,128)}, u32[]{:S(2)}) copy-start(s32[8,4]{0,1:T(4,128)} %constant.157.clone.1) | copy-start | bytes 388
  7.2 4.9 copy-start.5
  7.2 28.8 %all-gather.8.cloned.1.call-start = ((), (), s32[]{:S(2)}) async-start(), calls=%async_computation.6 | async-start | bytes 2359296 | tf_op jit(solution)/shard_map/all_gather | solution.py:92
  7.9 109.1 %all-gather.6.cloned.1.call-start = ((), (), s32[]{:S(2)}) async-start(), calls=%async_computation.4 | async-start | bytes 6684672 | tf_op jit(solution)/shard_map/all_gather | solution.py:45
  8.7 203.6 %all-gather.4.cloned.1.call-start = ((), (), s32[]{:S(2)}) async-start(), calls=%async_computation.3 | async-start | bytes 6684672 | tf_op jit(solution)/shard_map/all_gather | solution.py:46
  9.4 536.3 %all-reduce.2.cloned.1.call-start = ((), (), s32[]{:S(2)}) async-start(), calls=%async_computation.9 | async-start | bytes 9437184 | tf_op jit(solution)/shard_map/psum | solution.py:99
  40.4 85.3 %copy-start.3 = (bf16[256,768]{0,1:T(8,128)(2,1)}, bf16[256,768]{0,1:T(8,128)(2,1)S(1)}, u32[]{:S(2)}) copy-start(bf16[256,768]{0,1:T(8,128)(2,1)S(1)} %copy.31) | copy-start | bytes 1179652
  228.1 2.7 copy-start
  249.6 1.7 copy-start.7
  256.5 1.7 copy-start.7
  261.0 0.7 copy-start.1
  263.5 1.7 copy-start.7
  270.4 1.7 copy-start.7
  277.4 1.7 copy-start.7
  284.3 1.7 copy-start.7
  291.3 1.7 copy-start.7
  298.2 1.7 copy-start.7
  301.2 60.0 %copy-start.4 = (bf16[256,768]{0,1:T(8,128)(2,1)S(1)}, bf16[256,768]{0,1:T(8,128)(2,1)}, u32[]{:S(2)}) copy-start(bf16[256,768]{0,1:T(8,128)(2,1)} %copy-done.3) | copy-start | bytes 1179652
  367.5 1.1 copy-start.2
  367.5 1.2 copy-start.6
  367.5 328.4 %reduce-scatter.6.cloned.1.call-start = ((), (), s32[]{:S(2)}) async-start(), calls=%async_computation.7 | async-start | bytes 6684672 | tf_op jit(solution)/shard_map/reduce_scatter | solution.py:138
  476.8 370.8 %reduce-scatter.8.cloned.1.call-start = ((), (), s32[]{:S(2)}) async-start(), calls=%async_computation.8 | async-start | bytes 6684672 | tf_op jit(solution)/shard_map/reduce_scatter | solution.py:144
  495.8 365.8 %reduce-scatter.4.cloned.1.call-start = ((), (), s32[]{:S(2)}) async-start(), calls=%async_computation.5 | async-start | bytes 2359296 | tf_op jit(solution)/shard_map/reduce_scatter | solution.py:89
  (15 other events, 9.4 us)
Sparse Core Ops, SparseCore 0:
  9.6 11.6 all-gather.7
  24.0 92.9 all-gather.5
  119.8 92.4 all-gather.3
  367.6 178.0 all-reduce.1
  551.7 144.1 reduce-scatter.5
  701.8 145.7 reduce-scatter.7
  850.5 11.0 reduce-scatter.3
where the time goes:
time: 884 us; the launch traced here: 869 us
  waiting for transfers between devices  484 us (55%)
  local copies, waits for them, and re-layouts  140 us (16%)
  matrix products  131 us (15%)
  other arithmetic  97.6 us (11%)
  between operations  14.8 us (2%)
    reduce_scatter x1, waiting for transfers between devices, per_device(): lax.psum_scatter(value_parts.reshape(all_rows, local_width).astype(jnp.bf...  150 us
    reduce_scatter x1, waiting for transfers between devices, per_device(): lax.psum_scatter(key_parts.reshape(all_rows, local_width).astype(jnp.bflo...  143 us
    unnamed x31, local copies, waits for them, and re-layouts  80.9 us
    all_gather x1, waiting for transfers between devices, per_device(): lax.all_gather(key_vectors, 'ctx', axis=0, tiled=True)  75.7 us
    all_gather x1, waiting for transfers between devices, per_device(): lax.all_gather(value_vectors, 'ctx', axis=0, tiled=True)  58.1 us
    psum x1, waiting for transfers between devices, per_device(): lax.psum(weight_term.astype(jnp.bfloat16), 'ctx').astype(jnp.float32)  43.9 us
    or x48, other arithmetic, permitted_mask(): (query_col == 0) | (query_col == target_id) | (key_row == 0)  34.4 us
    dot_general x8, matrix products, value_step(): jnp.einsum('hqk,khd->qhd', weights, value_block, preferred_element_type=j...  31.2 us
  transfers between devices with their start and end apart: 7, of which 6 were waited for; matrix products, arithmetic and copies ran while one was open for 24% of the time, Pallas kernels for 0%

commit v1 on v0

v1 whole, which is shorter than its diff:
```python
import functools
import math

import jax
import jax.numpy as jnp
from jax import lax
from jax.experimental import pallas as pl
from jax.experimental.pallas import tpu as pltpu
from jax.sharding import PartitionSpec as P

HEAD = 128
BLK = 128
TXT_BLK = 4
RUNS = 5
TARGET = 5
LOG2E = math.log2(math.e)
NEG_BIG = -1e30

NT = (((1,), (1,)), ((), ()))
TN = (((0,), (0,)), ((), ()))
F32 = jnp.float32
BF16 = jnp.bfloat16


def dot(a, b, dims=(((1,), (0,)), ((), ()))):
    return lax.dot_general(a, b, dims, preferred_element_type=F32)


def gather_tiles(k_ref, kidx_ref, row, dst, tile, count):
    for j in range(count):
        dst[pl.ds(j * tile, tile), :] = k_ref[kidx_ref[row, j]]


def forward_kernel(tile, count, full_ref, kcnt_ref, kidx_ref, q_ref, k_ref, v_ref, out_ref, lse_ref, k_few, v_few):
    row = pl.program_id(0)
    q = q_ref[0, 0]

    def finish(s, v):
        top = jnp.max(s, axis=1, keepdims=True)
        p = jnp.exp2(s - top)
        mass = jnp.sum(p, axis=1, keepdims=True)
        out = dot(p.astype(BF16), v)
        out_ref[0, 0] = (out / mass).astype(BF16)
        lse_ref[...] = jnp.broadcast_to(top + jnp.log2(mass), lse_ref.shape)

    scale = HEAD ** -0.5 * LOG2E

    @pl.when(full_ref[row] == 1)
    def _():
        keys = k_ref[...].reshape(-1, HEAD)
        finish(dot(q, keys, NT) * scale, v_ref[...].reshape(-1, HEAD))

    @pl.when(full_ref[row] == 0)
    def _():
        gather_tiles(k_ref, kidx_ref, row, k_few, tile, count)
        gather_tiles(v_ref, kidx_ref, row, v_few, tile, count)
        s = dot(q, k_few[...], NT) * scale
        column = lax.broadcasted_iota(jnp.int32, s.shape, 1)
        s = jnp.where(column < kcnt_ref[row] * tile, s, NEG_BIG)
        finish(s, v_few[...])


def backward_kernel(tile, count, full_ref, kcnt_ref, kidx_ref, q_ref, g_ref, o_ref, lse_ref, k_ref, v_ref,
                    dq_ref, dkv_ref, k_few, v_few, dk_acc, dv_acc):
    row = pl.program_id(0)
    last = pl.num_programs(0) - 1

    @pl.when(row == 0)
    def _():
        dk_acc[...] = jnp.zeros_like(dk_acc)
        dv_acc[...] = jnp.zeros_like(dv_acc)

    q = q_ref[0, 0]
    g = g_ref[0, 0]
    delta = jnp.sum(g.astype(F32) * o_ref[0, 0].astype(F32), axis=1, keepdims=True)
    lse = lse_ref[:, :1]
    unit = HEAD ** -0.5
    scale = unit * LOG2E

    def gradients(keys, values, mask):
        s = dot(q, keys, NT)
        p = jnp.exp2(s * scale - lse)
        if mask is not None:
            p = jnp.where(mask(p.shape), p, 0.0)
        ds = (p * (dot(g, values, NT) - delta)).astype(BF16)
        dq_ref[0, 0] = (dot(ds, keys) * unit).astype(BF16)
        return dot(ds, q, TN) * unit, dot(p.astype(BF16), g, TN)

    @pl.when(full_ref[row] == 1)
    def _():
        dk, dv = gradients(k_ref[...].reshape(-1, HEAD), v_ref[...].reshape(-1, HEAD), None)
        dk_acc[...] += dk.reshape(dk_acc.shape)
        dv_acc[...] += dv.reshape(dv_acc.shape)

    @pl.when(full_ref[row] == 0)
    def _():
        gather_tiles(k_ref, kidx_ref, row, k_few, tile, count)
        gather_tiles(v_ref, kidx_ref, row, v_few, tile, count)

        def mask(shape):
            return lax.broadcasted_iota(jnp.int32, shape, 1) < kcnt_ref[row] * tile

        dk, dv = gradients(k_few[...], v_few[...], mask)
        for j in range(count):
            at = kidx_ref[row, j]
            dk_acc[at] += dk[j * tile:(j + 1) * tile]
            dv_acc[at] += dv[j * tile:(j + 1) * tile]

    @pl.when(row == last)
    def _():
        parts, _, chunks, rows, _ = dkv_ref.shape
        shape = (parts, chunks, rows, HEAD)
        dkv_ref[:, 0] = dk_acc[...].reshape(shape).astype(BF16)
        dkv_ref[:, 1] = dv_acc[...].reshape(shape).astype(BF16)


def whole_block(shape):
    return pl.BlockSpec(shape, lambda *_: (0,) * len(shape))


def tile_block(which, per_chunk, tile):
    return pl.BlockSpec(
        (1, 1, tile, HEAD), lambda r, *_: (r // per_chunk, which, r % per_chunk, 0)
    )


def shifts(t, s):
    return [(c, (c + s) % t) for c in range(t)]


def per_device(n, t, queries, key_vectors, value_vectors, out_weight, out_grad, block_segment):
    rows, width = queries.shape
    heads_here = width // HEAD
    heads = heads_here * t
    sub = rows // t
    tile = min(sub, BLK)
    per_chunk = sub // tile
    core = lax.axis_index("tp")
    chunks = [h * n // heads for h in range(heads)]

    def tp_order(stack):
        return [lax.dynamic_index_in_dim(stack, (core - p) % t, 0, False) for p in range(t)]

    def tp_split(pack):
        got = [lax.dynamic_index_in_dim(pack, core, 0, False)]
        for s in range(1, t):
            block = lax.dynamic_index_in_dim(pack, (core + s) % t, 0, False)
            got.append(lax.ppermute(block, "tp", shifts(t, s)))
        return tp_order(jnp.stack(got))

    def to_heads(arrays):
        pack = jnp.stack(
            [a.reshape(t, sub, heads_here, HEAD).transpose(0, 2, 1, 3) for a in arrays], axis=2
        )
        every = jnp.concatenate(tp_split(pack), axis=0)
        empty = jnp.zeros_like(every[0])
        sent = [empty] * n
        for h, chunk in enumerate(chunks):
            sent[chunk] = every[h]
        return lax.all_to_all(jnp.stack(sent), "ctx", 0, 0, tiled=True)

    def to_tokens(pack):
        got = lax.all_to_all(pack, "ctx", 0, 0, tiled=True)
        every = jnp.stack([got[chunk] for chunk in chunks])
        every = every.reshape((t, heads_here) + every.shape[1:])
        mine = jnp.stack(tp_split(every))
        return [
            mine[:, :, a].transpose(0, 2, 1, 3).reshape(rows, width) for a in range(pack.shape[1])
        ]

    chunk_row = jnp.arange(n)[:, None] * rows + jnp.arange(per_chunk)[None, :] * tile

    def tile_segments(part):
        return jnp.take(block_segment, ((chunk_row + part * sub) // BLK).reshape(-1))

    seg_parts = [tile_segments((core - s) % t) for s in range(t)]
    seg_q = seg_parts[0]
    seg_k = jnp.concatenate(seg_parts)
    full = (seg_q == 0) | (seg_q == TARGET)
    permitted = (seg_k[None] == 0) | (seg_k[None] == seg_q[:, None])
    total_blocks = block_segment.shape[0]
    count = (TXT_BLK + -(-(total_blocks - TXT_BLK) // RUNS)) * (BLK // tile)
    kcnt = jnp.sum(permitted.astype(jnp.int32), axis=1)
    tiles_k = seg_k.shape[0]
    ids = jnp.arange(tiles_k)
    place = jnp.sum((permitted[:, None, :] & (ids[None, None, :] < ids[None, :, None])).astype(jnp.int32), axis=2)
    hit = permitted[:, None, :] & (place[:, None, :] == jnp.arange(count)[None, :, None])
    kidx = jnp.sum(jnp.where(hit, ids[None, None, :], 0), axis=2).astype(jnp.int32)
    full = full.astype(jnp.int32)

    half = out_grad.shape[1]
    grads = [out_grad] + [lax.ppermute(out_grad, "tp", shifts(t, s)) for s in range(1, t)]
    full_grad = jnp.concatenate(tp_order(jnp.stack(grads)), axis=1)

    kv = to_heads([key_vectors, value_vectors])
    grad_attn = dot(full_grad, out_weight, NT).astype(BF16)
    qg = to_heads([queries, grad_attn])

    kv_parts = jnp.stack([kv] + [lax.ppermute(kv, "tp", shifts(t, s)) for s in range(1, t)])
    keys = kv_parts[:, :, 0].reshape(tiles_k, tile, HEAD)
    values = kv_parts[:, :, 1].reshape(tiles_k, tile, HEAD)

    tiles_q = n * per_chunk
    few = [pltpu.VMEM((count * tile, HEAD), BF16)] * 2
    params = pltpu.CompilerParams(vmem_limit_bytes=48 * 2**20)
    q_block = tile_block(0, per_chunk, tile)
    g_block = tile_block(1, per_chunk, tile)
    key_block = whole_block((tiles_k, tile, HEAD))
    lse_block = pl.BlockSpec((tile, HEAD), lambda r, *_: (r, 0))
    attn, lse = pl.pallas_call(
        functools.partial(forward_kernel, tile, count),
        grid_spec=pltpu.PrefetchScalarGridSpec(
            num_scalar_prefetch=3,
            grid=(tiles_q,),
            in_specs=[q_block, key_block, key_block],
            out_specs=[q_block, lse_block],
            scratch_shapes=few,
        ),
        out_shape=[
            jax.ShapeDtypeStruct((n, 1, sub, HEAD), BF16),
            jax.ShapeDtypeStruct((tiles_q * tile, HEAD), F32),
        ],
        compiler_params=params,
        cost_estimate=pl.CostEstimate(
            flops=tiles_q * tile * tiles_k * tile * HEAD * 2, bytes_accessed=5 * 2**20, transcendentals=2**22
        ),
        name="forward",
    )(full, kcnt, kidx, qg, keys, values)

    (attention,) = to_tokens(attn)
    projected = dot(attention, out_weight)
    own = lax.dynamic_slice_in_dim(projected, core * half, half, 1)
    for s in range(1, t):
        there = lax.dynamic_slice_in_dim(projected, (core + s) % t * half, half, 1)
        own = own + lax.ppermute(there.astype(BF16), "tp", shifts(t, s)).astype(F32)
    attention_out = own.astype(BF16)
    weight_term = dot(attention, full_grad, TN)
    grad_weight = lax.psum(weight_term.astype(BF16), "ctx").astype(F32)

    dq, dkv = pl.pallas_call(
        functools.partial(backward_kernel, tile, count),
        grid_spec=pltpu.PrefetchScalarGridSpec(
            num_scalar_prefetch=3,
            grid=(tiles_q,),
            in_specs=[q_block, g_block, q_block, lse_block, key_block, key_block],
            out_specs=[q_block, whole_block((t, 2, n, sub, HEAD))],
            scratch_shapes=few + [pltpu.VMEM((tiles_k, tile, HEAD), F32)] * 2,
        ),
        out_shape=[
            jax.ShapeDtypeStruct((n, 1, sub, HEAD), BF16),
            jax.ShapeDtypeStruct((t, 2, n, sub, HEAD), BF16),
        ],
        compiler_params=params,
        cost_estimate=pl.CostEstimate(
            flops=tiles_q * tile * tiles_k * tile * HEAD * 5, bytes_accessed=8 * 2**20, transcendentals=2**22
        ),
        name="backward",
    )(full, kcnt, kidx, qg, qg, attn, lse, keys, values)

    sums = dkv[0].astype(F32)
    for s in range(1, t):
        back = [(c, (c - s) % t) for c in range(t)]
        sums = sums + lax.ppermute(dkv[s], "tp", back).astype(F32)
    sums = sums.astype(BF16).transpose(1, 0, 2, 3)
    grad_queries, grad_keys, grad_values = to_tokens(jnp.concatenate([dq, sums], axis=1))
    return attention_out, grad_queries, grad_keys, grad_values, grad_weight


def solution(mesh):
    n, t = mesh.shape["ctx"], mesh.shape["tp"]
    in_specs = (P("ctx", "tp"), P("ctx", "tp"), P("ctx", "tp"), P("tp", None), P("ctx", "tp"), P())
    out_specs = (P("ctx", "tp"), P("ctx", "tp"), P("ctx", "tp"), P("ctx", "tp"), P("tp", None))
    return jax.shard_map(
        functools.partial(per_device, n, t), mesh=mesh, in_specs=in_specs, out_specs=out_specs, check_vma=False
    )
```

time: 884 us -> 377 us (0.43); the launches traced: 869 us -> 373 us
  waiting for transfers between devices: 484 us -> 221 us
  matrix products: 131 us -> 11.1 us
  local copies, waits for them, and re-layouts: 140 us -> 46 us
  other arithmetic: 97.6 us -> 18 us
  Pallas kernels: 0 us -> 33.4 us
  starting transfers between devices: 0.28 us -> 29.6 us
    reduce_scatter x3 -> x0, waiting for transfers between devices: 305 us -> none  [the longest x1 150 us: per_device(): lax.psum_scatter(value_parts.reshape(all_rows, local_width).astype(jnp.bf...]
    all_gather x3 -> x0, waiting for transfers between devices: 134 us -> none  [the longest x1 75.7 us: per_device(): lax.all_gather(key_vectors, 'ctx', axis=0, tiled=True)]
    dot_general x59 -> x3, matrix products: 131 us -> 11.1 us  [dot(): return lax.dot_general(a, b, dims, preferred_element_type=F32)]
    all_to_all x0 -> x4, waiting for transfers between devices: none -> 96.3 us  [the longest x2 65.6 us: to_tokens(): got = lax.all_to_all(pack, 'ctx', 0, 0, tiled=True)]
    psum x1, waiting for transfers between devices: 43.9 us -> 120 us  [per_device(): grad_weight = lax.psum(weight_term.astype(BF16), 'ctx').astype(F32)]
    unnamed x31 -> x72, local copies, waits for them, and re-layouts: 80.9 us -> 30.7 us
    or x48 -> x0, other arithmetic: 34.4 us -> none  [permitted_mask(): (query_col == 0) | (query_col == target_id) | (key_row == 0)]
    pallas_call x0 -> x2, Pallas kernels: none -> 33.4 us  [the longest x1 19.7 us: per_device(): pl.pallas_call(functools.partial(backward_kernel, tile, count), grid_spec...]
  transfers between devices with their start and end apart: 7 -> 13, of which waited for: 6 -> 7; matrix products, arithmetic and copies ran while one was open for 24% -> 13% of each run, Pallas kernels for 0% -> 5%
where the time goes in v1:
time: 377 us; the launch traced here: 373 us
  waiting for transfers between devices  221 us (59%)
  local copies, waits for them, and re-layouts  46 us (12%)
  Pallas kernels  33.4 us (9%)
  starting transfers between devices  29.6 us (8%)
  other arithmetic  18 us (5%)
  between operations  14.5 us (4%)
  matrix products  11.1 us (3%)
    psum x1, waiting for transfers between devices, per_device(): grad_weight = lax.psum(weight_term.astype(BF16), 'ctx').astype(F32)  120 us
    all_to_all x2, waiting for transfers between devices, to_tokens(): got = lax.all_to_all(pack, 'ctx', 0, 0, tiled=True)  65.6 us
    unnamed x72, local copies, waits for them, and re-layouts  30.7 us
    all_to_all x2, waiting for transfers between devices, to_heads(): return lax.all_to_all(jnp.stack(sent), 'ctx', 0, 0, tiled=True)  30.7 us
    pallas_call x1, Pallas kernels, per_device(): pl.pallas_call(functools.partial(backward_kernel, tile, count), grid_spec...  19.7 us
    pallas_call x1, Pallas kernels, per_device(): pl.pallas_call(functools.partial(forward_kernel, tile, count), grid_spec=...  13.7 us
    all_to_all x2, starting transfers between devices, to_heads(): return lax.all_to_all(jnp.stack(sent), 'ctx', 0, 0, tiled=True)  11.2 us
    dot_general x3, matrix products, dot(): return lax.dot_general(a, b, dims, preferred_element_type=F32)  11.1 us
  transfers between devices with their start and end apart: 13, of which 7 were waited for; matrix products, arithmetic and copies ran while one was open for 13% of the time, Pallas kernels for 5%

profile of v1, /device:TPU:13, one launch (start us, length us, event | category | flops | bytes accessed | tf_op | source)
XLA Modules:
  0.0 373.4 jit_solution(4188973483121225372)
XLA Ops:
  7.9 1.4 reshape.216
  10.9 1.4 reshape.213
  14.2 3.8 %convolution_convert_fusion.1 = bf16[256,768]{1,0:T(8,128)(2,1)S(1)} fusion(bf16[768,3072]{1,0:T(8,128)(2,1)} %param.11, bf16[256,1536]{1,0:T(8,128)(2,1)S(1)} %get-tuple-element.47, bf16[256,1536]{1,0:T(8,128)(2,1)S(1)} %get-tuple-element.46), kind=kOutput, calls=%fused_computation.23 | convolution fusion | flops 1211301888 | bytes 6684672 | tf_op jit(solution)/shard_map/dot_general | solution.py:26
  20.4 1.6 fusion.9
  32.0 6.6 %all-to-all-start.1 = ((bf16[16,2,128,128]{3,2,1,0:T(8,128)(2,1)}), bf16[16,2,128,128]{3,2,1,0:T(8,128)(2,1)S(1)}, u32[]{:S(2)}, u32[]{:S(2)}) async-start(bf16[16,2,128,128]{3,2,1,0:T(8,128)(2,1)} %constant_dynamic-update-slice_fusion.4), calls=%async_computation.1 | async-start | bytes 2097152 | tf_op jit(solution)/shard_map/all_to_all | solution.py:160
  48.8 14.6 %all-to-all-done.1 = bf16[16,2,128,128]{3,2,1,0:T(8,128)(2,1)S(1)} async-done(((bf16[16,2,128,128]{3,2,1,0:T(8,128)(2,1)}), bf16[16,2,128,128]{3,2,1,0:T(8,128)(2,1)S(1)}, u32[]{:S(2)}, u32[]{:S(2)}) %all-to-all-start.1) | async-done | bytes 1048608 | tf_op jit(solution)/shard_map/all_to_all | solution.py:160
  63.4 4.6 %all-to-all-start = ((bf16[16,2,128,128]{3,2,1,0:T(8,128)(2,1)}), bf16[16,2,128,128]{3,2,1,0:T(8,128)(2,1)S(1)}, u32[]{:S(2)}, u32[]{:S(2)}) async-start(bf16[16,2,128,128]{3,2,1,0:T(8,128)(2,1)} %constant_dynamic-update-slice_fusion), calls=%async_computation | async-start | bytes 2097152 | tf_op jit(solution)/shard_map/all_to_all | solution.py:160
  69.4 2.4 collective-permute-start.3
  75.1 1.7 pad_maximum_fusion.3
  76.8 16.0 %all-to-all-done.q_ref.g_ref = bf16[16,2,128,128]{3,2,1,0:T(8,128)(2,1)S(1)} async-done(((bf16[16,2,128,128]{3,2,1,0:T(8,128)(2,1)}), bf16[16,2,128,128]{3,2,1,0:T(8,128)(2,1)S(1)}, u32[]{:S(2)}, u32[]{:S(2)}) %all-to-all-start) | async-done | bytes 1048608 | tf_op jit(solution)/shard_map/all_to_all | solution.py:160
  92.8 13.7 %forward.1 = (bf16[16,1,128,128]{3,2,1,0:T(8,128)(2,1)S(1)}, f32[2048,128]{1,0:T(8,128)S(1)}) custom-call(s32[16]{0:T(128)S(1)} %get-tuple-element.38.full_ref, s32[16]{0:T(128)S(1)} %get-tuple-element.34.kcnt_ref, s32[16,10]{1,0:T(8,128)S(1)} %copy.76.kidx_ref, bf16[16,2,128,128]{3,2,1,0:T(8,128)(2,1)S(1)} %all-to-all-done.q_ref.g_ref, ...), custom_call_target="tpu_custom_call" | custom-call | flops 2147483648 | bytes 5242880 | tf_op jit(solution)/shard_map/forward/pallas_call | solution.py:210
  108.2 4.1 %all-to-all-start.2 = ((bf16[16,1,128,128]{3,2,1,0:T(8,128)(2,1)}), bf16[16,1,128,128]{3,2,1,0:T(8,128)(2,1)}, u32[]{:S(2)}, u32[]{:S(2)}) async-start(bf16[16,1,128,128]{3,2,1,0:T(8,128)(2,1)} %copy-done.2), calls=%async_computation.2 | async-start | bytes 1048576 | tf_op jit(solution)/shard_map/all_to_all | solution.py:163
  114.9 19.7 %backward.1 = (bf16[16,1,128,128]{3,2,1,0:T(8,128)(2,1)S(1)}, bf16[2,2,16,128,128]{4,3,2,1,0:T(8,128)(2,1)}) custom-call(s32[16]{0:T(128)S(1)} %get-tuple-element.38.full_ref, s32[16]{0:T(128)S(1)} %get-tuple-element.34.kcnt_ref, s32[16,10]{1,0:T(8,128)S(1)} %copy.76.kidx_ref, bf16[16,2,128,128]{3,2,1,0:T(8,128)(2,1)S(1)} %all-to-all-done.q_ref.g_ref, ...), custom_call_target="tpu_custom_call" | custom-call | flops 5368709120 | bytes 8388608 | tf_op jit(solution)/shard_map/backward/pallas_call | solution.py:240
  135.4 2.4 slice_bitcast_fusion
  137.8 2.6 collective-permute-start.6
  143.7 3.6 convolution_convert_fusion
  147.3 1.5 copy-done.14
  150.7 6.4 %all-to-all-start.3 = ((bf16[16,3,128,128]{3,2,1,0:T(8,128)(2,1)}), bf16[16,3,128,128]{3,2,1,0:T(8,128)(2,1)}, u32[]{:S(2)}, u32[]{:S(2)}) async-start(bf16[16,3,128,128]{3,2,1,0:T(8,128)(2,1)} %copy.81), calls=%async_computation.3 | async-start | bytes 3145728 | tf_op jit(solution)/shard_map/all_to_all | solution.py:163
  157.0 3.8 %fusion.24 = f32[256,3072]{1,0:T(8,128)S(1)} fusion(bf16[768,3072]{1,0:T(8,128)(2,1)} %param.11, bf16[96,8,2,128]{3,2,1,0:T(2,128)(2,1)S(1)} %bitcast.198), kind=kOutput, calls=%fused_computation.74 | convolution fusion | flops 1207959552 | bytes 8257536 | tf_op jit(solution)/shard_map/dot_general | solution.py:26
  162.6 65.6 %all-to-all-done.3 = bf16[16,3,128,128]{3,2,1,0:T(8,128)(2,1)} async-done(((bf16[16,3,128,128]{3,2,1,0:T(8,128)(2,1)}), bf16[16,3,128,128]{3,2,1,0:T(8,128)(2,1)}, u32[]{:S(2)}, u32[]{:S(2)}) %all-to-all-start.3) | async-done | bytes 1572896 | tf_op jit(solution)/shard_map/all_to_all | solution.py:163
  231.4 2.3 add_convert_fusion
  233.7 1.7 fusion.7
  238.7 120.4 %all-reduce.2.cloned.1.call-done = bf16[768,3072]{1,0:T(8,128)(2,1)} async-done(((bf16[768,3072]{1,0:T(8,128)(2,1)}), bf16[768,3072]{1,0:T(8,128)(2,1)}) %all-reduce.2.cloned.1.call-update) | async-done | bytes 4718608 | tf_op jit(solution)/shard_map/psum | solution.py:238
  359.1 7.4 %convert_element_type.51 = f32[768,3072]{1,0:T(8,128)} convert(bf16[768,3072]{1,0:T(8,128)(2,1)} %all-reduce.2.cloned.1.call-done) | non-fusion elementwise | flops 2359296 | bytes 14155776 | tf_op jit(solution)/shard_map/convert_element_type | solution.py:238
  (127 shorter events, 49.6 us)
Async XLA Ops:
  7.2 60.8 %copy-start = (s32[32]{0:T(128)S(1)}, s32[32]{0:T(128)}, u32[]{:S(2)}) copy-start(s32[32]{0:T(128)} %param.13) | copy-start | bytes 388
  7.2 2.3 copy-start.17
  7.2 5.2 %collective-permute-start = (bf16[256,1536]{1,0:T(8,128)(2,1)}, bf16[256,1536]{1,0:T(8,128)(2,1)S(1)}, u32[]{:S(2)}, u32[]{:S(2)}) collective-permute-start(bf16[256,1536]{1,0:T(8,128)(2,1)} %param.12), channel_id=1, source_target_pairs={{0,1},{1,0},{2,3},{3,2},{4,5},{5,4},{6,7},{7,6},{8,9},{9,8},{10,11... | collective-permute-start | bytes 2359304 | tf_op jit(solution)/shard_map/ppermute | solution.py:192
  10.0 2.4 copy-start.16
  10.8 8.2 %collective-permute-start.2 = (bf16[6,2,128,128]{3,2,1,0:T(8,128)(2,1)}, bf16[6,2,128,128]{3,2,1,0:T(8,128)(2,1)}, u32[]{:S(2)}, u32[]{:S(2)}) collective-permute-start(bf16[6,2,128,128]{3,2,1,0:T(8,128)(2,1)} %get-tuple-element.57), channel_id=1, source_target_pairs={{0,1},{1,0},{2,3},{3,2},{4,5},{5,4},{6,7},{7,6},{8,9},{9,8},{10,11... | collective-permute-start | bytes 1179656 | tf_op jit(solution)/shard_map/ppermute | solution.py:148
  18.5 1.9 collective-permute-start.1
  32.0 31.4 %all-to-all-start.1 = ((bf16[16,2,128,128]{3,2,1,0:T(8,128)(2,1)}), bf16[16,2,128,128]{3,2,1,0:T(8,128)(2,1)S(1)}, u32[]{:S(2)}, u32[]{:S(2)}) async-start(bf16[16,2,128,128]{3,2,1,0:T(8,128)(2,1)} %constant_dynamic-update-slice_fusion.4), calls=%async_computation.1 | async-start | bytes 2097152 | tf_op jit(solution)/shard_map/all_to_all | solution.py:160
  63.4 5.9 %copy-start.8 = (bf16[16,2,128,128]{3,2,1,0:T(8,128)(2,1)}, bf16[16,2,128,128]{3,2,1,0:T(8,128)(2,1)S(1)}, u32[]{:S(2)}) copy-start(bf16[16,2,128,128]{3,2,1,0:T(8,128)(2,1)S(1)} %all-to-all-done.1) | copy-start | bytes 3145732
  63.4 29.4 %all-to-all-start = ((bf16[16,2,128,128]{3,2,1,0:T(8,128)(2,1)}), bf16[16,2,128,128]{3,2,1,0:T(8,128)(2,1)S(1)}, u32[]{:S(2)}, u32[]{:S(2)}) async-start(bf16[16,2,128,128]{3,2,1,0:T(8,128)(2,1)} %constant_dynamic-update-slice_fusion), calls=%async_computation | async-start | bytes 2097152 | tf_op jit(solution)/shard_map/all_to_all | solution.py:160
  69.4 4.7 %collective-permute-start.3 = (bf16[16,2,128,128]{3,2,1,0:T(8,128)(2,1)S(1)}, bf16[16,2,128,128]{3,2,1,0:T(8,128)(2,1)S(1)}, u32[]{:S(2)}, u32[]{:S(2)}) collective-permute-start(bf16[16,2,128,128]{3,2,1,0:T(8,128)(2,1)S(1)} %all-to-all-done.1), channel_id=1, source_target_pairs={{0,1},{1,0},{2,3},{3,2},{4,5},{5,4},{6,7},{7,6},{8,9},{9,8},{10,11... | collective-permute-start | bytes 3145736 | tf_op jit(solution)/shard_map/ppermute | solution.py:199
  108.2 32.1 %all-to-all-start.2 = ((bf16[16,1,128,128]{3,2,1,0:T(8,128)(2,1)}), bf16[16,1,128,128]{3,2,1,0:T(8,128)(2,1)}, u32[]{:S(2)}, u32[]{:S(2)}) async-start(bf16[16,1,128,128]{3,2,1,0:T(8,128)(2,1)} %copy-done.2), calls=%async_computation.2 | async-start | bytes 1048576 | tf_op jit(solution)/shard_map/all_to_all | solution.py:163
  112.4 246.8 %all-reduce.2.cloned.1.call-start = ((), (), s32[]{:S(2)}) async-start(), calls=%async_computation.4 | async-start | bytes 9437184 | tf_op jit(solution)/shard_map/psum | solution.py:238
  113.7 1.2 copy-start.7
  137.8 9.5 %collective-permute-start.6 = (bf16[2,16,128,128]{3,2,1,0:T(8,128)(2,1)}, bf16[2,16,128,128]{3,2,1,0:T(8,128)(2,1)S(1)}, u32[]{:S(2)}, u32[]{:S(2)}) collective-permute-start(bf16[2,16,128,128]{3,2,1,0:T(8,128)(2,1)} %slice_bitcast_fusion), channel_id=1, source_target_pairs={{0,1},{1,0},{2,3},{3,2},{4,5},{5,4},{6,7},{7,6},{8,9},{9,8},{10,11... | collective-permute-start | bytes 3145736 | tf_op jit(solution)/shard_map/ppermute | solution.py:263
  141.5 2.2 copy-start.10
  141.5 2.2 copy-start.12
  141.5 1.5 collective-permute-start.4
  147.3 1.6 copy-start.14
  147.3 1.9 copy-start.5
  150.7 77.6 %all-to-all-start.3 = ((bf16[16,3,128,128]{3,2,1,0:T(8,128)(2,1)}), bf16[16,3,128,128]{3,2,1,0:T(8,128)(2,1)}, u32[]{:S(2)}, u32[]{:S(2)}) async-start(bf16[16,3,128,128]{3,2,1,0:T(8,128)(2,1)} %copy.81), calls=%async_computation.3 | async-start | bytes 3145728 | tf_op jit(solution)/shard_map/all_to_all | solution.py:163
  161.8 69.6 %collective-permute-start.5 = (bf16[256,1536]{1,0:T(8,128)(2,1)}, bf16[256,1536]{1,0:T(8,128)(2,1)}, u32[]{:S(2)}, u32[]{:S(2)}) collective-permute-start(bf16[256,1536]{1,0:T(8,128)(2,1)} %dynamic-slice_convert_fusion), channel_id=1, source_target_pairs={{0,1},{1,0},{2,3},{3,2},{4,5},{5,4},{6,7},{7,6},{8,9},{9,8},{10,11... | collective-permute-start | bytes 2359304 | tf_op jit(solution)/shard_map/ppermute | solution.py:235
  230.9 2.8 collective-permute-start.7
  231.4 2.3 copy-start.13
  359.1 7.4 %copy-start.1 = (s32[32]{0:T(128)S(1)}, s32[32]{0:T(128)}, u32[]{:S(2)}) copy-start(s32[32]{0:T(128)} %param.13) | copy-start | bytes 388
  (7 other events, 6.6 us)
Sparse Core Ops, SparseCore 0:
  147.4 211.6 all-reduce.1

commit v2 on v1

--- a/solution.py
+++ b/solution.py
@@ -13,6 +13,7 @@
 TXT_BLK = 4
 RUNS = 5
 TARGET = 5
+PLANES = 4
 LOG2E = math.log2(math.e)
 NEG_BIG = -1e30
 
@@ -31,9 +32,22 @@
         dst[pl.ds(j * tile, tile), :] = k_ref[kidx_ref[row, j]]
 
 
-def forward_kernel(tile, count, full_ref, kcnt_ref, kidx_ref, q_ref, k_ref, v_ref, out_ref, lse_ref, k_few, v_few):
+def join_parts(parts, k_all, v_all):
+    shape = (k_all.shape[0] // (len(parts) // 2),) + k_all.shape[1:]
+    for s in range(len(parts) // 2):
+        at = pl.ds(s * shape[0], shape[0])
+        k_all[at] = parts[2 * s][...].reshape(shape)
+        v_all[at] = parts[2 * s + 1][...].reshape(shape)
+
+
+def forward_kernel(t, tile, count, full_ref, kcnt_ref, kidx_ref, q_ref, *refs):
+    parts, (out_ref, lse_ref, k_few, v_few, k_ref, v_ref) = refs[:2 * t], refs[2 * t:]
     row = pl.program_id(0)
     q = q_ref[0, 0]
+
+    @pl.when(row == 0)
+    def _():
+        join_parts(parts, k_ref, v_ref)
 
     def finish(s, v):
         top = jnp.max(s, axis=1, keepdims=True)
@@ -60,13 +74,14 @@
         finish(s, v_few[...])
 
 
-def backward_kernel(tile, count, full_ref, kcnt_ref, kidx_ref, q_ref, g_ref, o_ref, lse_ref, k_ref, v_ref,
-                    dq_ref, dkv_ref, k_few, v_few, dk_acc, dv_acc):
+def backward_kernel(t, tile, count, full_ref, kcnt_ref, kidx_ref, q_ref, g_ref, o_ref, lse_ref, *refs):
+    parts, (dq_ref, dkv_ref, k_few, v_few, k_ref, v_ref, dk_acc, dv_acc) = refs[:2 * t], refs[2 * t:]
     row = pl.program_id(0)
     last = pl.num_programs(0) - 1
 
     @pl.when(row == 0)
     def _():
+        join_parts(parts, k_ref, v_ref)
         dk_acc[...] = jnp.zeros_like(dk_acc)
         dv_acc[...] = jnp.zeros_like(dv_acc)
 
@@ -118,6 +133,10 @@
     return pl.BlockSpec(shape, lambda *_: (0,) * len(shape))
 
 
+def one_array(which, n, sub):
+    return pl.BlockSpec((n, 1, sub, HEAD), lambda *_: (0, which, 0, 0))
+
+
 def tile_block(which, per_chunk, tile):
     return pl.BlockSpec(
         (1, 1, tile, HEAD), lambda r, *_: (r // per_chunk, which, r % per_chunk, 0)
@@ -136,34 +155,43 @@
     tile = min(sub, BLK)
     per_chunk = sub // tile
     core = lax.axis_index("tp")
-    chunks = [h * n // heads for h in range(heads)]
-
-    def tp_order(stack):
-        return [lax.dynamic_index_in_dim(stack, (core - p) % t, 0, False) for p in range(t)]
+    chip = lax.axis_index("ctx")
+    in_plane = n // PLANES
+    heads_plane = heads // PLANES
+    seat = chip % in_plane
+
+    def tp_swap(pick):
+        got = [pick(core)]
+        for s in range(1, t):
+            got.append(lax.ppermute(pick((core + s) % t), "tp", shifts(t, s)))
+        return [lax.select_n((core - p) % t, *got) for p in range(t)]
+
+    def tp_gather(x):
+        return tp_swap(lambda _: x)
 
     def tp_split(pack):
-        got = [lax.dynamic_index_in_dim(pack, core, 0, False)]
-        for s in range(1, t):
-            block = lax.dynamic_index_in_dim(pack, (core + s) % t, 0, False)
-            got.append(lax.ppermute(block, "tp", shifts(t, s)))
-        return tp_order(jnp.stack(got))
+        return tp_swap(lambda p: lax.dynamic_index_in_dim(pack, p, 0, False))
+
+    def plane_swap(pick):
+        got = [pick(seat)]
+        for k in range(1, in_plane):
+            got.append(lax.ppermute(pick(seat ^ k), "ctx", [(i, i ^ k) for i in range(n)]))
+        return [lax.select_n(seat ^ b, *got) for b in range(in_plane)]
 
     def to_heads(arrays):
         pack = jnp.stack(
             [a.reshape(t, sub, heads_here, HEAD).transpose(0, 2, 1, 3) for a in arrays], axis=2
         )
         every = jnp.concatenate(tp_split(pack), axis=0)
-        empty = jnp.zeros_like(every[0])
-        sent = [empty] * n
-        for h, chunk in enumerate(chunks):
-            sent[chunk] = every[h]
-        return lax.all_to_all(jnp.stack(sent), "ctx", 0, 0, tiled=True)
+        every = every.reshape((PLANES, heads_plane) + every.shape[1:])
+        spare = in_plane - heads_plane
+        sent = jnp.pad(every, ((0, 0), (0, spare), (0, 0), (0, 0), (0, 0)))
+        return lax.all_to_all(sent.reshape((n,) + every.shape[2:]), "ctx", 0, 0, tiled=True)
 
     def to_tokens(pack):
         got = lax.all_to_all(pack, "ctx", 0, 0, tiled=True)
-        every = jnp.stack([got[chunk] for chunk in chunks])
-        every = every.reshape((t, heads_here) + every.shape[1:])
-        mine = jnp.stack(tp_split(every))
+        every = got.reshape((PLANES, in_plane) + got.shape[1:])[:, :heads_plane]
+        mine = jnp.stack(tp_split(every.reshape((t, heads_here) + got.shape[1:])))
         return [
             mine[:, :, a].transpose(0, 2, 1, 3).reshape(rows, width) for a in range(pack.shape[1])
         ]
@@ -188,31 +216,38 @@
     kidx = jnp.sum(jnp.where(hit, ids[None, None, :], 0), axis=2).astype(jnp.int32)
     full = full.astype(jnp.int32)
 
+    qkv = to_heads([queries, key_vectors, value_vectors])
+
     half = out_grad.shape[1]
-    grads = [out_grad] + [lax.ppermute(out_grad, "tp", shifts(t, s)) for s in range(1, t)]
-    full_grad = jnp.concatenate(tp_order(jnp.stack(grads)), axis=1)
-
-    kv = to_heads([key_vectors, value_vectors])
+    model = half * t
+    full_grad = jnp.concatenate(tp_gather(out_grad), axis=1)
     grad_attn = dot(full_grad, out_weight, NT).astype(BF16)
-    qg = to_heads([queries, grad_attn])
-
-    kv_parts = jnp.stack([kv] + [lax.ppermute(kv, "tp", shifts(t, s)) for s in range(1, t)])
-    keys = kv_parts[:, :, 0].reshape(tiles_k, tile, HEAD)
-    values = kv_parts[:, :, 1].reshape(tiles_k, tile, HEAD)
+    g_heads = to_heads([grad_attn])
+
+    cols = model // in_plane
+    mine = lax.dynamic_slice_in_dim(full_grad, core * sub, sub, 0)
+    plane_grad = jnp.stack(
+        plane_swap(lambda b: lax.dynamic_slice_in_dim(mine, b * cols, cols, 1))
+    )
+    lines = [[a * in_plane + b for a in range(PLANES)] for b in range(in_plane)]
+    slice_grad = lax.all_gather(plane_grad, "ctx", axis_index_groups=lines)
+    slice_grad = slice_grad.reshape(n * sub, cols)
+
+    others = [lax.ppermute(qkv, "tp", shifts(t, s)) for s in range(1, t)]
 
     tiles_q = n * per_chunk
-    few = [pltpu.VMEM((count * tile, HEAD), BF16)] * 2
+    few = [pltpu.VMEM((count * tile, HEAD), BF16)] * 2 + [pltpu.VMEM((tiles_k, tile, HEAD), BF16)] * 2
     params = pltpu.CompilerParams(vmem_limit_bytes=48 * 2**20)
     q_block = tile_block(0, per_chunk, tile)
-    g_block = tile_block(1, per_chunk, tile)
-    key_block = whole_block((tiles_k, tile, HEAD))
+    part_blocks = [one_array(1, n, sub), one_array(2, n, sub)] * t
+    part_arrays = [a for pack in [qkv] + others for a in (pack, pack)]
     lse_block = pl.BlockSpec((tile, HEAD), lambda r, *_: (r, 0))
     attn, lse = pl.pallas_call(
-        functools.partial(forward_kernel, tile, count),
+        functools.partial(forward_kernel, t, tile, count),
         grid_spec=pltpu.PrefetchScalarGridSpec(
             num_scalar_prefetch=3,
             grid=(tiles_q,),
-            in_specs=[q_block, key_block, key_block],
+            in_specs=[q_block] + part_blocks,
             out_specs=[q_block, lse_block],
             scratch_shapes=few,
         ),
@@ -225,7 +260,22 @@
             flops=tiles_q * tile * tiles_k * tile * HEAD * 2, bytes_accessed=5 * 2**20, transcendentals=2**22
         ),
         name="forward",
-    )(full, kcnt, kidx, qg, keys, values)
+    )(full, kcnt, kidx, qkv, *part_arrays)
+
+    plane_attn = plane_swap(lambda _: attn)[:heads_plane]
+    plane_attn = jnp.stack([a.reshape(n * sub, HEAD) for a in plane_attn])
+    tile_term = jnp.einsum("hrd,rc->hdc", plane_attn, slice_grad, preferred_element_type=F32)
+    tile_rows = heads_plane * HEAD
+    piece = tile_rows // t
+    tile_term = tile_term.reshape(t, piece, cols)
+    tile_sum = lax.dynamic_index_in_dim(tile_term, core, 0, False)
+    for s in range(1, t):
+        there = lax.dynamic_index_in_dim(tile_term, (core + s) % t, 0, False)
+        tile_sum = tile_sum + lax.ppermute(there.astype(BF16), "tp", shifts(t, s)).astype(F32)
+    tiles = lax.all_gather(tile_sum.astype(BF16), "ctx")
+    planes_here = PLANES // t
+    tiles = jnp.stack(tp_split(tiles.reshape(t, planes_here, in_plane, piece, cols)))
+    grad_weight = tiles.transpose(1, 0, 3, 2, 4).reshape(width, model).astype(F32)
 
     (attention,) = to_tokens(attn)
     projected = dot(attention, out_weight)
@@ -234,15 +284,13 @@
         there = lax.dynamic_slice_in_dim(projected, (core + s) % t * half, half, 1)
         own = own + lax.ppermute(there.astype(BF16), "tp", shifts(t, s)).astype(F32)
     attention_out = own.astype(BF16)
-    weight_term = dot(attention, full_grad, TN)
-    grad_weight = lax.psum(weight_term.astype(BF16), "ctx").astype(F32)
 
     dq, dkv = pl.pallas_call(
-        functools.partial(backward_kernel, tile, count),
+        functools.partial(backward_kernel, t, tile, count),
         grid_spec=pltpu.PrefetchScalarGridSpec(
             num_scalar_prefetch=3,
             grid=(tiles_q,),
-            in_specs=[q_block, g_block, q_block, lse_block, key_block, key_block],
+            in_specs=[q_block, q_block, q_block, lse_block] + part_blocks,
             out_specs=[q_block, whole_block((t, 2, n, sub, HEAD))],
             scratch_shapes=few + [pltpu.VMEM((tiles_k, tile, HEAD), F32)] * 2,
         ),
@@ -255,7 +303,7 @@
             flops=tiles_q * tile * tiles_k * tile * HEAD * 5, bytes_accessed=8 * 2**20, transcendentals=2**22
         ),
         name="backward",
-    )(full, kcnt, kidx, qg, qg, attn, lse, keys, values)
+    )(full, kcnt, kidx, qkv, g_heads, attn, lse, *part_arrays)
 
     sums = dkv[0].astype(F32)
     for s in range(1, t):

time: 377 us -> 307 us (0.81)
  waiting for transfers between devices: 221 us -> 108 us
  blocking collectives: 0 us -> 21.5 us
  local copies, waits for them, and re-layouts: 46 us -> 55.2 us
  other arithmetic: 18 us -> 25.9 us
  Pallas kernels: 33.4 us -> 38 us
    psum x1 -> x0, waiting for transfers between devices: 120 us -> none  [per_device(): grad_weight = lax.psum(weight_term.astype(BF16), 'ctx').astype(F32)]
    ppermute x6 -> x14, waiting for transfers between devices: 4.04 us -> 40.8 us  [the longest x6 35.3 us: plane_swap(): lax.ppermute(pick(seat ^ k), 'ctx', [(i, i ^ k) for i in range(n)])]
    all_to_all x0 -> x1, blocking collectives: none -> 21.5 us  [to_heads(): lax.all_to_all(sent.reshape((n,) + every.shape[2:]), 'ctx', 0, 0, tiled=T...]
    all_to_all x2 -> x1, waiting for transfers between devices: 30.7 us -> 14.8 us  [to_heads(): lax.all_to_all(sent.reshape((n,) + every.shape[2:]), 'ctx', 0, 0, tiled=T...]
    unnamed x72 -> x30, local copies, waits for them, and re-layouts: 30.7 us -> 15.6 us
    all_to_all x2, waiting for transfers between devices: 65.6 us -> 50.6 us  [to_tokens(): got = lax.all_to_all(pack, 'ctx', 0, 0, tiled=True)]
    convert_element_type x0 -> x3, local copies, waits for them, and re-layouts: none -> 14.6 us  [the longest x1 13.4 us: per_device(): tiles.transpose(1, 0, 3, 2, 4).reshape(width, model).astype(F32)]
    ppermute x6 -> x14, starting transfers between devices: 4.32 us -> 11.4 us  [the longest x6 5.3 us: plane_swap(): lax.ppermute(pick(seat ^ k), 'ctx', [(i, i ^ k) for i in range(n)])]
  transfers between devices with their start and end apart: 13 -> 21, of which waited for: 7 -> 13; matrix products, arithmetic and copies ran while one was open for 13% -> 16% of each run, Pallas kernels for 5% -> 12%
where the time goes in v2:
time: 307 us; the launch traced here: 305 us
  waiting for transfers between devices  108 us (35%)
  local copies, waits for them, and re-layouts  55.2 us (18%)
  Pallas kernels  38 us (12%)
  starting transfers between devices  29.6 us (10%)
  other arithmetic  25.9 us (8%)
  blocking collectives  21.5 us (7%)
  between operations  14.5 us (5%)
  matrix products  12.3 us (4%)
    all_to_all x2, waiting for transfers between devices, to_tokens(): got = lax.all_to_all(pack, 'ctx', 0, 0, tiled=True)  50.6 us
    ppermute x6, waiting for transfers between devices, plane_swap(): lax.ppermute(pick(seat ^ k), 'ctx', [(i, i ^ k) for i in range(n)])  35.3 us
    pallas_call x1, Pallas kernels, per_device(): pl.pallas_call(functools.partial(backward_kernel, t, tile, count), grid_s...  21.7 us
    all_to_all x1, blocking collectives, to_heads(): lax.all_to_all(sent.reshape((n,) + every.shape[2:]), 'ctx', 0, 0, tiled=T...  21.5 us
    pallas_call x1, Pallas kernels, per_device(): pl.pallas_call(functools.partial(forward_kernel, t, tile, count), grid_sp...  16.3 us
    unnamed x30, local copies, waits for them, and re-layouts  15.6 us
    all_to_all x1, waiting for transfers between devices, to_heads(): lax.all_to_all(sent.reshape((n,) + every.shape[2:]), 'ctx', 0, 0, tiled=T...  14.8 us
    convert_element_type x1, local copies, waits for them, and re-layouts, per_device(): tiles.transpose(1, 0, 3, 2, 4).reshape(width, model).astype(F32)  13.4 us
  transfers between devices with their start and end apart: 21, of which 13 were waited for; matrix products, arithmetic and copies ran while one was open for 16% of the time, Pallas kernels for 12%

profile of v2, /device:TPU:13, one launch (start us, length us, event | category | flops | bytes accessed | tf_op | source)
XLA Modules:
  0.0 305.4 jit_solution(11590299943514790413)
XLA Ops:
  11.2 2.7 constant_dynamic-slice_fusion.1
  13.9 2.5 copy.109
  21.3 6.6 %all-to-all-start = ((bf16[16,3,128,128]{3,2,1,0:T(8,128)(2,1)}), bf16[16,3,128,128]{3,2,1,0:T(8,128)(2,1)S(1)}, u32[]{:S(2)}, u32[]{:S(2)}) async-start(bf16[16,3,128,128]{3,2,1,0:T(8,128)(2,1)} %bitcast.9), calls=%async_computation | async-start | bytes 3145728 | tf_op jit(solution)/shard_map/all_to_all | solution.py:189
  33.7 4.5 %collective-permute-done.11 = bf16[128,768]{1,0:T(8,128)(2,1)S(1)} collective-permute-done((bf16[128,768]{1,0:T(8,128)(2,1)}, bf16[128,768]{1,0:T(8,128)(2,1)S(1)}, u32[]{:S(2)}, u32[]{:S(2)}) %collective-permute-start.11) | collective-permute-done | bytes 196640 | tf_op jit(solution)/shard_map/ppermute | solution.py:178
  38.2 7.8 %collective-permute-done.12 = bf16[128,768]{1,0:T(8,128)(2,1)S(1)} collective-permute-done((bf16[128,768]{1,0:T(8,128)(2,1)}, bf16[128,768]{1,0:T(8,128)(2,1)S(1)}, u32[]{:S(2)}, u32[]{:S(2)}) %collective-permute-start.12) | collective-permute-done | bytes 196640 | tf_op jit(solution)/shard_map/ppermute | solution.py:178
  49.9 14.8 %all-to-all-done.q_ref.refs_0_.refs_1_ = bf16[16,3,128,128]{3,2,1,0:T(8,128)(2,1)S(1)} async-done(((bf16[16,3,128,128]{3,2,1,0:T(8,128)(2,1)}), bf16[16,3,128,128]{3,2,1,0:T(8,128)(2,1)S(1)}, u32[]{:S(2)}, u32[]{:S(2)}) %all-to-all-start) | async-done | bytes 1572896 | tf_op jit(solution)/shard_map/all_to_all | solution.py:189
  69.3 16.3 %forward.1 = (bf16[16,1,128,128]{3,2,1,0:T(8,128)(2,1)}, f32[2048,128]{1,0:T(8,128)S(1)}) custom-call(s32[16]{0:T(128)S(1)} %get-tuple-element.43.full_ref, s32[16]{0:T(128)S(1)} %get-tuple-element.39.kcnt_ref, s32[16,10]{1,0:T(8,128)S(1)} %copy.110.kidx_ref, bf16[16,3,128,128]{3,2,1,0:T(8,128)(2,1)S(1)} %all-to-all-done.q_ref.refs_0_.refs_1_, ...), custom_call_target="tpu_custom_call" | custom-call | flops 2147483648 | bytes 5242880 | tf_op jit(solution)/shard_map/forward/pallas_call | solution.py:245
  88.2 11.7 %collective-permute-done.10 = bf16[16,1,128,128]{3,2,1,0:T(8,128)(2,1)S(1)} collective-permute-done((bf16[16,1,128,128]{3,2,1,0:T(8,128)(2,1)}, bf16[16,1,128,128]{3,2,1,0:T(8,128)(2,1)S(1)}, u32[]{:S(2)}, u32[]{:S(2)}) %collective-permute-start.10) | collective-permute-done | bytes 524320 | tf_op jit(solution)/shard_map/ppermute | solution.py:178
  100.0 11.2 %collective-permute-done.9 = bf16[16,1,128,128]{3,2,1,0:T(8,128)(2,1)S(1)} collective-permute-done((bf16[16,1,128,128]{3,2,1,0:T(8,128)(2,1)}, bf16[16,1,128,128]{3,2,1,0:T(8,128)(2,1)S(1)}, u32[]{:S(2)}, u32[]{:S(2)}) %collective-permute-start.9) | collective-permute-done | bytes 524320 | tf_op jit(solution)/shard_map/ppermute | solution.py:178
  113.7 2.6 copy.123
  118.3 3.7 %fusion.26 = f32[2,192,768]{2,1,0:T(8,128)S(1)} fusion(bf16[2,192,2048]{2,1,0:T(8,128)(2,1)} %bitcast.177, bf16[2048,768,1]{1,0,2:T(8,128)(2,1)} %bitcast.189), kind=kOutput, calls=%fused_computation.109 | convolution fusion | flops 1207959552 | bytes 5898240 | tf_op jit(solution)/shard_map/hrd,rc->hdc/dot_general | solution.py:267
  125.0 4.8 %fusion.4 = bf16[256,768]{1,0:T(8,128)(2,1)} fusion(bf16[768,3072]{1,0:T(8,128)(2,1)} %param.11, bf16[256,1536]{1,0:T(8,128)(2,1)} %copy-done.2, bf16[256,1536]{1,0:T(8,128)(2,1)S(1)} %get-tuple-element.59), kind=kOutput, calls=%fused_computation.28 | convolution fusion | flops 1211301888 | bytes 6684672 | tf_op jit(solution)/shard_map/dot_general | solution.py:27
  136.6 21.5 %all_to_all.20.g_ref = bf16[16,1,128,128]{3,2,1,0:T(8,128)(2,1)S(1)} all-to-all(bf16[16,1,128,128]{3,2,1,0:T(8,128)(2,1)S(1)} %bitcast.175), channel_id=1, replica_groups=mesh['ctx'=16,'tp'=2] {'ctx'}, dimensions={0} | all-to-all | bytes 1048576 | tf_op jit(solution)/shard_map/all_to_all | solution.py:189
  158.1 21.7 %backward.1 = (bf16[16,1,128,128]{3,2,1,0:T(8,128)(2,1)S(1)}, bf16[2,2,16,128,128]{4,3,2,1,0:T(8,128)(2,1)}) custom-call(s32[16]{0:T(128)S(1)} %get-tuple-element.43.full_ref, s32[16]{0:T(128)S(1)} %get-tuple-element.39.kcnt_ref, s32[16,10]{1,0:T(8,128)S(1)} %copy.110.kidx_ref, bf16[16,3,128,128]{3,2,1,0:T(8,128)(2,1)S(1)} %all-to-all-done.q_ref.refs_0_.refs_1_, ...), custom_call_target="tpu_custom_call" | custom-call | flops 5368709120 | bytes 8388608 | tf_op jit(solution)/shard_map/backward/pallas_call | solution.py:288
  182.3 5.7 %all-to-all-start.1 = ((bf16[16,1,128,128]{3,2,1,0:T(8,128)(2,1)}), bf16[16,1,128,128]{3,2,1,0:T(8,128)(2,1)S(1)}, u32[]{:S(2)}, u32[]{:S(2)}) async-start(bf16[16,1,128,128]{3,2,1,0:T(8,128)(2,1)} %get-tuple-element.10.o_ref), calls=%async_computation.1 | async-start | bytes 1048576 | tf_op jit(solution)/shard_map/all_to_all | solution.py:192
  191.1 25.4 %all-to-all-done.1 = bf16[16,1,128,128]{3,2,1,0:T(8,128)(2,1)S(1)} async-done(((bf16[16,1,128,128]{3,2,1,0:T(8,128)(2,1)}), bf16[16,1,128,128]{3,2,1,0:T(8,128)(2,1)S(1)}, u32[]{:S(2)}, u32[]{:S(2)}) %all-to-all-start.1) | async-done | bytes 524320 | tf_op jit(solution)/shard_map/all_to_all | solution.py:192
  216.5 4.3 %all-to-all-start.3 = ((bf16[16,3,128,128]{3,2,1,0:T(8,128)(2,1)}), bf16[16,3,128,128]{3,2,1,0:T(8,128)(2,1)}, u32[]{:S(2)}, u32[]{:S(2)}) async-start(bf16[16,3,128,128]{3,2,1,0:T(8,128)(2,1)} %copy.119), calls=%async_computation.3 | async-start | bytes 3145728 | tf_op jit(solution)/shard_map/all_to_all | solution.py:192
  223.7 3.2 %dynamic-slice_bitcast_fusion = bf16[2,4,192,768]{3,2,1,0:T(8,128)(2,1)} fusion(bf16[2,2,4,192,768]{4,3,2,1,0:T(8,128)(2,1)} %bitcast.161, s32[]{:T(128)S(6)} %select_n.392), kind=kLoop, calls=%fused_computation.16 | loop fusion | bytes 4718596 | tf_op jit(solution)/shard_map/jit(dynamic_index_in_dim)/squeeze | solution.py:173
  227.3 3.8 %fusion.13 = f32[256,3072]{1,0:T(8,128)S(1)} fusion(bf16[768,3072]{1,0:T(8,128)(2,1)} %param.11, bf16[96,8,2,128]{3,2,1,0:T(2,128)(2,1)S(1)} %bitcast.168), kind=kOutput, calls=%fused_computation.56 | convolution fusion | flops 1207959552 | bytes 8257536 | tf_op jit(solution)/shard_map/dot_general | solution.py:27
  232.2 25.2 %all-to-all-done.3 = bf16[16,3,128,128]{3,2,1,0:T(8,128)(2,1)} async-done(((bf16[16,3,128,128]{3,2,1,0:T(8,128)(2,1)}), bf16[16,3,128,128]{3,2,1,0:T(8,128)(2,1)}, u32[]{:S(2)}, u32[]{:S(2)}) %all-to-all-start.3) | async-done | bytes 1572896 | tf_op jit(solution)/shard_map/all_to_all | solution.py:192
  262.3 2.4 add_convert_fusion
  271.1 4.4 %convert_bitcast_fusion = f32[2,2,192,4,768]{4,2,3,0,1:T(8,128)} fusion(bf16[1,2,4,192,768]{4,3,2,1,0:T(8,128)(2,1)S(1)} %get-tuple-element.46, bf16[1,2,4,192,768]{4,3,2,1,0:T(8,128)(2,1)S(1)} %get-tuple-element.45), kind=kLoop, calls=%fused_computation.2 | loop fusion | flops 4718592 | bytes 14155776 | tf_op jit(solution)/shard_map/convert_element_type | solution.py:278
  275.5 13.4 %copy.124 = f32[2,2,192,4,768]{4,3,2,1,0:T(4,128)} copy(f32[2,2,192,4,768]{4,2,3,0,1:T(8,128)} %convert_bitcast_fusion) | data formatting | bytes 18874368 | tf_op jit(solution)/shard_map/convert_element_type | solution.py:278
  288.9 9.6 %copy.138 = f32[96,8,4,768]{3,1,2,0:T(8,128)} copy(f32[96,8,4,768]{3,2,1,0:T(4,128)} %bitcast.159) | data formatting | bytes 18874368
  (117 shorter events, 61.0 us)
Async XLA Ops:
  7.2 59.0 %copy-start = (s32[32]{0:T(128)S(1)}, s32[32]{0:T(128)}, u32[]{:S(2)}) copy-start(s32[32]{0:T(128)} %param.13) | copy-start | bytes 388
  16.4 3.3 %collective-permute-start = (bf16[6,3,128,128]{3,2,1,0:T(8,128)(2,1)}, bf16[6,3,128,128]{3,2,1,0:T(8,128)(2,1)S(1)}, u32[]{:S(2)}, u32[]{:S(2)}) collective-permute-start(bf16[6,3,128,128]{3,2,1,0:T(8,128)(2,1)} %bitcast.184), channel_id=1, source_target_pairs={{0,1},{1,0},{2,3},{3,2},{4,5},{5,4},{6,7},{7,6},{8,9},{9,8},{10,11... | collective-permute-start | bytes 1769480 | tf_op jit(solution)/shard_map/ppermute | solution.py:166
  17.1 10.8 %collective-permute-start.4 = (bf16[256,1536]{1,0:T(8,128)(2,1)S(1)}, bf16[256,1536]{1,0:T(8,128)(2,1)}, u32[]{:S(2)}, u32[]{:S(2)}) collective-permute-start(bf16[256,1536]{1,0:T(8,128)(2,1)S(1)} %copy-done.5), channel_id=1, source_target_pairs={{0,1},{1,0},{2,3},{3,2},{4,5},{5,4},{6,7},{7,6},{8,9},{9,8},{10,11... | collective-permute-start | bytes 2359304 | tf_op jit(solution)/shard_map/ppermute | solution.py:166
  21.3 43.4 %all-to-all-start = ((bf16[16,3,128,128]{3,2,1,0:T(8,128)(2,1)}), bf16[16,3,128,128]{3,2,1,0:T(8,128)(2,1)S(1)}, u32[]{:S(2)}, u32[]{:S(2)}) async-start(bf16[16,3,128,128]{3,2,1,0:T(8,128)(2,1)} %bitcast.9), calls=%async_computation | async-start | bytes 3145728 | tf_op jit(solution)/shard_map/all_to_all | solution.py:189
  27.9 90.5 %all-gather.5.cloned.1.call-start = ((), (), s32[]{:S(2)}) async-start(), calls=%async_computation.4 | async-start | bytes 3932160 | tf_op jit(solution)/shard_map/all_gather | solution.py:233
  29.4 17.9 %copy-start.2 = (bf16[256,1536]{1,0:T(8,128)(2,1)}, bf16[256,1536]{1,0:T(8,128)(2,1)S(1)}, u32[]{:S(2)}) copy-start(bf16[256,1536]{1,0:T(8,128)(2,1)S(1)} %get-tuple-element.60) | copy-start | bytes 2359300
  31.0 7.2 %collective-permute-start.11 = (bf16[128,768]{1,0:T(8,128)(2,1)}, bf16[128,768]{1,0:T(8,128)(2,1)S(1)}, u32[]{:S(2)}, u32[]{:S(2)}) collective-permute-start(bf16[128,768]{1,0:T(8,128)(2,1)} %get-tuple-element.56), channel_id=1, source_target_pairs={{0,2},{2,0},{4,6},{6,4},{8,10},{10,8},{12,14},{14,12},{16,18},{18,... | collective-permute-start | bytes 589832 | tf_op jit(solution)/shard_map/ppermute | solution.py:178
  32.2 13.8 %collective-permute-start.12 = (bf16[128,768]{1,0:T(8,128)(2,1)}, bf16[128,768]{1,0:T(8,128)(2,1)S(1)}, u32[]{:S(2)}, u32[]{:S(2)}) collective-permute-start(bf16[128,768]{1,0:T(8,128)(2,1)} %get-tuple-element.57), channel_id=1, source_target_pairs={{0,4},{2,6},{4,0},{6,2},{8,12},{10,14},{12,8},{14,10},{16,20},{18,... | collective-permute-start | bytes 589832 | tf_op jit(solution)/shard_map/ppermute | solution.py:178
  32.5 13.5 %collective-permute-start.13 = (bf16[128,768]{1,0:T(8,128)(2,1)}, bf16[128,768]{1,0:T(8,128)(2,1)}, u32[]{:S(2)}, u32[]{:S(2)}) collective-permute-start(bf16[128,768]{1,0:T(8,128)(2,1)} %get-tuple-element.58), channel_id=1, source_target_pairs={{0,6},{2,4},{4,2},{6,0},{8,14},{10,12},{12,10},{14,8},{16,22},{18,... | collective-permute-start | bytes 589832 | tf_op jit(solution)/shard_map/ppermute | solution.py:178
  49.7 174.0 %all-gather.7.cloned.1.call-start = ((), (), s32[]{:S(2)}) async-start(), calls=%async_computation.5 | async-start | bytes 5013504 | tf_op jit(solution)/shard_map/all_gather | solution.py:275
  64.7 4.6 %collective-permute-start.1 = (bf16[16,3,128,128]{3,2,1,0:T(8,128)(2,1)S(1)}, bf16[16,3,128,128]{3,2,1,0:T(8,128)(2,1)}, u32[]{:S(2)}, u32[]{:S(2)}) collective-permute-start(bf16[16,3,128,128]{3,2,1,0:T(8,128)(2,1)S(1)} %all-to-all-done.q_ref.refs_0_.refs_1_), channel_id=1, source_target_pairs={{0,1},{1,0},{2,3},{3,2},{4,5},{5,4},{6,7},{7,6},{8,9},{9,8},{10,11... | collective-permute-start | bytes 4718600 | tf_op jit(solution)/shard_map/ppermute | solution.py:236
  85.6 14.4 %collective-permute-start.10 = (bf16[16,1,128,128]{3,2,1,0:T(8,128)(2,1)}, bf16[16,1,128,128]{3,2,1,0:T(8,128)(2,1)S(1)}, u32[]{:S(2)}, u32[]{:S(2)}) collective-permute-start(bf16[16,1,128,128]{3,2,1,0:T(8,128)(2,1)} %get-tuple-element.10.o_ref), channel_id=1, source_target_pairs={{0,6},{2,4},{4,2},{6,0},{8,14},{10,12},{12,10},{14,8},{16,22},{18,... | collective-permute-start | bytes 1572872 | tf_op jit(solution)/shard_map/ppermute | solution.py:178
  86.1 25.0 %collective-permute-start.9 = (bf16[16,1,128,128]{3,2,1,0:T(8,128)(2,1)}, bf16[16,1,128,128]{3,2,1,0:T(8,128)(2,1)S(1)}, u32[]{:S(2)}, u32[]{:S(2)}) collective-permute-start(bf16[16,1,128,128]{3,2,1,0:T(8,128)(2,1)} %get-tuple-element.10.o_ref), channel_id=1, source_target_pairs={{0,4},{2,6},{4,0},{6,2},{8,12},{10,14},{12,8},{14,10},{16,20},{18,... | collective-permute-start | bytes 1572872 | tf_op jit(solution)/shard_map/ppermute | solution.py:178
  87.5 23.6 %collective-permute-start.8 = (bf16[16,1,128,128]{3,2,1,0:T(8,128)(2,1)}, bf16[16,1,128,128]{3,2,1,0:T(8,128)(2,1)S(1)}, u32[]{:S(2)}, u32[]{:S(2)}) collective-permute-start(bf16[16,1,128,128]{3,2,1,0:T(8,128)(2,1)} %get-tuple-element.10.o_ref), channel_id=1, source_target_pairs={{0,2},{2,0},{4,6},{6,4},{8,10},{10,8},{12,14},{14,12},{16,18},{18,... | collective-permute-start | bytes 1572872 | tf_op jit(solution)/shard_map/ppermute | solution.py:178
  122.1 2.0 collective-permute-start.14
  133.8 1.6 collective-permute-start.5
  181.1 6.9 %collective-permute-start.6 = (bf16[2,16,128,128]{3,2,1,0:T(8,128)(2,1)S(1)}, bf16[2,16,128,128]{3,2,1,0:T(8,128)(2,1)S(1)}, u32[]{:S(2)}, u32[]{:S(2)}) collective-permute-start(bf16[2,16,128,128]{3,2,1,0:T(8,128)(2,1)S(1)} %slice_bitcast_fusion), channel_id=1, source_target_pairs={{0,1},{1,0},{2,3},{3,2},{4,5},{5,4},{6,7},{7,6},{8,9},{9,8},{10,11... | collective-permute-start | bytes 3145736 | tf_op jit(solution)/shard_map/ppermute | solution.py:311
  182.3 34.3 %all-to-all-start.1 = ((bf16[16,1,128,128]{3,2,1,0:T(8,128)(2,1)}), bf16[16,1,128,128]{3,2,1,0:T(8,128)(2,1)S(1)}, u32[]{:S(2)}, u32[]{:S(2)}) async-start(bf16[16,1,128,128]{3,2,1,0:T(8,128)(2,1)} %get-tuple-element.10.o_ref), calls=%async_computation.1 | async-start | bytes 1048576 | tf_op jit(solution)/shard_map/all_to_all | solution.py:192
  216.5 40.8 %all-to-all-start.3 = ((bf16[16,3,128,128]{3,2,1,0:T(8,128)(2,1)}), bf16[16,3,128,128]{3,2,1,0:T(8,128)(2,1)}, u32[]{:S(2)}, u32[]{:S(2)}) async-start(bf16[16,3,128,128]{3,2,1,0:T(8,128)(2,1)} %copy.119), calls=%async_computation.3 | async-start | bytes 3145728 | tf_op jit(solution)/shard_map/all_to_all | solution.py:192
  220.9 2.0 collective-permute-start.2
  226.9 42.2 %collective-permute-start.15 = (bf16[2,4,192,768]{3,2,1,0:T(8,128)(2,1)}, bf16[2,4,192,768]{3,2,1,0:T(8,128)(2,1)}, u32[]{:S(2)}, u32[]{:S(2)}) collective-permute-start(bf16[2,4,192,768]{3,2,1,0:T(8,128)(2,1)} %dynamic-slice_bitcast_fusion), channel_id=1, source_target_pairs={{0,1},{1,0},{2,3},{3,2},{4,5},{5,4},{6,7},{7,6},{8,9},{9,8},{10,11... | collective-permute-start | bytes 7077896 | tf_op jit(solution)/shard_map/ppermute | solution.py:166
  232.1 30.2 %collective-permute-start.3 = (bf16[256,1536]{1,0:T(8,128)(2,1)}, bf16[256,1536]{1,0:T(8,128)(2,1)}, u32[]{:S(2)}, u32[]{:S(2)}) collective-permute-start(bf16[256,1536]{1,0:T(8,128)(2,1)} %dynamic-slice_convert_fusion), channel_id=1, source_target_pairs={{0,1},{1,0},{2,3},{3,2},{4,5},{5,4},{6,7},{7,6},{8,9},{9,8},{10,11... | collective-permute-start | bytes 2359304 | tf_op jit(solution)/shard_map/ppermute | solution.py:285
  260.8 3.9 %collective-permute-start.7 = (bf16[6,3,128,128]{3,2,1,0:T(8,128)(2,1)}, bf16[6,3,128,128]{3,2,1,0:T(8,128)(2,1)}, u32[]{:S(2)}, u32[]{:S(2)}) collective-permute-start(bf16[6,3,128,128]{3,2,1,0:T(8,128)(2,1)} %dynamic-slice_bitcast_fusion.1), channel_id=1, source_target_pairs={{0,1},{1,0},{2,3},{3,2},{4,5},{5,4},{6,7},{7,6},{8,9},{9,8},{10,11... | collective-permute-start | bytes 1769480 | tf_op jit(solution)/shard_map/ppermute | solution.py:166
  288.9 9.6 %copy-start.1 = (s32[32]{0:T(128)S(1)}, s32[32]{0:T(128)}, u32[]{:S(2)}) copy-start(s32[32]{0:T(128)} %param.13) | copy-start | bytes 388
  (7 other events, 20.0 us)
Sparse Core Ops, SparseCore 0:
  49.8 68.4 all-gather.4
  125.1 90.5 all-gather.6

commit v3 on v2

--- a/solution.py
+++ b/solution.py
@@ -145,6 +145,60 @@
 
 def shifts(t, s):
     return [(c, (c + s) % t) for c in range(t)]
+
+
+def place_kernel(place_ref, *refs):
+    sources, out_ref = refs[:-1], refs[-1]
+    step = pl.program_id(0)
+    for u in range(2):
+        own, beside, above, upper, lower = sources[5 * u:5 * u + 5]
+        for v, source in enumerate((own, beside, above)):
+            @pl.when(step == 4 * u + v)
+            def _(source=source):
+                out_ref[...] = source[...].astype(F32)
+
+        @pl.when(step == 4 * u + 3)
+        def _(upper=upper, lower=lower):
+            middle = upper.shape[0]
+            out_ref[:middle] = upper[...].astype(F32)
+            out_ref[middle:] = lower[...].astype(F32)
+
+
+def gather_tiles_by_core(n, t, tile_sum, chip, core):
+    in_plane = n // PLANES
+    plane, seat = chip // in_plane, chip % in_plane
+    tile_rows, cols = tile_sum.shape
+    across = [
+        (i * t + c, (i ^ 2 * in_plane) * t + c)
+        for i in range(n) for c in range(t) if i // in_plane // 2 == c
+    ]
+    from_half = lax.ppermute(tile_sum, ("ctx", "tp"), across)
+
+    def swap(x, k):
+        return lax.ppermute(x, "ctx", [(i, i ^ k) for i in range(n)])
+
+    first = jnp.where(plane // 2 == core, tile_sum, from_half)
+    second = swap(first, in_plane)
+    middle = tile_rows // 2
+    sources = []
+    for mine in (first, second):
+        beside, above = swap(mine, 1), swap(mine, 2)
+        sources += [mine, beside, above, swap(beside[:middle], 2), swap(above[middle:], 1)]
+    place = jnp.stack([plane % 2, seat]).astype(jnp.int32)
+    return pl.pallas_call(
+        place_kernel,
+        grid_spec=pltpu.PrefetchScalarGridSpec(
+            num_scalar_prefetch=1,
+            grid=(8,),
+            in_specs=[whole_block(x.shape) for x in sources],
+            out_specs=pl.BlockSpec(
+                (tile_rows, cols), lambda s, place: (s // 4 ^ place[0], s % 4 ^ place[1])
+            ),
+        ),
+        out_shape=jax.ShapeDtypeStruct((2 * tile_rows, in_plane * cols), F32),
+        compiler_params=pltpu.CompilerParams(vmem_limit_bytes=48 * 2**20),
+        name="place",
+    )(place, *sources)
 
 
 def per_device(n, t, queries, key_vectors, value_vectors, out_weight, out_grad, block_segment):
@@ -257,33 +311,12 @@
         ],
         compiler_params=params,
         cost_estimate=pl.CostEstimate(
-            flops=tiles_q * tile * tiles_k * tile * HEAD * 2, bytes_accessed=5 * 2**20, transcendentals=2**22
+            flops=16 * 10**9, bytes_accessed=5 * 2**20, transcendentals=2**22
         ),
         name="forward",
     )(full, kcnt, kidx, qkv, *part_arrays)
 
-    plane_attn = plane_swap(lambda _: attn)[:heads_plane]
-    plane_attn = jnp.stack([a.reshape(n * sub, HEAD) for a in plane_attn])
-    tile_term = jnp.einsum("hrd,rc->hdc", plane_attn, slice_grad, preferred_element_type=F32)
-    tile_rows = heads_plane * HEAD
-    piece = tile_rows // t
-    tile_term = tile_term.reshape(t, piece, cols)
-    tile_sum = lax.dynamic_index_in_dim(tile_term, core, 0, False)
-    for s in range(1, t):
-        there = lax.dynamic_index_in_dim(tile_term, (core + s) % t, 0, False)
-        tile_sum = tile_sum + lax.ppermute(there.astype(BF16), "tp", shifts(t, s)).astype(F32)
-    tiles = lax.all_gather(tile_sum.astype(BF16), "ctx")
-    planes_here = PLANES // t
-    tiles = jnp.stack(tp_split(tiles.reshape(t, planes_here, in_plane, piece, cols)))
-    grad_weight = tiles.transpose(1, 0, 3, 2, 4).reshape(width, model).astype(F32)
-
-    (attention,) = to_tokens(attn)
-    projected = dot(attention, out_weight)
-    own = lax.dynamic_slice_in_dim(projected, core * half, half, 1)
-    for s in range(1, t):
-        there = lax.dynamic_slice_in_dim(projected, (core + s) % t * half, half, 1)
-        own = own + lax.ppermute(there.astype(BF16), "tp", shifts(t, s)).astype(F32)
-    attention_out = own.astype(BF16)
+    got_attn = plane_swap(lambda _: attn)[:heads_plane]
 
     dq, dkv = pl.pallas_call(
         functools.partial(backward_kernel, t, tile, count),
@@ -300,10 +333,41 @@
         ],
         compiler_params=params,
         cost_estimate=pl.CostEstimate(
-            flops=tiles_q * tile * tiles_k * tile * HEAD * 5, bytes_accessed=8 * 2**20, transcendentals=2**22
+            flops=20 * 10**9, bytes_accessed=8 * 2**20, transcendentals=2**22
         ),
         name="backward",
     )(full, kcnt, kidx, qkv, g_heads, attn, lse, *part_arrays)
+
+    got_attn, dq, dkv = lax.optimization_barrier((got_attn, dq, dkv))
+
+    plane_attn = jnp.stack([a.reshape(n * sub, HEAD) for a in got_attn])
+    tile_term = jnp.einsum("hrd,rc->hdc", plane_attn, slice_grad, preferred_element_type=F32)
+    tile_term = tile_term.reshape(heads_plane * HEAD, cols)
+    tile_rows = heads_plane * HEAD
+    planes_here = PLANES // t
+    if in_plane == 4 and t == 2:
+        tile_sum = tile_term
+        for s in range(1, t):
+            tile_sum = tile_sum + lax.ppermute(tile_term.astype(BF16), "tp", shifts(t, s)).astype(F32)
+        grad_weight = gather_tiles_by_core(n, t, tile_sum.astype(BF16), chip, core)
+    else:
+        piece = tile_rows // t
+        tile_term = tile_term.reshape(t, piece, cols)
+        tile_sum = lax.dynamic_index_in_dim(tile_term, core, 0, False)
+        for s in range(1, t):
+            there = lax.dynamic_index_in_dim(tile_term, (core + s) % t, 0, False)
+            tile_sum = tile_sum + lax.ppermute(there.astype(BF16), "tp", shifts(t, s)).astype(F32)
+        tiles = lax.all_gather(tile_sum.astype(BF16), "ctx")
+        tiles = jnp.stack(tp_split(tiles.reshape(t, planes_here, in_plane, piece, cols)))
+        grad_weight = tiles.transpose(1, 0, 3, 2, 4).reshape(width, model).astype(F32)
+
+    (attention,) = to_tokens(attn)
+    projected = dot(attention, out_weight)
+    own = lax.dynamic_slice_in_dim(projected, core * half, half, 1)
+    for s in range(1, t):
+        there = lax.dynamic_slice_in_dim(projected, (core + s) % t * half, half, 1)
+        own = own + lax.ppermute(there.astype(BF16), "tp", shifts(t, s)).astype(F32)
+    attention_out = own.astype(BF16)
 
     sums = dkv[0].astype(F32)
     for s in range(1, t):

time: 307 us -> 287 us (0.935)
  starting transfers between devices: 29.6 us -> 63.4 us
  local copies, waits for them, and re-layouts: 55.2 us -> 28.8 us
  blocking collectives: 21.5 us -> 0 us
  other arithmetic: 25.9 us -> 18.8 us
  waiting for transfers between devices: 108 us -> 102 us
  Pallas kernels: 38 us -> 43.5 us
    ppermute x1 -> x11, waiting for transfers between devices: 1.21 us -> 58.5 us  [the longest x9 30.2 us: swap(): return lax.ppermute(x, 'ctx', [(i, i ^ k) for i in range(n)])]
    all_to_all x2, waiting for transfers between devices: 50.6 us -> 0.01 us  [to_tokens(): got = lax.all_to_all(pack, 'ctx', 0, 0, tiled=True)]
    ppermute x6, waiting for transfers between devices: 35.3 us -> 0.02 us  [plane_swap(): lax.ppermute(pick(seat ^ k), 'ctx', [(i, i ^ k) for i in range(n)])]
    all_to_all x1 -> x0, blocking collectives: 21.5 us -> none  [to_heads(): lax.all_to_all(sent.reshape((n,) + every.shape[2:]), 'ctx', 0, 0, tiled=T...]
    ppermute x1 -> x11, starting transfers between devices: 0.83 us -> 20.8 us  [the longest x9 18.9 us: swap(): return lax.ppermute(x, 'ctx', [(i, i ^ k) for i in range(n)])]
    all_to_all x1 -> x2, waiting for transfers between devices: 14.8 us -> 31 us  [to_heads(): lax.all_to_all(sent.reshape((n,) + every.shape[2:]), 'ctx', 0, 0, tiled=T...]
    convert_element_type x2 -> x0, local copies, waits for them, and re-layouts: 13.5 us -> none  [the longest x1 13.4 us: per_device(): tiles.transpose(1, 0, 3, 2, 4).reshape(width, model).astype(F32)]
    all_gather x1, waiting for transfers between devices: 2.06 us -> 10.9 us  [per_device(): slice_grad = lax.all_gather(plane_grad, 'ctx', axis_index_groups=lines)]
  transfers between devices with their start and end apart: 21 -> 30, of which waited for: 13 -> 13; matrix products, arithmetic and copies ran while one was open for 16% -> 16% of each run, Pallas kernels for 12% -> 15%
where the time goes in v3:
time: 287 us; the launch traced here: 284 us
  waiting for transfers between devices  102 us (36%)
  starting transfers between devices  63.4 us (22%)
  Pallas kernels  43.5 us (15%)
  local copies, waits for them, and re-layouts  28.8 us (10%)
  other arithmetic  18.8 us (7%)
  between operations  14.6 us (5%)
  matrix products  12.2 us (4%)
    all_to_all x2, waiting for transfers between devices, to_heads(): lax.all_to_all(sent.reshape((n,) + every.shape[2:]), 'ctx', 0, 0, tiled=T...  31 us
    ppermute x9, waiting for transfers between devices, swap(): return lax.ppermute(x, 'ctx', [(i, i ^ k) for i in range(n)])  30.2 us
    ppermute x1, waiting for transfers between devices, gather_tiles_by_core(): from_half = lax.ppermute(tile_sum, ('ctx', 'tp'), across)  28.3 us
    pallas_call x1, Pallas kernels, per_device(): pl.pallas_call(functools.partial(backward_kernel, t, tile, count), grid_s...  21.7 us
    ppermute x9, starting transfers between devices, swap(): return lax.ppermute(x, 'ctx', [(i, i ^ k) for i in range(n)])  18.9 us
    pallas_call x1, Pallas kernels, per_device(): pl.pallas_call(functools.partial(forward_kernel, t, tile, count), grid_sp...  16.4 us
    all_to_all x2, starting transfers between devices, to_tokens(): got = lax.all_to_all(pack, 'ctx', 0, 0, tiled=True)  12 us
    all_to_all x2, starting transfers between devices, to_heads(): lax.all_to_all(sent.reshape((n,) + every.shape[2:]), 'ctx', 0, 0, tiled=T...  11.1 us
  transfers between devices with their start and end apart: 30, of which 13 were waited for; matrix products, arithmetic and copies ran while one was open for 16% of the time, Pallas kernels for 15%

profile of v3, /device:TPU:13, one launch (start us, length us, event | category | flops | bytes accessed | tf_op | source)
XLA Modules:
  0.0 283.5 jit_solution(14525280043568120544)
XLA Ops:
  11.2 2.7 constant_dynamic-slice_fusion.1
  18.8 6.7 %all-to-all-start = ((bf16[16,3,128,128]{3,2,1,0:T(8,128)(2,1)}), bf16[16,3,128,128]{3,2,1,0:T(8,128)(2,1)S(1)}, u32[]{:S(2)}, u32[]{:S(2)}) async-start(bf16[16,3,128,128]{3,2,1,0:T(8,128)(2,1)} %bitcast.9), calls=%async_computation | async-start | bytes 3145728 | tf_op jit(solution)/shard_map/all_to_all | solution.py:243
  34.8 27.6 %all-to-all-done.q_ref.refs_0_.refs_1_ = bf16[16,3,128,128]{3,2,1,0:T(8,128)(2,1)S(1)} async-done(((bf16[16,3,128,128]{3,2,1,0:T(8,128)(2,1)}), bf16[16,3,128,128]{3,2,1,0:T(8,128)(2,1)S(1)}, u32[]{:S(2)}, u32[]{:S(2)}) %all-to-all-start) | async-done | bytes 1572896 | tf_op jit(solution)/shard_map/all_to_all | solution.py:243
  63.8 3.8 %fusion.2 = bf16[256,768]{1,0:T(8,128)(2,1)S(1)} fusion(bf16[768,3072]{1,0:T(8,128)(2,1)} %param.11, bf16[256,1536]{1,0:T(8,128)(2,1)S(1)} %get-tuple-element.68, bf16[256,1536]{1,0:T(8,128)(2,1)S(1)} %get-tuple-element.67), kind=kOutput, calls=%fused_computation.22 | convolution fusion | flops 1211301888 | bytes 6684672 | tf_op jit(solution)/shard_map/dot_general | solution.py:27
  79.4 4.4 %all-to-all-start.2 = ((bf16[16,1,128,128]{3,2,1,0:T(8,128)(2,1)}), bf16[16,1,128,128]{3,2,1,0:T(8,128)(2,1)S(1)}, u32[]{:S(2)}, u32[]{:S(2)}) async-start(bf16[16,1,128,128]{3,2,1,0:T(8,128)(2,1)} %bitcast.25), calls=%async_computation.2 | async-start | bytes 1048576 | tf_op jit(solution)/shard_map/all_to_all | solution.py:243
  83.8 16.4 %forward.1 = (bf16[16,1,128,128]{3,2,1,0:T(8,128)(2,1)}, f32[2048,128]{1,0:T(8,128)S(1)}) custom-call(s32[16]{0:T(128)S(1)} %get-tuple-element.53.full_ref, s32[16]{0:T(128)S(1)} %get-tuple-element.49.kcnt_ref, s32[16,10]{1,0:T(8,128)S(1)} %copy.113.kidx_ref, bf16[16,3,128,128]{3,2,1,0:T(8,128)(2,1)S(1)} %all-to-all-done.q_ref.refs_0_.refs_1_, ...), custom_call_target="tpu_custom_call" | custom-call | flops 16000000000 | bytes 5242880 | tf_op jit(solution)/shard_map/forward/pallas_call | solution.py:299
  103.8 3.4 %all-to-all-done.2.g_ref = bf16[16,1,128,128]{3,2,1,0:T(8,128)(2,1)S(1)} async-done(((bf16[16,1,128,128]{3,2,1,0:T(8,128)(2,1)}), bf16[16,1,128,128]{3,2,1,0:T(8,128)(2,1)S(1)}, u32[]{:S(2)}, u32[]{:S(2)}) %all-to-all-start.2) | async-done | bytes 524320 | tf_op jit(solution)/shard_map/all_to_all | solution.py:243
  108.4 21.7 %backward.1 = (bf16[16,1,128,128]{3,2,1,0:T(8,128)(2,1)S(1)}, bf16[2,2,16,128,128]{4,3,2,1,0:T(8,128)(2,1)}) custom-call(s32[16]{0:T(128)S(1)} %get-tuple-element.53.full_ref, s32[16]{0:T(128)S(1)} %get-tuple-element.49.kcnt_ref, s32[16,10]{1,0:T(8,128)S(1)} %copy.113.kidx_ref, bf16[16,3,128,128]{3,2,1,0:T(8,128)(2,1)S(1)} %all-to-all-done.q_ref.refs_0_.refs_1_, ...), custom_call_target="tpu_custom_call" | custom-call | flops 20000000000 | bytes 8388608 | tf_op jit(solution)/shard_map/backward/pallas_call | solution.py:321
  133.2 5.0 %collective-permute-start.9 = (bf16[2,16,128,128]{3,2,1,0:T(8,128)(2,1)}, bf16[2,16,128,128]{3,2,1,0:T(8,128)(2,1)}, u32[]{:S(2)}, u32[]{:S(2)}) collective-permute-start(bf16[2,16,128,128]{3,2,1,0:T(8,128)(2,1)} %slice_bitcast_fusion), channel_id=1, source_target_pairs={{0,1},{1,0},{2,3},{3,2},{4,5},{5,4},{6,7},{7,6},{8,9},{9,8},{10,11... | collective-permute-start | bytes 3145736 | tf_op jit(solution)/shard_map/ppermute | solution.py:375
  138.1 4.3 %all-to-all-start.1 = ((bf16[16,1,128,128]{3,2,1,0:T(8,128)(2,1)}), bf16[16,1,128,128]{3,2,1,0:T(8,128)(2,1)S(1)}, u32[]{:S(2)}, u32[]{:S(2)}) async-start(bf16[16,1,128,128]{3,2,1,0:T(8,128)(2,1)} %get-tuple-element.15.o_ref), calls=%async_computation.1 | async-start | bytes 1048576 | tf_op jit(solution)/shard_map/all_to_all | solution.py:246
  144.5 10.9 %all-gather.3.cloned.1.call-done = bf16[16,128,768]{2,1,0:T(8,128)(2,1)} async-done(((bf16[4,128,768]{2,1,0:T(8,128)(2,1)}), bf16[16,128,768]{2,1,0:T(8,128)(2,1)}) %all-gather.3.cloned.1.call-update) | async-done | bytes 3145744 | tf_op jit(solution)/shard_map/all_gather | solution.py:287
  155.4 4.7 %fusion.22 = (bf16[384,768]{1,0:T(8,128)(2,1)}, f32[384,768]{1,0:T(8,128)S(1)}) fusion(bf16[384,2048]{1,0:T(8,128)(2,1)} %bitcast.145, bf16[2048,768]{1,0:T(8,128)(2,1)} %bitcast.157), kind=kOutput, calls=%fused_computation.102 | convolution fusion | flops 1208254464 | bytes 6488064 | tf_op jit(solution)/shard_map/hrd,rc->hdc/dot_general | solution.py:344
  163.6 7.6 %all-to-all-start.3 = ((bf16[16,3,128,128]{3,2,1,0:T(8,128)(2,1)}), bf16[16,3,128,128]{3,2,1,0:T(8,128)(2,1)}, u32[]{:S(2)}, u32[]{:S(2)}) async-start(bf16[16,3,128,128]{3,2,1,0:T(8,128)(2,1)} %copy.122), calls=%async_computation.3 | async-start | bytes 3145728 | tf_op jit(solution)/shard_map/all_to_all | solution.py:246
  174.0 3.7 %collective-permute-start.2 = (bf16[6,1,128,128]{3,2,0,1:T(8,128)(2,1)S(1)}, bf16[6,1,128,128]{3,2,0,1:T(8,128)(2,1)S(1)}, u32[]{:S(2)}, u32[]{:S(2)}) collective-permute-start(bf16[6,1,128,128]{3,2,0,1:T(8,128)(2,1)S(1)} %dynamic-slice_bitcast_fusion.3), channel_id=1, source_target_pairs={{0,1},{1,0},{2,3},{3,2},{4,5},{5,4},{6,7},{7,6},{8,9},{9,8},{10,11... | collective-permute-start | bytes 589832 | tf_op jit(solution)/shard_map/ppermute | solution.py:220
  179.3 28.3 %collective-permute-done.15 = bf16[384,768]{1,0:T(8,128)(2,1)S(1)} collective-permute-done((bf16[384,768]{1,0:T(8,128)(2,1)S(1)}, bf16[384,768]{1,0:T(8,128)(2,1)S(1)}, u32[]{:S(2)}, u32[]{:S(2)}) %collective-permute-start.15) | collective-permute-done | bytes 589856 | tf_op jit(solution)/shard_map/ppermute | solution.py:175
  207.7 14.8 %collective-permute-start.20 = (bf16[384,768]{1,0:T(8,128)(2,1)S(1)}, bf16[384,768]{1,0:T(8,128)(2,1)S(1)}, u32[]{:S(2)}, u32[]{:S(2)}) collective-permute-start(bf16[384,768]{1,0:T(8,128)(2,1)S(1)} %broadcast_select_fusion.2.refs_0_), channel_id=1, source_target_pairs={{0,8},{2,10},{4,12},{6,14},{8,0},{10,2},{12,4},{14,6},{16,24},{18,... | collective-permute-start | bytes 1769480 | tf_op jit(solution)/shard_map/ppermute | solution.py:178
  222.4 3.8 %fusion.10 = f32[256,3072]{1,0:T(8,128)S(1)} fusion(bf16[768,3072]{1,0:T(8,128)(2,1)} %param.11, bf16[96,8,2,128]{3,2,1,0:T(2,128)(2,1)S(1)} %bitcast.137), kind=kOutput, calls=%fused_computation.49 | convolution fusion | flops 1207959552 | bytes 8257536 | tf_op jit(solution)/shard_map/dot_general | solution.py:27
  227.8 7.3 %collective-permute-done.20.refs_5_ = bf16[384,768]{1,0:T(8,128)(2,1)S(1)} collective-permute-done((bf16[384,768]{1,0:T(8,128)(2,1)S(1)}, bf16[384,768]{1,0:T(8,128)(2,1)S(1)}, u32[]{:S(2)}, u32[]{:S(2)}) %collective-permute-start.20) | collective-permute-done | bytes 589856 | tf_op jit(solution)/shard_map/ppermute | solution.py:178
  237.6 4.1 %collective-permute-done.17.refs_2_ = bf16[384,768]{1,0:T(8,128)(2,1)S(1)} collective-permute-done((bf16[384,768]{1,0:T(8,128)(2,1)S(1)}, bf16[384,768]{1,0:T(8,128)(2,1)S(1)}, u32[]{:S(2)}, u32[]{:S(2)}) %collective-permute-start.17) | collective-permute-done | bytes 589856 | tf_op jit(solution)/shard_map/ppermute | solution.py:178
  241.7 2.3 collective-permute-start.10
  244.7 9.7 %collective-permute-done.22.refs_7_ = bf16[384,768]{1,0:T(8,128)(2,1)S(1)} collective-permute-done((bf16[384,768]{1,0:T(8,128)(2,1)S(1)}, bf16[384,768]{1,0:T(8,128)(2,1)S(1)}, u32[]{:S(2)}, u32[]{:S(2)}) %collective-permute-start.22) | collective-permute-done | bytes 589856 | tf_op jit(solution)/shard_map/ppermute | solution.py:178
  256.4 2.2 add_convert_fusion
  261.5 5.5 %collective-permute-done.24.refs_9_ = bf16[192,768]{1,0:T(8,128)(2,1)S(1)} collective-permute-done((bf16[192,768]{1,0:T(8,128)(2,1)S(1)}, bf16[192,768]{1,0:T(8,128)(2,1)S(1)}, u32[]{:S(2)}, u32[]{:S(2)}) %collective-permute-start.24) | collective-permute-done | bytes 294944 | tf_op jit(solution)/shard_map/ppermute | solution.py:178
  267.8 5.4 %place.1 = f32[768,3072]{1,0:T(8,128)} custom-call(s32[2]{0:T(128)S(1)} %pad_add_fusion.1.place_ref, bf16[384,768]{1,0:T(8,128)(2,1)S(1)} %broadcast_select_fusion.2.refs_0_, bf16[384,768]{1,0:T(8,128)(2,1)S(1)} %collective-permute-done.16.refs_1_, bf16[384,768]{1,0:T(8,128)(2,1)S(1)} %collective-permute-done.17.refs_2_, ...), custom_call_target="tpu_custom_call" | custom-call | tf_op jit(solution)/shard_map/place/pallas_call | solution.py:188
  (137 shorter events, 62.7 us)
Async XLA Ops:
  18.8 43.6 %all-to-all-start = ((bf16[16,3,128,128]{3,2,1,0:T(8,128)(2,1)}), bf16[16,3,128,128]{3,2,1,0:T(8,128)(2,1)S(1)}, u32[]{:S(2)}, u32[]{:S(2)}) async-start(bf16[16,3,128,128]{3,2,1,0:T(8,128)(2,1)} %bitcast.9), calls=%async_computation | async-start | bytes 3145728 | tf_op jit(solution)/shard_map/all_to_all | solution.py:243
  25.5 129.9 %all-gather.3.cloned.1.call-start = ((), (), s32[]{:S(2)}) async-start(), calls=%async_computation.4 | async-start | bytes 3932160 | tf_op jit(solution)/shard_map/all_gather | solution.py:287
  32.1 42.3 %collective-permute-start.11 = (bf16[128,768]{1,0:T(8,128)(2,1)}, bf16[128,768]{1,0:T(8,128)(2,1)}, u32[]{:S(2)}, u32[]{:S(2)}) collective-permute-start(bf16[128,768]{1,0:T(8,128)(2,1)} %get-tuple-element.64), channel_id=1, source_target_pairs={{0,2},{2,0},{4,6},{6,4},{8,10},{10,8},{12,14},{14,12},{16,18},{18,... | collective-permute-start | bytes 589832 | tf_op jit(solution)/shard_map/ppermute | solution.py:232
  33.3 41.1 %collective-permute-start.12 = (bf16[128,768]{1,0:T(8,128)(2,1)}, bf16[128,768]{1,0:T(8,128)(2,1)}, u32[]{:S(2)}, u32[]{:S(2)}) collective-permute-start(bf16[128,768]{1,0:T(8,128)(2,1)} %get-tuple-element.65), channel_id=1, source_target_pairs={{0,4},{2,6},{4,0},{6,2},{8,12},{10,14},{12,8},{14,10},{16,20},{18,... | collective-permute-start | bytes 589832 | tf_op jit(solution)/shard_map/ppermute | solution.py:232
  33.6 40.8 %collective-permute-start.13 = (bf16[128,768]{1,0:T(8,128)(2,1)}, bf16[128,768]{1,0:T(8,128)(2,1)}, u32[]{:S(2)}, u32[]{:S(2)}) collective-permute-start(bf16[128,768]{1,0:T(8,128)(2,1)} %get-tuple-element.66), channel_id=1, source_target_pairs={{0,6},{2,4},{4,2},{6,0},{8,14},{10,12},{12,10},{14,8},{16,22},{18,... | collective-permute-start | bytes 589832 | tf_op jit(solution)/shard_map/ppermute | solution.py:232
  62.4 21.4 %collective-permute-start.1 = (bf16[16,3,128,128]{3,2,1,0:T(8,128)(2,1)S(1)}, bf16[16,3,128,128]{3,2,1,0:T(8,128)(2,1)}, u32[]{:S(2)}, u32[]{:S(2)}) collective-permute-start(bf16[16,3,128,128]{3,2,1,0:T(8,128)(2,1)S(1)} %all-to-all-done.q_ref.refs_0_.refs_1_), channel_id=1, source_target_pairs={{0,1},{1,0},{2,3},{3,2},{4,5},{5,4},{6,7},{7,6},{8,9},{9,8},{10,11... | collective-permute-start | bytes 4718600 | tf_op jit(solution)/shard_map/ppermute | solution.py:290
  79.4 27.7 %all-to-all-start.2 = ((bf16[16,1,128,128]{3,2,1,0:T(8,128)(2,1)}), bf16[16,1,128,128]{3,2,1,0:T(8,128)(2,1)S(1)}, u32[]{:S(2)}, u32[]{:S(2)}) async-start(bf16[16,1,128,128]{3,2,1,0:T(8,128)(2,1)} %bitcast.25), calls=%async_computation.2 | async-start | bytes 1048576 | tf_op jit(solution)/shard_map/all_to_all | solution.py:243
  101.1 28.9 %collective-permute-start.6 = (bf16[16,1,128,128]{3,2,1,0:T(8,128)(2,1)}, bf16[16,1,128,128]{3,2,1,0:T(8,128)(2,1)S(1)}, u32[]{:S(2)}, u32[]{:S(2)}) collective-permute-start(bf16[16,1,128,128]{3,2,1,0:T(8,128)(2,1)} %get-tuple-element.15.o_ref), channel_id=1, source_target_pairs={{0,6},{2,4},{4,2},{6,0},{8,14},{10,12},{12,10},{14,8},{16,22},{18,... | collective-permute-start | bytes 1572872 | tf_op jit(solution)/shard_map/ppermute | solution.py:232
  102.3 27.8 %collective-permute-start.5 = (bf16[16,1,128,128]{3,2,1,0:T(8,128)(2,1)}, bf16[16,1,128,128]{3,2,1,0:T(8,128)(2,1)}, u32[]{:S(2)}, u32[]{:S(2)}) collective-permute-start(bf16[16,1,128,128]{3,2,1,0:T(8,128)(2,1)} %get-tuple-element.15.o_ref), channel_id=1, source_target_pairs={{0,4},{2,6},{4,0},{6,2},{8,12},{10,14},{12,8},{14,10},{16,20},{18,... | collective-permute-start | bytes 1572872 | tf_op jit(solution)/shard_map/ppermute | solution.py:232
  103.5 26.6 %collective-permute-start.4 = (bf16[16,1,128,128]{3,2,1,0:T(8,128)(2,1)}, bf16[16,1,128,128]{3,2,1,0:T(8,128)(2,1)}, u32[]{:S(2)}, u32[]{:S(2)}) collective-permute-start(bf16[16,1,128,128]{3,2,1,0:T(8,128)(2,1)} %get-tuple-element.15.o_ref), channel_id=1, source_target_pairs={{0,2},{2,0},{4,6},{6,4},{8,10},{10,8},{12,14},{14,12},{16,18},{18,... | collective-permute-start | bytes 1572872 | tf_op jit(solution)/shard_map/ppermute | solution.py:232
  133.2 27.4 %collective-permute-start.9 = (bf16[2,16,128,128]{3,2,1,0:T(8,128)(2,1)}, bf16[2,16,128,128]{3,2,1,0:T(8,128)(2,1)}, u32[]{:S(2)}, u32[]{:S(2)}) collective-permute-start(bf16[2,16,128,128]{3,2,1,0:T(8,128)(2,1)} %slice_bitcast_fusion), channel_id=1, source_target_pairs={{0,1},{1,0},{2,3},{3,2},{4,5},{5,4},{6,7},{7,6},{8,9},{9,8},{10,11... | collective-permute-start | bytes 3145736 | tf_op jit(solution)/shard_map/ppermute | solution.py:375
  138.1 25.5 %all-to-all-start.1 = ((bf16[16,1,128,128]{3,2,1,0:T(8,128)(2,1)}), bf16[16,1,128,128]{3,2,1,0:T(8,128)(2,1)S(1)}, u32[]{:S(2)}, u32[]{:S(2)}) async-start(bf16[16,1,128,128]{3,2,1,0:T(8,128)(2,1)} %get-tuple-element.15.o_ref), calls=%async_computation.1 | async-start | bytes 1048576 | tf_op jit(solution)/shard_map/all_to_all | solution.py:246
  163.6 72.6 %all-to-all-start.3 = ((bf16[16,3,128,128]{3,2,1,0:T(8,128)(2,1)}), bf16[16,3,128,128]{3,2,1,0:T(8,128)(2,1)}, u32[]{:S(2)}, u32[]{:S(2)}) async-start(bf16[16,3,128,128]{3,2,1,0:T(8,128)(2,1)} %copy.122), calls=%async_computation.3 | async-start | bytes 3145728 | tf_op jit(solution)/shard_map/all_to_all | solution.py:246
  172.5 35.1 %collective-permute-start.15 = (bf16[384,768]{1,0:T(8,128)(2,1)S(1)}, bf16[384,768]{1,0:T(8,128)(2,1)S(1)}, u32[]{:S(2)}, u32[]{:S(2)}) collective-permute-start(bf16[384,768]{1,0:T(8,128)(2,1)S(1)} %add_convert_fusion.1), channel_id=1, source_target_pairs={{0,16},{2,18},{4,20},{6,22},{8,24},{10,26},{12,28},{14,30},{17,1},... | collective-permute-start | bytes 1769480 | tf_op jit(solution)/shard_map/ppermute | solution.py:175
  207.7 27.4 %collective-permute-start.20 = (bf16[384,768]{1,0:T(8,128)(2,1)S(1)}, bf16[384,768]{1,0:T(8,128)(2,1)S(1)}, u32[]{:S(2)}, u32[]{:S(2)}) collective-permute-start(bf16[384,768]{1,0:T(8,128)(2,1)S(1)} %broadcast_select_fusion.2.refs_0_), channel_id=1, source_target_pairs={{0,8},{2,10},{4,12},{6,14},{8,0},{10,2},{12,4},{14,6},{16,24},{18,... | collective-permute-start | bytes 1769480 | tf_op jit(solution)/shard_map/ppermute | solution.py:178
  227.3 27.7 %collective-permute-start.3 = (bf16[256,1536]{1,0:T(8,128)(2,1)}, bf16[256,1536]{1,0:T(8,128)(2,1)}, u32[]{:S(2)}, u32[]{:S(2)}) collective-permute-start(bf16[256,1536]{1,0:T(8,128)(2,1)} %dynamic-slice_convert_fusion), channel_id=1, source_target_pairs={{0,1},{1,0},{2,3},{3,2},{4,5},{5,4},{6,7},{7,6},{8,9},{9,8},{10,11... | collective-permute-start | bytes 2359304 | tf_op jit(solution)/shard_map/ppermute | solution.py:369
  227.3 14.4 %collective-permute-start.17 = (bf16[384,768]{1,0:T(8,128)(2,1)S(1)}, bf16[384,768]{1,0:T(8,128)(2,1)S(1)}, u32[]{:S(2)}, u32[]{:S(2)}) collective-permute-start(bf16[384,768]{1,0:T(8,128)(2,1)S(1)} %broadcast_select_fusion.2.refs_0_), channel_id=1, source_target_pairs={{0,4},{2,6},{4,0},{6,2},{8,12},{10,14},{12,8},{14,10},{16,20},{18,... | collective-permute-start | bytes 1769480 | tf_op jit(solution)/shard_map/ppermute | solution.py:178
  227.3 16.8 %collective-permute-start.16 = (bf16[384,768]{1,0:T(8,128)(2,1)S(1)}, bf16[384,768]{1,0:T(8,128)(2,1)S(1)}, u32[]{:S(2)}, u32[]{:S(2)}) collective-permute-start(bf16[384,768]{1,0:T(8,128)(2,1)S(1)} %broadcast_select_fusion.2.refs_0_), channel_id=1, source_target_pairs={{0,2},{2,0},{4,6},{6,4},{8,10},{10,8},{12,14},{14,12},{16,18},{18,... | collective-permute-start | bytes 1769480 | tf_op jit(solution)/shard_map/ppermute | solution.py:178
  235.0 19.3 %collective-permute-start.22 = (bf16[384,768]{1,0:T(8,128)(2,1)S(1)}, bf16[384,768]{1,0:T(8,128)(2,1)S(1)}, u32[]{:S(2)}, u32[]{:S(2)}) collective-permute-start(bf16[384,768]{1,0:T(8,128)(2,1)S(1)} %collective-permute-done.20.refs_5_), channel_id=1, source_target_pairs={{0,4},{2,6},{4,0},{6,2},{8,12},{10,14},{12,8},{14,10},{16,20},{18,... | collective-permute-start | bytes 1769480 | tf_op jit(solution)/shard_map/ppermute | solution.py:178
  235.1 19.6 %collective-permute-start.21 = (bf16[384,768]{1,0:T(8,128)(2,1)S(1)}, bf16[384,768]{1,0:T(8,128)(2,1)S(1)}, u32[]{:S(2)}, u32[]{:S(2)}) collective-permute-start(bf16[384,768]{1,0:T(8,128)(2,1)S(1)} %collective-permute-done.20.refs_5_), channel_id=1, source_target_pairs={{0,2},{2,0},{4,6},{6,4},{8,10},{10,8},{12,14},{14,12},{16,18},{18,... | collective-permute-start | bytes 1769480 | tf_op jit(solution)/shard_map/ppermute | solution.py:178
  241.7 31.5 %collective-permute-start.10 = (bf16[6,3,128,128]{3,2,1,0:T(8,128)(2,1)S(1)}, bf16[6,3,128,128]{3,2,1,0:T(8,128)(2,1)S(1)}, u32[]{:S(2)}, u32[]{:S(2)}) collective-permute-start(bf16[6,3,128,128]{3,2,1,0:T(8,128)(2,1)S(1)} %dynamic-slice_bitcast_fusion), channel_id=1, source_target_pairs={{0,1},{1,0},{2,3},{3,2},{4,5},{5,4},{6,7},{7,6},{8,9},{9,8},{10,11... | collective-permute-start | bytes 1769480 | tf_op jit(solution)/shard_map/ppermute | solution.py:220
  244.1 16.5 %collective-permute-start.19 = (bf16[192,768]{1,0:T(8,128)(2,1)S(1)}, bf16[192,768]{1,0:T(8,128)(2,1)S(1)}, u32[]{:S(2)}, u32[]{:S(2)}) collective-permute-start(bf16[192,768]{1,0:T(8,128)(2,1)S(1)} %slice.55), channel_id=1, source_target_pairs={{0,2},{2,0},{4,6},{6,4},{8,10},{10,8},{12,14},{14,12},{16,18},{18,... | collective-permute-start | bytes 884744 | tf_op jit(solution)/shard_map/ppermute | solution.py:178
  254.7 12.3 %collective-permute-start.24 = (bf16[192,768]{1,0:T(8,128)(2,1)S(1)}, bf16[192,768]{1,0:T(8,128)(2,1)S(1)}, u32[]{:S(2)}, u32[]{:S(2)}) collective-permute-start(bf16[192,768]{1,0:T(8,128)(2,1)S(1)} %slice.57), channel_id=1, source_target_pairs={{0,2},{2,0},{4,6},{6,4},{8,10},{10,8},{12,14},{14,12},{16,18},{18,... | collective-permute-start | bytes 884744 | tf_op jit(solution)/shard_map/ppermute | solution.py:178
  255.0 12.8 %collective-permute-start.23 = (bf16[192,768]{1,0:T(8,128)(2,1)S(1)}, bf16[192,768]{1,0:T(8,128)(2,1)S(1)}, u32[]{:S(2)}, u32[]{:S(2)}) collective-permute-start(bf16[192,768]{1,0:T(8,128)(2,1)S(1)} %slice.56), channel_id=1, source_target_pairs={{0,4},{2,6},{4,0},{6,2},{8,12},{10,14},{12,8},{14,10},{16,20},{18,... | collective-permute-start | bytes 884744 | tf_op jit(solution)/shard_map/ppermute | solution.py:178
  (17 other events, 101.5 us)
Sparse Core Ops, SparseCore 0:
  78.6 76.8 all-gather.2

commit v4 on v3

--- a/solution.py
+++ b/solution.py
@@ -40,10 +40,85 @@
         v_all[at] = parts[2 * s + 1][...].reshape(shape)
 
 
+def head_of(chip, in_plane, heads_plane):
+    place = (chip % in_plane + in_plane - chip // in_plane % in_plane) % in_plane
+    return place < heads_plane, chip // in_plane * heads_plane + jnp.minimum(place, heads_plane - 1)
+
+
+def pack_kernel(n, t, where_ref, *refs):
+    arrays, got, outs, heads_all = refs[:4], refs[4:4 + 2 * (t - 1)], refs[4 + 2 * (t - 1):-1], refs[-1]
+    chip, core = where_ref[0], where_ref[1]
+    sub = heads_all.shape[2]
+    heads_here = heads_all.shape[0] // t
+    for a in range(4):
+        for h in range(heads_here):
+            column = pl.ds(h * HEAD, HEAD)
+            heads_all[core * heads_here + h, a] = arrays[a][pl.ds(core * sub, sub), column]
+            for s in range(1, t):
+                first = (core + t - s) % t * heads_here
+                source = got[2 * (s - 1)] if a < 3 else got[2 * (s - 1) + 1]
+                heads_all[first + h, a] = source[a % 3, :, column]
+    for k in range(n):
+        _, head = head_of(chip ^ k, n // PLANES, heads_all.shape[0] // PLANES)
+        outs[k][...] = heads_all[head]
+
+
+def join_kernel(n, where_ref, *refs):
+    chunks, (qg_ref, kv_ref) = refs[:n], refs[n:]
+    chip = where_ref[0]
+    for k in range(n):
+        sub = chunks[k].shape[1]
+        at = pl.ds(pl.multiple_of((chip ^ k) * sub, sub), sub)
+        qg_ref[0, at] = chunks[k][0]
+        kv_ref[0, at] = chunks[k][1]
+        kv_ref[1, at] = chunks[k][2]
+        qg_ref[1, at] = chunks[k][3]
+
+
+def unjoin_kernel(n, t, where_ref, attn_ref, dq_ref, dkv_ref, *refs):
+    got, outs = refs[:t - 1], refs[t - 1:]
+    chip = where_ref[0]
+    for k in range(n):
+        sub = outs[k].shape[1]
+        at = pl.ds(pl.multiple_of((chip ^ k) * sub, sub), sub)
+        outs[k][0] = attn_ref[at]
+        outs[k][1] = dq_ref[at]
+        for a in range(2):
+            total = dkv_ref[a, at].astype(F32)
+            for other in got:
+                total = total + other[a, at].astype(F32)
+            outs[k][2 + a] = total.astype(BF16)
+
+
+def by_core_kernel(n, t, where_ref, *refs):
+    chunks, outs, heads_all = refs[:n], refs[n:n + t], refs[-1]
+    chip, core = where_ref[0], where_ref[1]
+    heads_here = heads_all.shape[0] // t
+    for k in range(n):
+        held, head = head_of(chip ^ k, n // PLANES, heads_all.shape[0] // PLANES)
+
+        @pl.when(held)
+        def _(k=k, head=head):
+            heads_all[head] = chunks[k][...]
+    for s in range(t):
+        outs[s][...] = heads_all[pl.ds((core + s) % t * heads_here, heads_here)]
+
+
+def unpack_kernel(t, where_ref, *refs):
+    parts, outs = refs[:t], refs[t:]
+    core = where_ref[1]
+    heads_here, _, sub, _ = parts[0].shape
+    for s in range(t):
+        at = pl.ds(pl.multiple_of((core + t - s) % t * sub, sub), sub)
+        for a in range(4):
+            for h in range(heads_here):
+                outs[a][at, pl.ds(h * HEAD, HEAD)] = parts[s][h, a]
+
+
 def forward_kernel(t, tile, count, full_ref, kcnt_ref, kidx_ref, q_ref, *refs):
     parts, (out_ref, lse_ref, k_few, v_few, k_ref, v_ref) = refs[:2 * t], refs[2 * t:]
     row = pl.program_id(0)
-    q = q_ref[0, 0]
+    q = q_ref[0]
 
     @pl.when(row == 0)
     def _():
@@ -54,7 +129,7 @@
         p = jnp.exp2(s - top)
         mass = jnp.sum(p, axis=1, keepdims=True)
         out = dot(p.astype(BF16), v)
-        out_ref[0, 0] = (out / mass).astype(BF16)
+        out_ref[...] = (out / mass).astype(BF16)
         lse_ref[...] = jnp.broadcast_to(top + jnp.log2(mass), lse_ref.shape)
 
     scale = HEAD ** -0.5 * LOG2E
@@ -75,7 +150,9 @@
 
 
 def backward_kernel(t, tile, count, full_ref, kcnt_ref, kidx_ref, q_ref, g_ref, o_ref, lse_ref, *refs):
-    parts, (dq_ref, dkv_ref, k_few, v_few, k_ref, v_ref, dk_acc, dv_acc) = refs[:2 * t], refs[2 * t:]
+    parts, dkv_refs = refs[:2 * t], refs[2 * t + 1:3 * t + 1]
+    dq_ref = refs[2 * t]
+    k_few, v_few, k_ref, v_ref, dk_acc, dv_acc = refs[3 * t + 1:]
     row = pl.program_id(0)
     last = pl.num_programs(0) - 1
 
@@ -85,9 +162,9 @@
         dk_acc[...] = jnp.zeros_like(dk_acc)
         dv_acc[...] = jnp.zeros_like(dv_acc)
 
-    q = q_ref[0, 0]
-    g = g_ref[0, 0]
-    delta = jnp.sum(g.astype(F32) * o_ref[0, 0].astype(F32), axis=1, keepdims=True)
+    q = q_ref[0]
+    g = g_ref[0]
+    delta = jnp.sum(g.astype(F32) * o_ref[...].astype(F32), axis=1, keepdims=True)
     lse = lse_ref[:, :1]
     unit = HEAD ** -0.5
     scale = unit * LOG2E
@@ -98,7 +175,7 @@
         if mask is not None:
             p = jnp.where(mask(p.shape), p, 0.0)
         ds = (p * (dot(g, values, NT) - delta)).astype(BF16)
-        dq_ref[0, 0] = (dot(ds, keys) * unit).astype(BF16)
+        dq_ref[...] = (dot(ds, keys) * unit).astype(BF16)
         return dot(ds, q, TN) * unit, dot(p.astype(BF16), g, TN)
 
     @pl.when(full_ref[row] == 1)
@@ -123,24 +200,41 @@
 
     @pl.when(row == last)
     def _():
-        parts, _, chunks, rows, _ = dkv_ref.shape
-        shape = (parts, chunks, rows, HEAD)
-        dkv_ref[:, 0] = dk_acc[...].reshape(shape).astype(BF16)
-        dkv_ref[:, 1] = dv_acc[...].reshape(shape).astype(BF16)
+        tiles = dk_acc.shape[0] // t
+        for s, dkv_ref in enumerate(dkv_refs):
+            at = pl.ds(s * tiles, tiles)
+            dkv_ref[0] = dk_acc[at].reshape(dkv_ref.shape[1:]).astype(BF16)
+            dkv_ref[1] = dv_acc[at].reshape(dkv_ref.shape[1:]).astype(BF16)
 
 
 def whole_block(shape):
     return pl.BlockSpec(shape, lambda *_: (0,) * len(shape))
 
 
-def one_array(which, n, sub):
-    return pl.BlockSpec((n, 1, sub, HEAD), lambda *_: (0, which, 0, 0))
-
-
-def tile_block(which, per_chunk, tile):
-    return pl.BlockSpec(
-        (1, 1, tile, HEAD), lambda r, *_: (r // per_chunk, which, r % per_chunk, 0)
-    )
+def one_array(which, length):
+    return pl.BlockSpec((1, length, HEAD), lambda *_: (which, 0, 0))
+
+
+def tile_block(which, tile):
+    return pl.BlockSpec((1, tile, HEAD), lambda r, *_: (which, r, 0))
+
+
+def simple_call(kernel, name, scalars, inputs, outputs, scratch=()):
+    size = sum(2 * math.prod(x.shape) for x in list(inputs) + list(outputs))
+    return pl.pallas_call(
+        kernel,
+        grid_spec=pltpu.PrefetchScalarGridSpec(
+            num_scalar_prefetch=1,
+            grid=(1,),
+            in_specs=[whole_block(x.shape) for x in inputs],
+            out_specs=[whole_block(x.shape) for x in outputs],
+            scratch_shapes=scratch,
+        ),
+        out_shape=outputs,
+        compiler_params=pltpu.CompilerParams(vmem_limit_bytes=48 * 2**20),
+        cost_estimate=pl.CostEstimate(flops=0, bytes_accessed=2 * size, transcendentals=0),
+        name=name,
+    )(scalars, *inputs)
 
 
 def shifts(t, s):
@@ -232,23 +326,11 @@
             got.append(lax.ppermute(pick(seat ^ k), "ctx", [(i, i ^ k) for i in range(n)]))
         return [lax.select_n(seat ^ b, *got) for b in range(in_plane)]
 
-    def to_heads(arrays):
-        pack = jnp.stack(
-            [a.reshape(t, sub, heads_here, HEAD).transpose(0, 2, 1, 3) for a in arrays], axis=2
-        )
-        every = jnp.concatenate(tp_split(pack), axis=0)
-        every = every.reshape((PLANES, heads_plane) + every.shape[1:])
-        spare = in_plane - heads_plane
-        sent = jnp.pad(every, ((0, 0), (0, spare), (0, 0), (0, 0), (0, 0)))
-        return lax.all_to_all(sent.reshape((n,) + every.shape[2:]), "ctx", 0, 0, tiled=True)
-
-    def to_tokens(pack):
-        got = lax.all_to_all(pack, "ctx", 0, 0, tiled=True)
-        every = got.reshape((PLANES, in_plane) + got.shape[1:])[:, :heads_plane]
-        mine = jnp.stack(tp_split(every.reshape((t, heads_here) + got.shape[1:])))
-        return [
-            mine[:, :, a].transpose(0, 2, 1, 3).reshape(rows, width) for a in range(pack.shape[1])
-        ]
+    def shape(*dims):
+        return jax.ShapeDtypeStruct(dims, BF16)
+
+    where = jnp.stack([chip, core]).astype(jnp.int32)
+    held = [(i % in_plane - i // in_plane) % in_plane < heads_plane for i in range(n)]
 
     chunk_row = jnp.arange(n)[:, None] * rows + jnp.arange(per_chunk)[None, :] * tile
 
@@ -270,13 +352,24 @@
     kidx = jnp.sum(jnp.where(hit, ids[None, None, :], 0), axis=2).astype(jnp.int32)
     full = full.astype(jnp.int32)
 
-    qkv = to_heads([queries, key_vectors, value_vectors])
+    def other_rows(*arrays):
+        return [
+            lax.ppermute(
+                jnp.stack([
+                    lax.dynamic_slice_in_dim(x, (core + s) % t * sub, sub, 0) for x in arrays
+                ]),
+                "tp", shifts(t, s),
+            )
+            for s in range(1, t)
+        ]
+
+    got_qkv = other_rows(queries, key_vectors, value_vectors)
 
     half = out_grad.shape[1]
     model = half * t
     full_grad = jnp.concatenate(tp_gather(out_grad), axis=1)
     grad_attn = dot(full_grad, out_weight, NT).astype(BF16)
-    g_heads = to_heads([grad_attn])
+    got_g = other_rows(grad_attn)
 
     cols = model // in_plane
     mine = lax.dynamic_slice_in_dim(full_grad, core * sub, sub, 0)
@@ -287,58 +380,67 @@
     slice_grad = lax.all_gather(plane_grad, "ctx", axis_index_groups=lines)
     slice_grad = slice_grad.reshape(n * sub, cols)
 
-    others = [lax.ppermute(qkv, "tp", shifts(t, s)) for s in range(1, t)]
+    got = [x for pair in zip(got_qkv, got_g) for x in pair]
+    sent = simple_call(
+        functools.partial(pack_kernel, n, t), "pack", where,
+        [queries, key_vectors, value_vectors, grad_attn] + got,
+        [shape(4, sub, HEAD)] * n,
+        [pltpu.VMEM((heads, 4, sub, HEAD), BF16)],
+    )
+    chunks = [sent[0]] + [
+        lax.ppermute(sent[k], "ctx", [(i, i ^ k) for i in range(n) if held[i ^ k]]) for k in range(1, n)
+    ]
+    length = n * sub
+    qg, kv = simple_call(
+        functools.partial(join_kernel, n), "join", where, chunks, [shape(2, length, HEAD)] * 2
+    )
+    kv_all = [kv] + [lax.ppermute(kv, "tp", shifts(t, s)) for s in range(1, t)]
 
     tiles_q = n * per_chunk
     few = [pltpu.VMEM((count * tile, HEAD), BF16)] * 2 + [pltpu.VMEM((tiles_k, tile, HEAD), BF16)] * 2
     params = pltpu.CompilerParams(vmem_limit_bytes=48 * 2**20)
-    q_block = tile_block(0, per_chunk, tile)
-    part_blocks = [one_array(1, n, sub), one_array(2, n, sub)] * t
-    part_arrays = [a for pack in [qkv] + others for a in (pack, pack)]
-    lse_block = pl.BlockSpec((tile, HEAD), lambda r, *_: (r, 0))
+    part_blocks = [one_array(0, length), one_array(1, length)] * t
+    part_arrays = [a for pack in kv_all for a in (pack, pack)]
+    row_block = pl.BlockSpec((tile, HEAD), lambda r, *_: (r, 0))
     attn, lse = pl.pallas_call(
         functools.partial(forward_kernel, t, tile, count),
         grid_spec=pltpu.PrefetchScalarGridSpec(
             num_scalar_prefetch=3,
             grid=(tiles_q,),
-            in_specs=[q_block] + part_blocks,
-            out_specs=[q_block, lse_block],
+            in_specs=[tile_block(0, tile)] + part_blocks,
+            out_specs=[row_block, row_block],
             scratch_shapes=few,
         ),
-        out_shape=[
-            jax.ShapeDtypeStruct((n, 1, sub, HEAD), BF16),
-            jax.ShapeDtypeStruct((tiles_q * tile, HEAD), F32),
-        ],
+        out_shape=[shape(length, HEAD), jax.ShapeDtypeStruct((length, HEAD), F32)],
         compiler_params=params,
-        cost_estimate=pl.CostEstimate(
-            flops=16 * 10**9, bytes_accessed=5 * 2**20, transcendentals=2**22
-        ),
+        cost_estimate=pl.CostEstimate(flops=16 * 10**9, bytes_accessed=5 * 2**20, transcendentals=2**22),
         name="forward",
-    )(full, kcnt, kidx, qkv, *part_arrays)
-
-    got_attn = plane_swap(lambda _: attn)[:heads_plane]
-
-    dq, dkv = pl.pallas_call(
+    )(full, kcnt, kidx, qg, *part_arrays)
+
+    plane = chip // in_plane
+    travel = [attn] + [
+        lax.ppermute(attn, "ctx", [(i, i ^ k) for i in range(n) if held[i]]) for k in range(1, in_plane)
+    ]
+    got_attn = [
+        lax.select_n(seat ^ ((plane + j) % in_plane), *travel) for j in range(heads_plane)
+    ]
+
+    dq, *dkv = pl.pallas_call(
         functools.partial(backward_kernel, t, tile, count),
         grid_spec=pltpu.PrefetchScalarGridSpec(
             num_scalar_prefetch=3,
             grid=(tiles_q,),
-            in_specs=[q_block, q_block, q_block, lse_block] + part_blocks,
-            out_specs=[q_block, whole_block((t, 2, n, sub, HEAD))],
+            in_specs=[tile_block(0, tile), tile_block(1, tile), row_block, row_block] + part_blocks,
+            out_specs=[row_block] + [whole_block((2, length, HEAD))] * t,
             scratch_shapes=few + [pltpu.VMEM((tiles_k, tile, HEAD), F32)] * 2,
         ),
-        out_shape=[
-            jax.ShapeDtypeStruct((n, 1, sub, HEAD), BF16),
-            jax.ShapeDtypeStruct((t, 2, n, sub, HEAD), BF16),
-        ],
+        out_shape=[shape(length, HEAD)] + [shape(2, length, HEAD)] * t,
         compiler_params=params,
-        cost_estimate=pl.CostEstimate(
-            flops=20 * 10**9, bytes_accessed=8 * 2**20, transcendentals=2**22
-        ),
+        cost_estimate=pl.CostEstimate(flops=20 * 10**9, bytes_accessed=8 * 2**20, transcendentals=2**22),
         name="backward",
-    )(full, kcnt, kidx, qkv, g_heads, attn, lse, *part_arrays)
-
-    got_attn, dq, dkv = lax.optimization_barrier((got_attn, dq, dkv))
+    )(full, kcnt, kidx, qg, qg, attn, lse, *part_arrays)
+
+    got_attn, dq = lax.optimization_barrier((got_attn, dq))
 
     plane_attn = jnp.stack([a.reshape(n * sub, HEAD) for a in got_attn])
     tile_term = jnp.einsum("hrd,rc->hdc", plane_attn, slice_grad, preferred_element_type=F32)
@@ -361,7 +463,24 @@
         tiles = jnp.stack(tp_split(tiles.reshape(t, planes_here, in_plane, piece, cols)))
         grad_weight = tiles.transpose(1, 0, 3, 2, 4).reshape(width, model).astype(F32)
 
-    (attention,) = to_tokens(attn)
+    got_dkv = [
+        lax.ppermute(dkv[s], "tp", [(c, (c - s) % t) for c in range(t)]) for s in range(1, t)
+    ]
+    sent = simple_call(
+        functools.partial(unjoin_kernel, n, t), "unjoin", where,
+        [attn, dq, dkv[0]] + got_dkv, [shape(4, sub, HEAD)] * n,
+    )
+    chunks = [sent[0]] + [
+        lax.ppermute(sent[k], "ctx", [(i, i ^ k) for i in range(n) if held[i]]) for k in range(1, n)
+    ]
+    mine = simple_call(
+        functools.partial(by_core_kernel, n, t), "by_core", where, chunks,
+        [shape(heads_here, 4, sub, HEAD)] * t, [pltpu.VMEM((heads, 4, sub, HEAD), BF16)],
+    )
+    parts = [mine[0]] + [lax.ppermute(mine[s], "tp", shifts(t, s)) for s in range(1, t)]
+    attention, grad_queries, grad_keys, grad_values = simple_call(
+        functools.partial(unpack_kernel, t), "unpack", where, parts, [shape(rows, width)] * 4
+    )
     projected = dot(attention, out_weight)
     own = lax.dynamic_slice_in_dim(projected, core * half, half, 1)
     for s in range(1, t):
@@ -369,12 +488,6 @@
         own = own + lax.ppermute(there.astype(BF16), "tp", shifts(t, s)).astype(F32)
     attention_out = own.astype(BF16)
 
-    sums = dkv[0].astype(F32)
-    for s in range(1, t):
-        back = [(c, (c - s) % t) for c in range(t)]
-        sums = sums + lax.ppermute(dkv[s], "tp", back).astype(F32)
-    sums = sums.astype(BF16).transpose(1, 0, 2, 3)
-    grad_queries, grad_keys, grad_values = to_tokens(jnp.concatenate([dq, sums], axis=1))
     return attention_out, grad_queries, grad_keys, grad_values, grad_weight
 
 

time: 287 us -> 317 us (1.10)
  starting transfers between devices: 63.4 us -> 136 us
  waiting for transfers between devices: 102 us -> 77.6 us
  local copies, waits for them, and re-layouts: 28.8 us -> 11 us
  other arithmetic: 18.8 us -> 12.2 us
  Pallas kernels: 43.5 us -> 49.3 us
    ppermute x2 -> x38, starting transfers between devices: 6.38 us -> 111 us  [the longest x15 50.6 us: per_device(): lax.ppermute(sent[k], 'ctx', [(i, i ^ k) for i in range(n) if held[i]])]
    all_to_all x4 -> x0, waiting for transfers between devices: 31 us -> none  [the longest x2 31 us: to_heads(): lax.all_to_all(sent.reshape((n,) + every.shape[2:]), 'ctx', 0, 0, tiled=T...]
    ppermute x2 -> x38, waiting for transfers between devices: 0.01 us -> 26.4 us  [the longest x15 16.9 us: per_device(): lax.ppermute(sent[k], 'ctx', [(i, i ^ k) for i in range(n) if held[i]])]
    all_to_all x4 -> x0, starting transfers between devices: 23.1 us -> none  [the longest x2 12 us: to_tokens(): got = lax.all_to_all(pack, 'ctx', 0, 0, tiled=True)]
    ppermute x1, waiting for transfers between devices: 28.3 us -> 8.06 us  [gather_tiles_by_core(): from_half = lax.ppermute(tile_sum, ('ctx', 'tp'), across)]
    pallas_call x0 -> x5, Pallas kernels: none -> 7.08 us  [simple_call(): pl.pallas_call(kernel, grid_spec=pltpu.PrefetchScalarGridSpec(num_scalar_...]
    ppermute x5 -> x1, starting transfers between devices: 7.76 us -> 0.74 us  [tp_swap(): got.append(lax.ppermute(pick((core + s) % t), 'tp', shifts(t, s)))]
    dynamic_slice x3 -> x0, local copies, waits for them, and re-layouts: 4.67 us -> none  [tp_split(): return tp_swap(lambda p: lax.dynamic_index_in_dim(pack, p, 0, False))]
  transfers between devices with their start and end apart: 30 -> 55, of which waited for: 13 -> 15; matrix products, arithmetic and copies ran while one was open for 16% -> 10% of each run, Pallas kernels for 15% -> 13%
where the time goes in v4:
time: 317 us; the launch traced here: 313 us
  starting transfers between devices  136 us (43%)
  waiting for transfers between devices  77.6 us (24%)
  Pallas kernels  49.3 us (16%)
  between operations  15 us (5%)
  other arithmetic  12.2 us (4%)
  matrix products  11.9 us (4%)
  local copies, waits for them, and re-layouts  11 us (3%)
    ppermute x15, starting transfers between devices, per_device(): lax.ppermute(sent[k], 'ctx', [(i, i ^ k) for i in range(n) if held[i]])  50.6 us
    ppermute x15, starting transfers between devices, per_device(): lax.ppermute(sent[k], 'ctx', [(i, i ^ k) for i in range(n) if held[i ^ k]])  46.2 us
    ppermute x9, waiting for transfers between devices, swap(): return lax.ppermute(x, 'ctx', [(i, i ^ k) for i in range(n)])  31.1 us
    pallas_call x1, Pallas kernels, per_device(): pl.pallas_call(functools.partial(backward_kernel, t, tile, count), grid_s...  21.2 us
    ppermute x9, starting transfers between devices, swap(): return lax.ppermute(x, 'ctx', [(i, i ^ k) for i in range(n)])  18.4 us
    ppermute x15, waiting for transfers between devices, per_device(): lax.ppermute(sent[k], 'ctx', [(i, i ^ k) for i in range(n) if held[i]])  16.9 us
    pallas_call x1, Pallas kernels, per_device(): pl.pallas_call(functools.partial(forward_kernel, t, tile, count), grid_sp...  15.5 us
    all_gather x1, waiting for transfers between devices, per_device(): slice_grad = lax.all_gather(plane_grad, 'ctx', axis_index_groups=lines)  12.1 us
  transfers between devices with their start and end apart: 55, of which 15 were waited for; matrix products, arithmetic and copies ran while one was open for 10% of the time, Pallas kernels for 13%

profile of v4, /device:TPU:13, one launch (start us, length us, event | category | flops | bytes accessed | tf_op | source)
XLA Modules:
  0.0 312.6 jit_solution(10018107307518531857)
XLA Ops:
  10.4 4.4 %fusion.1.refs_3_ = bf16[256,768]{1,0:T(8,128)(2,1)S(1)} fusion(bf16[768,3072]{1,0:T(8,128)(2,1)} %param.11, bf16[256,1536]{1,0:T(8,128)(2,1)S(1)} %get-tuple-element.121, bf16[256,1536]{1,0:T(8,128)(2,1)S(1)} %get-tuple-element.120), kind=kOutput, calls=%fused_computation.15 | convolution fusion | flops 1211301888 | bytes 6684672 | tf_op jit(solution)/shard_map/dot_general | solution.py:27
  33.7 5.0 %collective-permute-start.8 = (bf16[4,128,128]{2,1,0:T(8,128)(2,1)}, bf16[4,128,128]{2,1,0:T(8,128)(2,1)S(1)}, u32[]{:S(2)}, u32[]{:S(2)}) collective-permute-start(bf16[4,128,128]{2,1,0:T(8,128)(2,1)} %copy-done.10), channel_id=1, source_target_pairs={{0,12},{2,14},{6,10},{8,4},{12,0},{14,2},{18,30},{20,24},{22,26},{... | collective-permute-start | bytes 393224 | tf_op jit(solution)/shard_map/ppermute | solution.py:391
  38.7 4.1 %collective-permute-start.9 = (bf16[4,128,128]{2,1,0:T(8,128)(2,1)}, bf16[4,128,128]{2,1,0:T(8,128)(2,1)S(1)}, u32[]{:S(2)}, u32[]{:S(2)}) collective-permute-start(bf16[4,128,128]{2,1,0:T(8,128)(2,1)} %copy-done.9), channel_id=1, source_target_pairs={{0,14},{2,12},{4,10},{10,4},{12,2},{14,0},{16,30},{20,26},{22,24},... | collective-permute-start | bytes 393224 | tf_op jit(solution)/shard_map/ppermute | solution.py:391
  47.8 5.2 %collective-permute-start.12 = (bf16[4,128,128]{2,1,0:T(8,128)(2,1)S(1)}, bf16[4,128,128]{2,1,0:T(8,128)(2,1)S(1)}, u32[]{:S(2)}, u32[]{:S(2)}) collective-permute-start(bf16[4,128,128]{2,1,0:T(8,128)(2,1)S(1)} %get-tuple-element.65), channel_id=1, source_target_pairs={{0,20},{2,22},{4,16},{10,30},{12,24},{14,26},{16,4},{20,0},{22,2},... | collective-permute-start | bytes 393224 | tf_op jit(solution)/shard_map/ppermute | solution.py:391
  54.9 4.3 %collective-permute-start.14 = (bf16[4,128,128]{2,1,0:T(8,128)(2,1)S(1)}, bf16[4,128,128]{2,1,0:T(8,128)(2,1)S(1)}, u32[]{:S(2)}, u32[]{:S(2)}) collective-permute-start(bf16[4,128,128]{2,1,0:T(8,128)(2,1)S(1)} %get-tuple-element.67), channel_id=1, source_target_pairs={{0,24},{2,26},{6,30},{8,16},{12,20},{14,22},{18,10},{20,12},{22,14... | collective-permute-start | bytes 393224 | tf_op jit(solution)/shard_map/ppermute | solution.py:391
  69.1 6.1 %collective-permute-start.16 = (bf16[4,128,128]{2,1,0:T(8,128)(2,1)S(1)}, bf16[4,128,128]{2,1,0:T(8,128)(2,1)S(1)}, u32[]{:S(2)}, u32[]{:S(2)}) collective-permute-start(bf16[4,128,128]{2,1,0:T(8,128)(2,1)S(1)} %get-tuple-element.69), channel_id=1, source_target_pairs={{2,30},{4,24},{6,26},{8,20},{10,22},{12,16},{16,12},{18,14},{22,10... | collective-permute-start | bytes 393224 | tf_op jit(solution)/shard_map/ppermute | solution.py:391
  76.7 4.1 %collective-permute-done.16.refs_14_ = bf16[4,128,128]{2,1,0:T(8,128)(2,1)S(1)} collective-permute-done((bf16[4,128,128]{2,1,0:T(8,128)(2,1)S(1)}, bf16[4,128,128]{2,1,0:T(8,128)(2,1)S(1)}, u32[]{:S(2)}, u32[]{:S(2)}) %collective-permute-start.16) | collective-permute-done | bytes 131104 | tf_op jit(solution)/shard_map/ppermute | solution.py:391
  92.8 15.5 %forward.1 = (bf16[2048,128]{1,0:T(8,128)(2,1)S(1)}, f32[2048,128]{1,0:T(8,128)S(1)}) custom-call(s32[16]{0:T(128)S(1)} %get-tuple-element.108.full_ref, s32[16]{0:T(128)S(1)} %get-tuple-element.104.kcnt_ref, s32[16,10]{1,0:T(8,128)S(1)} %copy.13.kidx_ref, bf16[2,2048,128]{2,1,0:T(8,128)(2,1)S(1)} %copy-done.6, ...), custom_call_target="tpu_custom_call" | custom-call | flops 16000000000 | bytes 5242880 | tf_op jit(solution)/shard_map/forward/pallas_call | solution.py:405
  116.9 21.2 %backward.1 = (bf16[2048,128]{1,0:T(8,128)(2,1)S(1)}, bf16[2,2048,128]{2,1,0:T(8,128)(2,1)S(1)}, bf16[2,2048,128]{2,1,0:T(8,128)(2,1)}) custom-call(s32[16]{0:T(128)S(1)} %get-tuple-element.108.full_ref, s32[16]{0:T(128)S(1)} %get-tuple-element.104.kcnt_ref, s32[16,10]{1,0:T(8,128)S(1)} %copy.13.kidx_ref, bf16[2,2048,128]{2,1,0:T(8,128)(2,1)S(1)} %copy-done.7, ...), custom_call_target="tpu_custom_call" | custom-call | flops 20000000000 | bytes 8388608 | tf_op jit(solution)/shard_map/backward/pallas_call | solution.py:428
  143.5 12.1 %all-gather.3.cloned.1.call-done = bf16[16,128,768]{2,1,0:T(8,128)(2,1)} async-done(((bf16[4,128,768]{2,1,0:T(8,128)(2,1)}), bf16[16,128,768]{2,1,0:T(8,128)(2,1)}) %all-gather.3.cloned.1.call-update) | async-done | bytes 3145744 | tf_op jit(solution)/shard_map/all_gather | solution.py:380
  174.2 5.8 %collective-permute-start.28 = (bf16[4,128,128]{2,1,0:T(8,128)(2,1)S(1)}, bf16[4,128,128]{2,1,0:T(8,128)(2,1)S(1)}, u32[]{:S(2)}, u32[]{:S(2)}) collective-permute-start(bf16[4,128,128]{2,1,0:T(8,128)(2,1)S(1)} %get-tuple-element.85), channel_id=1, source_target_pairs={{0,12},{2,14},{4,8},{10,6},{12,0},{14,2},{16,28},{20,24},{22,26},{... | collective-permute-start | bytes 393224 | tf_op jit(solution)/shard_map/ppermute | solution.py:474
  183.3 5.8 %collective-permute-start.31 = (bf16[4,128,128]{2,1,0:T(8,128)(2,1)S(1)}, bf16[4,128,128]{2,1,0:T(8,128)(2,1)S(1)}, u32[]{:S(2)}, u32[]{:S(2)}) collective-permute-start(bf16[4,128,128]{2,1,0:T(8,128)(2,1)S(1)} %get-tuple-element.88), channel_id=1, source_target_pairs={{0,18},{2,16},{4,22},{10,24},{12,30},{14,28},{16,2},{20,6},{22,4},... | collective-permute-start | bytes 393224 | tf_op jit(solution)/shard_map/ppermute | solution.py:474
  194.6 6.7 %collective-permute-start.34 = (bf16[4,128,128]{2,1,0:T(8,128)(2,1)S(1)}, bf16[4,128,128]{2,1,0:T(8,128)(2,1)S(1)}, u32[]{:S(2)}, u32[]{:S(2)}) collective-permute-start(bf16[4,128,128]{2,1,0:T(8,128)(2,1)S(1)} %get-tuple-element.91), channel_id=1, source_target_pairs={{0,24},{2,26},{4,28},{10,18},{12,20},{14,22},{16,8},{20,12},{22,14... | collective-permute-start | bytes 393224 | tf_op jit(solution)/shard_map/ppermute | solution.py:474
  202.1 4.1 %collective-permute-start.35 = (bf16[4,128,128]{2,1,0:T(8,128)(2,1)S(1)}, bf16[4,128,128]{2,1,0:T(8,128)(2,1)S(1)}, u32[]{:S(2)}, u32[]{:S(2)}) collective-permute-start(bf16[4,128,128]{2,1,0:T(8,128)(2,1)S(1)} %get-tuple-element.92), channel_id=1, source_target_pairs={{0,26},{2,24},{4,30},{10,16},{12,22},{14,20},{16,10},{20,14},{22,1... | collective-permute-start | bytes 393224 | tf_op jit(solution)/shard_map/ppermute | solution.py:474
  206.1 5.1 %collective-permute-start.36 = (bf16[4,128,128]{2,1,0:T(8,128)(2,1)S(1)}, bf16[4,128,128]{2,1,0:T(8,128)(2,1)S(1)}, u32[]{:S(2)}, u32[]{:S(2)}) collective-permute-start(bf16[4,128,128]{2,1,0:T(8,128)(2,1)S(1)} %get-tuple-element.93), channel_id=1, source_target_pairs={{0,28},{2,30},{4,24},{10,22},{12,16},{14,18},{16,12},{20,8},{22,10... | collective-permute-start | bytes 393224 | tf_op jit(solution)/shard_map/ppermute | solution.py:474
  212.6 11.6 %collective-permute-done.35.refs_13_ = bf16[4,128,128]{2,1,0:T(8,128)(2,1)S(1)} collective-permute-done((bf16[4,128,128]{2,1,0:T(8,128)(2,1)S(1)}, bf16[4,128,128]{2,1,0:T(8,128)(2,1)S(1)}, u32[]{:S(2)}, u32[]{:S(2)}) %collective-permute-start.35) | collective-permute-done | bytes 131104 | tf_op jit(solution)/shard_map/ppermute | solution.py:474
  224.2 4.6 %collective-permute-done.36.refs_14_ = bf16[4,128,128]{2,1,0:T(8,128)(2,1)S(1)} collective-permute-done((bf16[4,128,128]{2,1,0:T(8,128)(2,1)S(1)}, bf16[4,128,128]{2,1,0:T(8,128)(2,1)S(1)}, u32[]{:S(2)}, u32[]{:S(2)}) %collective-permute-start.36) | collective-permute-done | bytes 131104 | tf_op jit(solution)/shard_map/ppermute | solution.py:474
  234.6 8.1 %collective-permute-done.44 = bf16[384,768]{1,0:T(8,128)(2,1)S(1)} collective-permute-done((bf16[384,768]{1,0:T(8,128)(2,1)S(1)}, bf16[384,768]{1,0:T(8,128)(2,1)S(1)}, u32[]{:S(2)}, u32[]{:S(2)}) %collective-permute-start.44) | collective-permute-done | bytes 589856 | tf_op jit(solution)/shard_map/ppermute | solution.py:269
  242.7 12.3 %collective-permute-start.49 = (bf16[384,768]{1,0:T(8,128)(2,1)S(1)}, bf16[384,768]{1,0:T(8,128)(2,1)S(1)}, u32[]{:S(2)}, u32[]{:S(2)}) collective-permute-start(bf16[384,768]{1,0:T(8,128)(2,1)S(1)} %broadcast_select_fusion.2.refs_0_), channel_id=1, source_target_pairs={{0,8},{2,10},{4,12},{6,14},{8,0},{10,2},{12,4},{14,6},{16,24},{18,... | collective-permute-start | bytes 1769480 | tf_op jit(solution)/shard_map/ppermute | solution.py:272
  261.7 7.0 %collective-permute-done.49.refs_5_ = bf16[384,768]{1,0:T(8,128)(2,1)S(1)} collective-permute-done((bf16[384,768]{1,0:T(8,128)(2,1)S(1)}, bf16[384,768]{1,0:T(8,128)(2,1)S(1)}, u32[]{:S(2)}, u32[]{:S(2)}) %collective-permute-start.49) | collective-permute-done | bytes 589856 | tf_op jit(solution)/shard_map/ppermute | solution.py:272
  270.2 4.8 %collective-permute-done.46.refs_2_ = bf16[384,768]{1,0:T(8,128)(2,1)S(1)} collective-permute-done((bf16[384,768]{1,0:T(8,128)(2,1)S(1)}, bf16[384,768]{1,0:T(8,128)(2,1)S(1)}, u32[]{:S(2)}, u32[]{:S(2)}) %collective-permute-start.46) | collective-permute-done | bytes 589856 | tf_op jit(solution)/shard_map/ppermute | solution.py:272
  276.6 11.0 %collective-permute-done.51.refs_7_ = bf16[384,768]{1,0:T(8,128)(2,1)S(1)} collective-permute-done((bf16[384,768]{1,0:T(8,128)(2,1)S(1)}, bf16[384,768]{1,0:T(8,128)(2,1)S(1)}, u32[]{:S(2)}, u32[]{:S(2)}) %collective-permute-start.51) | collective-permute-done | bytes 589856 | tf_op jit(solution)/shard_map/ppermute | solution.py:272
  294.0 6.3 %collective-permute-done.53.refs_9_ = bf16[192,768]{1,0:T(8,128)(2,1)S(1)} collective-permute-done((bf16[192,768]{1,0:T(8,128)(2,1)S(1)}, bf16[192,768]{1,0:T(8,128)(2,1)S(1)}, u32[]{:S(2)}, u32[]{:S(2)}) %collective-permute-start.53) | collective-permute-done | bytes 294944 | tf_op jit(solution)/shard_map/ppermute | solution.py:272
  300.3 5.4 %place.1 = f32[768,3072]{1,0:T(8,128)} custom-call(s32[2]{0:T(128)S(1)} %pad_add_fusion.2.place_ref, bf16[384,768]{1,0:T(8,128)(2,1)S(1)} %broadcast_select_fusion.2.refs_0_, bf16[384,768]{1,0:T(8,128)(2,1)S(1)} %collective-permute-done.45.refs_1_, bf16[384,768]{1,0:T(8,128)(2,1)S(1)} %collective-permute-done.46.refs_2_, ...), custom_call_target="tpu_custom_call" | custom-call | tf_op jit(solution)/shard_map/place/pallas_call | solution.py:282
  (173 shorter events, 117.2 us)
Async XLA Ops:
  7.2 148.3 %all-gather.3.cloned.1.call-start = ((), (), s32[]{:S(2)}) async-start(), calls=%async_computation | async-start | bytes 3932160 | tf_op jit(solution)/shard_map/all_gather | solution.py:380
  33.7 19.3 %collective-permute-start.8 = (bf16[4,128,128]{2,1,0:T(8,128)(2,1)}, bf16[4,128,128]{2,1,0:T(8,128)(2,1)S(1)}, u32[]{:S(2)}, u32[]{:S(2)}) collective-permute-start(bf16[4,128,128]{2,1,0:T(8,128)(2,1)} %copy-done.10), channel_id=1, source_target_pairs={{0,12},{2,14},{6,10},{8,4},{12,0},{14,2},{18,30},{20,24},{22,26},{... | collective-permute-start | bytes 393224 | tf_op jit(solution)/shard_map/ppermute | solution.py:391
  44.2 20.9 %collective-permute-start.11 = (bf16[4,128,128]{2,1,0:T(8,128)(2,1)S(1)}, bf16[4,128,128]{2,1,0:T(8,128)(2,1)S(1)}, u32[]{:S(2)}, u32[]{:S(2)}) collective-permute-start(bf16[4,128,128]{2,1,0:T(8,128)(2,1)S(1)} %get-tuple-element.64), channel_id=1, source_target_pairs={{2,16},{4,22},{6,20},{8,26},{10,24},{12,30},{16,2},{18,0},{22,4},{... | collective-permute-start | bytes 393224 | tf_op jit(solution)/shard_map/ppermute | solution.py:391
  47.8 18.5 %collective-permute-start.12 = (bf16[4,128,128]{2,1,0:T(8,128)(2,1)S(1)}, bf16[4,128,128]{2,1,0:T(8,128)(2,1)S(1)}, u32[]{:S(2)}, u32[]{:S(2)}) collective-permute-start(bf16[4,128,128]{2,1,0:T(8,128)(2,1)S(1)} %get-tuple-element.65), channel_id=1, source_target_pairs={{0,20},{2,22},{4,16},{10,30},{12,24},{14,26},{16,4},{20,0},{22,2},... | collective-permute-start | bytes 393224 | tf_op jit(solution)/shard_map/ppermute | solution.py:391
  65.0 22.8 %collective-permute-start.40 = (bf16[128,768]{1,0:T(8,128)(2,1)}, bf16[128,768]{1,0:T(8,128)(2,1)}, u32[]{:S(2)}, u32[]{:S(2)}) collective-permute-start(bf16[128,768]{1,0:T(8,128)(2,1)} %get-tuple-element.117), channel_id=1, source_target_pairs={{0,2},{2,0},{4,6},{6,4},{8,10},{10,8},{12,14},{14,12},{16,18},{18,... | collective-permute-start | bytes 589832 | tf_op jit(solution)/shard_map/ppermute | solution.py:326
  66.3 21.6 %collective-permute-start.41 = (bf16[128,768]{1,0:T(8,128)(2,1)}, bf16[128,768]{1,0:T(8,128)(2,1)S(1)}, u32[]{:S(2)}, u32[]{:S(2)}) collective-permute-start(bf16[128,768]{1,0:T(8,128)(2,1)} %get-tuple-element.118), channel_id=1, source_target_pairs={{0,4},{2,6},{4,0},{6,2},{8,12},{10,14},{12,8},{14,10},{16,20},{18,... | collective-permute-start | bytes 589832 | tf_op jit(solution)/shard_map/ppermute | solution.py:326
  66.3 21.6 %collective-permute-start.42 = (bf16[128,768]{1,0:T(8,128)(2,1)}, bf16[128,768]{1,0:T(8,128)(2,1)}, u32[]{:S(2)}, u32[]{:S(2)}) collective-permute-start(bf16[128,768]{1,0:T(8,128)(2,1)} %get-tuple-element.119), channel_id=1, source_target_pairs={{0,6},{2,4},{4,2},{6,0},{8,14},{10,12},{12,10},{14,8},{16,22},{18,... | collective-permute-start | bytes 589832 | tf_op jit(solution)/shard_map/ppermute | solution.py:326
  108.3 31.0 %collective-permute-start.21 = (bf16[2048,128]{1,0:T(8,128)(2,1)S(1)}, bf16[2048,128]{1,0:T(8,128)(2,1)S(1)}, u32[]{:S(2)}, u32[]{:S(2)}) collective-permute-start(bf16[2048,128]{1,0:T(8,128)(2,1)S(1)} %get-tuple-element.73.o_ref.attn_ref), channel_id=1, source_target_pairs={{0,6},{2,4},{4,2},{10,12},{12,10},{14,8},{16,22},{20,18},{22,16},{... | collective-permute-start | bytes 1572872 | tf_op jit(solution)/shard_map/ppermute | solution.py:422
  111.9 27.5 %collective-permute-start.20 = (bf16[2048,128]{1,0:T(8,128)(2,1)S(1)}, bf16[2048,128]{1,0:T(8,128)(2,1)S(1)}, u32[]{:S(2)}, u32[]{:S(2)}) collective-permute-start(bf16[2048,128]{1,0:T(8,128)(2,1)S(1)} %get-tuple-element.73.o_ref.attn_ref), channel_id=1, source_target_pairs={{0,4},{2,6},{4,0},{10,14},{12,8},{14,10},{16,20},{20,16},{22,18},{... | collective-permute-start | bytes 1572872 | tf_op jit(solution)/shard_map/ppermute | solution.py:422
  113.2 26.1 %collective-permute-start.19 = (bf16[2048,128]{1,0:T(8,128)(2,1)S(1)}, bf16[2048,128]{1,0:T(8,128)(2,1)S(1)}, u32[]{:S(2)}, u32[]{:S(2)}) collective-permute-start(bf16[2048,128]{1,0:T(8,128)(2,1)S(1)} %get-tuple-element.73.o_ref.attn_ref), channel_id=1, source_target_pairs={{0,2},{2,0},{4,6},{10,8},{12,14},{14,12},{16,18},{20,22},{22,20},{... | collective-permute-start | bytes 1572872 | tf_op jit(solution)/shard_map/ppermute | solution.py:422
  138.1 22.0 %collective-permute-start.22 = (bf16[2,2048,128]{2,1,0:T(8,128)(2,1)}, bf16[2,2048,128]{2,1,0:T(8,128)(2,1)S(1)}, u32[]{:S(2)}, u32[]{:S(2)}) collective-permute-start(bf16[2,2048,128]{2,1,0:T(8,128)(2,1)} %get-tuple-element.78), channel_id=1, source_target_pairs={{0,1},{1,0},{2,3},{3,2},{4,5},{5,4},{6,7},{7,6},{8,9},{9,8},{10,11... | collective-permute-start | bytes 3145736 | tf_op jit(solution)/shard_map/ppermute | solution.py:467
  159.3 71.6 %collective-permute-start.43 = (bf16[384,768]{1,0:T(8,128)(2,1)S(1)}, bf16[384,768]{1,0:T(8,128)(2,1)S(1)}, u32[]{:S(2)}, u32[]{:S(2)}) collective-permute-start(bf16[384,768]{1,0:T(8,128)(2,1)S(1)} %get-tuple-element.122), channel_id=1, source_target_pairs={{0,1},{1,0},{2,3},{3,2},{4,5},{5,4},{6,7},{7,6},{8,9},{9,8},{10,11... | collective-permute-start | bytes 1769480 | tf_op jit(solution)/shard_map/ppermute | solution.py:453
  183.3 18.8 %collective-permute-start.31 = (bf16[4,128,128]{2,1,0:T(8,128)(2,1)S(1)}, bf16[4,128,128]{2,1,0:T(8,128)(2,1)S(1)}, u32[]{:S(2)}, u32[]{:S(2)}) collective-permute-start(bf16[4,128,128]{2,1,0:T(8,128)(2,1)S(1)} %get-tuple-element.88), channel_id=1, source_target_pairs={{0,18},{2,16},{4,22},{10,24},{12,30},{14,28},{16,2},{20,6},{22,4},... | collective-permute-start | bytes 393224 | tf_op jit(solution)/shard_map/ppermute | solution.py:474
  192.7 18.6 %collective-permute-start.33 = (bf16[4,128,128]{2,1,0:T(8,128)(2,1)S(1)}, bf16[4,128,128]{2,1,0:T(8,128)(2,1)S(1)}, u32[]{:S(2)}, u32[]{:S(2)}) collective-permute-start(bf16[4,128,128]{2,1,0:T(8,128)(2,1)S(1)} %get-tuple-element.90), channel_id=1, source_target_pairs={{0,22},{2,20},{4,18},{10,28},{12,26},{14,24},{16,6},{20,2},{22,0},... | collective-permute-start | bytes 393224 | tf_op jit(solution)/shard_map/ppermute | solution.py:474
  194.6 18.0 %collective-permute-start.34 = (bf16[4,128,128]{2,1,0:T(8,128)(2,1)S(1)}, bf16[4,128,128]{2,1,0:T(8,128)(2,1)S(1)}, u32[]{:S(2)}, u32[]{:S(2)}) collective-permute-start(bf16[4,128,128]{2,1,0:T(8,128)(2,1)S(1)} %get-tuple-element.91), channel_id=1, source_target_pairs={{0,24},{2,26},{4,28},{10,18},{12,20},{14,22},{16,8},{20,12},{22,14... | collective-permute-start | bytes 393224 | tf_op jit(solution)/shard_map/ppermute | solution.py:474
  202.1 22.1 %collective-permute-start.35 = (bf16[4,128,128]{2,1,0:T(8,128)(2,1)S(1)}, bf16[4,128,128]{2,1,0:T(8,128)(2,1)S(1)}, u32[]{:S(2)}, u32[]{:S(2)}) collective-permute-start(bf16[4,128,128]{2,1,0:T(8,128)(2,1)S(1)} %get-tuple-element.92), channel_id=1, source_target_pairs={{0,26},{2,24},{4,30},{10,16},{12,22},{14,20},{16,10},{20,14},{22,1... | collective-permute-start | bytes 393224 | tf_op jit(solution)/shard_map/ppermute | solution.py:474
  206.1 22.6 %collective-permute-start.36 = (bf16[4,128,128]{2,1,0:T(8,128)(2,1)S(1)}, bf16[4,128,128]{2,1,0:T(8,128)(2,1)S(1)}, u32[]{:S(2)}, u32[]{:S(2)}) collective-permute-start(bf16[4,128,128]{2,1,0:T(8,128)(2,1)S(1)} %get-tuple-element.93), channel_id=1, source_target_pairs={{0,28},{2,30},{4,24},{10,22},{12,16},{14,18},{16,12},{20,8},{22,10... | collective-permute-start | bytes 393224 | tf_op jit(solution)/shard_map/ppermute | solution.py:474
  211.3 17.4 %collective-permute-start.37 = (bf16[4,128,128]{2,1,0:T(8,128)(2,1)S(1)}, bf16[4,128,128]{2,1,0:T(8,128)(2,1)S(1)}, u32[]{:S(2)}, u32[]{:S(2)}) collective-permute-start(bf16[4,128,128]{2,1,0:T(8,128)(2,1)S(1)} %get-tuple-element.94), channel_id=1, source_target_pairs={{0,30},{2,28},{4,26},{10,20},{12,18},{14,16},{16,14},{20,10},{22,8... | collective-permute-start | bytes 393224 | tf_op jit(solution)/shard_map/ppermute | solution.py:474
  242.7 26.0 %collective-permute-start.49 = (bf16[384,768]{1,0:T(8,128)(2,1)S(1)}, bf16[384,768]{1,0:T(8,128)(2,1)S(1)}, u32[]{:S(2)}, u32[]{:S(2)}) collective-permute-start(bf16[384,768]{1,0:T(8,128)(2,1)S(1)} %broadcast_select_fusion.2.refs_0_), channel_id=1, source_target_pairs={{0,8},{2,10},{4,12},{6,14},{8,0},{10,2},{12,4},{14,6},{16,24},{18,... | collective-permute-start | bytes 1769480 | tf_op jit(solution)/shard_map/ppermute | solution.py:272
  259.8 29.4 %collective-permute-start.39 = (bf16[256,1536]{1,0:T(8,128)(2,1)}, bf16[256,1536]{1,0:T(8,128)(2,1)}, u32[]{:S(2)}, u32[]{:S(2)}) collective-permute-start(bf16[256,1536]{1,0:T(8,128)(2,1)} %dynamic-slice_convert_fusion), channel_id=1, source_target_pairs={{0,1},{1,0},{2,3},{3,2},{4,5},{5,4},{6,7},{7,6},{8,9},{9,8},{10,11... | collective-permute-start | bytes 2359304 | tf_op jit(solution)/shard_map/ppermute | solution.py:488
  268.7 19.0 %collective-permute-start.51 = (bf16[384,768]{1,0:T(8,128)(2,1)S(1)}, bf16[384,768]{1,0:T(8,128)(2,1)S(1)}, u32[]{:S(2)}, u32[]{:S(2)}) collective-permute-start(bf16[384,768]{1,0:T(8,128)(2,1)S(1)} %collective-permute-done.49.refs_5_), channel_id=1, source_target_pairs={{0,4},{2,6},{4,0},{6,2},{8,12},{10,14},{12,8},{14,10},{16,20},{18,... | collective-permute-start | bytes 1769480 | tf_op jit(solution)/shard_map/ppermute | solution.py:272
  268.9 20.0 %collective-permute-start.50 = (bf16[384,768]{1,0:T(8,128)(2,1)S(1)}, bf16[384,768]{1,0:T(8,128)(2,1)S(1)}, u32[]{:S(2)}, u32[]{:S(2)}) collective-permute-start(bf16[384,768]{1,0:T(8,128)(2,1)S(1)} %collective-permute-done.49.refs_5_), channel_id=1, source_target_pairs={{0,2},{2,0},{4,6},{6,4},{8,10},{10,8},{12,14},{14,12},{16,18},{18,... | collective-permute-start | bytes 1769480 | tf_op jit(solution)/shard_map/ppermute | solution.py:272
  275.0 18.9 %collective-permute-start.48 = (bf16[192,768]{1,0:T(8,128)(2,1)S(1)}, bf16[192,768]{1,0:T(8,128)(2,1)S(1)}, u32[]{:S(2)}, u32[]{:S(2)}) collective-permute-start(bf16[192,768]{1,0:T(8,128)(2,1)S(1)} %slice.21), channel_id=1, source_target_pairs={{0,2},{2,0},{4,6},{6,4},{8,10},{10,8},{12,14},{14,12},{16,18},{18,... | collective-permute-start | bytes 884744 | tf_op jit(solution)/shard_map/ppermute | solution.py:272
  276.3 17.7 %collective-permute-start.47 = (bf16[192,768]{1,0:T(8,128)(2,1)S(1)}, bf16[192,768]{1,0:T(8,128)(2,1)S(1)}, u32[]{:S(2)}, u32[]{:S(2)}) collective-permute-start(bf16[192,768]{1,0:T(8,128)(2,1)S(1)} %slice.20), channel_id=1, source_target_pairs={{0,4},{2,6},{4,0},{6,2},{8,12},{10,14},{12,8},{14,10},{16,20},{18,... | collective-permute-start | bytes 884744 | tf_op jit(solution)/shard_map/ppermute | solution.py:272
  (51 other events, 523.4 us)
Sparse Core Ops, SparseCore 0:
  91.9 63.5 all-gather.2

commit v5 on v4

--- a/solution.py
+++ b/solution.py
@@ -41,13 +41,13 @@
 
 
 def head_of(chip, in_plane, heads_plane):
-    place = (chip % in_plane + in_plane - chip // in_plane % in_plane) % in_plane
-    return place < heads_plane, chip // in_plane * heads_plane + jnp.minimum(place, heads_plane - 1)
+    place = (chip % in_plane - chip // in_plane) % in_plane
+    return place < heads_plane, chip // in_plane * heads_plane + min(place, heads_plane - 1)
 
 
 def pack_kernel(n, t, where_ref, *refs):
     arrays, got, outs, heads_all = refs[:4], refs[4:4 + 2 * (t - 1)], refs[4 + 2 * (t - 1):-1], refs[-1]
-    chip, core = where_ref[0], where_ref[1]
+    core = where_ref[1]
     sub = heads_all.shape[2]
     heads_here = heads_all.shape[0] // t
     for a in range(4):
@@ -58,50 +58,89 @@
                 first = (core + t - s) % t * heads_here
                 source = got[2 * (s - 1)] if a < 3 else got[2 * (s - 1) + 1]
                 heads_all[first + h, a] = source[a % 3, :, column]
+    out_ref = outs[0]
     for k in range(n):
-        _, head = head_of(chip ^ k, n // PLANES, heads_all.shape[0] // PLANES)
-        outs[k][...] = heads_all[head]
-
-
-def join_kernel(n, where_ref, *refs):
-    chunks, (qg_ref, kv_ref) = refs[:n], refs[n:]
-    chip = where_ref[0]
+        held, head = head_of(k, n // PLANES, heads_all.shape[0] // PLANES)
+        out_ref[k] = heads_all[head] if held else jnp.zeros_like(heads_all[0])
+
+
+def join_kernel(n, where_ref, chunks_ref, qg_ref, kv_ref):
+    sub = chunks_ref.shape[2]
     for k in range(n):
-        sub = chunks[k].shape[1]
-        at = pl.ds(pl.multiple_of((chip ^ k) * sub, sub), sub)
-        qg_ref[0, at] = chunks[k][0]
-        kv_ref[0, at] = chunks[k][1]
-        kv_ref[1, at] = chunks[k][2]
-        qg_ref[1, at] = chunks[k][3]
+        at = pl.ds(k * sub, sub)
+        qg_ref[0, at] = chunks_ref[k, 0]
+        kv_ref[0, at] = chunks_ref[k, 1]
+        kv_ref[1, at] = chunks_ref[k, 2]
+        qg_ref[1, at] = chunks_ref[k, 3]
 
 
 def unjoin_kernel(n, t, where_ref, attn_ref, dq_ref, dkv_ref, *refs):
-    got, outs = refs[:t - 1], refs[t - 1:]
-    chip = where_ref[0]
+    got, out_ref = refs[:t - 1], refs[t - 1]
+    sub = out_ref.shape[2]
     for k in range(n):
-        sub = outs[k].shape[1]
-        at = pl.ds(pl.multiple_of((chip ^ k) * sub, sub), sub)
-        outs[k][0] = attn_ref[at]
-        outs[k][1] = dq_ref[at]
+        at = pl.ds(k * sub, sub)
+        out_ref[k, 0] = attn_ref[at]
+        out_ref[k, 1] = dq_ref[at]
         for a in range(2):
             total = dkv_ref[a, at].astype(F32)
             for other in got:
                 total = total + other[a, at].astype(F32)
-            outs[k][2 + a] = total.astype(BF16)
-
-
-def by_core_kernel(n, t, where_ref, *refs):
-    chunks, outs, heads_all = refs[:n], refs[n:n + t], refs[-1]
-    chip, core = where_ref[0], where_ref[1]
+            out_ref[k, 2 + a] = total.astype(BF16)
+
+
+def by_core_kernel(n, t, where_ref, chunks_ref, *refs):
+    outs, heads_all = refs[:t], refs[t]
+    core = where_ref[1]
     heads_here = heads_all.shape[0] // t
     for k in range(n):
-        held, head = head_of(chip ^ k, n // PLANES, heads_all.shape[0] // PLANES)
-
-        @pl.when(held)
-        def _(k=k, head=head):
-            heads_all[head] = chunks[k][...]
+        held, head = head_of(k, n // PLANES, heads_all.shape[0] // PLANES)
+        if held:
+            heads_all[head] = chunks_ref[k]
     for s in range(t):
         outs[s][...] = heads_all[pl.ds((core + s) % t * heads_here, heads_here)]
+
+
+def seats_kernel(in_plane, where_ref, *refs):
+    got, out_ref = refs[:in_plane], refs[in_plane]
+    seat = where_ref[0] % in_plane
+    for k in range(in_plane):
+        out_ref[seat ^ k] = got[k][...]
+
+
+def tile_kernel(in_plane, heads_plane, t, where_ref, *refs):
+    attns, (grad_ref, own_ref), sends = refs[:in_plane], refs[in_plane:in_plane + 2], refs[in_plane + 2:-2]
+    seats, total = refs[-2:]
+    chip, core = where_ref[0], where_ref[1]
+    seat = chip % in_plane
+    plane = chip // in_plane
+    step = pl.program_id(0)
+    for k in range(in_plane):
+        seats[seat ^ k] = attns[k][...]
+
+    @pl.when(step == 0)
+    def _():
+        total[...] = jnp.zeros_like(total)
+
+    grad = grad_ref[...]
+    for j in range(heads_plane):
+        total[pl.ds(j * HEAD, HEAD)] += dot(seats[(plane + j) % in_plane], grad, TN)
+
+    @pl.when(step == pl.num_programs(0) - 1)
+    def _():
+        piece = own_ref.shape[0]
+        own_ref[...] = total[pl.ds(pl.multiple_of(core * piece, piece), piece)]
+        for s in range(1, t):
+            at = pl.ds(pl.multiple_of((core + s) % t * piece, piece), piece)
+            sends[s - 1][...] = total[at].astype(BF16)
+
+
+def place_kernel(t, where_ref, *refs):
+    parts, out_ref = refs[:t], refs[t]
+    core = where_ref[1]
+    piece = parts[0].shape[1]
+    for s in range(t):
+        at = pl.ds(pl.multiple_of((core + t - s) % t * piece, piece), piece)
+        out_ref[at] = parts[s][0].astype(F32)
 
 
 def unpack_kernel(t, where_ref, *refs):
@@ -241,60 +280,6 @@
     return [(c, (c + s) % t) for c in range(t)]
 
 
-def place_kernel(place_ref, *refs):
-    sources, out_ref = refs[:-1], refs[-1]
-    step = pl.program_id(0)
-    for u in range(2):
-        own, beside, above, upper, lower = sources[5 * u:5 * u + 5]
-        for v, source in enumerate((own, beside, above)):
-            @pl.when(step == 4 * u + v)
-            def _(source=source):
-                out_ref[...] = source[...].astype(F32)
-
-        @pl.when(step == 4 * u + 3)
-        def _(upper=upper, lower=lower):
-            middle = upper.shape[0]
-            out_ref[:middle] = upper[...].astype(F32)
-            out_ref[middle:] = lower[...].astype(F32)
-
-
-def gather_tiles_by_core(n, t, tile_sum, chip, core):
-    in_plane = n // PLANES
-    plane, seat = chip // in_plane, chip % in_plane
-    tile_rows, cols = tile_sum.shape
-    across = [
-        (i * t + c, (i ^ 2 * in_plane) * t + c)
-        for i in range(n) for c in range(t) if i // in_plane // 2 == c
-    ]
-    from_half = lax.ppermute(tile_sum, ("ctx", "tp"), across)
-
-    def swap(x, k):
-        return lax.ppermute(x, "ctx", [(i, i ^ k) for i in range(n)])
-
-    first = jnp.where(plane // 2 == core, tile_sum, from_half)
-    second = swap(first, in_plane)
-    middle = tile_rows // 2
-    sources = []
-    for mine in (first, second):
-        beside, above = swap(mine, 1), swap(mine, 2)
-        sources += [mine, beside, above, swap(beside[:middle], 2), swap(above[middle:], 1)]
-    place = jnp.stack([plane % 2, seat]).astype(jnp.int32)
-    return pl.pallas_call(
-        place_kernel,
-        grid_spec=pltpu.PrefetchScalarGridSpec(
-            num_scalar_prefetch=1,
-            grid=(8,),
-            in_specs=[whole_block(x.shape) for x in sources],
-            out_specs=pl.BlockSpec(
-                (tile_rows, cols), lambda s, place: (s // 4 ^ place[0], s % 4 ^ place[1])
-            ),
-        ),
-        out_shape=jax.ShapeDtypeStruct((2 * tile_rows, in_plane * cols), F32),
-        compiler_params=pltpu.CompilerParams(vmem_limit_bytes=48 * 2**20),
-        name="place",
-    )(place, *sources)
-
-
 def per_device(n, t, queries, key_vectors, value_vectors, out_weight, out_grad, block_segment):
     rows, width = queries.shape
     heads_here = width // HEAD
@@ -316,15 +301,6 @@
 
     def tp_gather(x):
         return tp_swap(lambda _: x)
-
-    def tp_split(pack):
-        return tp_swap(lambda p: lax.dynamic_index_in_dim(pack, p, 0, False))
-
-    def plane_swap(pick):
-        got = [pick(seat)]
-        for k in range(1, in_plane):
-            got.append(lax.ppermute(pick(seat ^ k), "ctx", [(i, i ^ k) for i in range(n)]))
-        return [lax.select_n(seat ^ b, *got) for b in range(in_plane)]
 
     def shape(*dims):
         return jax.ShapeDtypeStruct(dims, BF16)
@@ -373,26 +349,28 @@
 
     cols = model // in_plane
     mine = lax.dynamic_slice_in_dim(full_grad, core * sub, sub, 0)
-    plane_grad = jnp.stack(
-        plane_swap(lambda b: lax.dynamic_slice_in_dim(mine, b * cols, cols, 1))
-    )
+    plane_got = [lax.dynamic_slice_in_dim(mine, seat * cols, cols, 1)]
+    for k in range(1, in_plane):
+        there = lax.dynamic_slice_in_dim(mine, (seat ^ k) * cols, cols, 1)
+        plane_got.append(lax.ppermute(there, "ctx", [(i, i ^ k) for i in range(n)]))
+    (plane_grad,) = simple_call(
+        functools.partial(seats_kernel, in_plane), "seats", where, plane_got, [shape(in_plane, sub, cols)]
+    )
+    got = [x for pair in zip(got_qkv, got_g) for x in pair]
+    (sent,) = simple_call(
+        functools.partial(pack_kernel, n, t), "pack", where,
+        [queries, key_vectors, value_vectors, grad_attn] + got,
+        [shape(n, 4, sub, HEAD)],
+        [pltpu.VMEM((heads, 4, sub, HEAD), BF16)],
+    )
+    sent, plane_grad = lax.optimization_barrier((sent, plane_grad))
     lines = [[a * in_plane + b for a in range(PLANES)] for b in range(in_plane)]
     slice_grad = lax.all_gather(plane_grad, "ctx", axis_index_groups=lines)
     slice_grad = slice_grad.reshape(n * sub, cols)
-
-    got = [x for pair in zip(got_qkv, got_g) for x in pair]
-    sent = simple_call(
-        functools.partial(pack_kernel, n, t), "pack", where,
-        [queries, key_vectors, value_vectors, grad_attn] + got,
-        [shape(4, sub, HEAD)] * n,
-        [pltpu.VMEM((heads, 4, sub, HEAD), BF16)],
-    )
-    chunks = [sent[0]] + [
-        lax.ppermute(sent[k], "ctx", [(i, i ^ k) for i in range(n) if held[i ^ k]]) for k in range(1, n)
-    ]
+    chunks = lax.all_to_all(sent, "ctx", 0, 0, tiled=True)
     length = n * sub
     qg, kv = simple_call(
-        functools.partial(join_kernel, n), "join", where, chunks, [shape(2, length, HEAD)] * 2
+        functools.partial(join_kernel, n), "join", where, [chunks], [shape(2, length, HEAD)] * 2
     )
     kv_all = [kv] + [lax.ppermute(kv, "tp", shifts(t, s)) for s in range(1, t)]
 
@@ -417,14 +395,9 @@
         name="forward",
     )(full, kcnt, kidx, qg, *part_arrays)
 
-    plane = chip // in_plane
     travel = [attn] + [
         lax.ppermute(attn, "ctx", [(i, i ^ k) for i in range(n) if held[i]]) for k in range(1, in_plane)
     ]
-    got_attn = [
-        lax.select_n(seat ^ ((plane + j) % in_plane), *travel) for j in range(heads_plane)
-    ]
-
     dq, *dkv = pl.pallas_call(
         functools.partial(backward_kernel, t, tile, count),
         grid_spec=pltpu.PrefetchScalarGridSpec(
@@ -440,41 +413,64 @@
         name="backward",
     )(full, kcnt, kidx, qg, qg, attn, lse, *part_arrays)
 
-    got_attn, dq = lax.optimization_barrier((got_attn, dq))
-
-    plane_attn = jnp.stack([a.reshape(n * sub, HEAD) for a in got_attn])
-    tile_term = jnp.einsum("hrd,rc->hdc", plane_attn, slice_grad, preferred_element_type=F32)
-    tile_term = tile_term.reshape(heads_plane * HEAD, cols)
+    *travel, dq = lax.optimization_barrier((*travel, dq))
+
     tile_rows = heads_plane * HEAD
-    planes_here = PLANES // t
-    if in_plane == 4 and t == 2:
-        tile_sum = tile_term
-        for s in range(1, t):
-            tile_sum = tile_sum + lax.ppermute(tile_term.astype(BF16), "tp", shifts(t, s)).astype(F32)
-        grad_weight = gather_tiles_by_core(n, t, tile_sum.astype(BF16), chip, core)
-    else:
-        piece = tile_rows // t
-        tile_term = tile_term.reshape(t, piece, cols)
-        tile_sum = lax.dynamic_index_in_dim(tile_term, core, 0, False)
-        for s in range(1, t):
-            there = lax.dynamic_index_in_dim(tile_term, (core + s) % t, 0, False)
-            tile_sum = tile_sum + lax.ppermute(there.astype(BF16), "tp", shifts(t, s)).astype(F32)
-        tiles = lax.all_gather(tile_sum.astype(BF16), "ctx")
-        tiles = jnp.stack(tp_split(tiles.reshape(t, planes_here, in_plane, piece, cols)))
-        grad_weight = tiles.transpose(1, 0, 3, 2, 4).reshape(width, model).astype(F32)
+    piece = tile_rows // t
+    step_rows = length // 4
+    tile_own, *tile_sends = pl.pallas_call(
+        functools.partial(tile_kernel, in_plane, heads_plane, t),
+        grid_spec=pltpu.PrefetchScalarGridSpec(
+            num_scalar_prefetch=1,
+            grid=(4,),
+            in_specs=[pl.BlockSpec((step_rows, HEAD), lambda r, *_: (r, 0))] * in_plane
+            + [pl.BlockSpec((step_rows, cols), lambda r, *_: (r, 0))],
+            out_specs=[whole_block((piece, cols))] * t,
+            scratch_shapes=[
+                pltpu.VMEM((in_plane, step_rows, HEAD), BF16), pltpu.VMEM((tile_rows, cols), F32)
+            ],
+        ),
+        out_shape=[jax.ShapeDtypeStruct((piece, cols), F32)] + [shape(piece, cols)] * (t - 1),
+        compiler_params=params,
+        cost_estimate=pl.CostEstimate(flops=5 * 10**9, bytes_accessed=2**22, transcendentals=0),
+        name="tile",
+    )(where, *travel, slice_grad)
+    tile_sum = tile_own
+    for s in range(1, t):
+        tile_sum = tile_sum + lax.ppermute(tile_sends[s - 1], "tp", shifts(t, s)).astype(F32)
+    tiles = lax.all_gather(tile_sum.astype(BF16), "ctx")
+    here = n // t
+    tiles_core = [tiles] + [
+        lax.ppermute(
+            lax.dynamic_slice_in_dim(tiles, (core + s) % t * here, here, 0), "tp", shifts(t, s)
+        )
+        for s in range(1, t)
+    ]
+    grad_weight = pl.pallas_call(
+        functools.partial(place_kernel, t),
+        grid_spec=pltpu.PrefetchScalarGridSpec(
+            num_scalar_prefetch=1,
+            grid=(here,),
+            in_specs=[pl.BlockSpec((1, piece, cols), lambda r, where: (where[1] * here + r, 0, 0))]
+            + [pl.BlockSpec((1, piece, cols), lambda r, *_: (r, 0, 0))] * (t - 1),
+            out_specs=pl.BlockSpec((tile_rows, cols), lambda r, *_: (r // in_plane, r % in_plane)),
+        ),
+        out_shape=jax.ShapeDtypeStruct((width, model), F32),
+        compiler_params=params,
+        cost_estimate=pl.CostEstimate(flops=0, bytes_accessed=2**24, transcendentals=0),
+        name="place",
+    )(where, *tiles_core)
 
     got_dkv = [
         lax.ppermute(dkv[s], "tp", [(c, (c - s) % t) for c in range(t)]) for s in range(1, t)
     ]
-    sent = simple_call(
+    (sent,) = simple_call(
         functools.partial(unjoin_kernel, n, t), "unjoin", where,
-        [attn, dq, dkv[0]] + got_dkv, [shape(4, sub, HEAD)] * n,
-    )
-    chunks = [sent[0]] + [
-        lax.ppermute(sent[k], "ctx", [(i, i ^ k) for i in range(n) if held[i]]) for k in range(1, n)
-    ]
+        [attn, dq, dkv[0]] + got_dkv, [shape(n, 4, sub, HEAD)],
+    )
+    chunks = lax.all_to_all(sent, "ctx", 0, 0, tiled=True)
     mine = simple_call(
-        functools.partial(by_core_kernel, n, t), "by_core", where, chunks,
+        functools.partial(by_core_kernel, n, t), "by_core", where, [chunks],
         [shape(heads_here, 4, sub, HEAD)] * t, [pltpu.VMEM((heads, 4, sub, HEAD), BF16)],
     )
     parts = [mine[0]] + [lax.ppermute(mine[s], "tp", shifts(t, s)) for s in range(1, t)]

time: 317 us -> 332 us (1.047)
  starting transfers between devices: 136 us -> 28.6 us
  blocking collectives: 0 us -> 74.1 us
  waiting for transfers between devices: 77.6 us -> 124 us
  local copies, waits for them, and re-layouts: 11 us -> 19.4 us
  Pallas kernels: 49.3 us -> 56.8 us
  other arithmetic: 12.2 us -> 5.75 us
  matrix products: 11.9 us -> 7.51 us
    ppermute x44 -> x5, starting transfers between devices: 120 us -> 5.91 us  [the longest x3 2.74 us: per_device(): plane_got.append(lax.ppermute(there, 'ctx', [(i, i ^ k) for i in range(n)]))]
    all_to_all x0 -> x1, waiting for transfers between devices: none -> 90 us  [per_device(): chunks = lax.all_to_all(sent, 'ctx', 0, 0, tiled=True)]
    all_to_all x0 -> x1, blocking collectives: none -> 74.1 us  [per_device(): chunks = lax.all_to_all(sent, 'ctx', 0, 0, tiled=True)]
    ppermute x44 -> x5, waiting for transfers between devices: 64.1 us -> 8.09 us  [the longest x3 6.88 us: per_device(): plane_got.append(lax.ppermute(there, 'ctx', [(i, i ^ k) for i in range(n)]))]
    all_gather x0 -> x1, waiting for transfers between devices: none -> 18.8 us  [per_device(): tiles = lax.all_gather(tile_sum.astype(BF16), 'ctx')]
    all_gather x1, waiting for transfers between devices: 12.1 us -> 0.01 us  [per_device(): slice_grad = lax.all_gather(plane_grad, 'ctx', axis_index_groups=lines)]
    unnamed x40 -> x36, local copies, waits for them, and re-layouts: 3.33 us -> 12.6 us
    all_to_all x0 -> x1, starting transfers between devices: none -> 6.61 us  [per_device(): chunks = lax.all_to_all(sent, 'ctx', 0, 0, tiled=True)]
  transfers between devices with their start and end apart: 55 -> 18, of which waited for: 15 -> 9; matrix products, arithmetic and copies ran while one was open for 10% -> 6% of each run, Pallas kernels for 13% -> 14%
where the time goes in v5:
time: 332 us; the launch traced here: 330 us
  waiting for transfers between devices  124 us (37%)
  blocking collectives  74.1 us (22%)
  Pallas kernels  56.8 us (17%)
  starting transfers between devices  28.6 us (9%)
  local copies, waits for them, and re-layouts  19.4 us (6%)
  between operations  14.3 us (4%)
  matrix products  7.51 us (2%)
  other arithmetic  5.75 us (2%)
    all_to_all x1, waiting for transfers between devices, per_device(): chunks = lax.all_to_all(sent, 'ctx', 0, 0, tiled=True)  90 us
    all_to_all x1, blocking collectives, per_device(): chunks = lax.all_to_all(sent, 'ctx', 0, 0, tiled=True)  74.1 us
    pallas_call x1, Pallas kernels, per_device(): pl.pallas_call(functools.partial(backward_kernel, t, tile, count), grid_s...  20.2 us
    all_gather x1, waiting for transfers between devices, per_device(): tiles = lax.all_gather(tile_sum.astype(BF16), 'ctx')  18.8 us
    pallas_call x1, Pallas kernels, per_device(): pl.pallas_call(functools.partial(forward_kernel, t, tile, count), grid_sp...  15.2 us
    unnamed x36, local copies, waits for them, and re-layouts  12.6 us
    pallas_call x6, Pallas kernels, simple_call(): pl.pallas_call(kernel, grid_spec=pltpu.PrefetchScalarGridSpec(num_scalar_...  10.8 us
    ppermute x3, starting transfers between devices, per_device(): lax.ppermute(attn, 'ctx', [(i, i ^ k) for i in range(n) if held[i]])  8.37 us
  transfers between devices with their start and end apart: 18, of which 9 were waited for; matrix products, arithmetic and copies ran while one was open for 6% of the time, Pallas kernels for 14%

profile of v5, /device:TPU:13, one launch (start us, length us, event | category | flops | bytes accessed | tf_op | source)
XLA Modules:
  0.0 330.2 jit_solution(8492030529659447985)
XLA Ops:
  10.3 3.8 %fusion.1.refs_3_ = bf16[256,768]{1,0:T(8,128)(2,1)S(1)} fusion(bf16[768,3072]{1,0:T(8,128)(2,1)} %param.11, bf16[256,1536]{1,0:T(8,128)(2,1)S(1)} %get-tuple-element.61, bf16[256,1536]{1,0:T(8,128)(2,1)S(1)} %get-tuple-element.60), kind=kOutput, calls=%fused_computation.14 | convolution fusion | flops 1211301888 | bytes 6684672 | tf_op jit(solution)/shard_map/dot_general | solution.py:27
  18.6 2.3 pack.1
  20.9 2.3 collective-permute-done.5.refs_3_
  23.2 3.1 collective-permute-done.3.refs_1_
  29.2 6.6 %all-to-all-start = ((bf16[16,4,128,128]{3,2,1,0:T(8,128)(2,1)}), bf16[16,4,128,128]{3,2,1,0:T(8,128)(2,1)S(1)}, u32[]{:S(2)}, u32[]{:S(2)}) async-start(bf16[16,4,128,128]{3,2,1,0:T(8,128)(2,1)} %pack.1), calls=%async_computation | async-start | bytes 4194304 | tf_op jit(solution)/shard_map/all_to_all | solution.py:370
  38.0 90.0 %all-to-all-done.chunks_ref = bf16[16,4,128,128]{3,2,1,0:T(8,128)(2,1)S(1)} async-done(((bf16[16,4,128,128]{3,2,1,0:T(8,128)(2,1)}), bf16[16,4,128,128]{3,2,1,0:T(8,128)(2,1)S(1)}, u32[]{:S(2)}, u32[]{:S(2)}) %all-to-all-start) | async-done | bytes 2097184 | tf_op jit(solution)/shard_map/all_to_all | solution.py:370
  130.6 3.5 %collective-permute-start.6 = (bf16[2,2048,128]{2,1,0:T(8,128)(2,1)}, bf16[2,2048,128]{2,1,0:T(8,128)(2,1)S(1)}, u32[]{:S(2)}, u32[]{:S(2)}) collective-permute-start(bf16[2,2048,128]{2,1,0:T(8,128)(2,1)} %get-tuple-element.30.refs_0_.refs_1_), channel_id=1, source_target_pairs={{0,1},{1,0},{2,3},{3,2},{4,5},{5,4},{6,7},{7,6},{8,9},{9,8},{10,11... | collective-permute-start | bytes 3145736 | tf_op jit(solution)/shard_map/ppermute | solution.py:375
  138.2 15.2 %forward.1 = (bf16[2048,128]{1,0:T(8,128)(2,1)S(1)}, f32[2048,128]{1,0:T(8,128)S(1)}) custom-call(s32[16]{0:T(128)S(1)} %get-tuple-element.54.full_ref, s32[16]{0:T(128)S(1)} %get-tuple-element.50.kcnt_ref, s32[16,10]{1,0:T(8,128)S(1)} %copy.11.kidx_ref, bf16[2,2048,128]{2,1,0:T(8,128)(2,1)S(1)} %copy-done.6, ...), custom_call_target="tpu_custom_call" | custom-call | flops 16000000000 | bytes 5242880 | tf_op jit(solution)/shard_map/forward/pallas_call | solution.py:383
  153.4 1.9 collective-permute-start.9
  156.7 5.1 %collective-permute-start.7 = (bf16[2048,128]{1,0:T(8,128)(2,1)S(1)}, bf16[2048,128]{1,0:T(8,128)(2,1)S(1)}, u32[]{:S(2)}, u32[]{:S(2)}) collective-permute-start(bf16[2048,128]{1,0:T(8,128)(2,1)S(1)} %get-tuple-element.43.o_ref.attn_ref.refs_0_), channel_id=1, source_target_pairs={{0,2},{2,0},{4,6},{10,8},{12,14},{14,12},{16,18},{20,22},{22,20},{... | collective-permute-start | bytes 1572872 | tf_op jit(solution)/shard_map/ppermute | solution.py:399
  161.8 20.2 %backward.1 = (bf16[2048,128]{1,0:T(8,128)(2,1)S(1)}, bf16[2,2048,128]{2,1,0:T(8,128)(2,1)S(1)}, bf16[2,2048,128]{2,1,0:T(8,128)(2,1)S(1)}) custom-call(s32[16]{0:T(128)S(1)} %get-tuple-element.54.full_ref, s32[16]{0:T(128)S(1)} %get-tuple-element.50.kcnt_ref, s32[16,10]{1,0:T(8,128)S(1)} %copy.11.kidx_ref, bf16[2,2048,128]{2,1,0:T(8,128)(2,1)S(1)} %copy-done.6, ...), custom_call_target="tpu_custom_call" | custom-call | flops 20000000000 | bytes 8388608 | tf_op jit(solution)/shard_map/backward/pallas_call | solution.py:401
  185.3 1.9 copy-done.4
  190.4 3.0 tile.1
  197.1 2.3 collective-permute-done.10.refs_0_
  200.2 74.1 %all_to_all.10.chunks_ref = bf16[16,4,128,128]{3,2,1,0:T(8,128)(2,1)S(1)} all-to-all(bf16[16,4,128,128]{3,2,1,0:T(8,128)(2,1)S(1)} %unjoin.1), channel_id=1, replica_groups=mesh['ctx'=16,'tp'=2] {'ctx'}, dimensions={0} | all-to-all | bytes 4194304 | tf_op jit(solution)/shard_map/all_to_all | solution.py:471
  276.0 2.3 collective-permute-start.11
  278.3 18.8 %all-gather.7.cloned.1.call-done = bf16[3072,768]{1,0:T(8,128)(2,1)} async-done(((bf16[192,768]{1,0:T(8,128)(2,1)}), bf16[3072,768]{1,0:T(8,128)(2,1)}) %all-gather.7.cloned.1.call-update) | async-done | bytes 4718608 | tf_op jit(solution)/shard_map/all_gather | solution.py:441
  297.1 3.2 constant_dynamic-slice_fusion
  300.3 1.9 collective-permute-start.14
  302.2 2.9 unpack.1
  305.1 3.7 %fusion.8 = f32[256,3072]{1,0:T(8,128)S(1)} fusion(bf16[256,768]{1,0:T(8,128)(2,1)S(1)} %get-tuple-element.39, bf16[768,3072]{1,0:T(8,128)(2,1)} %param.11), kind=kOutput, calls=%fused_computation.55 | convolution fusion | flops 1207959552 | bytes 8257536 | tf_op jit(solution)/shard_map/dot_general | solution.py:27
  310.7 2.4 collective-permute-done.12
  313.1 2.7 add_convert_fusion
  315.8 7.6 %place.1 = f32[768,3072]{1,0:T(8,128)} custom-call(s32[2]{0:T(128)S(1)} %pad_add_fusion.where_ref, bf16[16,192,768]{2,1,0:T(8,128)(2,1)} %bitcast.17, bf16[8,192,768]{2,1,0:T(8,128)(2,1)S(1)} %collective-permute-done.14.refs_1_), custom_call_target="tpu_custom_call" | custom-call | bytes 16777216 | tf_op jit(solution)/shard_map/place/pallas_call | solution.py:449
  (87 shorter events, 35.0 us)
Async XLA Ops:
  7.2 29.5 %copy-start = (s32[32]{0:T(128)S(1)}, s32[32]{0:T(128)}, u32[]{:S(2)}) copy-start(s32[32]{0:T(128)} %param.13) | copy-start | bytes 388
  7.2 3.0 collective-permute-start
  10.0 8.5 %collective-permute-start.1 = (bf16[3,128,768]{2,1,0:T(8,128)(2,1)S(1)}, bf16[3,128,768]{2,1,0:T(8,128)(2,1)S(1)}, u32[]{:S(2)}, u32[]{:S(2)}) collective-permute-start(bf16[3,128,768]{2,1,0:T(8,128)(2,1)S(1)} %pad_maximum_fusion.4), channel_id=1, source_target_pairs={{0,1},{1,0},{2,3},{3,2},{4,5},{5,4},{6,7},{7,6},{8,9},{9,8},{10,11... | collective-permute-start | bytes 1769480 | tf_op jit(solution)/shard_map/ppermute | solution.py:333
  14.1 4.5 %copy-start.1 = (bf16[256,768]{1,0:T(8,128)(2,1)S(1)}, bf16[256,768]{1,0:T(8,128)(2,1)}, u32[]{:S(2)}) copy-start(bf16[256,768]{1,0:T(8,128)(2,1)} %refs_0_.1) | copy-start | bytes 1179652
  14.1 4.5 %copy-start.2 = (bf16[256,768]{1,0:T(8,128)(2,1)S(1)}, bf16[256,768]{1,0:T(8,128)(2,1)}, u32[]{:S(2)}) copy-start(bf16[256,768]{1,0:T(8,128)(2,1)} %refs_1_.1) | copy-start | bytes 1179652
  14.1 4.5 %copy-start.3 = (bf16[256,768]{1,0:T(8,128)(2,1)S(1)}, bf16[256,768]{1,0:T(8,128)(2,1)}, u32[]{:S(2)}) copy-start(bf16[256,768]{1,0:T(8,128)(2,1)} %refs_2_.1) | copy-start | bytes 1179652
  14.2 4.4 %collective-permute-start.2 = (bf16[1,128,768]{2,1,0:T(8,128)(2,1)S(1)}, bf16[1,128,768]{2,1,0:T(8,128)(2,1)S(1)}, u32[]{:S(2)}, u32[]{:S(2)}) collective-permute-start(bf16[1,128,768]{2,1,0:T(8,128)(2,1)S(1)} %dynamic-slice_bitcast_fusion), channel_id=1, source_target_pairs={{0,1},{1,0},{2,3},{3,2},{4,5},{5,4},{6,7},{7,6},{8,9},{9,8},{10,11... | collective-permute-start | bytes 589832 | tf_op jit(solution)/shard_map/ppermute | solution.py:333
  15.7 7.5 %collective-permute-start.5 = (bf16[128,768]{1,0:T(8,128)(2,1)S(1)}, bf16[128,768]{1,0:T(8,128)(2,1)S(1)}, u32[]{:S(2)}, u32[]{:S(2)}) collective-permute-start(bf16[128,768]{1,0:T(8,128)(2,1)S(1)} %get-tuple-element.56), channel_id=1, source_target_pairs={{0,6},{2,4},{4,2},{6,0},{8,14},{10,12},{12,10},{14,8},{16,22},{18,... | collective-permute-start | bytes 589832 | tf_op jit(solution)/shard_map/ppermute | solution.py:355
  17.0 9.4 %collective-permute-start.3 = (bf16[128,768]{1,0:T(8,128)(2,1)S(1)}, bf16[128,768]{1,0:T(8,128)(2,1)S(1)}, u32[]{:S(2)}, u32[]{:S(2)}) collective-permute-start(bf16[128,768]{1,0:T(8,128)(2,1)S(1)} %get-tuple-element.58), channel_id=1, source_target_pairs={{0,2},{2,0},{4,6},{6,4},{8,10},{10,8},{12,14},{14,12},{16,18},{18,... | collective-permute-start | bytes 589832 | tf_op jit(solution)/shard_map/ppermute | solution.py:355
  17.2 10.6 %collective-permute-start.4 = (bf16[128,768]{1,0:T(8,128)(2,1)S(1)}, bf16[128,768]{1,0:T(8,128)(2,1)S(1)}, u32[]{:S(2)}, u32[]{:S(2)}) collective-permute-start(bf16[128,768]{1,0:T(8,128)(2,1)S(1)} %get-tuple-element.59), channel_id=1, source_target_pairs={{0,4},{2,6},{4,0},{6,2},{8,12},{10,14},{12,8},{14,10},{16,20},{18,... | collective-permute-start | bytes 589832 | tf_op jit(solution)/shard_map/ppermute | solution.py:355
  29.2 98.7 %all-to-all-start = ((bf16[16,4,128,128]{3,2,1,0:T(8,128)(2,1)}), bf16[16,4,128,128]{3,2,1,0:T(8,128)(2,1)S(1)}, u32[]{:S(2)}, u32[]{:S(2)}) async-start(bf16[16,4,128,128]{3,2,1,0:T(8,128)(2,1)} %pack.1), calls=%async_computation | async-start | bytes 4194304 | tf_op jit(solution)/shard_map/all_to_all | solution.py:370
  35.8 149.5 %all-gather.5.cloned.1.call-start = ((), (), s32[]{:S(2)}) async-start(), calls=%async_computation.2 | async-start | bytes 3932160 | tf_op jit(solution)/shard_map/all_gather | solution.py:368
  36.6 260.5 %all-gather.7.cloned.1.call-start = ((), (), s32[]{:S(2)}) async-start(), calls=%async_computation.3 | async-start | bytes 5013504 | tf_op jit(solution)/shard_map/all_gather | solution.py:441
  130.6 6.0 %collective-permute-start.6 = (bf16[2,2048,128]{2,1,0:T(8,128)(2,1)}, bf16[2,2048,128]{2,1,0:T(8,128)(2,1)S(1)}, u32[]{:S(2)}, u32[]{:S(2)}) collective-permute-start(bf16[2,2048,128]{2,1,0:T(8,128)(2,1)} %get-tuple-element.30.refs_0_.refs_1_), channel_id=1, source_target_pairs={{0,1},{1,0},{2,3},{3,2},{4,5},{5,4},{6,7},{7,6},{8,9},{9,8},{10,11... | collective-permute-start | bytes 3145736 | tf_op jit(solution)/shard_map/ppermute | solution.py:375
  136.6 16.8 %copy-start.7 = (bf16[2,2048,128]{2,1,0:T(8,128)(2,1)}, bf16[2,2048,128]{2,1,0:T(8,128)(2,1)S(1)}, u32[]{:S(2)}) copy-start(bf16[2,2048,128]{2,1,0:T(8,128)(2,1)S(1)} %collective-permute-done.6.refs_2_.refs_3_) | copy-start | bytes 3145732
  153.4 29.5 %collective-permute-start.9 = (bf16[2048,128]{1,0:T(8,128)(2,1)S(1)}, bf16[2048,128]{1,0:T(8,128)(2,1)S(1)}, u32[]{:S(2)}, u32[]{:S(2)}) collective-permute-start(bf16[2048,128]{1,0:T(8,128)(2,1)S(1)} %get-tuple-element.43.o_ref.attn_ref.refs_0_), channel_id=1, source_target_pairs={{0,6},{2,4},{4,2},{10,12},{12,10},{14,8},{16,22},{20,18},{22,16},{... | collective-permute-start | bytes 1572872 | tf_op jit(solution)/shard_map/ppermute | solution.py:399
  155.3 28.4 %collective-permute-start.8 = (bf16[2048,128]{1,0:T(8,128)(2,1)S(1)}, bf16[2048,128]{1,0:T(8,128)(2,1)S(1)}, u32[]{:S(2)}, u32[]{:S(2)}) collective-permute-start(bf16[2048,128]{1,0:T(8,128)(2,1)S(1)} %get-tuple-element.43.o_ref.attn_ref.refs_0_), channel_id=1, source_target_pairs={{0,4},{2,6},{4,0},{10,14},{12,8},{14,10},{16,20},{20,16},{22,18},{... | collective-permute-start | bytes 1572872 | tf_op jit(solution)/shard_map/ppermute | solution.py:399
  156.7 27.9 %collective-permute-start.7 = (bf16[2048,128]{1,0:T(8,128)(2,1)S(1)}, bf16[2048,128]{1,0:T(8,128)(2,1)S(1)}, u32[]{:S(2)}, u32[]{:S(2)}) collective-permute-start(bf16[2048,128]{1,0:T(8,128)(2,1)S(1)} %get-tuple-element.43.o_ref.attn_ref.refs_0_), channel_id=1, source_target_pairs={{0,2},{2,0},{4,6},{10,8},{12,14},{14,12},{16,18},{20,22},{22,20},{... | collective-permute-start | bytes 1572872 | tf_op jit(solution)/shard_map/ppermute | solution.py:399
  190.3 6.3 %copy-start.9 = (bf16[2,2048,128]{2,1,0:T(8,128)(2,1)S(1)}, bf16[2,2048,128]{2,1,0:T(8,128)(2,1)}, u32[]{:S(2)}) copy-start(bf16[2,2048,128]{2,1,0:T(8,128)(2,1)} %copy-done.8) | copy-start | bytes 3145732
  193.4 2.5 collective-permute-start.13
  196.7 2.7 collective-permute-start.10
  276.0 26.2 %collective-permute-start.11 = (bf16[6,4,128,128]{3,2,1,0:T(8,128)(2,1)}, bf16[6,4,128,128]{3,2,1,0:T(8,128)(2,1)}, u32[]{:S(2)}, u32[]{:S(2)}) collective-permute-start(bf16[6,4,128,128]{3,2,1,0:T(8,128)(2,1)} %get-tuple-element.38), channel_id=1, source_target_pairs={{0,1},{1,0},{2,3},{3,2},{4,5},{5,4},{6,7},{7,6},{8,9},{9,8},{10,11... | collective-permute-start | bytes 2359304 | tf_op jit(solution)/shard_map/ppermute | solution.py:476
  300.3 15.5 %collective-permute-start.14 = (bf16[8,192,768]{2,1,0:T(8,128)(2,1)}, bf16[8,192,768]{2,1,0:T(8,128)(2,1)S(1)}, u32[]{:S(2)}, u32[]{:S(2)}) collective-permute-start(bf16[8,192,768]{2,1,0:T(8,128)(2,1)} %constant_dynamic-slice_fusion), channel_id=1, source_target_pairs={{0,1},{1,0},{2,3},{3,2},{4,5},{5,4},{6,7},{7,6},{8,9},{9,8},{10,11... | collective-permute-start | bytes 7077896 | tf_op jit(solution)/shard_map/ppermute | solution.py:444
  310.6 2.5 collective-permute-start.12
  (12 other events, 15.6 us)
Sparse Core Ops, SparseCore 0:
  38.8 93.3 all-gather.4
  196.8 100.1 all-gather.6

commit v6 on v5

--- a/solution.py
+++ b/solution.py
@@ -45,33 +45,30 @@
     return place < heads_plane, chip // in_plane * heads_plane + min(place, heads_plane - 1)
 
 
-def pack_kernel(n, t, where_ref, *refs):
-    arrays, got, outs, heads_all = refs[:4], refs[4:4 + 2 * (t - 1)], refs[4 + 2 * (t - 1):-1], refs[-1]
+def pack_kernel(n, t, count, where_ref, *refs):
+    arrays, got, (out_ref, heads_all) = refs[:count], refs[count:count + t - 1], refs[count + t - 1:]
     core = where_ref[1]
     sub = heads_all.shape[2]
     heads_here = heads_all.shape[0] // t
-    for a in range(4):
+    for a in range(count):
         for h in range(heads_here):
             column = pl.ds(h * HEAD, HEAD)
             heads_all[core * heads_here + h, a] = arrays[a][pl.ds(core * sub, sub), column]
             for s in range(1, t):
                 first = (core + t - s) % t * heads_here
-                source = got[2 * (s - 1)] if a < 3 else got[2 * (s - 1) + 1]
-                heads_all[first + h, a] = source[a % 3, :, column]
-    out_ref = outs[0]
+                heads_all[first + h, a] = got[s - 1][a, :, column]
     for k in range(n):
         held, head = head_of(k, n // PLANES, heads_all.shape[0] // PLANES)
         out_ref[k] = heads_all[head] if held else jnp.zeros_like(heads_all[0])
 
 
-def join_kernel(n, where_ref, chunks_ref, qg_ref, kv_ref):
+def join_kernel(n, where_ref, chunks_ref, q_ref, kv_ref):
     sub = chunks_ref.shape[2]
     for k in range(n):
         at = pl.ds(k * sub, sub)
-        qg_ref[0, at] = chunks_ref[k, 0]
+        q_ref[at] = chunks_ref[k, 0]
         kv_ref[0, at] = chunks_ref[k, 1]
         kv_ref[1, at] = chunks_ref[k, 2]
-        qg_ref[1, at] = chunks_ref[k, 3]
 
 
 def unjoin_kernel(n, t, where_ref, attn_ref, dq_ref, dkv_ref, *refs):
@@ -128,6 +125,10 @@
     @pl.when(step == pl.num_programs(0) - 1)
     def _():
         piece = own_ref.shape[0]
+        if piece == total.shape[0]:
+            own_ref[...] = total[...]
+            sends[0][...] = total[...].astype(BF16)
+            return
         own_ref[...] = total[pl.ds(pl.multiple_of(core * piece, piece), piece)]
         for s in range(1, t):
             at = pl.ds(pl.multiple_of((core + s) % t * piece, piece), piece)
@@ -157,7 +158,7 @@
 def forward_kernel(t, tile, count, full_ref, kcnt_ref, kidx_ref, q_ref, *refs):
     parts, (out_ref, lse_ref, k_few, v_few, k_ref, v_ref) = refs[:2 * t], refs[2 * t:]
     row = pl.program_id(0)
-    q = q_ref[0]
+    q = q_ref[...]
 
     @pl.when(row == 0)
     def _():
@@ -201,8 +202,8 @@
         dk_acc[...] = jnp.zeros_like(dk_acc)
         dv_acc[...] = jnp.zeros_like(dv_acc)
 
-    q = q_ref[0]
-    g = g_ref[0]
+    q = q_ref[...]
+    g = g_ref[...]
     delta = jnp.sum(g.astype(F32) * o_ref[...].astype(F32), axis=1, keepdims=True)
     lse = lse_ref[:, :1]
     unit = HEAD ** -0.5
@@ -252,10 +253,6 @@
 
 def one_array(which, length):
     return pl.BlockSpec((1, length, HEAD), lambda *_: (which, 0, 0))
-
-
-def tile_block(which, tile):
-    return pl.BlockSpec((1, tile, HEAD), lambda r, *_: (which, r, 0))
 
 
 def simple_call(kernel, name, scalars, inputs, outputs, scratch=()):
@@ -280,6 +277,61 @@
     return [(c, (c + s) % t) for c in range(t)]
 
 
+def place_xor_kernel(place_ref, *refs):
+    sources, out_ref = refs[:-1], refs[-1]
+    step = pl.program_id(0)
+    for u in range(2):
+        own, beside, above, upper, lower = sources[5 * u:5 * u + 5]
+        for v, source in enumerate((own, beside, above)):
+            @pl.when(step == 4 * u + v)
+            def _(source=source):
+                out_ref[...] = source[...].astype(F32)
+
+        @pl.when(step == 4 * u + 3)
+        def _(upper=upper, lower=lower):
+            middle = upper.shape[0]
+            out_ref[:middle] = upper[...].astype(F32)
+            out_ref[middle:] = lower[...].astype(F32)
+
+
+def gather_tiles_by_core(n, t, tile_sum, chip, core):
+    in_plane = n // PLANES
+    plane, seat = chip // in_plane, chip % in_plane
+    tile_rows, cols = tile_sum.shape
+    across = [
+        (i * t + c, (i ^ 2 * in_plane) * t + c)
+        for i in range(n) for c in range(t) if i // in_plane // 2 == c
+    ]
+    from_half = lax.ppermute(tile_sum, ("ctx", "tp"), across)
+
+    def swap(x, k):
+        return lax.ppermute(x, "ctx", [(i, i ^ k) for i in range(n)])
+
+    first = jnp.where(plane // 2 == core, tile_sum, from_half)
+    second = swap(first, in_plane)
+    middle = tile_rows // 2
+    sources = []
+    for mine in (first, second):
+        beside, above = swap(mine, 1), swap(mine, 2)
+        sources += [mine, beside, above, swap(beside[:middle], 2), swap(above[middle:], 1)]
+    place = jnp.stack([plane % 2, seat]).astype(jnp.int32)
+    return pl.pallas_call(
+        place_xor_kernel,
+        grid_spec=pltpu.PrefetchScalarGridSpec(
+            num_scalar_prefetch=1,
+            grid=(8,),
+            in_specs=[whole_block(x.shape) for x in sources],
+            out_specs=pl.BlockSpec(
+                (tile_rows, cols), lambda s, place: (s // 4 ^ place[0], s % 4 ^ place[1])
+            ),
+        ),
+        out_shape=jax.ShapeDtypeStruct((2 * tile_rows, in_plane * cols), F32),
+        compiler_params=pltpu.CompilerParams(vmem_limit_bytes=48 * 2**20),
+        cost_estimate=pl.CostEstimate(flops=0, bytes_accessed=2**24, transcendentals=0),
+        name="place",
+    )(place, *sources)
+
+
 def per_device(n, t, queries, key_vectors, value_vectors, out_weight, out_grad, block_segment):
     rows, width = queries.shape
     heads_here = width // HEAD
@@ -356,21 +408,25 @@
     (plane_grad,) = simple_call(
         functools.partial(seats_kernel, in_plane), "seats", where, plane_got, [shape(in_plane, sub, cols)]
     )
-    got = [x for pair in zip(got_qkv, got_g) for x in pair]
-    (sent,) = simple_call(
-        functools.partial(pack_kernel, n, t), "pack", where,
-        [queries, key_vectors, value_vectors, grad_attn] + got,
-        [shape(n, 4, sub, HEAD)],
-        [pltpu.VMEM((heads, 4, sub, HEAD), BF16)],
-    )
-    sent, plane_grad = lax.optimization_barrier((sent, plane_grad))
+    def pack(arrays, got):
+        (sent,) = simple_call(
+            functools.partial(pack_kernel, n, t, len(arrays)), "pack", where,
+            arrays + got, [shape(n, len(arrays), sub, HEAD)],
+            [pltpu.VMEM((heads, len(arrays), sub, HEAD), BF16)],
+        )
+        return sent
+
+    sent_qkv = pack([queries, key_vectors, value_vectors], got_qkv)
+    sent_g = pack([grad_attn], got_g)
+    chunks = lax.all_to_all(sent_qkv, "ctx", 0, 0, tiled=True)
+    chunks, sent_g, plane_grad = lax.optimization_barrier((chunks, sent_g, plane_grad))
     lines = [[a * in_plane + b for a in range(PLANES)] for b in range(in_plane)]
     slice_grad = lax.all_gather(plane_grad, "ctx", axis_index_groups=lines)
     slice_grad = slice_grad.reshape(n * sub, cols)
-    chunks = lax.all_to_all(sent, "ctx", 0, 0, tiled=True)
+    g_rows = lax.all_to_all(sent_g, "ctx", 0, 0, tiled=True).reshape(n * sub, HEAD)
     length = n * sub
-    qg, kv = simple_call(
-        functools.partial(join_kernel, n), "join", where, [chunks], [shape(2, length, HEAD)] * 2
+    q_rows, kv = simple_call(
+        functools.partial(join_kernel, n), "join", where, [chunks], [shape(length, HEAD), shape(2, length, HEAD)]
     )
     kv_all = [kv] + [lax.ppermute(kv, "tp", shifts(t, s)) for s in range(1, t)]
 
@@ -385,7 +441,7 @@
         grid_spec=pltpu.PrefetchScalarGridSpec(
             num_scalar_prefetch=3,
             grid=(tiles_q,),
-            in_specs=[tile_block(0, tile)] + part_blocks,
+            in_specs=[row_block] + part_blocks,
             out_specs=[row_block, row_block],
             scratch_shapes=few,
         ),
@@ -393,7 +449,7 @@
         compiler_params=params,
         cost_estimate=pl.CostEstimate(flops=16 * 10**9, bytes_accessed=5 * 2**20, transcendentals=2**22),
         name="forward",
-    )(full, kcnt, kidx, qg, *part_arrays)
+    )(full, kcnt, kidx, q_rows, *part_arrays)
 
     travel = [attn] + [
         lax.ppermute(attn, "ctx", [(i, i ^ k) for i in range(n) if held[i]]) for k in range(1, in_plane)
@@ -403,7 +459,7 @@
         grid_spec=pltpu.PrefetchScalarGridSpec(
             num_scalar_prefetch=3,
             grid=(tiles_q,),
-            in_specs=[tile_block(0, tile), tile_block(1, tile), row_block, row_block] + part_blocks,
+            in_specs=[row_block] * 4 + part_blocks,
             out_specs=[row_block] + [whole_block((2, length, HEAD))] * t,
             scratch_shapes=few + [pltpu.VMEM((tiles_k, tile, HEAD), F32)] * 2,
         ),
@@ -411,12 +467,13 @@
         compiler_params=params,
         cost_estimate=pl.CostEstimate(flops=20 * 10**9, bytes_accessed=8 * 2**20, transcendentals=2**22),
         name="backward",
-    )(full, kcnt, kidx, qg, qg, attn, lse, *part_arrays)
+    )(full, kcnt, kidx, q_rows, g_rows, attn, lse, *part_arrays)
 
     *travel, dq = lax.optimization_barrier((*travel, dq))
 
     tile_rows = heads_plane * HEAD
-    piece = tile_rows // t
+    by_core = in_plane == 4 and t == 2
+    piece = tile_rows if by_core else tile_rows // t
     step_rows = length // 4
     tile_own, *tile_sends = pl.pallas_call(
         functools.partial(tile_kernel, in_plane, heads_plane, t),
@@ -438,28 +495,31 @@
     tile_sum = tile_own
     for s in range(1, t):
         tile_sum = tile_sum + lax.ppermute(tile_sends[s - 1], "tp", shifts(t, s)).astype(F32)
-    tiles = lax.all_gather(tile_sum.astype(BF16), "ctx")
-    here = n // t
-    tiles_core = [tiles] + [
-        lax.ppermute(
-            lax.dynamic_slice_in_dim(tiles, (core + s) % t * here, here, 0), "tp", shifts(t, s)
-        )
-        for s in range(1, t)
-    ]
-    grad_weight = pl.pallas_call(
-        functools.partial(place_kernel, t),
-        grid_spec=pltpu.PrefetchScalarGridSpec(
-            num_scalar_prefetch=1,
-            grid=(here,),
-            in_specs=[pl.BlockSpec((1, piece, cols), lambda r, where: (where[1] * here + r, 0, 0))]
-            + [pl.BlockSpec((1, piece, cols), lambda r, *_: (r, 0, 0))] * (t - 1),
-            out_specs=pl.BlockSpec((tile_rows, cols), lambda r, *_: (r // in_plane, r % in_plane)),
-        ),
-        out_shape=jax.ShapeDtypeStruct((width, model), F32),
-        compiler_params=params,
-        cost_estimate=pl.CostEstimate(flops=0, bytes_accessed=2**24, transcendentals=0),
-        name="place",
-    )(where, *tiles_core)
+    if by_core:
+        grad_weight = gather_tiles_by_core(n, t, tile_sum.astype(BF16), chip, core)
+    else:
+        tiles = lax.all_gather(tile_sum.astype(BF16), "ctx")
+        here = n // t
+        tiles_core = [tiles] + [
+            lax.ppermute(
+                lax.dynamic_slice_in_dim(tiles, (core + s) % t * here, here, 0), "tp", shifts(t, s)
+            )
+            for s in range(1, t)
+        ]
+        grad_weight = pl.pallas_call(
+            functools.partial(place_kernel, t),
+            grid_spec=pltpu.PrefetchScalarGridSpec(
+                num_scalar_prefetch=1,
+                grid=(here,),
+                in_specs=[pl.BlockSpec((1, piece, cols), lambda r, where: (where[1] * here + r, 0, 0))]
+                + [pl.BlockSpec((1, piece, cols), lambda r, *_: (r, 0, 0))] * (t - 1),
+                out_specs=pl.BlockSpec((tile_rows, cols), lambda r, *_: (r // in_plane, r % in_plane)),
+            ),
+            out_shape=jax.ShapeDtypeStruct((width, model), F32),
+            compiler_params=params,
+            cost_estimate=pl.CostEstimate(flops=0, bytes_accessed=2**24, transcendentals=0),
+            name="place",
+        )(where, *tiles_core)
 
     got_dkv = [
         lax.ppermute(dkv[s], "tp", [(c, (c - s) % t) for c in range(t)]) for s in range(1, t)

time: 332 us -> 272 us (0.82)
  blocking collectives: 74.1 us -> 0 us
  starting transfers between devices: 28.6 us -> 50.7 us
  waiting for transfers between devices: 124 us -> 112 us
    all_to_all x1 -> x0, blocking collectives: 74.1 us -> none  [per_device(): chunks = lax.all_to_all(sent, 'ctx', 0, 0, tiled=True)]
    all_to_all x1, waiting for transfers between devices: 90 us -> 41.9 us  [per_device(): chunks = lax.all_to_all(sent, 'ctx', 0, 0, tiled=True)]
    ppermute x1 -> x10, waiting for transfers between devices: 0.01 us -> 22.9 us  [the longest x9 22.8 us: swap(): return lax.ppermute(x, 'ctx', [(i, i ^ k) for i in range(n)])]
    all_gather x1 -> x0, waiting for transfers between devices: 18.8 us -> none  [per_device(): tiles = lax.all_gather(tile_sum.astype(BF16), 'ctx')]
    ppermute x3, waiting for transfers between devices: 0.01 us -> 15.9 us  [per_device(): lax.ppermute(attn, 'ctx', [(i, i ^ k) for i in range(n) if held[i]])]
    all_to_all x0 -> x2, waiting for transfers between devices: none -> 13.2 us  [the longest x1 7.29 us: per_device(): lax.all_to_all(sent_g, 'ctx', 0, 0, tiled=True).reshape(n * sub, HEAD)]
    all_to_all x0 -> x2, starting transfers between devices: none -> 11.5 us  [the longest x1 6.74 us: per_device(): chunks = lax.all_to_all(sent_qkv, 'ctx', 0, 0, tiled=True)]
    ppermute x1 -> x10, starting transfers between devices: 1.87 us -> 9.1 us  [the longest x9 7.81 us: swap(): return lax.ppermute(x, 'ctx', [(i, i ^ k) for i in range(n)])]
  transfers between devices with their start and end apart: 18 -> 28, of which waited for: 9 -> 15; matrix products, arithmetic and copies ran while one was open for 6% -> 7% of each run, Pallas kernels for 14% -> 20%
where the time goes in v6:
time: 272 us; the launch traced here: 268 us
  waiting for transfers between devices  112 us (41%)
  Pallas kernels  56.5 us (21%)
  starting transfers between devices  50.7 us (19%)
  local copies, waits for them, and re-layouts  20.2 us (7%)
  between operations  14.4 us (5%)
  matrix products  7.51 us (3%)
  other arithmetic  6.53 us (2%)
    all_to_all x1, waiting for transfers between devices, per_device(): chunks = lax.all_to_all(sent, 'ctx', 0, 0, tiled=True)  41.9 us
    ppermute x9, waiting for transfers between devices, swap(): return lax.ppermute(x, 'ctx', [(i, i ^ k) for i in range(n)])  22.8 us
    pallas_call x1, Pallas kernels, per_device(): pl.pallas_call(functools.partial(backward_kernel, t, tile, count), grid_s...  20.1 us
    ppermute x3, waiting for transfers between devices, per_device(): lax.ppermute(attn, 'ctx', [(i, i ^ k) for i in range(n) if held[i]])  15.9 us
    pallas_call x1, Pallas kernels, per_device(): pl.pallas_call(functools.partial(forward_kernel, t, tile, count), grid_sp...  13.9 us
    ppermute x3, waiting for transfers between devices, per_device(): plane_got.append(lax.ppermute(there, 'ctx', [(i, i ^ k) for i in range(n)]))  13.1 us
    unnamed x42, local copies, waits for them, and re-layouts  11.9 us
    pallas_call x7, Pallas kernels, simple_call(): pl.pallas_call(kernel, grid_spec=pltpu.PrefetchScalarGridSpec(num_scalar_...  10.9 us
  transfers between devices with their start and end apart: 28, of which 15 were waited for; matrix products, arithmetic and copies ran while one was open for 7% of the time, Pallas kernels for 20%

profile of v6, /device:TPU:13, one launch (start us, length us, event | category | flops | bytes accessed | tf_op | source)
XLA Modules:
  0.0 268.0 jit_solution(5845113751747040158)
XLA Ops:
  13.8 6.7 %all-to-all-start = ((bf16[16,3,128,128]{3,2,1,0:T(8,128)(2,1)}), bf16[16,3,128,128]{3,2,1,0:T(8,128)(2,1)S(1)}, u32[]{:S(2)}, u32[]{:S(2)}) async-start(bf16[16,3,128,128]{3,2,1,0:T(8,128)(2,1)} %pack.2), calls=%async_computation | async-start | bytes 3145728 | tf_op jit(solution)/shard_map/all_to_all | solution.py:421
  24.9 3.8 %fusion.1.refs_0_ = bf16[256,768]{1,0:T(8,128)(2,1)S(1)} fusion(bf16[768,3072]{1,0:T(8,128)(2,1)} %param.11, bf16[256,1536]{1,0:T(8,128)(2,1)S(1)} %get-tuple-element.63, bf16[256,1536]{1,0:T(8,128)(2,1)S(1)} %get-tuple-element.62), kind=kOutput, calls=%fused_computation.14 | convolution fusion | flops 1211301888 | bytes 6684672 | tf_op jit(solution)/shard_map/dot_general | solution.py:27
  36.9 11.1 %collective-permute-done.5.refs_3_ = bf16[128,768]{1,0:T(8,128)(2,1)S(1)} collective-permute-done((bf16[128,768]{1,0:T(8,128)(2,1)}, bf16[128,768]{1,0:T(8,128)(2,1)S(1)}, u32[]{:S(2)}, u32[]{:S(2)}) %collective-permute-start.5) | collective-permute-done | bytes 196640 | tf_op jit(solution)/shard_map/ppermute | solution.py:407
  51.5 5.9 %all-to-all-done.chunks_ref = bf16[16,3,128,128]{3,2,1,0:T(8,128)(2,1)S(1)} async-done(((bf16[16,3,128,128]{3,2,1,0:T(8,128)(2,1)}), bf16[16,3,128,128]{3,2,1,0:T(8,128)(2,1)S(1)}, u32[]{:S(2)}, u32[]{:S(2)}) %all-to-all-start) | async-done | bytes 1572896 | tf_op jit(solution)/shard_map/all_to_all | solution.py:421
  60.6 4.8 %all-to-all-start.1 = ((bf16[16,1,128,128]{3,2,1,0:T(8,128)(2,1)}), bf16[16,1,128,128]{3,2,1,0:T(8,128)(2,1)S(1)}, u32[]{:S(2)}, u32[]{:S(2)}) async-start(bf16[16,1,128,128]{3,2,1,0:T(8,128)(2,1)} %pack.3), calls=%async_computation.1 | async-start | bytes 1048576 | tf_op jit(solution)/shard_map/all_to_all | solution.py:426
  67.0 13.9 %forward.1 = (bf16[2048,128]{1,0:T(8,128)(2,1)S(1)}, f32[2048,128]{1,0:T(8,128)S(1)}) custom-call(s32[16]{0:T(128)S(1)} %get-tuple-element.56.full_ref, s32[16]{0:T(128)S(1)} %get-tuple-element.52.kcnt_ref, s32[16,10]{1,0:T(8,128)S(1)} %copy.11.kidx_ref, bf16[2048,128]{1,0:T(8,128)(2,1)S(1)} %get-tuple-element.30.q_ref, bf16[2,2048,128]{2,1,0:T(8,128)(2,1)S(1)} %copy-done.8, ...), custom_call_target="tpu_custom_call" | custom-call | flops 16000000000 | bytes 5242880 | tf_op jit(solution)/shard_map/forward/pallas_call | solution.py:439
  82.0 7.3 %all-to-all-done.1 = bf16[16,1,128,128]{3,2,1,0:T(8,128)(2,1)S(1)} async-done(((bf16[16,1,128,128]{3,2,1,0:T(8,128)(2,1)}), bf16[16,1,128,128]{3,2,1,0:T(8,128)(2,1)S(1)}, u32[]{:S(2)}, u32[]{:S(2)}) %all-to-all-start.1) | async-done | bytes 524320 | tf_op jit(solution)/shard_map/all_to_all | solution.py:426
  90.5 20.1 %backward.1 = (bf16[2048,128]{1,0:T(8,128)(2,1)S(1)}, bf16[2,2048,128]{2,1,0:T(8,128)(2,1)S(1)}, bf16[2,2048,128]{2,1,0:T(8,128)(2,1)S(1)}) custom-call(s32[16]{0:T(128)S(1)} %get-tuple-element.56.full_ref, s32[16]{0:T(128)S(1)} %get-tuple-element.52.kcnt_ref, s32[16,10]{1,0:T(8,128)S(1)} %copy.11.kidx_ref, bf16[2048,128]{1,0:T(8,128)(2,1)S(1)} %get-tuple-element.30.q_ref, ...), custom_call_target="tpu_custom_call" | custom-call | flops 20000000000 | bytes 8388608 | tf_op jit(solution)/shard_map/backward/pallas_call | solution.py:457
  110.7 4.1 %collective-permute-start.10 = (bf16[2,2048,128]{2,1,0:T(8,128)(2,1)S(1)}, bf16[2,2048,128]{2,1,0:T(8,128)(2,1)S(1)}, u32[]{:S(2)}, u32[]{:S(2)}) collective-permute-start(bf16[2,2048,128]{2,1,0:T(8,128)(2,1)S(1)} %get-tuple-element.38), channel_id=1, source_target_pairs={{0,1},{1,0},{2,3},{3,2},{4,5},{5,4},{6,7},{7,6},{8,9},{9,8},{10,11... | collective-permute-start | bytes 3145736 | tf_op jit(solution)/shard_map/ppermute | solution.py:525
  118.0 5.1 %collective-permute-start.7 = (bf16[2048,128]{1,0:T(8,128)(2,1)S(1)}, bf16[2048,128]{1,0:T(8,128)(2,1)S(1)}, u32[]{:S(2)}, u32[]{:S(2)}) collective-permute-start(bf16[2048,128]{1,0:T(8,128)(2,1)S(1)} %get-tuple-element.45.o_ref.attn_ref.refs_0_), channel_id=1, source_target_pairs={{0,2},{2,0},{4,6},{10,8},{12,14},{14,12},{16,18},{20,22},{22,20},{... | collective-permute-start | bytes 1572872 | tf_op jit(solution)/shard_map/ppermute | solution.py:455
  123.2 7.9 %collective-permute-done.9.refs_3_ = bf16[2048,128]{1,0:T(8,128)(2,1)S(1)} collective-permute-done((bf16[2048,128]{1,0:T(8,128)(2,1)S(1)}, bf16[2048,128]{1,0:T(8,128)(2,1)S(1)}, u32[]{:S(2)}, u32[]{:S(2)}) %collective-permute-start.9) | collective-permute-done | bytes 524320 | tf_op jit(solution)/shard_map/ppermute | solution.py:455
  131.9 7.1 %collective-permute-done.8.refs_2_ = bf16[2048,128]{1,0:T(8,128)(2,1)S(1)} collective-permute-done((bf16[2048,128]{1,0:T(8,128)(2,1)S(1)}, bf16[2048,128]{1,0:T(8,128)(2,1)S(1)}, u32[]{:S(2)}, u32[]{:S(2)}) %collective-permute-start.8) | collective-permute-done | bytes 524320 | tf_op jit(solution)/shard_map/ppermute | solution.py:455
  142.8 7.2 %all-to-all-start.2 = ((bf16[16,4,128,128]{3,2,1,0:T(8,128)(2,1)}), bf16[16,4,128,128]{3,2,1,0:T(8,128)(2,1)S(1)}, u32[]{:S(2)}, u32[]{:S(2)}) async-start(bf16[16,4,128,128]{3,2,1,0:T(8,128)(2,1)} %copy-done.1), calls=%async_computation.2 | async-start | bytes 4194304 | tf_op jit(solution)/shard_map/all_to_all | solution.py:531
  153.2 4.8 %tile.1 = (f32[384,768]{1,0:T(8,128)S(1)}, bf16[384,768]{1,0:T(8,128)(2,1)S(1)}) custom-call(s32[2]{0:T(128)S(1)} %pad_add_fusion.where_ref, bf16[2048,128]{1,0:T(8,128)(2,1)S(1)} %get-tuple-element.45.o_ref.attn_ref.refs_0_, bf16[2048,128]{1,0:T(8,128)(2,1)S(1)} %copy-done.15, bf16[2048,128]{1,0:T(8,128)(2,1)S(1)} %copy-done.13, ...), custom_call_target="tpu_custom_call" | custom-call | flops 5000000000 | bytes 4194304 | tf_op jit(solution)/shard_map/tile/pallas_call | solution.py:478
  162.2 41.9 %all-to-all-done.2.chunks_ref = bf16[16,4,128,128]{3,2,1,0:T(8,128)(2,1)S(1)} async-done(((bf16[16,4,128,128]{3,2,1,0:T(8,128)(2,1)}), bf16[16,4,128,128]{3,2,1,0:T(8,128)(2,1)S(1)}, u32[]{:S(2)}, u32[]{:S(2)}) %all-to-all-start.2) | async-done | bytes 2097184 | tf_op jit(solution)/shard_map/all_to_all | solution.py:531
  206.6 2.4 collective-permute-start.11
  209.1 3.3 %collective-permute-start.19 = (bf16[384,768]{1,0:T(8,128)(2,1)S(1)}, bf16[384,768]{1,0:T(8,128)(2,1)S(1)}, u32[]{:S(2)}, u32[]{:S(2)}) collective-permute-start(bf16[384,768]{1,0:T(8,128)(2,1)S(1)} %broadcast_select_fusion.2.refs_0_), channel_id=1, source_target_pairs={{0,8},{2,10},{4,12},{6,14},{8,0},{10,2},{12,4},{14,6},{16,24},{18,... | collective-permute-start | bytes 1769480 | tf_op jit(solution)/shard_map/ppermute | solution.py:308
  212.8 12.0 %collective-permute-done.19.refs_5_ = bf16[384,768]{1,0:T(8,128)(2,1)S(1)} collective-permute-done((bf16[384,768]{1,0:T(8,128)(2,1)S(1)}, bf16[384,768]{1,0:T(8,128)(2,1)S(1)}, u32[]{:S(2)}, u32[]{:S(2)}) %collective-permute-start.19) | collective-permute-done | bytes 589856 | tf_op jit(solution)/shard_map/ppermute | solution.py:308
  227.3 2.9 %unpack.1 = (bf16[256,768]{1,0:T(8,128)(2,1)S(1)}, bf16[256,768]{1,0:T(8,128)(2,1)}, bf16[256,768]{1,0:T(8,128)(2,1)}, bf16[256,768]{1,0:T(8,128)(2,1)}) custom-call(s32[2]{0:T(128)S(1)} %pad_add_fusion.where_ref, bf16[6,4,128,128]{3,2,1,0:T(8,128)(2,1)S(1)} %copy-done.6, bf16[6,4,128,128]{3,2,1,0:T(8,128)(2,1)} %collective-permute-done.11.refs_1_), custom_call_target="tpu_custom_call" | custom-call | bytes 6291456 | tf_op jit(solution)/shard_map/unpack/pallas_call | solution.py:260
  230.2 3.7 %fusion.8 = f32[256,3072]{1,0:T(8,128)S(1)} fusion(bf16[256,768]{1,0:T(8,128)(2,1)S(1)} %get-tuple-element.41, bf16[768,3072]{1,0:T(8,128)(2,1)} %param.11), kind=kOutput, calls=%fused_computation.56 | convolution fusion | flops 1207959552 | bytes 8257536 | tf_op jit(solution)/shard_map/dot_general | solution.py:27
  242.8 3.1 %collective-permute-done.18.refs_4_ = bf16[192,768]{1,0:T(8,128)(2,1)} collective-permute-done((bf16[192,768]{1,0:T(8,128)(2,1)}, bf16[192,768]{1,0:T(8,128)(2,1)}, u32[]{:S(2)}, u32[]{:S(2)}) %collective-permute-start.18) | collective-permute-done | bytes 294944 | tf_op jit(solution)/shard_map/ppermute | solution.py:308
  245.9 6.3 %collective-permute-done.23.refs_9_ = bf16[192,768]{1,0:T(8,128)(2,1)} collective-permute-done((bf16[192,768]{1,0:T(8,128)(2,1)}, bf16[192,768]{1,0:T(8,128)(2,1)}, u32[]{:S(2)}, u32[]{:S(2)}) %collective-permute-start.23) | collective-permute-done | bytes 294944 | tf_op jit(solution)/shard_map/ppermute | solution.py:308
  252.2 6.7 %place.1 = f32[768,3072]{1,0:T(8,128)} custom-call(s32[2]{0:T(128)S(1)} %pad_add_fusion.2.place_ref, bf16[384,768]{1,0:T(8,128)(2,1)S(1)} %broadcast_select_fusion.2.refs_0_, bf16[384,768]{1,0:T(8,128)(2,1)S(1)} %collective-permute-done.15.refs_1_, bf16[384,768]{1,0:T(8,128)(2,1)S(1)} %collective-permute-done.16.refs_2_, ...), custom_call_target="tpu_custom_call" | custom-call | bytes 16777216 | tf_op jit(solution)/shard_map/place/pallas_call | solution.py:318
  258.9 2.2 add_convert_fusion
  (117 shorter events, 58.8 us)
Async XLA Ops:
  13.8 43.6 %all-to-all-start = ((bf16[16,3,128,128]{3,2,1,0:T(8,128)(2,1)}), bf16[16,3,128,128]{3,2,1,0:T(8,128)(2,1)S(1)}, u32[]{:S(2)}, u32[]{:S(2)}) async-start(bf16[16,3,128,128]{3,2,1,0:T(8,128)(2,1)} %pack.2), calls=%async_computation | async-start | bytes 3145728 | tf_op jit(solution)/shard_map/all_to_all | solution.py:421
  20.5 129.5 %all-gather.3.cloned.1.call-start = ((), (), s32[]{:S(2)}) async-start(), calls=%async_computation.3 | async-start | bytes 3932160 | tf_op jit(solution)/shard_map/all_gather | solution.py:424
  31.5 16.6 %collective-permute-start.5 = (bf16[128,768]{1,0:T(8,128)(2,1)}, bf16[128,768]{1,0:T(8,128)(2,1)S(1)}, u32[]{:S(2)}, u32[]{:S(2)}) collective-permute-start(bf16[128,768]{1,0:T(8,128)(2,1)} %get-tuple-element.58), channel_id=1, source_target_pairs={{0,6},{2,4},{4,2},{6,0},{8,14},{10,12},{12,10},{14,8},{16,22},{18,... | collective-permute-start | bytes 589832 | tf_op jit(solution)/shard_map/ppermute | solution.py:407
  32.6 17.4 %collective-permute-start.3 = (bf16[128,768]{1,0:T(8,128)(2,1)S(1)}, bf16[128,768]{1,0:T(8,128)(2,1)S(1)}, u32[]{:S(2)}, u32[]{:S(2)}) collective-permute-start(bf16[128,768]{1,0:T(8,128)(2,1)S(1)} %get-tuple-element.60), channel_id=1, source_target_pairs={{0,2},{2,0},{4,6},{6,4},{8,10},{10,8},{12,14},{14,12},{16,18},{18,... | collective-permute-start | bytes 589832 | tf_op jit(solution)/shard_map/ppermute | solution.py:407
  32.9 17.1 %collective-permute-start.4 = (bf16[128,768]{1,0:T(8,128)(2,1)S(1)}, bf16[128,768]{1,0:T(8,128)(2,1)S(1)}, u32[]{:S(2)}, u32[]{:S(2)}) collective-permute-start(bf16[128,768]{1,0:T(8,128)(2,1)S(1)} %get-tuple-element.61), channel_id=1, source_target_pairs={{0,4},{2,6},{4,0},{6,2},{8,12},{10,14},{12,8},{14,10},{16,20},{18,... | collective-permute-start | bytes 589832 | tf_op jit(solution)/shard_map/ppermute | solution.py:407
  58.0 7.3 %collective-permute-start.6 = (bf16[2,2048,128]{2,1,0:T(8,128)(2,1)S(1)}, bf16[2,2048,128]{2,1,0:T(8,128)(2,1)S(1)}, u32[]{:S(2)}, u32[]{:S(2)}) collective-permute-start(bf16[2,2048,128]{2,1,0:T(8,128)(2,1)S(1)} %get-tuple-element.31.refs_0_.refs_1_), channel_id=1, source_target_pairs={{0,1},{1,0},{2,3},{3,2},{4,5},{5,4},{6,7},{7,6},{8,9},{9,8},{10,11... | collective-permute-start | bytes 3145736 | tf_op jit(solution)/shard_map/ppermute | solution.py:431
  60.6 28.7 %all-to-all-start.1 = ((bf16[16,1,128,128]{3,2,1,0:T(8,128)(2,1)}), bf16[16,1,128,128]{3,2,1,0:T(8,128)(2,1)S(1)}, u32[]{:S(2)}, u32[]{:S(2)}) async-start(bf16[16,1,128,128]{3,2,1,0:T(8,128)(2,1)} %pack.3), calls=%async_computation.1 | async-start | bytes 1048576 | tf_op jit(solution)/shard_map/all_to_all | solution.py:426
  110.7 30.0 %collective-permute-start.10 = (bf16[2,2048,128]{2,1,0:T(8,128)(2,1)S(1)}, bf16[2,2048,128]{2,1,0:T(8,128)(2,1)S(1)}, u32[]{:S(2)}, u32[]{:S(2)}) collective-permute-start(bf16[2,2048,128]{2,1,0:T(8,128)(2,1)S(1)} %get-tuple-element.38), channel_id=1, source_target_pairs={{0,1},{1,0},{2,3},{3,2},{4,5},{5,4},{6,7},{7,6},{8,9},{9,8},{10,11... | collective-permute-start | bytes 3145736 | tf_op jit(solution)/shard_map/ppermute | solution.py:525
  114.8 16.3 %collective-permute-start.9 = (bf16[2048,128]{1,0:T(8,128)(2,1)S(1)}, bf16[2048,128]{1,0:T(8,128)(2,1)S(1)}, u32[]{:S(2)}, u32[]{:S(2)}) collective-permute-start(bf16[2048,128]{1,0:T(8,128)(2,1)S(1)} %get-tuple-element.45.o_ref.attn_ref.refs_0_), channel_id=1, source_target_pairs={{0,6},{2,4},{4,2},{10,12},{12,10},{14,8},{16,22},{20,18},{22,16},{... | collective-permute-start | bytes 1572872 | tf_op jit(solution)/shard_map/ppermute | solution.py:455
  116.7 22.3 %collective-permute-start.8 = (bf16[2048,128]{1,0:T(8,128)(2,1)S(1)}, bf16[2048,128]{1,0:T(8,128)(2,1)S(1)}, u32[]{:S(2)}, u32[]{:S(2)}) collective-permute-start(bf16[2048,128]{1,0:T(8,128)(2,1)S(1)} %get-tuple-element.45.o_ref.attn_ref.refs_0_), channel_id=1, source_target_pairs={{0,4},{2,6},{4,0},{10,14},{12,8},{14,10},{16,20},{20,16},{22,18},{... | collective-permute-start | bytes 1572872 | tf_op jit(solution)/shard_map/ppermute | solution.py:455
  118.0 21.9 %collective-permute-start.7 = (bf16[2048,128]{1,0:T(8,128)(2,1)S(1)}, bf16[2048,128]{1,0:T(8,128)(2,1)S(1)}, u32[]{:S(2)}, u32[]{:S(2)}) collective-permute-start(bf16[2048,128]{1,0:T(8,128)(2,1)S(1)} %get-tuple-element.45.o_ref.attn_ref.refs_0_), channel_id=1, source_target_pairs={{0,2},{2,0},{4,6},{10,8},{12,14},{14,12},{16,18},{20,22},{22,20},{... | collective-permute-start | bytes 1572872 | tf_op jit(solution)/shard_map/ppermute | solution.py:455
  142.8 61.3 %all-to-all-start.2 = ((bf16[16,4,128,128]{3,2,1,0:T(8,128)(2,1)}), bf16[16,4,128,128]{3,2,1,0:T(8,128)(2,1)S(1)}, u32[]{:S(2)}, u32[]{:S(2)}) async-start(bf16[16,4,128,128]{3,2,1,0:T(8,128)(2,1)} %copy-done.1), calls=%async_computation.2 | async-start | bytes 4194304 | tf_op jit(solution)/shard_map/all_to_all | solution.py:531
  160.9 48.2 %collective-permute-start.14 = (bf16[384,768]{1,0:T(8,128)(2,1)S(1)}, bf16[384,768]{1,0:T(8,128)(2,1)S(1)}, u32[]{:S(2)}, u32[]{:S(2)}) collective-permute-start(bf16[384,768]{1,0:T(8,128)(2,1)S(1)} %add_convert_fusion.1), channel_id=1, source_target_pairs={{0,16},{2,18},{4,20},{6,22},{8,24},{10,26},{12,28},{14,30},{17,1},... | collective-permute-start | bytes 1769480 | tf_op jit(solution)/shard_map/ppermute | solution.py:305
  206.6 19.6 %collective-permute-start.11 = (bf16[6,4,128,128]{3,2,1,0:T(8,128)(2,1)}, bf16[6,4,128,128]{3,2,1,0:T(8,128)(2,1)}, u32[]{:S(2)}, u32[]{:S(2)}) collective-permute-start(bf16[6,4,128,128]{3,2,1,0:T(8,128)(2,1)} %get-tuple-element.40), channel_id=1, source_target_pairs={{0,1},{1,0},{2,3},{3,2},{4,5},{5,4},{6,7},{7,6},{8,9},{9,8},{10,11... | collective-permute-start | bytes 2359304 | tf_op jit(solution)/shard_map/ppermute | solution.py:536
  209.1 15.7 %collective-permute-start.19 = (bf16[384,768]{1,0:T(8,128)(2,1)S(1)}, bf16[384,768]{1,0:T(8,128)(2,1)S(1)}, u32[]{:S(2)}, u32[]{:S(2)}) collective-permute-start(bf16[384,768]{1,0:T(8,128)(2,1)S(1)} %broadcast_select_fusion.2.refs_0_), channel_id=1, source_target_pairs={{0,8},{2,10},{4,12},{6,14},{8,0},{10,2},{12,4},{14,6},{16,24},{18,... | collective-permute-start | bytes 1769480 | tf_op jit(solution)/shard_map/ppermute | solution.py:308
  212.5 23.1 %collective-permute-start.16 = (bf16[384,768]{1,0:T(8,128)(2,1)S(1)}, bf16[384,768]{1,0:T(8,128)(2,1)S(1)}, u32[]{:S(2)}, u32[]{:S(2)}) collective-permute-start(bf16[384,768]{1,0:T(8,128)(2,1)S(1)} %broadcast_select_fusion.2.refs_0_), channel_id=1, source_target_pairs={{0,4},{2,6},{4,0},{6,2},{8,12},{10,14},{12,8},{14,10},{16,20},{18,... | collective-permute-start | bytes 1769480 | tf_op jit(solution)/shard_map/ppermute | solution.py:308
  212.5 24.1 %collective-permute-start.15 = (bf16[384,768]{1,0:T(8,128)(2,1)S(1)}, bf16[384,768]{1,0:T(8,128)(2,1)S(1)}, u32[]{:S(2)}, u32[]{:S(2)}) collective-permute-start(bf16[384,768]{1,0:T(8,128)(2,1)S(1)} %broadcast_select_fusion.2.refs_0_), channel_id=1, source_target_pairs={{0,2},{2,0},{4,6},{6,4},{8,10},{10,8},{12,14},{14,12},{16,18},{18,... | collective-permute-start | bytes 1769480 | tf_op jit(solution)/shard_map/ppermute | solution.py:308
  224.9 15.3 %collective-permute-start.21 = (bf16[384,768]{1,0:T(8,128)(2,1)S(1)}, bf16[384,768]{1,0:T(8,128)(2,1)S(1)}, u32[]{:S(2)}, u32[]{:S(2)}) collective-permute-start(bf16[384,768]{1,0:T(8,128)(2,1)S(1)} %collective-permute-done.19.refs_5_), channel_id=1, source_target_pairs={{0,4},{2,6},{4,0},{6,2},{8,12},{10,14},{12,8},{14,10},{16,20},{18,... | collective-permute-start | bytes 1769480 | tf_op jit(solution)/shard_map/ppermute | solution.py:308
  224.9 16.4 %collective-permute-start.20 = (bf16[384,768]{1,0:T(8,128)(2,1)S(1)}, bf16[384,768]{1,0:T(8,128)(2,1)S(1)}, u32[]{:S(2)}, u32[]{:S(2)}) collective-permute-start(bf16[384,768]{1,0:T(8,128)(2,1)S(1)} %collective-permute-done.19.refs_5_), channel_id=1, source_target_pairs={{0,2},{2,0},{4,6},{6,4},{8,10},{10,8},{12,14},{14,12},{16,18},{18,... | collective-permute-start | bytes 1769480 | tf_op jit(solution)/shard_map/ppermute | solution.py:308
  235.1 23.8 %collective-permute-start.12 = (bf16[256,1536]{1,0:T(8,128)(2,1)}, bf16[256,1536]{1,0:T(8,128)(2,1)}, u32[]{:S(2)}, u32[]{:S(2)}) collective-permute-start(bf16[256,1536]{1,0:T(8,128)(2,1)} %dynamic-slice_convert_fusion), channel_id=1, source_target_pairs={{0,1},{1,0},{2,3},{3,2},{4,5},{5,4},{6,7},{7,6},{8,9},{9,8},{10,11... | collective-permute-start | bytes 2359304 | tf_op jit(solution)/shard_map/ppermute | solution.py:544
  236.3 9.6 %collective-permute-start.18 = (bf16[192,768]{1,0:T(8,128)(2,1)}, bf16[192,768]{1,0:T(8,128)(2,1)}, u32[]{:S(2)}, u32[]{:S(2)}) collective-permute-start(bf16[192,768]{1,0:T(8,128)(2,1)} %slice.21), channel_id=1, source_target_pairs={{0,2},{2,0},{4,6},{6,4},{8,10},{10,8},{12,14},{14,12},{16,18},{18,... | collective-permute-start | bytes 884744 | tf_op jit(solution)/shard_map/ppermute | solution.py:308
  237.3 8.6 %collective-permute-start.17 = (bf16[192,768]{1,0:T(8,128)(2,1)}, bf16[192,768]{1,0:T(8,128)(2,1)}, u32[]{:S(2)}, u32[]{:S(2)}) collective-permute-start(bf16[192,768]{1,0:T(8,128)(2,1)} %slice.20), channel_id=1, source_target_pairs={{0,4},{2,6},{4,0},{6,2},{8,12},{10,14},{12,8},{14,10},{16,20},{18,... | collective-permute-start | bytes 884744 | tf_op jit(solution)/shard_map/ppermute | solution.py:308
  240.9 11.3 %collective-permute-start.23 = (bf16[192,768]{1,0:T(8,128)(2,1)}, bf16[192,768]{1,0:T(8,128)(2,1)}, u32[]{:S(2)}, u32[]{:S(2)}) collective-permute-start(bf16[192,768]{1,0:T(8,128)(2,1)} %slice.23), channel_id=1, source_target_pairs={{0,2},{2,0},{4,6},{6,4},{8,10},{10,8},{12,14},{14,12},{16,18},{18,... | collective-permute-start | bytes 884744 | tf_op jit(solution)/shard_map/ppermute | solution.py:308
  242.0 10.2 %collective-permute-start.22 = (bf16[192,768]{1,0:T(8,128)(2,1)}, bf16[192,768]{1,0:T(8,128)(2,1)}, u32[]{:S(2)}, u32[]{:S(2)}) collective-permute-start(bf16[192,768]{1,0:T(8,128)(2,1)} %slice.22), channel_id=1, source_target_pairs={{0,4},{2,6},{4,0},{6,2},{8,12},{10,14},{12,8},{14,10},{16,20},{18,... | collective-permute-start | bytes 884744 | tf_op jit(solution)/shard_map/ppermute | solution.py:308
  (25 other events, 122.0 us)
Sparse Core Ops, SparseCore 0:
  60.7 67.5 all-gather.2

commit v7 on v6

--- a/solution.py
+++ b/solution.py
@@ -294,7 +294,7 @@
             out_ref[middle:] = lower[...].astype(F32)
 
 
-def gather_tiles_by_core(n, t, tile_sum, chip, core):
+def gather_tiles_by_core(n, t, tile_sum, chip, core, beside_chunks):
     in_plane = n // PLANES
     plane, seat = chip // in_plane, chip % in_plane
     tile_rows, cols = tile_sum.shape
@@ -309,11 +309,12 @@
 
     first = jnp.where(plane // 2 == core, tile_sum, from_half)
     second = swap(first, in_plane)
+    beside, above = swap(first, 1), swap(first, 2)
+    second, beside, above, beside_chunks = lax.optimization_barrier((second, beside, above, beside_chunks))
     middle = tile_rows // 2
-    sources = []
-    for mine in (first, second):
-        beside, above = swap(mine, 1), swap(mine, 2)
-        sources += [mine, beside, above, swap(beside[:middle], 2), swap(above[middle:], 1)]
+    sources = [first, beside, above, swap(beside[:middle], 2), swap(above[middle:], 1)]
+    beside, above = swap(second, 1), swap(second, 2)
+    sources += [second, beside, above, swap(beside[:middle], 2), swap(above[middle:], 1)]
     place = jnp.stack([plane % 2, seat]).astype(jnp.int32)
     return pl.pallas_call(
         place_xor_kernel,
@@ -329,7 +330,7 @@
         compiler_params=pltpu.CompilerParams(vmem_limit_bytes=48 * 2**20),
         cost_estimate=pl.CostEstimate(flops=0, bytes_accessed=2**24, transcendentals=0),
         name="place",
-    )(place, *sources)
+    )(place, *sources), beside_chunks
 
 
 def per_device(n, t, queries, key_vectors, value_vectors, out_weight, out_grad, block_segment):
@@ -454,6 +455,8 @@
     travel = [attn] + [
         lax.ppermute(attn, "ctx", [(i, i ^ k) for i in range(n) if held[i]]) for k in range(1, in_plane)
     ]
+    *travel, attn = lax.optimization_barrier((*travel, attn))
+
     dq, *dkv = pl.pallas_call(
         functools.partial(backward_kernel, t, tile, count),
         grid_spec=pltpu.PrefetchScalarGridSpec(
@@ -469,7 +472,14 @@
         name="backward",
     )(full, kcnt, kidx, q_rows, g_rows, attn, lse, *part_arrays)
 
-    *travel, dq = lax.optimization_barrier((*travel, dq))
+    got_dkv = [
+        lax.ppermute(dkv[s], "tp", [(c, (c - s) % t) for c in range(t)]) for s in range(1, t)
+    ]
+    (sent,) = simple_call(
+        functools.partial(unjoin_kernel, n, t), "unjoin", where,
+        [attn, dq, dkv[0]] + got_dkv, [shape(n, 4, sub, HEAD)],
+    )
+    chunks = lax.all_to_all(sent, "ctx", 0, 0, tiled=True)
 
     tile_rows = heads_plane * HEAD
     by_core = in_plane == 4 and t == 2
@@ -496,7 +506,7 @@
     for s in range(1, t):
         tile_sum = tile_sum + lax.ppermute(tile_sends[s - 1], "tp", shifts(t, s)).astype(F32)
     if by_core:
-        grad_weight = gather_tiles_by_core(n, t, tile_sum.astype(BF16), chip, core)
+        grad_weight, chunks = gather_tiles_by_core(n, t, tile_sum.astype(BF16), chip, core, chunks)
     else:
         tiles = lax.all_gather(tile_sum.astype(BF16), "ctx")
         here = n // t
@@ -521,14 +531,6 @@
             name="place",
         )(where, *tiles_core)
 
-    got_dkv = [
-        lax.ppermute(dkv[s], "tp", [(c, (c - s) % t) for c in range(t)]) for s in range(1, t)
-    ]
-    (sent,) = simple_call(
-        functools.partial(unjoin_kernel, n, t), "unjoin", where,
-        [attn, dq, dkv[0]] + got_dkv, [shape(n, 4, sub, HEAD)],
-    )
-    chunks = lax.all_to_all(sent, "ctx", 0, 0, tiled=True)
     mine = simple_call(
         functools.partial(by_core_kernel, n, t), "by_core", where, [chunks],
         [shape(heads_here, 4, sub, HEAD)] * t, [pltpu.VMEM((heads, 4, sub, HEAD), BF16)],

time: 272 us -> 271 us (level)
  waiting for transfers between devices: 112 us -> 101 us
  starting transfers between devices: 50.7 us -> 60.5 us
    all_to_all x1, waiting for transfers between devices: 41.9 us -> 0.01 us  [per_device(): chunks = lax.all_to_all(sent, 'ctx', 0, 0, tiled=True)]
    ppermute x1, waiting for transfers between devices: 0.01 us -> 32.8 us  [gather_tiles_by_core(): from_half = lax.ppermute(tile_sum, ('ctx', 'tp'), across)]
    ppermute x9, starting transfers between devices: 7.81 us -> 23.1 us  [swap(): return lax.ppermute(x, 'ctx', [(i, i ^ k) for i in range(n)])]
    all_to_all x1, waiting for transfers between devices: 7.29 us -> 0.01 us  [per_device(): lax.all_to_all(sent_g, 'ctx', 0, 0, tiled=True).reshape(n * sub, HEAD)]
    ppermute x1, starting transfers between devices: 4.14 us -> 1.4 us  [per_device(): lax.ppermute(dkv[s], 'tp', [(c, (c - s) % t) for c in range(t)])]
    unnamed x42 -> x46, local copies, waits for them, and re-layouts: 11.9 us -> 11.6 us
where the time goes in v7:
time: 271 us; the launch traced here: 268 us
  waiting for transfers between devices  101 us (37%)
  starting transfers between devices  60.5 us (22%)
  Pallas kernels  56.6 us (21%)
  local copies, waits for them, and re-layouts  19.7 us (7%)
  between operations  14.4 us (5%)
  other arithmetic  7.67 us (3%)
  matrix products  7.5 us (3%)
    ppermute x1, waiting for transfers between devices, gather_tiles_by_core(): from_half = lax.ppermute(tile_sum, ('ctx', 'tp'), across)  32.8 us
    ppermute x9, starting transfers between devices, swap(): return lax.ppermute(x, 'ctx', [(i, i ^ k) for i in range(n)])  23.1 us
    ppermute x9, waiting for transfers between devices, swap(): return lax.ppermute(x, 'ctx', [(i, i ^ k) for i in range(n)])  22.7 us
    pallas_call x1, Pallas kernels, per_device(): pl.pallas_call(functools.partial(backward_kernel, t, tile, count), grid_s...  20.1 us
    ppermute x3, waiting for transfers between devices, per_device(): lax.ppermute(attn, 'ctx', [(i, i ^ k) for i in range(n) if held[i]])  18.6 us
    pallas_call x1, Pallas kernels, per_device(): pl.pallas_call(functools.partial(forward_kernel, t, tile, count), grid_sp...  13.9 us
    ppermute x3, waiting for transfers between devices, per_device(): plane_got.append(lax.ppermute(there, 'ctx', [(i, i ^ k) for i in range(n)]))  13.1 us
    unnamed x46, local copies, waits for them, and re-layouts  11.6 us
  transfers between devices with their start and end apart: 28, of which 15 were waited for; matrix products, arithmetic and copies ran while one was open for 7% of the time, Pallas kernels for 20%

profile of v7, /device:TPU:13, one launch (start us, length us, event | category | flops | bytes accessed | tf_op | source)
XLA Modules:
  0.0 267.6 jit_solution(1440853072460124689)
XLA Ops:
  13.8 6.7 %all-to-all-start = ((bf16[16,3,128,128]{3,2,1,0:T(8,128)(2,1)}), bf16[16,3,128,128]{3,2,1,0:T(8,128)(2,1)S(1)}, u32[]{:S(2)}, u32[]{:S(2)}) async-start(bf16[16,3,128,128]{3,2,1,0:T(8,128)(2,1)} %pack.2), calls=%async_computation | async-start | bytes 3145728 | tf_op jit(solution)/shard_map/all_to_all | solution.py:422
  21.6 2.0 collective-permute-done.1
  24.9 3.8 %fusion.1.refs_0_ = bf16[256,768]{1,0:T(8,128)(2,1)S(1)} fusion(bf16[768,3072]{1,0:T(8,128)(2,1)} %param.11, bf16[256,1536]{1,0:T(8,128)(2,1)S(1)} %get-tuple-element.71, bf16[256,1536]{1,0:T(8,128)(2,1)S(1)} %get-tuple-element.70), kind=kOutput, calls=%fused_computation.14 | convolution fusion | flops 1211301888 | bytes 6684672 | tf_op jit(solution)/shard_map/dot_general | solution.py:27
  37.0 11.1 %collective-permute-done.5.refs_3_ = bf16[128,768]{1,0:T(8,128)(2,1)S(1)} collective-permute-done((bf16[128,768]{1,0:T(8,128)(2,1)}, bf16[128,768]{1,0:T(8,128)(2,1)S(1)}, u32[]{:S(2)}, u32[]{:S(2)}) %collective-permute-start.5) | collective-permute-done | bytes 196640 | tf_op jit(solution)/shard_map/ppermute | solution.py:408
  51.5 5.8 %all-to-all-done.chunks_ref = bf16[16,3,128,128]{3,2,1,0:T(8,128)(2,1)S(1)} async-done(((bf16[16,3,128,128]{3,2,1,0:T(8,128)(2,1)}), bf16[16,3,128,128]{3,2,1,0:T(8,128)(2,1)S(1)}, u32[]{:S(2)}, u32[]{:S(2)}) %all-to-all-start) | async-done | bytes 1572896 | tf_op jit(solution)/shard_map/all_to_all | solution.py:422
  60.6 4.8 %all-to-all-start.1 = ((bf16[16,1,128,128]{3,2,1,0:T(8,128)(2,1)}), bf16[16,1,128,128]{3,2,1,0:T(8,128)(2,1)S(1)}, u32[]{:S(2)}, u32[]{:S(2)}) async-start(bf16[16,1,128,128]{3,2,1,0:T(8,128)(2,1)} %pack.3), calls=%async_computation.1 | async-start | bytes 1048576 | tf_op jit(solution)/shard_map/all_to_all | solution.py:427
  67.1 13.9 %forward.1 = (bf16[2048,128]{1,0:T(8,128)(2,1)S(1)}, f32[2048,128]{1,0:T(8,128)S(1)}) custom-call(s32[16]{0:T(128)S(1)} %get-tuple-element.64.full_ref, s32[16]{0:T(128)S(1)} %get-tuple-element.60.kcnt_ref, s32[16,10]{1,0:T(8,128)S(1)} %copy.11.kidx_ref, bf16[2048,128]{1,0:T(8,128)(2,1)S(1)} %get-tuple-element.34.q_ref, ...), custom_call_target="tpu_custom_call" | custom-call | flops 16000000000 | bytes 5242880 | tf_op jit(solution)/shard_map/forward/pallas_call | solution.py:440
  82.0 3.1 %collective-permute-start.9 = (bf16[2048,128]{1,0:T(8,128)(2,1)S(1)}, bf16[2048,128]{1,0:T(8,128)(2,1)S(1)}, u32[]{:S(2)}, u32[]{:S(2)}) collective-permute-start(bf16[2048,128]{1,0:T(8,128)(2,1)S(1)} %get-tuple-element.44.refs_0_.o_ref.attn_ref), channel_id=1, source_target_pairs={{0,6},{2,4},{4,2},{10,12},{12,10},{14,8},{16,22},{20,18},{22,16},{... | collective-permute-start | bytes 1572872 | tf_op jit(solution)/shard_map/ppermute | solution.py:456
  86.4 4.0 %collective-permute-start.7 = (bf16[2048,128]{1,0:T(8,128)(2,1)S(1)}, bf16[2048,128]{1,0:T(8,128)(2,1)S(1)}, u32[]{:S(2)}, u32[]{:S(2)}) collective-permute-start(bf16[2048,128]{1,0:T(8,128)(2,1)S(1)} %get-tuple-element.44.refs_0_.o_ref.attn_ref), channel_id=1, source_target_pairs={{0,2},{2,0},{4,6},{10,8},{12,14},{14,12},{16,18},{20,22},{22,20},{... | collective-permute-start | bytes 1572872 | tf_op jit(solution)/shard_map/ppermute | solution.py:456
  90.4 8.1 %collective-permute-done.9.refs_3_ = bf16[2048,128]{1,0:T(8,128)(2,1)S(1)} collective-permute-done((bf16[2048,128]{1,0:T(8,128)(2,1)S(1)}, bf16[2048,128]{1,0:T(8,128)(2,1)S(1)}, u32[]{:S(2)}, u32[]{:S(2)}) %collective-permute-start.9) | collective-permute-done | bytes 524320 | tf_op jit(solution)/shard_map/ppermute | solution.py:456
  98.6 9.8 %collective-permute-done.8.refs_2_ = bf16[2048,128]{1,0:T(8,128)(2,1)S(1)} collective-permute-done((bf16[2048,128]{1,0:T(8,128)(2,1)S(1)}, bf16[2048,128]{1,0:T(8,128)(2,1)S(1)}, u32[]{:S(2)}, u32[]{:S(2)}) %collective-permute-start.8) | collective-permute-done | bytes 524320 | tf_op jit(solution)/shard_map/ppermute | solution.py:456
  110.4 20.1 %backward.1 = (bf16[2048,128]{1,0:T(8,128)(2,1)S(1)}, bf16[2,2048,128]{2,1,0:T(8,128)(2,1)S(1)}, bf16[2,2048,128]{2,1,0:T(8,128)(2,1)S(1)}) custom-call(s32[16]{0:T(128)S(1)} %get-tuple-element.64.full_ref, s32[16]{0:T(128)S(1)} %get-tuple-element.60.kcnt_ref, s32[16,10]{1,0:T(8,128)S(1)} %copy.11.kidx_ref, bf16[2048,128]{1,0:T(8,128)(2,1)S(1)} %get-tuple-element.34.q_ref, ...), custom_call_target="tpu_custom_call" | custom-call | flops 20000000000 | bytes 8388608 | tf_op jit(solution)/shard_map/backward/pallas_call | solution.py:460
  132.0 2.3 collective-permute-done.15.refs_0_
  136.4 7.1 %all-to-all-start.2 = ((bf16[16,4,128,128]{3,2,1,0:T(8,128)(2,1)}), bf16[16,4,128,128]{3,2,1,0:T(8,128)(2,1)S(1)}, u32[]{:S(2)}, u32[]{:S(2)}) async-start(bf16[16,4,128,128]{3,2,1,0:T(8,128)(2,1)} %copy-done.1), calls=%async_computation.2 | async-start | bytes 4194304 | tf_op jit(solution)/shard_map/all_to_all | solution.py:482
  146.7 4.8 %tile.1 = (f32[384,768]{1,0:T(8,128)S(1)}, bf16[384,768]{1,0:T(8,128)(2,1)S(1)}) custom-call(s32[2]{0:T(128)S(1)} %pad_add_fusion.where_ref, bf16[2048,128]{1,0:T(8,128)(2,1)S(1)} %get-tuple-element.44.refs_0_.o_ref.attn_ref, bf16[2048,128]{1,0:T(8,128)(2,1)S(1)} %copy-done.17, bf16[2048,128]{1,0:T(8,128)(2,1)S(1)} %copy-done.15, ...), custom_call_target="tpu_custom_call" | custom-call | flops 5000000000 | bytes 4194304 | tf_op jit(solution)/shard_map/tile/pallas_call | solution.py:488
  155.7 32.8 %collective-permute-done.11 = bf16[384,768]{1,0:T(8,128)(2,1)} collective-permute-done((bf16[384,768]{1,0:T(8,128)(2,1)S(1)}, bf16[384,768]{1,0:T(8,128)(2,1)}, u32[]{:S(2)}, u32[]{:S(2)}) %collective-permute-start.11) | collective-permute-done | bytes 589856 | tf_op jit(solution)/shard_map/ppermute | solution.py:305
  190.4 17.2 %collective-permute-start.12 = (bf16[384,768]{1,0:T(8,128)(2,1)S(1)}, bf16[384,768]{1,0:T(8,128)(2,1)}, u32[]{:S(2)}, u32[]{:S(2)}) collective-permute-start(bf16[384,768]{1,0:T(8,128)(2,1)S(1)} %broadcast_select_fusion.2.refs_0_), channel_id=1, source_target_pairs={{0,8},{2,10},{4,12},{6,14},{8,0},{10,2},{12,4},{14,6},{16,24},{18,... | collective-permute-start | bytes 1769480 | tf_op jit(solution)/shard_map/ppermute | solution.py:308
  208.4 11.7 %collective-permute-done.12.refs_5_ = bf16[384,768]{1,0:T(8,128)(2,1)} collective-permute-done((bf16[384,768]{1,0:T(8,128)(2,1)S(1)}, bf16[384,768]{1,0:T(8,128)(2,1)}, u32[]{:S(2)}, u32[]{:S(2)}) %collective-permute-start.12) | collective-permute-done | bytes 589856 | tf_op jit(solution)/shard_map/ppermute | solution.py:308
  226.4 2.9 %unpack.1 = (bf16[256,768]{1,0:T(8,128)(2,1)S(1)}, bf16[256,768]{1,0:T(8,128)(2,1)}, bf16[256,768]{1,0:T(8,128)(2,1)}, bf16[256,768]{1,0:T(8,128)(2,1)}) custom-call(s32[2]{0:T(128)S(1)} %pad_add_fusion.where_ref, bf16[6,4,128,128]{3,2,1,0:T(8,128)(2,1)S(1)} %copy-done.8, bf16[6,4,128,128]{3,2,1,0:T(8,128)(2,1)} %collective-permute-done.16.refs_1_), custom_call_target="tpu_custom_call" | custom-call | bytes 6291456 | tf_op jit(solution)/shard_map/unpack/pallas_call | solution.py:260
  229.3 3.7 %fusion.8 = f32[256,3072]{1,0:T(8,128)S(1)} fusion(bf16[256,768]{1,0:T(8,128)(2,1)S(1)} %get-tuple-element.53, bf16[768,3072]{1,0:T(8,128)(2,1)} %param.11), kind=kOutput, calls=%fused_computation.56 | convolution fusion | flops 1207959552 | bytes 8257536 | tf_op jit(solution)/shard_map/dot_general | solution.py:27
  240.7 4.7 %collective-permute-done.19.refs_4_ = bf16[192,768]{1,0:T(8,128)(2,1)S(1)} collective-permute-done((bf16[192,768]{1,0:T(8,128)(2,1)}, bf16[192,768]{1,0:T(8,128)(2,1)S(1)}, u32[]{:S(2)}, u32[]{:S(2)}) %collective-permute-start.19) | collective-permute-done | bytes 294944 | tf_op jit(solution)/shard_map/ppermute | solution.py:308
  245.4 6.3 %collective-permute-done.23.refs_9_ = bf16[192,768]{1,0:T(8,128)(2,1)} collective-permute-done((bf16[192,768]{1,0:T(8,128)(2,1)}, bf16[192,768]{1,0:T(8,128)(2,1)}, u32[]{:S(2)}, u32[]{:S(2)}) %collective-permute-start.23) | collective-permute-done | bytes 294944 | tf_op jit(solution)/shard_map/ppermute | solution.py:308
  251.8 6.8 %place.1 = f32[768,3072]{1,0:T(8,128)} custom-call(s32[2]{0:T(128)S(1)} %pad_add_fusion.2.place_ref, bf16[384,768]{1,0:T(8,128)(2,1)S(1)} %broadcast_select_fusion.2.refs_0_, bf16[384,768]{1,0:T(8,128)(2,1)S(1)} %copy-done.3, bf16[384,768]{1,0:T(8,128)(2,1)S(1)} %collective-permute-done.14.refs_2_, bf16[192,768]{1,0:T(8,128)(2,1)} %collective-permute-done.18.refs_3_, ...), custom_call_target="tpu_custom_call" | custom-call | bytes 16777216 | tf_op jit(solution)/shard_map/place/pallas_call | solution.py:319
  258.5 2.2 add_convert_fusion
  (121 shorter events, 57.2 us)
Async XLA Ops:
  13.8 43.6 %all-to-all-start = ((bf16[16,3,128,128]{3,2,1,0:T(8,128)(2,1)}), bf16[16,3,128,128]{3,2,1,0:T(8,128)(2,1)S(1)}, u32[]{:S(2)}, u32[]{:S(2)}) async-start(bf16[16,3,128,128]{3,2,1,0:T(8,128)(2,1)} %pack.2), calls=%async_computation | async-start | bytes 3145728 | tf_op jit(solution)/shard_map/all_to_all | solution.py:422
  20.5 123.0 %all-gather.3.cloned.1.call-start = ((), (), s32[]{:S(2)}) async-start(), calls=%async_computation.3 | async-start | bytes 3932160 | tf_op jit(solution)/shard_map/all_gather | solution.py:425
  29.3 6.2 %collective-permute-start.2 = (bf16[1,128,768]{2,1,0:T(8,128)(2,1)}, bf16[1,128,768]{2,1,0:T(8,128)(2,1)S(1)}, u32[]{:S(2)}, u32[]{:S(2)}) collective-permute-start(bf16[1,128,768]{2,1,0:T(8,128)(2,1)} %dynamic-slice_bitcast_fusion), channel_id=1, source_target_pairs={{0,1},{1,0},{2,3},{3,2},{4,5},{5,4},{6,7},{7,6},{8,9},{9,8},{10,11... | collective-permute-start | bytes 589832 | tf_op jit(solution)/shard_map/ppermute | solution.py:386
  31.5 16.6 %collective-permute-start.5 = (bf16[128,768]{1,0:T(8,128)(2,1)}, bf16[128,768]{1,0:T(8,128)(2,1)S(1)}, u32[]{:S(2)}, u32[]{:S(2)}) collective-permute-start(bf16[128,768]{1,0:T(8,128)(2,1)} %get-tuple-element.66), channel_id=1, source_target_pairs={{0,6},{2,4},{4,2},{6,0},{8,14},{10,12},{12,10},{14,8},{16,22},{18,... | collective-permute-start | bytes 589832 | tf_op jit(solution)/shard_map/ppermute | solution.py:408
  32.7 17.4 %collective-permute-start.3 = (bf16[128,768]{1,0:T(8,128)(2,1)}, bf16[128,768]{1,0:T(8,128)(2,1)S(1)}, u32[]{:S(2)}, u32[]{:S(2)}) collective-permute-start(bf16[128,768]{1,0:T(8,128)(2,1)} %get-tuple-element.68), channel_id=1, source_target_pairs={{0,2},{2,0},{4,6},{6,4},{8,10},{10,8},{12,14},{14,12},{16,18},{18,... | collective-permute-start | bytes 589832 | tf_op jit(solution)/shard_map/ppermute | solution.py:408
  33.0 17.1 %collective-permute-start.4 = (bf16[128,768]{1,0:T(8,128)(2,1)S(1)}, bf16[128,768]{1,0:T(8,128)(2,1)S(1)}, u32[]{:S(2)}, u32[]{:S(2)}) collective-permute-start(bf16[128,768]{1,0:T(8,128)(2,1)S(1)} %get-tuple-element.69), channel_id=1, source_target_pairs={{0,4},{2,6},{4,0},{6,2},{8,12},{10,14},{12,8},{14,10},{16,20},{18,... | collective-permute-start | bytes 589832 | tf_op jit(solution)/shard_map/ppermute | solution.py:408
  58.0 7.3 %collective-permute-start.6 = (bf16[2,2048,128]{2,1,0:T(8,128)(2,1)S(1)}, bf16[2,2048,128]{2,1,0:T(8,128)(2,1)S(1)}, u32[]{:S(2)}, u32[]{:S(2)}) collective-permute-start(bf16[2,2048,128]{2,1,0:T(8,128)(2,1)S(1)} %get-tuple-element.35.refs_0_.refs_1_), channel_id=1, source_target_pairs={{0,1},{1,0},{2,3},{3,2},{4,5},{5,4},{6,7},{7,6},{8,9},{9,8},{10,11... | collective-permute-start | bytes 3145736 | tf_op jit(solution)/shard_map/ppermute | solution.py:432
  60.6 48.5 %all-to-all-start.1 = ((bf16[16,1,128,128]{3,2,1,0:T(8,128)(2,1)}), bf16[16,1,128,128]{3,2,1,0:T(8,128)(2,1)S(1)}, u32[]{:S(2)}, u32[]{:S(2)}) async-start(bf16[16,1,128,128]{3,2,1,0:T(8,128)(2,1)} %pack.3), calls=%async_computation.1 | async-start | bytes 1048576 | tf_op jit(solution)/shard_map/all_to_all | solution.py:427
  82.0 16.5 %collective-permute-start.9 = (bf16[2048,128]{1,0:T(8,128)(2,1)S(1)}, bf16[2048,128]{1,0:T(8,128)(2,1)S(1)}, u32[]{:S(2)}, u32[]{:S(2)}) collective-permute-start(bf16[2048,128]{1,0:T(8,128)(2,1)S(1)} %get-tuple-element.44.refs_0_.o_ref.attn_ref), channel_id=1, source_target_pairs={{0,6},{2,4},{4,2},{10,12},{12,10},{14,8},{16,22},{20,18},{22,16},{... | collective-permute-start | bytes 1572872 | tf_op jit(solution)/shard_map/ppermute | solution.py:456
  85.1 23.3 %collective-permute-start.8 = (bf16[2048,128]{1,0:T(8,128)(2,1)S(1)}, bf16[2048,128]{1,0:T(8,128)(2,1)S(1)}, u32[]{:S(2)}, u32[]{:S(2)}) collective-permute-start(bf16[2048,128]{1,0:T(8,128)(2,1)S(1)} %get-tuple-element.44.refs_0_.o_ref.attn_ref), channel_id=1, source_target_pairs={{0,4},{2,6},{4,0},{10,14},{12,8},{14,10},{16,20},{20,16},{22,18},{... | collective-permute-start | bytes 1572872 | tf_op jit(solution)/shard_map/ppermute | solution.py:456
  86.4 22.6 %collective-permute-start.7 = (bf16[2048,128]{1,0:T(8,128)(2,1)S(1)}, bf16[2048,128]{1,0:T(8,128)(2,1)S(1)}, u32[]{:S(2)}, u32[]{:S(2)}) collective-permute-start(bf16[2048,128]{1,0:T(8,128)(2,1)S(1)} %get-tuple-element.44.refs_0_.o_ref.attn_ref), channel_id=1, source_target_pairs={{0,2},{2,0},{4,6},{10,8},{12,14},{14,12},{16,18},{20,22},{22,20},{... | collective-permute-start | bytes 1572872 | tf_op jit(solution)/shard_map/ppermute | solution.py:456
  130.6 3.7 %collective-permute-start.15 = (bf16[2,2048,128]{2,1,0:T(8,128)(2,1)S(1)}, bf16[2,2048,128]{2,1,0:T(8,128)(2,1)S(1)}, u32[]{:S(2)}, u32[]{:S(2)}) collective-permute-start(bf16[2,2048,128]{2,1,0:T(8,128)(2,1)S(1)} %get-tuple-element.49), channel_id=1, source_target_pairs={{0,1},{1,0},{2,3},{3,2},{4,5},{5,4},{6,7},{7,6},{8,9},{9,8},{10,11... | collective-permute-start | bytes 3145736 | tf_op jit(solution)/shard_map/ppermute | solution.py:476
  136.4 83.7 %all-to-all-start.2 = ((bf16[16,4,128,128]{3,2,1,0:T(8,128)(2,1)}), bf16[16,4,128,128]{3,2,1,0:T(8,128)(2,1)S(1)}, u32[]{:S(2)}, u32[]{:S(2)}) async-start(bf16[16,4,128,128]{3,2,1,0:T(8,128)(2,1)} %copy-done.1), calls=%async_computation.2 | async-start | bytes 4194304 | tf_op jit(solution)/shard_map/all_to_all | solution.py:482
  154.3 34.1 %collective-permute-start.11 = (bf16[384,768]{1,0:T(8,128)(2,1)S(1)}, bf16[384,768]{1,0:T(8,128)(2,1)}, u32[]{:S(2)}, u32[]{:S(2)}) collective-permute-start(bf16[384,768]{1,0:T(8,128)(2,1)S(1)} %add_convert_fusion.1), channel_id=1, source_target_pairs={{0,16},{2,18},{4,20},{6,22},{8,24},{10,26},{12,28},{14,30},{17,1},... | collective-permute-start | bytes 1769480 | tf_op jit(solution)/shard_map/ppermute | solution.py:305
  189.6 18.0 %collective-permute-start.14 = (bf16[384,768]{1,0:T(8,128)(2,1)S(1)}, bf16[384,768]{1,0:T(8,128)(2,1)S(1)}, u32[]{:S(2)}, u32[]{:S(2)}) collective-permute-start(bf16[384,768]{1,0:T(8,128)(2,1)S(1)} %broadcast_select_fusion.2.refs_0_), channel_id=1, source_target_pairs={{0,4},{2,6},{4,0},{6,2},{8,12},{10,14},{12,8},{14,10},{16,20},{18,... | collective-permute-start | bytes 1769480 | tf_op jit(solution)/shard_map/ppermute | solution.py:308
  189.6 17.9 %collective-permute-start.13 = (bf16[384,768]{1,0:T(8,128)(2,1)S(1)}, bf16[384,768]{1,0:T(8,128)(2,1)S(1)}, u32[]{:S(2)}, u32[]{:S(2)}) collective-permute-start(bf16[384,768]{1,0:T(8,128)(2,1)S(1)} %broadcast_select_fusion.2.refs_0_), channel_id=1, source_target_pairs={{0,2},{2,0},{4,6},{6,4},{8,10},{10,8},{12,14},{14,12},{16,18},{18,... | collective-permute-start | bytes 1769480 | tf_op jit(solution)/shard_map/ppermute | solution.py:308
  190.4 29.7 %collective-permute-start.12 = (bf16[384,768]{1,0:T(8,128)(2,1)S(1)}, bf16[384,768]{1,0:T(8,128)(2,1)}, u32[]{:S(2)}, u32[]{:S(2)}) collective-permute-start(bf16[384,768]{1,0:T(8,128)(2,1)S(1)} %broadcast_select_fusion.2.refs_0_), channel_id=1, source_target_pairs={{0,8},{2,10},{4,12},{6,14},{8,0},{10,2},{12,4},{14,6},{16,24},{18,... | collective-permute-start | bytes 1769480 | tf_op jit(solution)/shard_map/ppermute | solution.py:308
  222.6 15.3 %collective-permute-start.21 = (bf16[384,768]{1,0:T(8,128)(2,1)}, bf16[384,768]{1,0:T(8,128)(2,1)S(1)}, u32[]{:S(2)}, u32[]{:S(2)}) collective-permute-start(bf16[384,768]{1,0:T(8,128)(2,1)} %collective-permute-done.12.refs_5_), channel_id=1, source_target_pairs={{0,4},{2,6},{4,0},{6,2},{8,12},{10,14},{12,8},{14,10},{16,20},{18,... | collective-permute-start | bytes 1769480 | tf_op jit(solution)/shard_map/ppermute | solution.py:308
  224.3 15.6 %collective-permute-start.20 = (bf16[384,768]{1,0:T(8,128)(2,1)}, bf16[384,768]{1,0:T(8,128)(2,1)S(1)}, u32[]{:S(2)}, u32[]{:S(2)}) collective-permute-start(bf16[384,768]{1,0:T(8,128)(2,1)} %collective-permute-done.12.refs_5_), channel_id=1, source_target_pairs={{0,2},{2,0},{4,6},{6,4},{8,10},{10,8},{12,14},{14,12},{16,18},{18,... | collective-permute-start | bytes 1769480 | tf_op jit(solution)/shard_map/ppermute | solution.py:308
  234.1 24.5 %collective-permute-start.17 = (bf16[256,1536]{1,0:T(8,128)(2,1)}, bf16[256,1536]{1,0:T(8,128)(2,1)}, u32[]{:S(2)}, u32[]{:S(2)}) collective-permute-start(bf16[256,1536]{1,0:T(8,128)(2,1)} %dynamic-slice_convert_fusion), channel_id=1, source_target_pairs={{0,1},{1,0},{2,3},{3,2},{4,5},{5,4},{6,7},{7,6},{8,9},{9,8},{10,11... | collective-permute-start | bytes 2359304 | tf_op jit(solution)/shard_map/ppermute | solution.py:546
  236.0 9.4 %collective-permute-start.19 = (bf16[192,768]{1,0:T(8,128)(2,1)}, bf16[192,768]{1,0:T(8,128)(2,1)S(1)}, u32[]{:S(2)}, u32[]{:S(2)}) collective-permute-start(bf16[192,768]{1,0:T(8,128)(2,1)} %slice.13), channel_id=1, source_target_pairs={{0,2},{2,0},{4,6},{6,4},{8,10},{10,8},{12,14},{14,12},{16,18},{18,... | collective-permute-start | bytes 884744 | tf_op jit(solution)/shard_map/ppermute | solution.py:308
  237.1 8.3 %collective-permute-start.18 = (bf16[192,768]{1,0:T(8,128)(2,1)}, bf16[192,768]{1,0:T(8,128)(2,1)}, u32[]{:S(2)}, u32[]{:S(2)}) collective-permute-start(bf16[192,768]{1,0:T(8,128)(2,1)} %slice.12), channel_id=1, source_target_pairs={{0,4},{2,6},{4,0},{6,2},{8,12},{10,14},{12,8},{14,10},{16,20},{18,... | collective-permute-start | bytes 884744 | tf_op jit(solution)/shard_map/ppermute | solution.py:308
  238.7 13.0 %collective-permute-start.23 = (bf16[192,768]{1,0:T(8,128)(2,1)}, bf16[192,768]{1,0:T(8,128)(2,1)}, u32[]{:S(2)}, u32[]{:S(2)}) collective-permute-start(bf16[192,768]{1,0:T(8,128)(2,1)} %slice.21), channel_id=1, source_target_pairs={{0,2},{2,0},{4,6},{6,4},{8,10},{10,8},{12,14},{14,12},{16,18},{18,... | collective-permute-start | bytes 884744 | tf_op jit(solution)/shard_map/ppermute | solution.py:308
  240.7 11.1 %collective-permute-start.22 = (bf16[192,768]{1,0:T(8,128)(2,1)}, bf16[192,768]{1,0:T(8,128)(2,1)}, u32[]{:S(2)}, u32[]{:S(2)}) collective-permute-start(bf16[192,768]{1,0:T(8,128)(2,1)} %slice.20), channel_id=1, source_target_pairs={{0,4},{2,6},{4,0},{6,2},{8,12},{10,14},{12,8},{14,10},{16,20},{18,... | collective-permute-start | bytes 884744 | tf_op jit(solution)/shard_map/ppermute | solution.py:308
  (27 other events, 193.4 us)
Sparse Core Ops, SparseCore 0:
  60.7 67.5 all-gather.2

commit v8 on v7

--- a/solution.py
+++ b/solution.py
@@ -40,13 +40,12 @@
         v_all[at] = parts[2 * s + 1][...].reshape(shape)
 
 
-def head_of(chip, in_plane, heads_plane):
-    place = (chip % in_plane - chip // in_plane) % in_plane
-    return place < heads_plane, chip // in_plane * heads_plane + min(place, heads_plane - 1)
+def place_of(chip, seat, in_plane):
+    return (seat + in_plane - chip // in_plane % in_plane) % in_plane
 
 
 def pack_kernel(n, t, count, where_ref, *refs):
-    arrays, got, (out_ref, heads_all) = refs[:count], refs[count:count + t - 1], refs[count + t - 1:]
+    arrays, got, outs, heads_all = refs[:count], refs[count:count + t - 1], refs[count + t - 1:-1], refs[-1]
     core = where_ref[1]
     sub = heads_all.shape[2]
     heads_here = heads_all.shape[0] // t
@@ -57,42 +56,74 @@
             for s in range(1, t):
                 first = (core + t - s) % t * heads_here
                 heads_all[first + h, a] = got[s - 1][a, :, column]
-    for k in range(n):
-        held, head = head_of(k, n // PLANES, heads_all.shape[0] // PLANES)
-        out_ref[k] = heads_all[head] if held else jnp.zeros_like(heads_all[0])
-
-
-def join_kernel(n, where_ref, chunks_ref, q_ref, kv_ref):
-    sub = chunks_ref.shape[2]
-    for k in range(n):
-        at = pl.ds(k * sub, sub)
-        q_ref[at] = chunks_ref[k, 0]
-        kv_ref[0, at] = chunks_ref[k, 1]
-        kv_ref[1, at] = chunks_ref[k, 2]
+    plane = where_ref[0] // (n // PLANES)
+    heads_plane = outs[0].shape[0]
+    for k in range(PLANES):
+        outs[k][...] = heads_all[pl.ds((plane ^ k) * heads_plane, heads_plane)]
+
+
+def to_seats_kernel(n, where_ref, *refs):
+    got, outs = refs[:PLANES], refs[PLANES:]
+    chip = where_ref[0]
+    in_plane = n // PLANES
+    for m in range(in_plane):
+        place = place_of(chip, chip % in_plane ^ m, in_plane)
+        head = jnp.minimum(place, got[0].shape[0] - 1)
+        for k in range(PLANES):
+            outs[m][chip // in_plane ^ k] = got[k][head]
+
+
+def join_kernel(n, where_ref, *refs):
+    in_plane = n // PLANES
+    chunks, outs = refs[:in_plane], refs[in_plane:]
+    seat = where_ref[0] % in_plane
+    sub = chunks[0].shape[2]
+    for m in range(in_plane):
+        for p in range(PLANES):
+            at = pl.ds(pl.multiple_of((p * in_plane + (seat ^ m)) * sub, sub), sub)
+            outs[0][at] = chunks[m][p, 0]
+            if len(outs) > 1:
+                outs[1][0, at] = chunks[m][p, 1]
+                outs[1][1, at] = chunks[m][p, 2]
 
 
 def unjoin_kernel(n, t, where_ref, attn_ref, dq_ref, dkv_ref, *refs):
-    got, out_ref = refs[:t - 1], refs[t - 1]
-    sub = out_ref.shape[2]
-    for k in range(n):
-        at = pl.ds(k * sub, sub)
-        out_ref[k, 0] = attn_ref[at]
-        out_ref[k, 1] = dq_ref[at]
-        for a in range(2):
-            total = dkv_ref[a, at].astype(F32)
-            for other in got:
-                total = total + other[a, at].astype(F32)
-            out_ref[k, 2 + a] = total.astype(BF16)
-
-
-def by_core_kernel(n, t, where_ref, chunks_ref, *refs):
-    outs, heads_all = refs[:t], refs[t]
-    core = where_ref[1]
+    got, outs = refs[:t - 1], refs[t - 1:]
+    in_plane = n // PLANES
+    seat = where_ref[0] % in_plane
+    sub = outs[0].shape[2]
+    for m in range(in_plane):
+        for p in range(PLANES):
+            at = pl.ds(pl.multiple_of((p * in_plane + (seat ^ m)) * sub, sub), sub)
+            outs[m][p, 0] = attn_ref[at]
+            outs[m][p, 1] = dq_ref[at]
+            for a in range(2):
+                total = dkv_ref[a, at].astype(F32)
+                for other in got:
+                    total = total + other[a, at].astype(F32)
+                outs[m][p, 2 + a] = total.astype(BF16)
+
+
+def to_planes_kernel(n, where_ref, *refs):
+    in_plane = n // PLANES
+    got, outs = refs[:in_plane], refs[in_plane:]
+    chip = where_ref[0]
+    for m in range(in_plane):
+        place = place_of(chip, chip % in_plane ^ m, in_plane)
+
+        @pl.when(place < outs[0].shape[0])
+        def _(m=m, place=place):
+            for k in range(PLANES):
+                outs[k][place] = got[m][chip // in_plane ^ k]
+
+
+def by_core_kernel(n, t, where_ref, *refs):
+    got, outs, heads_all = refs[:PLANES], refs[PLANES:PLANES + t], refs[-1]
+    plane, core = where_ref[0] // (n // PLANES), where_ref[1]
     heads_here = heads_all.shape[0] // t
-    for k in range(n):
-        held, head = head_of(k, n // PLANES, heads_all.shape[0] // PLANES)
-        if held:
-            heads_all[head] = chunks_ref[k]
+    heads_plane = got[0].shape[0]
+    for k in range(PLANES):
+        heads_all[pl.ds((plane ^ k) * heads_plane, heads_plane)] = got[k][...]
     for s in range(t):
         outs[s][...] = heads_all[pl.ds((core + s) % t * heads_here, heads_here)]
 
@@ -294,7 +325,7 @@
             out_ref[middle:] = lower[...].astype(F32)
 
 
-def gather_tiles_by_core(n, t, tile_sum, chip, core, beside_chunks):
+def gather_tiles_by_core(n, t, tile_sum, chip, core):
     in_plane = n // PLANES
     plane, seat = chip // in_plane, chip % in_plane
     tile_rows, cols = tile_sum.shape
@@ -310,7 +341,6 @@
     first = jnp.where(plane // 2 == core, tile_sum, from_half)
     second = swap(first, in_plane)
     beside, above = swap(first, 1), swap(first, 2)
-    second, beside, above, beside_chunks = lax.optimization_barrier((second, beside, above, beside_chunks))
     middle = tile_rows // 2
     sources = [first, beside, above, swap(beside[:middle], 2), swap(above[middle:], 1)]
     beside, above = swap(second, 1), swap(second, 2)
@@ -330,7 +360,7 @@
         compiler_params=pltpu.CompilerParams(vmem_limit_bytes=48 * 2**20),
         cost_estimate=pl.CostEstimate(flops=0, bytes_accessed=2**24, transcendentals=0),
         name="place",
-    )(place, *sources), beside_chunks
+    )(place, *sources)
 
 
 def per_device(n, t, queries, key_vectors, value_vectors, out_weight, out_grad, block_segment):
@@ -409,25 +439,48 @@
     (plane_grad,) = simple_call(
         functools.partial(seats_kernel, in_plane), "seats", where, plane_got, [shape(in_plane, sub, cols)]
     )
+    def along_z(packs):
+        return [packs[0]] + [
+            lax.ppermute(packs[k], "ctx", [(i, i ^ k * in_plane) for i in range(n)])
+            for k in range(1, PLANES)
+        ]
+
+    def in_the_plane(packs, pairs):
+        return [packs[0]] + [lax.ppermute(packs[m], "ctx", pairs(m)) for m in range(1, in_plane)]
+
+    def to_held(m):
+        return [(i, i ^ m) for i in range(n) if held[i ^ m]]
+
+    def from_held(m):
+        return [(i, i ^ m) for i in range(n) if held[i]]
+
     def pack(arrays, got):
-        (sent,) = simple_call(
+        return simple_call(
             functools.partial(pack_kernel, n, t, len(arrays)), "pack", where,
-            arrays + got, [shape(n, len(arrays), sub, HEAD)],
+            arrays + got, [shape(heads_plane, len(arrays), sub, HEAD)] * PLANES,
             [pltpu.VMEM((heads, len(arrays), sub, HEAD), BF16)],
         )
-        return sent
-
-    sent_qkv = pack([queries, key_vectors, value_vectors], got_qkv)
-    sent_g = pack([grad_attn], got_g)
-    chunks = lax.all_to_all(sent_qkv, "ctx", 0, 0, tiled=True)
-    chunks, sent_g, plane_grad = lax.optimization_barrier((chunks, sent_g, plane_grad))
+
+    def to_seats(packs):
+        return simple_call(
+            functools.partial(to_seats_kernel, n), "to_seats", where, packs,
+            [shape(PLANES, packs[0].shape[1], sub, HEAD)] * in_plane,
+        )
+
+    length = n * sub
+    seats_qkv = to_seats(along_z(pack([queries, key_vectors, value_vectors], got_qkv)))
+    packs_g = pack([grad_attn], got_g)
+    *seats_qkv, plane_grad, p0, p1, p2, p3 = lax.optimization_barrier((*seats_qkv, plane_grad, *packs_g))
     lines = [[a * in_plane + b for a in range(PLANES)] for b in range(in_plane)]
     slice_grad = lax.all_gather(plane_grad, "ctx", axis_index_groups=lines)
-    slice_grad = slice_grad.reshape(n * sub, cols)
-    g_rows = lax.all_to_all(sent_g, "ctx", 0, 0, tiled=True).reshape(n * sub, HEAD)
-    length = n * sub
+    slice_grad = slice_grad.reshape(length, cols)
+    chunks = in_the_plane(seats_qkv, to_held)
     q_rows, kv = simple_call(
-        functools.partial(join_kernel, n), "join", where, [chunks], [shape(length, HEAD), shape(2, length, HEAD)]
+        functools.partial(join_kernel, n), "join", where, chunks, [shape(length, HEAD), shape(2, length, HEAD)]
+    )
+    seats_g = to_seats(along_z([p0, p1, p2, p3]))
+    (g_rows,) = simple_call(
+        functools.partial(join_kernel, n), "join_g", where, in_the_plane(seats_g, to_held), [shape(length, HEAD)]
     )
     kv_all = [kv] + [lax.ppermute(kv, "tp", shifts(t, s)) for s in range(1, t)]
 
@@ -475,11 +528,14 @@
     got_dkv = [
         lax.ppermute(dkv[s], "tp", [(c, (c - s) % t) for c in range(t)]) for s in range(1, t)
     ]
-    (sent,) = simple_call(
+    back = simple_call(
         functools.partial(unjoin_kernel, n, t), "unjoin", where,
-        [attn, dq, dkv[0]] + got_dkv, [shape(n, 4, sub, HEAD)],
-    )
-    chunks = lax.all_to_all(sent, "ctx", 0, 0, tiled=True)
+        [attn, dq, dkv[0]] + got_dkv, [shape(PLANES, 4, sub, HEAD)] * in_plane,
+    )
+    packs = simple_call(
+        functools.partial(to_planes_kernel, n), "to_planes", where, in_the_plane(back, from_held),
+        [shape(heads_plane, 4, sub, HEAD)] * PLANES,
+    )
 
     tile_rows = heads_plane * HEAD
     by_core = in_plane == 4 and t == 2
@@ -506,7 +562,7 @@
     for s in range(1, t):
         tile_sum = tile_sum + lax.ppermute(tile_sends[s - 1], "tp", shifts(t, s)).astype(F32)
     if by_core:
-        grad_weight, chunks = gather_tiles_by_core(n, t, tile_sum.astype(BF16), chip, core, chunks)
+        grad_weight = gather_tiles_by_core(n, t, tile_sum.astype(BF16), chip, core)
     else:
         tiles = lax.all_gather(tile_sum.astype(BF16), "ctx")
         here = n // t
@@ -532,7 +588,7 @@
         )(where, *tiles_core)
 
     mine = simple_call(
-        functools.partial(by_core_kernel, n, t), "by_core", where, [chunks],
+        functools.partial(by_core_kernel, n, t), "by_core", where, along_z(packs),
         [shape(heads_here, 4, sub, HEAD)] * t, [pltpu.VMEM((heads, 4, sub, HEAD), BF16)],
     )
     parts = [mine[0]] + [lax.ppermute(mine[s], "tp", shifts(t, s)) for s in range(1, t)]

time: 271 us -> 310 us (1.14)
  waiting for transfers between devices: 101 us -> 147 us
  local copies, waits for them, and re-layouts: 19.7 us -> 9.11 us
  starting transfers between devices: 60.5 us -> 68.8 us
    ppermute x0 -> x18, waiting for transfers between devices: none -> 99.7 us  [the longest x9 72.3 us: along_z(): lax.ppermute(packs[k], 'ctx', [(i, i ^ k * in_plane) for i in range(n)])]
    ppermute x0 -> x18, starting transfers between devices: none -> 31.1 us  [the longest x9 23.3 us: in_the_plane(): lax.ppermute(packs[m], 'ctx', pairs(m))]
    ppermute x1, waiting for transfers between devices: 32.8 us -> 8.06 us  [gather_tiles_by_core(): from_half = lax.ppermute(tile_sum, ('ctx', 'tp'), across)]
    all_to_all x3 -> x0, starting transfers between devices: 18.7 us -> none  [the longest x1 7.15 us: per_device(): chunks = lax.all_to_all(sent, 'ctx', 0, 0, tiled=True)]
    ppermute x3, waiting for transfers between devices: 18.6 us -> 0.01 us  [per_device(): lax.ppermute(attn, 'ctx', [(i, i ^ k) for i in range(n) if held[i]])]
    ppermute x3, waiting for transfers between devices: 13.1 us -> 0.01 us  [per_device(): plane_got.append(lax.ppermute(there, 'ctx', [(i, i ^ k) for i in range(n)]))]
    ppermute x9, starting transfers between devices: 23.1 us -> 12.6 us  [swap(): return lax.ppermute(x, 'ctx', [(i, i ^ k) for i in range(n)])]
    ppermute x9, waiting for transfers between devices: 22.7 us -> 32.7 us  [swap(): return lax.ppermute(x, 'ctx', [(i, i ^ k) for i in range(n)])]
  transfers between devices with their start and end apart: 28 -> 43, of which waited for: 15 -> 27; matrix products, arithmetic and copies ran while one was open for 7% -> 5% of each run, Pallas kernels for 20% -> 16%
where the time goes in v8:
time: 310 us; the launch traced here: 308 us
  waiting for transfers between devices  147 us (47%)
  starting transfers between devices  68.8 us (22%)
  Pallas kernels  57.1 us (18%)
  between operations  14.6 us (5%)
  local copies, waits for them, and re-layouts  9.11 us (3%)
  other arithmetic  6.08 us (2%)
  matrix products  5.2 us (2%)
    ppermute x9, waiting for transfers between devices, along_z(): lax.ppermute(packs[k], 'ctx', [(i, i ^ k * in_plane) for i in range(n)])  72.3 us
    ppermute x9, waiting for transfers between devices, swap(): return lax.ppermute(x, 'ctx', [(i, i ^ k) for i in range(n)])  32.7 us
    ppermute x9, waiting for transfers between devices, in_the_plane(): lax.ppermute(packs[m], 'ctx', pairs(m))  27.4 us
    ppermute x9, starting transfers between devices, in_the_plane(): lax.ppermute(packs[m], 'ctx', pairs(m))  23.3 us
    pallas_call x1, Pallas kernels, per_device(): pl.pallas_call(functools.partial(backward_kernel, t, tile, count), grid_s...  20.1 us
    pallas_call x1, Pallas kernels, per_device(): pl.pallas_call(functools.partial(forward_kernel, t, tile, count), grid_sp...  15.2 us
    ppermute x9, starting transfers between devices, swap(): return lax.ppermute(x, 'ctx', [(i, i ^ k) for i in range(n)])  12.6 us
    pallas_call x11, Pallas kernels, simple_call(): pl.pallas_call(kernel, grid_spec=pltpu.PrefetchScalarGridSpec(num_scalar_...  11.5 us
  transfers between devices with their start and end apart: 43, of which 27 were waited for; matrix products, arithmetic and copies ran while one was open for 5% of the time, Pallas kernels for 16%

profile of v8, /device:TPU:13, one launch (start us, length us, event | category | flops | bytes accessed | tf_op | source)
XLA Modules:
  0.0 307.6 jit_solution(6297443300031150282)
XLA Ops:
  21.7 4.7 %collective-permute-done.1.refs_1_ = bf16[3,3,128,128]{3,2,1,0:T(8,128)(2,1)S(1)} collective-permute-done((bf16[3,3,128,128]{3,2,1,0:T(8,128)(2,1)S(1)}, bf16[3,3,128,128]{3,2,1,0:T(8,128)(2,1)S(1)}, u32[]{:S(2)}, u32[]{:S(2)}) %collective-permute-start.1) | collective-permute-done | bytes 294944 | tf_op jit(solution)/shard_map/ppermute | solution.py:444
  27.5 7.5 %collective-permute-done.2.refs_2_ = bf16[3,3,128,128]{3,2,1,0:T(8,128)(2,1)S(1)} collective-permute-done((bf16[3,3,128,128]{3,2,1,0:T(8,128)(2,1)S(1)}, bf16[3,3,128,128]{3,2,1,0:T(8,128)(2,1)S(1)}, u32[]{:S(2)}, u32[]{:S(2)}) %collective-permute-start.2) | collective-permute-done | bytes 294944 | tf_op jit(solution)/shard_map/ppermute | solution.py:444
  35.2 7.1 %collective-permute-done.3.refs_3_ = bf16[3,3,128,128]{3,2,1,0:T(8,128)(2,1)S(1)} collective-permute-done((bf16[3,3,128,128]{3,2,1,0:T(8,128)(2,1)S(1)}, bf16[3,3,128,128]{3,2,1,0:T(8,128)(2,1)S(1)}, u32[]{:S(2)}, u32[]{:S(2)}) %collective-permute-start.3) | collective-permute-done | bytes 294944 | tf_op jit(solution)/shard_map/ppermute | solution.py:444
  56.5 11.3 %collective-permute-done.10.refs_2_ = bf16[4,3,128,128]{3,2,1,0:T(8,128)(2,1)S(1)} collective-permute-done((bf16[4,3,128,128]{3,2,1,0:T(8,128)(2,1)S(1)}, bf16[4,3,128,128]{3,2,1,0:T(8,128)(2,1)S(1)}, u32[]{:S(2)}, u32[]{:S(2)}) %collective-permute-start.10) | collective-permute-done | bytes 393248 | tf_op jit(solution)/shard_map/ppermute | solution.py:449
  74.3 15.2 %forward.1 = (bf16[2048,128]{1,0:T(8,128)(2,1)S(1)}, f32[2048,128]{1,0:T(8,128)S(1)}) custom-call(s32[16]{0:T(128)S(1)} %get-tuple-element.116.full_ref, s32[16]{0:T(128)S(1)} %get-tuple-element.112.kcnt_ref, s32[16,10]{1,0:T(8,128)S(1)} %copy.11.kidx_ref, bf16[2048,128]{1,0:T(8,128)(2,1)S(1)} %get-tuple-element.75.q_ref, ...), custom_call_target="tpu_custom_call" | custom-call | flops 16000000000 | bytes 5242880 | tf_op jit(solution)/shard_map/forward/pallas_call | solution.py:493
  92.8 5.1 %collective-permute-start.13 = (bf16[2048,128]{1,0:T(8,128)(2,1)S(1)}, bf16[2048,128]{1,0:T(8,128)(2,1)S(1)}, u32[]{:S(2)}, u32[]{:S(2)}) collective-permute-start(bf16[2048,128]{1,0:T(8,128)(2,1)S(1)} %get-tuple-element.105.o_ref.attn_ref.refs_0_), channel_id=1, source_target_pairs={{0,2},{2,0},{4,6},{10,8},{12,14},{14,12},{16,18},{20,22},{22,20},{... | collective-permute-start | bytes 1572872 | tf_op jit(solution)/shard_map/ppermute | solution.py:509
  99.2 7.8 %collective-permute-done.16.refs_1_ = bf16[3,1,128,128]{3,2,1,0:T(8,128)(2,1)S(1)} collective-permute-done((bf16[3,1,128,128]{3,2,1,0:T(8,128)(2,1)S(1)}, bf16[3,1,128,128]{3,2,1,0:T(8,128)(2,1)S(1)}, u32[]{:S(2)}, u32[]{:S(2)}) %collective-permute-start.16) | collective-permute-done | bytes 98336 | tf_op jit(solution)/shard_map/ppermute | solution.py:444
  108.4 11.6 %collective-permute-done.18.refs_3_ = bf16[3,1,128,128]{3,2,1,0:T(8,128)(2,1)S(1)} collective-permute-done((bf16[3,1,128,128]{3,2,1,0:T(8,128)(2,1)S(1)}, bf16[3,1,128,128]{3,2,1,0:T(8,128)(2,1)S(1)}, u32[]{:S(2)}, u32[]{:S(2)}) %collective-permute-start.18) | collective-permute-done | bytes 98336 | tf_op jit(solution)/shard_map/ppermute | solution.py:444
  129.5 4.2 %collective-permute-done.21.refs_3_ = bf16[4,1,128,128]{3,2,1,0:T(8,128)(2,1)S(1)} collective-permute-done((bf16[4,1,128,128]{3,2,1,0:T(8,128)(2,1)S(1)}, bf16[4,1,128,128]{3,2,1,0:T(8,128)(2,1)S(1)}, u32[]{:S(2)}, u32[]{:S(2)}) %collective-permute-start.21) | collective-permute-done | bytes 131104 | tf_op jit(solution)/shard_map/ppermute | solution.py:449
  136.7 20.1 %backward.1 = (bf16[2048,128]{1,0:T(8,128)(2,1)S(1)}, bf16[2,2048,128]{2,1,0:T(8,128)(2,1)S(1)}, bf16[2,2048,128]{2,1,0:T(8,128)(2,1)S(1)}) custom-call(s32[16]{0:T(128)S(1)} %get-tuple-element.116.full_ref, s32[16]{0:T(128)S(1)} %get-tuple-element.112.kcnt_ref, s32[16,10]{1,0:T(8,128)S(1)} %copy.11.kidx_ref, bf16[2048,128]{1,0:T(8,128)(2,1)S(1)} %get-tuple-element.75.q_ref, ...), custom_call_target="tpu_custom_call" | custom-call | flops 20000000000 | bytes 8388608 | tf_op jit(solution)/shard_map/backward/pallas_call | solution.py:513
  156.9 4.7 %collective-permute-start.22 = (bf16[2,2048,128]{2,1,0:T(8,128)(2,1)S(1)}, bf16[2,2048,128]{2,1,0:T(8,128)(2,1)S(1)}, u32[]{:S(2)}, u32[]{:S(2)}) collective-permute-start(bf16[2,2048,128]{2,1,0:T(8,128)(2,1)S(1)} %get-tuple-element.90), channel_id=1, source_target_pairs={{0,1},{1,0},{2,3},{3,2},{4,5},{5,4},{6,7},{7,6},{8,9},{9,8},{10,11... | collective-permute-start | bytes 3145736 | tf_op jit(solution)/shard_map/ppermute | solution.py:529
  169.4 4.9 %collective-permute-start.25 = (bf16[4,4,128,128]{3,2,1,0:T(8,128)(2,1)}, bf16[4,4,128,128]{3,2,1,0:T(8,128)(2,1)S(1)}, u32[]{:S(2)}, u32[]{:S(2)}) collective-permute-start(bf16[4,4,128,128]{3,2,1,0:T(8,128)(2,1)} %get-tuple-element.94), channel_id=1, source_target_pairs={{0,6},{2,4},{4,2},{10,12},{12,10},{14,8},{16,22},{20,18},{22,16},{... | collective-permute-start | bytes 1572872 | tf_op jit(solution)/shard_map/ppermute | solution.py:449
  176.4 4.9 %tile.1 = (f32[384,768]{1,0:T(8,128)S(1)}, bf16[384,768]{1,0:T(8,128)(2,1)S(1)}) custom-call(s32[2]{0:T(128)S(1)} %pad_add_fusion.where_ref, bf16[2048,128]{1,0:T(8,128)(2,1)S(1)} %get-tuple-element.105.o_ref.attn_ref.refs_0_, bf16[2048,128]{1,0:T(8,128)(2,1)S(1)} %copy-done.11, bf16[2048,128]{1,0:T(8,128)(2,1)S(1)} %copy-done.9, ...), custom_call_target="tpu_custom_call" | custom-call | flops 5000000000 | bytes 4194304 | tf_op jit(solution)/shard_map/tile/pallas_call | solution.py:544
  182.6 8.0 %collective-permute-done.25.refs_3_ = bf16[4,4,128,128]{3,2,1,0:T(8,128)(2,1)S(1)} collective-permute-done((bf16[4,4,128,128]{3,2,1,0:T(8,128)(2,1)}, bf16[4,4,128,128]{3,2,1,0:T(8,128)(2,1)S(1)}, u32[]{:S(2)}, u32[]{:S(2)}) %collective-permute-start.25) | collective-permute-done | bytes 524320 | tf_op jit(solution)/shard_map/ppermute | solution.py:449
  195.0 9.7 %collective-permute-done.26.refs_1_ = bf16[3,4,128,128]{3,2,1,0:T(8,128)(2,1)S(1)} collective-permute-done((bf16[3,4,128,128]{3,2,1,0:T(8,128)(2,1)S(1)}, bf16[3,4,128,128]{3,2,1,0:T(8,128)(2,1)S(1)}, u32[]{:S(2)}, u32[]{:S(2)}) %collective-permute-start.26) | collective-permute-done | bytes 393248 | tf_op jit(solution)/shard_map/ppermute | solution.py:444
  204.6 14.1 %collective-permute-done.27.refs_2_ = bf16[3,4,128,128]{3,2,1,0:T(8,128)(2,1)S(1)} collective-permute-done((bf16[3,4,128,128]{3,2,1,0:T(8,128)(2,1)S(1)}, bf16[3,4,128,128]{3,2,1,0:T(8,128)(2,1)S(1)}, u32[]{:S(2)}, u32[]{:S(2)}) %collective-permute-start.27) | collective-permute-done | bytes 393248 | tf_op jit(solution)/shard_map/ppermute | solution.py:444
  218.7 8.6 %collective-permute-done.28.refs_3_ = bf16[3,4,128,128]{3,2,1,0:T(8,128)(2,1)S(1)} collective-permute-done((bf16[3,4,128,128]{3,2,1,0:T(8,128)(2,1)S(1)}, bf16[3,4,128,128]{3,2,1,0:T(8,128)(2,1)S(1)}, u32[]{:S(2)}, u32[]{:S(2)}) %collective-permute-start.28) | collective-permute-done | bytes 393248 | tf_op jit(solution)/shard_map/ppermute | solution.py:444
  234.1 8.1 %collective-permute-done.32 = bf16[384,768]{1,0:T(8,128)(2,1)S(1)} collective-permute-done((bf16[384,768]{1,0:T(8,128)(2,1)S(1)}, bf16[384,768]{1,0:T(8,128)(2,1)S(1)}, u32[]{:S(2)}, u32[]{:S(2)}) %collective-permute-start.32) | collective-permute-done | bytes 589856 | tf_op jit(solution)/shard_map/ppermute | solution.py:336
  242.3 6.7 %collective-permute-start.37 = (bf16[384,768]{1,0:T(8,128)(2,1)S(1)}, bf16[384,768]{1,0:T(8,128)(2,1)S(1)}, u32[]{:S(2)}, u32[]{:S(2)}) collective-permute-start(bf16[384,768]{1,0:T(8,128)(2,1)S(1)} %broadcast_select_fusion.2.refs_0_), channel_id=1, source_target_pairs={{0,8},{2,10},{4,12},{6,14},{8,0},{10,2},{12,4},{14,6},{16,24},{18,... | collective-permute-start | bytes 1769480 | tf_op jit(solution)/shard_map/ppermute | solution.py:339
  255.9 5.6 %collective-permute-done.37.refs_5_ = bf16[384,768]{1,0:T(8,128)(2,1)S(1)} collective-permute-done((bf16[384,768]{1,0:T(8,128)(2,1)S(1)}, bf16[384,768]{1,0:T(8,128)(2,1)S(1)}, u32[]{:S(2)}, u32[]{:S(2)}) %collective-permute-start.37) | collective-permute-done | bytes 589856 | tf_op jit(solution)/shard_map/ppermute | solution.py:339
  264.2 4.9 %collective-permute-done.34.refs_2_ = bf16[384,768]{1,0:T(8,128)(2,1)S(1)} collective-permute-done((bf16[384,768]{1,0:T(8,128)(2,1)S(1)}, bf16[384,768]{1,0:T(8,128)(2,1)S(1)}, u32[]{:S(2)}, u32[]{:S(2)}) %collective-permute-start.34) | collective-permute-done | bytes 589856 | tf_op jit(solution)/shard_map/ppermute | solution.py:339
  270.5 11.3 %collective-permute-done.39.refs_7_ = bf16[384,768]{1,0:T(8,128)(2,1)S(1)} collective-permute-done((bf16[384,768]{1,0:T(8,128)(2,1)S(1)}, bf16[384,768]{1,0:T(8,128)(2,1)S(1)}, u32[]{:S(2)}, u32[]{:S(2)}) %collective-permute-start.39) | collective-permute-done | bytes 589856 | tf_op jit(solution)/shard_map/ppermute | solution.py:339
  289.0 6.3 %collective-permute-done.41.refs_9_ = bf16[192,768]{1,0:T(8,128)(2,1)S(1)} collective-permute-done((bf16[192,768]{1,0:T(8,128)(2,1)S(1)}, bf16[192,768]{1,0:T(8,128)(2,1)S(1)}, u32[]{:S(2)}, u32[]{:S(2)}) %collective-permute-start.41) | collective-permute-done | bytes 294944 | tf_op jit(solution)/shard_map/ppermute | solution.py:339
  295.3 5.4 %place.1 = f32[768,3072]{1,0:T(8,128)} custom-call(s32[2]{0:T(128)S(1)} %pad_add_fusion.2.place_ref, bf16[384,768]{1,0:T(8,128)(2,1)S(1)} %broadcast_select_fusion.2.refs_0_, bf16[384,768]{1,0:T(8,128)(2,1)S(1)} %collective-permute-done.33.refs_1_, bf16[384,768]{1,0:T(8,128)(2,1)S(1)} %collective-permute-done.34.refs_2_, ...), custom_call_target="tpu_custom_call" | custom-call | bytes 16777216 | tf_op jit(solution)/shard_map/place/pallas_call | solution.py:349
  (139 shorter events, 95.2 us)
Async XLA Ops:
  7.2 167.1 %all-gather.3.cloned.1.call-start = ((), (), s32[]{:S(2)}) async-start(), calls=%async_computation | async-start | bytes 3932160 | tf_op jit(solution)/shard_map/all_gather | solution.py:475
  14.2 20.8 %collective-permute-start.2 = (bf16[3,3,128,128]{3,2,1,0:T(8,128)(2,1)S(1)}, bf16[3,3,128,128]{3,2,1,0:T(8,128)(2,1)S(1)}, u32[]{:S(2)}, u32[]{:S(2)}) collective-permute-start(bf16[3,3,128,128]{3,2,1,0:T(8,128)(2,1)S(1)} %get-tuple-element.61), channel_id=1, source_target_pairs={{0,16},{2,18},{4,20},{6,22},{8,24},{10,26},{12,28},{14,30},{16,0},... | collective-permute-start | bytes 884744 | tf_op jit(solution)/shard_map/ppermute | solution.py:444
  16.5 25.9 %collective-permute-start.3 = (bf16[3,3,128,128]{3,2,1,0:T(8,128)(2,1)S(1)}, bf16[3,3,128,128]{3,2,1,0:T(8,128)(2,1)S(1)}, u32[]{:S(2)}, u32[]{:S(2)}) collective-permute-start(bf16[3,3,128,128]{3,2,1,0:T(8,128)(2,1)S(1)} %get-tuple-element.62), channel_id=1, source_target_pairs={{0,24},{2,26},{4,28},{6,30},{8,16},{10,18},{12,20},{14,22},{16,8},... | collective-permute-start | bytes 884744 | tf_op jit(solution)/shard_map/ppermute | solution.py:444
  18.3 24.8 %collective-permute-start.8 = (bf16[1,128,768]{2,1,0:T(8,128)(2,1)S(1)}, bf16[1,128,768]{2,1,0:T(8,128)(2,1)S(1)}, u32[]{:S(2)}, u32[]{:S(2)}) collective-permute-start(bf16[1,128,768]{2,1,0:T(8,128)(2,1)S(1)} %dynamic-slice_bitcast_fusion), channel_id=1, source_target_pairs={{0,1},{1,0},{2,3},{3,2},{4,5},{5,4},{6,7},{7,6},{8,9},{9,8},{10,11... | collective-permute-start | bytes 589832 | tf_op jit(solution)/shard_map/ppermute | solution.py:416
  20.4 23.3 %collective-permute-start.7 = (bf16[128,768]{1,0:T(8,128)(2,1)S(1)}, bf16[128,768]{1,0:T(8,128)(2,1)S(1)}, u32[]{:S(2)}, u32[]{:S(2)}) collective-permute-start(bf16[128,768]{1,0:T(8,128)(2,1)S(1)} %get-tuple-element.118), channel_id=1, source_target_pairs={{0,6},{2,4},{4,2},{6,0},{8,14},{10,12},{12,10},{14,8},{16,22},{18,... | collective-permute-start | bytes 589832 | tf_op jit(solution)/shard_map/ppermute | solution.py:438
  26.3 17.4 %collective-permute-start.5 = (bf16[128,768]{1,0:T(8,128)(2,1)S(1)}, bf16[128,768]{1,0:T(8,128)(2,1)S(1)}, u32[]{:S(2)}, u32[]{:S(2)}) collective-permute-start(bf16[128,768]{1,0:T(8,128)(2,1)S(1)} %get-tuple-element.120), channel_id=1, source_target_pairs={{0,2},{2,0},{4,6},{6,4},{8,10},{10,8},{12,14},{14,12},{16,18},{18,... | collective-permute-start | bytes 589832 | tf_op jit(solution)/shard_map/ppermute | solution.py:438
  48.3 19.4 %collective-permute-start.10 = (bf16[4,3,128,128]{3,2,1,0:T(8,128)(2,1)S(1)}, bf16[4,3,128,128]{3,2,1,0:T(8,128)(2,1)S(1)}, u32[]{:S(2)}, u32[]{:S(2)}) collective-permute-start(bf16[4,3,128,128]{3,2,1,0:T(8,128)(2,1)S(1)} %get-tuple-element.73), channel_id=1, source_target_pairs={{0,4},{4,0},{6,2},{8,12},{10,14},{14,10},{16,20},{18,22},{20,16},{... | collective-permute-start | bytes 1179656 | tf_op jit(solution)/shard_map/ppermute | solution.py:449
  49.6 18.1 %collective-permute-start.11 = (bf16[4,3,128,128]{3,2,1,0:T(8,128)(2,1)S(1)}, bf16[4,3,128,128]{3,2,1,0:T(8,128)(2,1)S(1)}, u32[]{:S(2)}, u32[]{:S(2)}) collective-permute-start(bf16[4,3,128,128]{3,2,1,0:T(8,128)(2,1)S(1)} %get-tuple-element.74), channel_id=1, source_target_pairs={{2,4},{4,2},{6,0},{8,14},{10,12},{12,10},{16,22},{18,20},{22,16},{... | collective-permute-start | bytes 1179656 | tf_op jit(solution)/shard_map/ppermute | solution.py:449
  89.5 44.8 %collective-permute-start.15 = (bf16[2048,128]{1,0:T(8,128)(2,1)S(1)}, bf16[2048,128]{1,0:T(8,128)(2,1)S(1)}, u32[]{:S(2)}, u32[]{:S(2)}) collective-permute-start(bf16[2048,128]{1,0:T(8,128)(2,1)S(1)} %get-tuple-element.105.o_ref.attn_ref.refs_0_), channel_id=1, source_target_pairs={{0,6},{2,4},{4,2},{10,12},{12,10},{14,8},{16,22},{20,18},{22,16},{... | collective-permute-start | bytes 1572872 | tf_op jit(solution)/shard_map/ppermute | solution.py:509
  91.4 43.7 %collective-permute-start.14 = (bf16[2048,128]{1,0:T(8,128)(2,1)S(1)}, bf16[2048,128]{1,0:T(8,128)(2,1)S(1)}, u32[]{:S(2)}, u32[]{:S(2)}) collective-permute-start(bf16[2048,128]{1,0:T(8,128)(2,1)S(1)} %get-tuple-element.105.o_ref.attn_ref.refs_0_), channel_id=1, source_target_pairs={{0,4},{2,6},{4,0},{10,14},{12,8},{14,10},{16,20},{20,16},{22,18},{... | collective-permute-start | bytes 1572872 | tf_op jit(solution)/shard_map/ppermute | solution.py:509
  92.8 43.1 %collective-permute-start.13 = (bf16[2048,128]{1,0:T(8,128)(2,1)S(1)}, bf16[2048,128]{1,0:T(8,128)(2,1)S(1)}, u32[]{:S(2)}, u32[]{:S(2)}) collective-permute-start(bf16[2048,128]{1,0:T(8,128)(2,1)S(1)} %get-tuple-element.105.o_ref.attn_ref.refs_0_), channel_id=1, source_target_pairs={{0,2},{2,0},{4,6},{10,8},{12,14},{14,12},{16,18},{20,22},{22,20},{... | collective-permute-start | bytes 1572872 | tf_op jit(solution)/shard_map/ppermute | solution.py:509
  165.7 16.8 %collective-permute-start.23 = (bf16[4,4,128,128]{3,2,1,0:T(8,128)(2,1)}, bf16[4,4,128,128]{3,2,1,0:T(8,128)(2,1)S(1)}, u32[]{:S(2)}, u32[]{:S(2)}) collective-permute-start(bf16[4,4,128,128]{3,2,1,0:T(8,128)(2,1)} %get-tuple-element.92), channel_id=1, source_target_pairs={{0,2},{2,0},{4,6},{10,8},{12,14},{14,12},{16,18},{20,22},{22,20},{... | collective-permute-start | bytes 1572872 | tf_op jit(solution)/shard_map/ppermute | solution.py:449
  168.0 14.5 %collective-permute-start.24 = (bf16[4,4,128,128]{3,2,1,0:T(8,128)(2,1)}, bf16[4,4,128,128]{3,2,1,0:T(8,128)(2,1)S(1)}, u32[]{:S(2)}, u32[]{:S(2)}) collective-permute-start(bf16[4,4,128,128]{3,2,1,0:T(8,128)(2,1)} %get-tuple-element.93), channel_id=1, source_target_pairs={{0,4},{2,6},{4,0},{10,14},{12,8},{14,10},{16,20},{20,16},{22,18},{... | collective-permute-start | bytes 1572872 | tf_op jit(solution)/shard_map/ppermute | solution.py:449
  169.4 21.2 %collective-permute-start.25 = (bf16[4,4,128,128]{3,2,1,0:T(8,128)(2,1)}, bf16[4,4,128,128]{3,2,1,0:T(8,128)(2,1)S(1)}, u32[]{:S(2)}, u32[]{:S(2)}) collective-permute-start(bf16[4,4,128,128]{3,2,1,0:T(8,128)(2,1)} %get-tuple-element.94), channel_id=1, source_target_pairs={{0,6},{2,4},{4,2},{10,12},{12,10},{14,8},{16,22},{20,18},{22,16},{... | collective-permute-start | bytes 1572872 | tf_op jit(solution)/shard_map/ppermute | solution.py:449
  181.3 49.2 %collective-permute-start.31 = (bf16[384,768]{1,0:T(8,128)(2,1)S(1)}, bf16[384,768]{1,0:T(8,128)(2,1)S(1)}, u32[]{:S(2)}, u32[]{:S(2)}) collective-permute-start(bf16[384,768]{1,0:T(8,128)(2,1)S(1)} %get-tuple-element.111), channel_id=1, source_target_pairs={{0,1},{1,0},{2,3},{3,2},{4,5},{5,4},{6,7},{7,6},{8,9},{9,8},{10,11... | collective-permute-start | bytes 1769480 | tf_op jit(solution)/shard_map/ppermute | solution.py:563
  191.3 27.4 %collective-permute-start.27 = (bf16[3,4,128,128]{3,2,1,0:T(8,128)(2,1)S(1)}, bf16[3,4,128,128]{3,2,1,0:T(8,128)(2,1)S(1)}, u32[]{:S(2)}, u32[]{:S(2)}) collective-permute-start(bf16[3,4,128,128]{3,2,1,0:T(8,128)(2,1)S(1)} %get-tuple-element.97), channel_id=1, source_target_pairs={{0,16},{2,18},{4,20},{6,22},{8,24},{10,26},{12,28},{14,30},{16,0},... | collective-permute-start | bytes 1179656 | tf_op jit(solution)/shard_map/ppermute | solution.py:444
  194.9 32.3 %collective-permute-start.28 = (bf16[3,4,128,128]{3,2,1,0:T(8,128)(2,1)S(1)}, bf16[3,4,128,128]{3,2,1,0:T(8,128)(2,1)S(1)}, u32[]{:S(2)}, u32[]{:S(2)}) collective-permute-start(bf16[3,4,128,128]{3,2,1,0:T(8,128)(2,1)S(1)} %get-tuple-element.98), channel_id=1, source_target_pairs={{0,24},{2,26},{4,28},{6,30},{8,16},{10,18},{12,20},{14,22},{16,8},... | collective-permute-start | bytes 1179656 | tf_op jit(solution)/shard_map/ppermute | solution.py:444
  242.3 19.3 %collective-permute-start.37 = (bf16[384,768]{1,0:T(8,128)(2,1)S(1)}, bf16[384,768]{1,0:T(8,128)(2,1)S(1)}, u32[]{:S(2)}, u32[]{:S(2)}) collective-permute-start(bf16[384,768]{1,0:T(8,128)(2,1)S(1)} %broadcast_select_fusion.2.refs_0_), channel_id=1, source_target_pairs={{0,8},{2,10},{4,12},{6,14},{8,0},{10,2},{12,4},{14,6},{16,24},{18,... | collective-permute-start | bytes 1769480 | tf_op jit(solution)/shard_map/ppermute | solution.py:339
  253.9 29.3 %collective-permute-start.30 = (bf16[256,1536]{1,0:T(8,128)(2,1)}, bf16[256,1536]{1,0:T(8,128)(2,1)}, u32[]{:S(2)}, u32[]{:S(2)}) collective-permute-start(bf16[256,1536]{1,0:T(8,128)(2,1)} %dynamic-slice_convert_fusion), channel_id=1, source_target_pairs={{0,1},{1,0},{2,3},{3,2},{4,5},{5,4},{6,7},{7,6},{8,9},{9,8},{10,11... | collective-permute-start | bytes 2359304 | tf_op jit(solution)/shard_map/ppermute | solution.py:602
  253.9 15.3 %collective-permute-start.34 = (bf16[384,768]{1,0:T(8,128)(2,1)S(1)}, bf16[384,768]{1,0:T(8,128)(2,1)S(1)}, u32[]{:S(2)}, u32[]{:S(2)}) collective-permute-start(bf16[384,768]{1,0:T(8,128)(2,1)S(1)} %broadcast_select_fusion.2.refs_0_), channel_id=1, source_target_pairs={{0,4},{2,6},{4,0},{6,2},{8,12},{10,14},{12,8},{14,10},{16,20},{18,... | collective-permute-start | bytes 1769480 | tf_op jit(solution)/shard_map/ppermute | solution.py:339
  261.5 20.3 %collective-permute-start.39 = (bf16[384,768]{1,0:T(8,128)(2,1)S(1)}, bf16[384,768]{1,0:T(8,128)(2,1)S(1)}, u32[]{:S(2)}, u32[]{:S(2)}) collective-permute-start(bf16[384,768]{1,0:T(8,128)(2,1)S(1)} %collective-permute-done.37.refs_5_), channel_id=1, source_target_pairs={{0,4},{2,6},{4,0},{6,2},{8,12},{10,14},{12,8},{14,10},{16,20},{18,... | collective-permute-start | bytes 1769480 | tf_op jit(solution)/shard_map/ppermute | solution.py:339
  264.2 18.5 %collective-permute-start.38 = (bf16[384,768]{1,0:T(8,128)(2,1)S(1)}, bf16[384,768]{1,0:T(8,128)(2,1)S(1)}, u32[]{:S(2)}, u32[]{:S(2)}) collective-permute-start(bf16[384,768]{1,0:T(8,128)(2,1)S(1)} %collective-permute-done.37.refs_5_), channel_id=1, source_target_pairs={{0,2},{2,0},{4,6},{6,4},{8,10},{10,8},{12,14},{14,12},{16,18},{18,... | collective-permute-start | bytes 1769480 | tf_op jit(solution)/shard_map/ppermute | solution.py:339
  269.2 19.8 %collective-permute-start.36 = (bf16[192,768]{1,0:T(8,128)(2,1)S(1)}, bf16[192,768]{1,0:T(8,128)(2,1)S(1)}, u32[]{:S(2)}, u32[]{:S(2)}) collective-permute-start(bf16[192,768]{1,0:T(8,128)(2,1)S(1)} %slice.21), channel_id=1, source_target_pairs={{0,2},{2,0},{4,6},{6,4},{8,10},{10,8},{12,14},{14,12},{16,18},{18,... | collective-permute-start | bytes 884744 | tf_op jit(solution)/shard_map/ppermute | solution.py:339
  270.0 18.9 %collective-permute-start.35 = (bf16[192,768]{1,0:T(8,128)(2,1)S(1)}, bf16[192,768]{1,0:T(8,128)(2,1)S(1)}, u32[]{:S(2)}, u32[]{:S(2)}) collective-permute-start(bf16[192,768]{1,0:T(8,128)(2,1)S(1)} %slice.20), channel_id=1, source_target_pairs={{0,4},{2,6},{4,0},{6,2},{8,12},{10,14},{12,8},{14,10},{16,20},{18,... | collective-permute-start | bytes 884744 | tf_op jit(solution)/shard_map/ppermute | solution.py:339
  (34 other events, 296.0 us)
Sparse Core Ops, SparseCore 0:
  73.0 66.9 all-gather.2

commit v9 on v8

--- a/solution.py
+++ b/solution.py
@@ -325,7 +325,7 @@
             out_ref[middle:] = lower[...].astype(F32)
 
 
-def gather_tiles_by_core(n, t, tile_sum, chip, core):
+def gather_tiles_by_core(n, t, tile_sum, chip, core, packs, along_z):
     in_plane = n // PLANES
     plane, seat = chip // in_plane, chip % in_plane
     tile_rows, cols = tile_sum.shape
@@ -339,8 +339,10 @@
         return lax.ppermute(x, "ctx", [(i, i ^ k) for i in range(n)])
 
     first = jnp.where(plane // 2 == core, tile_sum, from_half)
+    first, *packs = lax.optimization_barrier((first, *packs))
     second = swap(first, in_plane)
     beside, above = swap(first, 1), swap(first, 2)
+    second, beside, above, *packs = lax.optimization_barrier((second, beside, above, *along_z(packs)))
     middle = tile_rows // 2
     sources = [first, beside, above, swap(beside[:middle], 2), swap(above[middle:], 1)]
     beside, above = swap(second, 1), swap(second, 2)
@@ -360,7 +362,7 @@
         compiler_params=pltpu.CompilerParams(vmem_limit_bytes=48 * 2**20),
         cost_estimate=pl.CostEstimate(flops=0, bytes_accessed=2**24, transcendentals=0),
         name="place",
-    )(place, *sources)
+    )(place, *sources), packs
 
 
 def per_device(n, t, queries, key_vectors, value_vectors, out_weight, out_grad, block_segment):
@@ -475,13 +477,16 @@
     slice_grad = lax.all_gather(plane_grad, "ctx", axis_index_groups=lines)
     slice_grad = slice_grad.reshape(length, cols)
     chunks = in_the_plane(seats_qkv, to_held)
+    seats_g = to_seats(along_z([p0, p1, p2, p3]))
+    tied = lax.optimization_barrier((*chunks, *seats_g))
+    chunks, seats_g = list(tied[:in_plane]), list(tied[in_plane:])
     q_rows, kv = simple_call(
         functools.partial(join_kernel, n), "join", where, chunks, [shape(length, HEAD), shape(2, length, HEAD)]
     )
-    seats_g = to_seats(along_z([p0, p1, p2, p3]))
     (g_rows,) = simple_call(
         functools.partial(join_kernel, n), "join_g", where, in_the_plane(seats_g, to_held), [shape(length, HEAD)]
     )
+    q_rows, g_rows = lax.optimization_barrier((q_rows, g_rows))
     kv_all = [kv] + [lax.ppermute(kv, "tp", shifts(t, s)) for s in range(1, t)]
 
     tiles_q = n * per_chunk
@@ -562,8 +567,11 @@
     for s in range(1, t):
         tile_sum = tile_sum + lax.ppermute(tile_sends[s - 1], "tp", shifts(t, s)).astype(F32)
     if by_core:
-        grad_weight = gather_tiles_by_core(n, t, tile_sum.astype(BF16), chip, core)
+        grad_weight, back = gather_tiles_by_core(
+            n, t, tile_sum.astype(BF16), chip, core, packs, along_z
+        )
     else:
+        back = along_z(packs)
         tiles = lax.all_gather(tile_sum.astype(BF16), "ctx")
         here = n // t
         tiles_core = [tiles] + [
@@ -588,7 +596,7 @@
         )(where, *tiles_core)
 
     mine = simple_call(
-        functools.partial(by_core_kernel, n, t), "by_core", where, along_z(packs),
+        functools.partial(by_core_kernel, n, t), "by_core", where, back,
         [shape(heads_here, 4, sub, HEAD)] * t, [pltpu.VMEM((heads, 4, sub, HEAD), BF16)],
     )
     parts = [mine[0]] + [lax.ppermute(mine[s], "tp", shifts(t, s)) for s in range(1, t)]

time: 310 us -> 291 us (0.939)
  waiting for transfers between devices: 147 us -> 106 us
  starting transfers between devices: 68.8 us -> 80.7 us
  local copies, waits for them, and re-layouts: 9.11 us -> 15.9 us
    ppermute x9, waiting for transfers between devices: 72.3 us -> 50.1 us  [along_z(): lax.ppermute(packs[k], 'ctx', [(i, i ^ k * in_plane) for i in range(n)])]
    ppermute x9, waiting for transfers between devices: 32.7 us -> 11.6 us  [swap(): return lax.ppermute(x, 'ctx', [(i, i ^ k) for i in range(n)])]
    ppermute x3, waiting for transfers between devices: 0.01 us -> 17.8 us  [per_device(): lax.ppermute(attn, 'ctx', [(i, i ^ k) for i in range(n) if held[i]])]
    ppermute x9, starting transfers between devices: 7.75 us -> 22.5 us  [along_z(): lax.ppermute(packs[k], 'ctx', [(i, i ^ k * in_plane) for i in range(n)])]
    ppermute x1, waiting for transfers between devices: 8.06 us -> 0.01 us  [gather_tiles_by_core(): from_half = lax.ppermute(tile_sum, ('ctx', 'tp'), across)]
    ppermute x1, starting transfers between devices: 4.74 us -> 0.13 us  [per_device(): lax.ppermute(dkv[s], 'tp', [(c, (c - s) % t) for c in range(t)])]
    ppermute x9, waiting for transfers between devices: 27.4 us -> 22.8 us  [in_the_plane(): lax.ppermute(packs[m], 'ctx', pairs(m))]
    unnamed x30 -> x46, local copies, waits for them, and re-layouts: 4.54 us -> 8.41 us
  transfers between devices with their start and end apart: 43 -> 43, of which waited for: 27 -> 24; matrix products, arithmetic and copies ran while one was open for 5% -> 6% of each run, Pallas kernels for 16% -> 19%
where the time goes in v9:
time: 291 us; the launch traced here: 289 us
  waiting for transfers between devices  106 us (36%)
  starting transfers between devices  80.7 us (28%)
  Pallas kernels  58.9 us (20%)
  local copies, waits for them, and re-layouts  15.9 us (5%)
  between operations  14.6 us (5%)
  other arithmetic  7.48 us (3%)
  matrix products  5.18 us (2%)
    ppermute x9, waiting for transfers between devices, along_z(): lax.ppermute(packs[k], 'ctx', [(i, i ^ k * in_plane) for i in range(n)])  50.1 us
    ppermute x9, starting transfers between devices, in_the_plane(): lax.ppermute(packs[m], 'ctx', pairs(m))  26.6 us
    ppermute x9, waiting for transfers between devices, in_the_plane(): lax.ppermute(packs[m], 'ctx', pairs(m))  22.8 us
    ppermute x9, starting transfers between devices, along_z(): lax.ppermute(packs[k], 'ctx', [(i, i ^ k * in_plane) for i in range(n)])  22.5 us
    pallas_call x1, Pallas kernels, per_device(): pl.pallas_call(functools.partial(backward_kernel, t, tile, count), grid_s...  21.1 us
    ppermute x3, waiting for transfers between devices, per_device(): lax.ppermute(attn, 'ctx', [(i, i ^ k) for i in range(n) if held[i]])  17.8 us
    pallas_call x1, Pallas kernels, per_device(): pl.pallas_call(functools.partial(forward_kernel, t, tile, count), grid_sp...  13.8 us
    pallas_call x11, Pallas kernels, simple_call(): pl.pallas_call(kernel, grid_spec=pltpu.PrefetchScalarGridSpec(num_scalar_...  12.5 us
  transfers between devices with their start and end apart: 43, of which 24 were waited for; matrix products, arithmetic and copies ran while one was open for 6% of the time, Pallas kernels for 19%

profile of v9, /device:TPU:13, one launch (start us, length us, event | category | flops | bytes accessed | tf_op | source)
XLA Modules:
  0.0 288.6 jit_solution(17187226686227321137)
XLA Ops:
  21.7 4.6 %collective-permute-done.1.refs_1_ = bf16[3,3,128,128]{3,2,1,0:T(8,128)(2,1)S(1)} collective-permute-done((bf16[3,3,128,128]{3,2,1,0:T(8,128)(2,1)S(1)}, bf16[3,3,128,128]{3,2,1,0:T(8,128)(2,1)S(1)}, u32[]{:S(2)}, u32[]{:S(2)}) %collective-permute-start.1) | collective-permute-done | bytes 294944 | tf_op jit(solution)/shard_map/ppermute | solution.py:446
  26.6 8.4 %collective-permute-done.2.refs_2_ = bf16[3,3,128,128]{3,2,1,0:T(8,128)(2,1)S(1)} collective-permute-done((bf16[3,3,128,128]{3,2,1,0:T(8,128)(2,1)S(1)}, bf16[3,3,128,128]{3,2,1,0:T(8,128)(2,1)S(1)}, u32[]{:S(2)}, u32[]{:S(2)}) %collective-permute-start.2) | collective-permute-done | bytes 294944 | tf_op jit(solution)/shard_map/ppermute | solution.py:446
  36.2 6.2 %collective-permute-done.3.refs_3_ = bf16[3,3,128,128]{3,2,1,0:T(8,128)(2,1)S(1)} collective-permute-done((bf16[3,3,128,128]{3,2,1,0:T(8,128)(2,1)S(1)}, bf16[3,3,128,128]{3,2,1,0:T(8,128)(2,1)S(1)}, u32[]{:S(2)}, u32[]{:S(2)}) %collective-permute-start.3) | collective-permute-done | bytes 294944 | tf_op jit(solution)/shard_map/ppermute | solution.py:446
  46.5 4.9 %collective-permute-start.11 = (bf16[4,3,128,128]{3,2,1,0:T(8,128)(2,1)S(1)}, bf16[4,3,128,128]{3,2,1,0:T(8,128)(2,1)S(1)}, u32[]{:S(2)}, u32[]{:S(2)}) collective-permute-start(bf16[4,3,128,128]{3,2,1,0:T(8,128)(2,1)S(1)} %get-tuple-element.96), channel_id=1, source_target_pairs={{2,4},{4,2},{6,0},{8,14},{10,12},{12,10},{16,22},{18,20},{22,16},{... | collective-permute-start | bytes 1179656 | tf_op jit(solution)/shard_map/ppermute | solution.py:451
  59.6 5.4 %collective-permute-done.14.refs_3_ = bf16[3,1,128,128]{3,2,1,0:T(8,128)(2,1)S(1)} collective-permute-done((bf16[3,1,128,128]{3,2,1,0:T(8,128)(2,1)S(1)}, bf16[3,1,128,128]{3,2,1,0:T(8,128)(2,1)S(1)}, u32[]{:S(2)}, u32[]{:S(2)}) %collective-permute-start.14) | collective-permute-done | bytes 98336 | tf_op jit(solution)/shard_map/ppermute | solution.py:446
  71.0 4.1 %collective-permute-start.15 = (bf16[4,1,128,128]{3,2,1,0:T(8,128)(2,1)}, bf16[4,1,128,128]{3,2,1,0:T(8,128)(2,1)S(1)}, u32[]{:S(2)}, u32[]{:S(2)}) collective-permute-start(bf16[4,1,128,128]{3,2,1,0:T(8,128)(2,1)} %copy-done.18), channel_id=1, source_target_pairs={{0,2},{2,0},{6,4},{8,10},{12,14},{14,12},{18,16},{20,22},{22,20},{... | collective-permute-start | bytes 393224 | tf_op jit(solution)/shard_map/ppermute | solution.py:451
  76.4 3.7 %collective-permute-start.17 = (bf16[4,1,128,128]{3,2,1,0:T(8,128)(2,1)S(1)}, bf16[4,1,128,128]{3,2,1,0:T(8,128)(2,1)S(1)}, u32[]{:S(2)}, u32[]{:S(2)}) collective-permute-start(bf16[4,1,128,128]{3,2,1,0:T(8,128)(2,1)S(1)} %get-tuple-element.113), channel_id=1, source_target_pairs={{2,4},{4,2},{6,0},{8,14},{10,12},{12,10},{16,22},{18,20},{22,16},{... | collective-permute-start | bytes 393224 | tf_op jit(solution)/shard_map/ppermute | solution.py:451
  87.5 13.8 %forward.1 = (bf16[2048,128]{1,0:T(8,128)(2,1)S(1)}, f32[2048,128]{1,0:T(8,128)S(1)}) custom-call(s32[16]{0:T(128)S(1)} %get-tuple-element.160.full_ref, s32[16]{0:T(128)S(1)} %get-tuple-element.156.kcnt_ref, s32[16,10]{1,0:T(8,128)S(1)} %copy.11.kidx_ref, bf16[2048,128]{1,0:T(8,128)(2,1)S(1)} %copy-done.13, bf16[2,2048,128]{2,1,0:T(8,128)(2,1)S(1)} %copy-done.10, ...), custom_call_target="tpu_custom_call" | custom-call | flops 16000000000 | bytes 5242880 | tf_op jit(solution)/shard_map/forward/pallas_call | solution.py:498
  105.5 4.4 %collective-permute-start.21 = (bf16[2048,128]{1,0:T(8,128)(2,1)S(1)}, bf16[2048,128]{1,0:T(8,128)(2,1)S(1)}, u32[]{:S(2)}, u32[]{:S(2)}) collective-permute-start(bf16[2048,128]{1,0:T(8,128)(2,1)S(1)} %get-tuple-element.124.refs_0_.o_ref.attn_ref), channel_id=1, source_target_pairs={{0,6},{2,4},{4,2},{10,12},{12,10},{14,8},{16,22},{20,18},{22,16},{... | collective-permute-start | bytes 1572872 | tf_op jit(solution)/shard_map/ppermute | solution.py:514
  109.9 5.7 %collective-permute-done.19.refs_1_ = bf16[2048,128]{1,0:T(8,128)(2,1)S(1)} collective-permute-done((bf16[2048,128]{1,0:T(8,128)(2,1)S(1)}, bf16[2048,128]{1,0:T(8,128)(2,1)S(1)}, u32[]{:S(2)}, u32[]{:S(2)}) %collective-permute-start.19) | collective-permute-done | bytes 524320 | tf_op jit(solution)/shard_map/ppermute | solution.py:514
  115.6 12.1 %collective-permute-done.20.refs_2_ = bf16[2048,128]{1,0:T(8,128)(2,1)S(1)} collective-permute-done((bf16[2048,128]{1,0:T(8,128)(2,1)S(1)}, bf16[2048,128]{1,0:T(8,128)(2,1)S(1)}, u32[]{:S(2)}, u32[]{:S(2)}) %collective-permute-start.20) | collective-permute-done | bytes 524320 | tf_op jit(solution)/shard_map/ppermute | solution.py:514
  127.7 21.1 %backward.1 = (bf16[2048,128]{1,0:T(8,128)(2,1)S(1)}, bf16[2,2048,128]{2,1,0:T(8,128)(2,1)S(1)}, bf16[2,2048,128]{2,1,0:T(8,128)(2,1)}) custom-call(s32[16]{0:T(128)S(1)} %get-tuple-element.160.full_ref, s32[16]{0:T(128)S(1)} %get-tuple-element.156.kcnt_ref, s32[16,10]{1,0:T(8,128)S(1)} %copy.11.kidx_ref, bf16[2048,128]{1,0:T(8,128)(2,1)S(1)} %copy-done.13, ...), custom_call_target="tpu_custom_call" | custom-call | flops 20000000000 | bytes 8388608 | tf_op jit(solution)/shard_map/backward/pallas_call | solution.py:518
  151.8 4.8 %tile.1 = (f32[384,768]{1,0:T(8,128)S(1)}, bf16[384,768]{1,0:T(8,128)(2,1)S(1)}) custom-call(s32[2]{0:T(128)S(1)} %pad_add_fusion.where_ref, bf16[2048,128]{1,0:T(8,128)(2,1)S(1)} %get-tuple-element.124.refs_0_.o_ref.attn_ref, bf16[2048,128]{1,0:T(8,128)(2,1)S(1)} %collective-permute-done.19.refs_1_, bf16[2048,128]{1,0:T(8,128)(2,1)S(1)} %copy-done.15, ...), custom_call_target="tpu_custom_call" | custom-call | flops 5000000000 | bytes 4194304 | tf_op jit(solution)/shard_map/tile/pallas_call | solution.py:549
  168.5 3.7 %collective-permute-start.27 = (bf16[4,4,128,128]{3,2,1,0:T(8,128)(2,1)}, bf16[4,4,128,128]{3,2,1,0:T(8,128)(2,1)S(1)}, u32[]{:S(2)}, u32[]{:S(2)}) collective-permute-start(bf16[4,4,128,128]{3,2,1,0:T(8,128)(2,1)} %get-tuple-element.133), channel_id=1, source_target_pairs={{0,6},{2,4},{4,2},{10,12},{12,10},{14,8},{16,22},{20,18},{22,16},{... | collective-permute-start | bytes 1572872 | tf_op jit(solution)/shard_map/ppermute | solution.py:451
  173.9 7.2 %collective-permute-done.26.refs_2_ = bf16[4,4,128,128]{3,2,1,0:T(8,128)(2,1)S(1)} collective-permute-done((bf16[4,4,128,128]{3,2,1,0:T(8,128)(2,1)}, bf16[4,4,128,128]{3,2,1,0:T(8,128)(2,1)S(1)}, u32[]{:S(2)}, u32[]{:S(2)}) %collective-permute-start.26) | collective-permute-done | bytes 524320 | tf_op jit(solution)/shard_map/ppermute | solution.py:451
  181.1 9.3 %collective-permute-done.27.refs_3_ = bf16[4,4,128,128]{3,2,1,0:T(8,128)(2,1)S(1)} collective-permute-done((bf16[4,4,128,128]{3,2,1,0:T(8,128)(2,1)}, bf16[4,4,128,128]{3,2,1,0:T(8,128)(2,1)S(1)}, u32[]{:S(2)}, u32[]{:S(2)}) %collective-permute-start.27) | collective-permute-done | bytes 524320 | tf_op jit(solution)/shard_map/ppermute | solution.py:451
  196.9 3.1 %collective-permute-start.32 = (bf16[3,4,128,128]{3,2,1,0:T(8,128)(2,1)S(1)}, bf16[3,4,128,128]{3,2,1,0:T(8,128)(2,1)S(1)}, u32[]{:S(2)}, u32[]{:S(2)}) collective-permute-start(bf16[3,4,128,128]{3,2,1,0:T(8,128)(2,1)S(1)} %get-tuple-element.141), channel_id=1, source_target_pairs={{0,16},{2,18},{4,20},{6,22},{8,24},{10,26},{12,28},{14,30},{16,0},... | collective-permute-start | bytes 1179656 | tf_op jit(solution)/shard_map/ppermute | solution.py:446
  200.9 12.3 %collective-permute-start.33 = (bf16[3,4,128,128]{3,2,1,0:T(8,128)(2,1)S(1)}, bf16[3,4,128,128]{3,2,1,0:T(8,128)(2,1)S(1)}, u32[]{:S(2)}, u32[]{:S(2)}) collective-permute-start(bf16[3,4,128,128]{3,2,1,0:T(8,128)(2,1)S(1)} %get-tuple-element.142), channel_id=1, source_target_pairs={{0,24},{2,26},{4,28},{6,30},{8,16},{10,18},{12,20},{14,22},{16,8},... | collective-permute-start | bytes 1179656 | tf_op jit(solution)/shard_map/ppermute | solution.py:446
  213.1 13.8 %collective-permute-done.32.refs_2_ = bf16[3,4,128,128]{3,2,1,0:T(8,128)(2,1)S(1)} collective-permute-done((bf16[3,4,128,128]{3,2,1,0:T(8,128)(2,1)S(1)}, bf16[3,4,128,128]{3,2,1,0:T(8,128)(2,1)S(1)}, u32[]{:S(2)}, u32[]{:S(2)}) %collective-permute-start.32) | collective-permute-done | bytes 393248 | tf_op jit(solution)/shard_map/ppermute | solution.py:446
  227.0 10.3 %collective-permute-done.33.refs_3_ = bf16[3,4,128,128]{3,2,1,0:T(8,128)(2,1)S(1)} collective-permute-done((bf16[3,4,128,128]{3,2,1,0:T(8,128)(2,1)S(1)}, bf16[3,4,128,128]{3,2,1,0:T(8,128)(2,1)S(1)}, u32[]{:S(2)}, u32[]{:S(2)}) %collective-permute-start.33) | collective-permute-done | bytes 393248 | tf_op jit(solution)/shard_map/ppermute | solution.py:446
  249.6 3.8 %fusion.8 = f32[256,3072]{1,0:T(8,128)S(1)} fusion(bf16[256,768]{1,0:T(8,128)(2,1)S(1)} %get-tuple-element.149, bf16[768,3072]{1,0:T(8,128)(2,1)} %param.11), kind=kOutput, calls=%fused_computation.56 | convolution fusion | flops 1207959552 | bytes 8257536 | tf_op jit(solution)/shard_map/dot_general | solution.py:27
  261.9 4.5 %collective-permute-done.36.refs_3_ = bf16[192,768]{1,0:T(8,128)(2,1)} collective-permute-done((bf16[192,768]{1,0:T(8,128)(2,1)}, bf16[192,768]{1,0:T(8,128)(2,1)}, u32[]{:S(2)}, u32[]{:S(2)}) %collective-permute-start.36) | collective-permute-done | bytes 294944 | tf_op jit(solution)/shard_map/ppermute | solution.py:339
  266.5 6.2 %collective-permute-done.40.refs_8_ = bf16[192,768]{1,0:T(8,128)(2,1)} collective-permute-done((bf16[192,768]{1,0:T(8,128)(2,1)}, bf16[192,768]{1,0:T(8,128)(2,1)}, u32[]{:S(2)}, u32[]{:S(2)}) %collective-permute-start.40) | collective-permute-done | bytes 294944 | tf_op jit(solution)/shard_map/ppermute | solution.py:339
  272.9 6.7 %place.1 = f32[768,3072]{1,0:T(8,128)} custom-call(s32[2]{0:T(128)S(1)} %pad_add_fusion.2.place_ref, bf16[384,768]{1,0:T(8,128)(2,1)S(1)} %broadcast_select_fusion.2.refs_0_, bf16[384,768]{1,0:T(8,128)(2,1)S(1)} %collective-permute-done.29.refs_1_, bf16[384,768]{1,0:T(8,128)(2,1)S(1)} %collective-permute-done.30.refs_2_, ...), custom_call_target="tpu_custom_call" | custom-call | bytes 16777216 | tf_op jit(solution)/shard_map/place/pallas_call | solution.py:351
  (155 shorter events, 93.8 us)
Async XLA Ops:
  7.2 142.5 %all-gather.3.cloned.1.call-start = ((), (), s32[]{:S(2)}) async-start(), calls=%async_computation | async-start | bytes 3932160 | tf_op jit(solution)/shard_map/all_gather | solution.py:477
  14.2 20.8 %collective-permute-start.2 = (bf16[3,3,128,128]{3,2,1,0:T(8,128)(2,1)S(1)}, bf16[3,3,128,128]{3,2,1,0:T(8,128)(2,1)S(1)}, u32[]{:S(2)}, u32[]{:S(2)}) collective-permute-start(bf16[3,3,128,128]{3,2,1,0:T(8,128)(2,1)S(1)} %get-tuple-element.83), channel_id=1, source_target_pairs={{0,16},{2,18},{4,20},{6,22},{8,24},{10,26},{12,28},{14,30},{16,0},... | collective-permute-start | bytes 884744 | tf_op jit(solution)/shard_map/ppermute | solution.py:446
  16.5 25.9 %collective-permute-start.3 = (bf16[3,3,128,128]{3,2,1,0:T(8,128)(2,1)S(1)}, bf16[3,3,128,128]{3,2,1,0:T(8,128)(2,1)S(1)}, u32[]{:S(2)}, u32[]{:S(2)}) collective-permute-start(bf16[3,3,128,128]{3,2,1,0:T(8,128)(2,1)S(1)} %get-tuple-element.84), channel_id=1, source_target_pairs={{0,24},{2,26},{4,28},{6,30},{8,16},{10,18},{12,20},{14,22},{16,8},... | collective-permute-start | bytes 884744 | tf_op jit(solution)/shard_map/ppermute | solution.py:446
  18.3 24.8 %collective-permute-start.8 = (bf16[1,128,768]{2,1,0:T(8,128)(2,1)S(1)}, bf16[1,128,768]{2,1,0:T(8,128)(2,1)S(1)}, u32[]{:S(2)}, u32[]{:S(2)}) collective-permute-start(bf16[1,128,768]{2,1,0:T(8,128)(2,1)S(1)} %dynamic-slice_bitcast_fusion), channel_id=1, source_target_pairs={{0,1},{1,0},{2,3},{3,2},{4,5},{5,4},{6,7},{7,6},{8,9},{9,8},{10,11... | collective-permute-start | bytes 589832 | tf_op jit(solution)/shard_map/ppermute | solution.py:418
  20.4 23.3 %collective-permute-start.5 = (bf16[128,768]{1,0:T(8,128)(2,1)S(1)}, bf16[128,768]{1,0:T(8,128)(2,1)S(1)}, u32[]{:S(2)}, u32[]{:S(2)}) collective-permute-start(bf16[128,768]{1,0:T(8,128)(2,1)S(1)} %get-tuple-element.164), channel_id=1, source_target_pairs={{0,2},{2,0},{4,6},{6,4},{8,10},{10,8},{12,14},{14,12},{16,18},{18,... | collective-permute-start | bytes 589832 | tf_op jit(solution)/shard_map/ppermute | solution.py:440
  26.3 17.4 %collective-permute-start.6 = (bf16[128,768]{1,0:T(8,128)(2,1)S(1)}, bf16[128,768]{1,0:T(8,128)(2,1)S(1)}, u32[]{:S(2)}, u32[]{:S(2)}) collective-permute-start(bf16[128,768]{1,0:T(8,128)(2,1)S(1)} %get-tuple-element.165), channel_id=1, source_target_pairs={{0,4},{2,6},{4,0},{6,2},{8,12},{10,14},{12,8},{14,10},{16,20},{18,... | collective-permute-start | bytes 589832 | tf_op jit(solution)/shard_map/ppermute | solution.py:440
  45.2 20.3 %collective-permute-start.10 = (bf16[4,3,128,128]{3,2,1,0:T(8,128)(2,1)S(1)}, bf16[4,3,128,128]{3,2,1,0:T(8,128)(2,1)S(1)}, u32[]{:S(2)}, u32[]{:S(2)}) collective-permute-start(bf16[4,3,128,128]{3,2,1,0:T(8,128)(2,1)S(1)} %get-tuple-element.95), channel_id=1, source_target_pairs={{0,4},{4,0},{6,2},{8,12},{10,14},{14,10},{16,20},{18,22},{20,16},{... | collective-permute-start | bytes 1179656 | tf_op jit(solution)/shard_map/ppermute | solution.py:451
  46.5 19.1 %collective-permute-start.11 = (bf16[4,3,128,128]{3,2,1,0:T(8,128)(2,1)S(1)}, bf16[4,3,128,128]{3,2,1,0:T(8,128)(2,1)S(1)}, u32[]{:S(2)}, u32[]{:S(2)}) collective-permute-start(bf16[4,3,128,128]{3,2,1,0:T(8,128)(2,1)S(1)} %get-tuple-element.96), channel_id=1, source_target_pairs={{2,4},{4,2},{6,0},{8,14},{10,12},{12,10},{16,22},{18,20},{22,16},{... | collective-permute-start | bytes 1179656 | tf_op jit(solution)/shard_map/ppermute | solution.py:451
  51.4 15.4 %collective-permute-start.9 = (bf16[4,3,128,128]{3,2,1,0:T(8,128)(2,1)S(1)}, bf16[4,3,128,128]{3,2,1,0:T(8,128)(2,1)S(1)}, u32[]{:S(2)}, u32[]{:S(2)}) collective-permute-start(bf16[4,3,128,128]{3,2,1,0:T(8,128)(2,1)S(1)} %get-tuple-element.94), channel_id=1, source_target_pairs={{0,2},{2,0},{6,4},{8,10},{12,14},{14,12},{18,16},{20,22},{22,20},{... | collective-permute-start | bytes 1179656 | tf_op jit(solution)/shard_map/ppermute | solution.py:451
  68.3 16.5 %collective-permute-start.18 = (bf16[2,2048,128]{2,1,0:T(8,128)(2,1)S(1)}, bf16[2,2048,128]{2,1,0:T(8,128)(2,1)S(1)}, u32[]{:S(2)}, u32[]{:S(2)}) collective-permute-start(bf16[2,2048,128]{2,1,0:T(8,128)(2,1)S(1)} %get-tuple-element.115.refs_0_.refs_1_), channel_id=1, source_target_pairs={{0,1},{1,0},{2,3},{3,2},{4,5},{5,4},{6,7},{7,6},{8,9},{9,8},{10,11... | collective-permute-start | bytes 3145736 | tf_op jit(solution)/shard_map/ppermute | solution.py:490
  101.3 14.3 %collective-permute-start.19 = (bf16[2048,128]{1,0:T(8,128)(2,1)S(1)}, bf16[2048,128]{1,0:T(8,128)(2,1)S(1)}, u32[]{:S(2)}, u32[]{:S(2)}) collective-permute-start(bf16[2048,128]{1,0:T(8,128)(2,1)S(1)} %get-tuple-element.124.refs_0_.o_ref.attn_ref), channel_id=1, source_target_pairs={{0,2},{2,0},{4,6},{10,8},{12,14},{14,12},{16,18},{20,22},{22,20},{... | collective-permute-start | bytes 1572872 | tf_op jit(solution)/shard_map/ppermute | solution.py:514
  104.2 23.6 %collective-permute-start.20 = (bf16[2048,128]{1,0:T(8,128)(2,1)S(1)}, bf16[2048,128]{1,0:T(8,128)(2,1)S(1)}, u32[]{:S(2)}, u32[]{:S(2)}) collective-permute-start(bf16[2048,128]{1,0:T(8,128)(2,1)S(1)} %get-tuple-element.124.refs_0_.o_ref.attn_ref), channel_id=1, source_target_pairs={{0,4},{2,6},{4,0},{10,14},{12,8},{14,10},{16,20},{20,16},{22,18},{... | collective-permute-start | bytes 1572872 | tf_op jit(solution)/shard_map/ppermute | solution.py:514
  105.5 22.2 %collective-permute-start.21 = (bf16[2048,128]{1,0:T(8,128)(2,1)S(1)}, bf16[2048,128]{1,0:T(8,128)(2,1)S(1)}, u32[]{:S(2)}, u32[]{:S(2)}) collective-permute-start(bf16[2048,128]{1,0:T(8,128)(2,1)S(1)} %get-tuple-element.124.refs_0_.o_ref.attn_ref), channel_id=1, source_target_pairs={{0,6},{2,4},{4,2},{10,12},{12,10},{14,8},{16,22},{20,18},{22,16},{... | collective-permute-start | bytes 1572872 | tf_op jit(solution)/shard_map/ppermute | solution.py:514
  159.7 31.5 %collective-permute-start.23 = (bf16[384,768]{1,0:T(8,128)(2,1)}, bf16[384,768]{1,0:T(8,128)(2,1)}, u32[]{:S(2)}, u32[]{:S(2)}) collective-permute-start(bf16[384,768]{1,0:T(8,128)(2,1)} %add_convert_fusion.1), channel_id=1, source_target_pairs={{0,16},{2,18},{4,20},{6,22},{8,24},{10,26},{12,28},{14,30},{17,1},... | collective-permute-start | bytes 1769480 | tf_op jit(solution)/shard_map/ppermute | solution.py:336
  165.9 15.3 %collective-permute-start.26 = (bf16[4,4,128,128]{3,2,1,0:T(8,128)(2,1)}, bf16[4,4,128,128]{3,2,1,0:T(8,128)(2,1)S(1)}, u32[]{:S(2)}, u32[]{:S(2)}) collective-permute-start(bf16[4,4,128,128]{3,2,1,0:T(8,128)(2,1)} %get-tuple-element.132), channel_id=1, source_target_pairs={{0,4},{2,6},{4,0},{10,14},{12,8},{14,10},{16,20},{20,16},{22,18},{... | collective-permute-start | bytes 1572872 | tf_op jit(solution)/shard_map/ppermute | solution.py:451
  168.5 22.0 %collective-permute-start.27 = (bf16[4,4,128,128]{3,2,1,0:T(8,128)(2,1)}, bf16[4,4,128,128]{3,2,1,0:T(8,128)(2,1)S(1)}, u32[]{:S(2)}, u32[]{:S(2)}) collective-permute-start(bf16[4,4,128,128]{3,2,1,0:T(8,128)(2,1)} %get-tuple-element.133), channel_id=1, source_target_pairs={{0,6},{2,4},{4,2},{10,12},{12,10},{14,8},{16,22},{20,18},{22,16},{... | collective-permute-start | bytes 1572872 | tf_op jit(solution)/shard_map/ppermute | solution.py:451
  192.4 44.9 %collective-permute-start.28 = (bf16[384,768]{1,0:T(8,128)(2,1)S(1)}, bf16[384,768]{1,0:T(8,128)(2,1)S(1)}, u32[]{:S(2)}, u32[]{:S(2)}) collective-permute-start(bf16[384,768]{1,0:T(8,128)(2,1)S(1)} %broadcast_select_fusion.2.refs_0_), channel_id=1, source_target_pairs={{0,8},{2,10},{4,12},{6,14},{8,0},{10,2},{12,4},{14,6},{16,24},{18,... | collective-permute-start | bytes 1769480 | tf_op jit(solution)/shard_map/ppermute | solution.py:339
  193.9 43.4 %collective-permute-start.29 = (bf16[384,768]{1,0:T(8,128)(2,1)S(1)}, bf16[384,768]{1,0:T(8,128)(2,1)S(1)}, u32[]{:S(2)}, u32[]{:S(2)}) collective-permute-start(bf16[384,768]{1,0:T(8,128)(2,1)S(1)} %broadcast_select_fusion.2.refs_0_), channel_id=1, source_target_pairs={{0,2},{2,0},{4,6},{6,4},{8,10},{10,8},{12,14},{14,12},{16,18},{18,... | collective-permute-start | bytes 1769480 | tf_op jit(solution)/shard_map/ppermute | solution.py:339
  194.8 42.5 %collective-permute-start.30 = (bf16[384,768]{1,0:T(8,128)(2,1)S(1)}, bf16[384,768]{1,0:T(8,128)(2,1)S(1)}, u32[]{:S(2)}, u32[]{:S(2)}) collective-permute-start(bf16[384,768]{1,0:T(8,128)(2,1)S(1)} %broadcast_select_fusion.2.refs_0_), channel_id=1, source_target_pairs={{0,4},{2,6},{4,0},{6,2},{8,12},{10,14},{12,8},{14,10},{16,20},{18,... | collective-permute-start | bytes 1769480 | tf_op jit(solution)/shard_map/ppermute | solution.py:339
  196.9 30.1 %collective-permute-start.32 = (bf16[3,4,128,128]{3,2,1,0:T(8,128)(2,1)S(1)}, bf16[3,4,128,128]{3,2,1,0:T(8,128)(2,1)S(1)}, u32[]{:S(2)}, u32[]{:S(2)}) collective-permute-start(bf16[3,4,128,128]{3,2,1,0:T(8,128)(2,1)S(1)} %get-tuple-element.141), channel_id=1, source_target_pairs={{0,16},{2,18},{4,20},{6,22},{8,24},{10,26},{12,28},{14,30},{16,0},... | collective-permute-start | bytes 1179656 | tf_op jit(solution)/shard_map/ppermute | solution.py:446
  200.9 36.4 %collective-permute-start.33 = (bf16[3,4,128,128]{3,2,1,0:T(8,128)(2,1)S(1)}, bf16[3,4,128,128]{3,2,1,0:T(8,128)(2,1)S(1)}, u32[]{:S(2)}, u32[]{:S(2)}) collective-permute-start(bf16[3,4,128,128]{3,2,1,0:T(8,128)(2,1)S(1)} %get-tuple-element.142), channel_id=1, source_target_pairs={{0,24},{2,26},{4,28},{6,30},{8,16},{10,18},{12,20},{14,22},{16,8},... | collective-permute-start | bytes 1179656 | tf_op jit(solution)/shard_map/ppermute | solution.py:446
  242.6 16.5 %collective-permute-start.38 = (bf16[384,768]{1,0:T(8,128)(2,1)S(1)}, bf16[384,768]{1,0:T(8,128)(2,1)S(1)}, u32[]{:S(2)}, u32[]{:S(2)}) collective-permute-start(bf16[384,768]{1,0:T(8,128)(2,1)S(1)} %collective-permute-done.28.refs_5_), channel_id=1, source_target_pairs={{0,2},{2,0},{4,6},{6,4},{8,10},{10,8},{12,14},{14,12},{16,18},{18,... | collective-permute-start | bytes 1769480 | tf_op jit(solution)/shard_map/ppermute | solution.py:339
  245.5 15.2 %collective-permute-start.39 = (bf16[384,768]{1,0:T(8,128)(2,1)S(1)}, bf16[384,768]{1,0:T(8,128)(2,1)S(1)}, u32[]{:S(2)}, u32[]{:S(2)}) collective-permute-start(bf16[384,768]{1,0:T(8,128)(2,1)S(1)} %collective-permute-done.28.refs_5_), channel_id=1, source_target_pairs={{0,4},{2,6},{4,0},{6,2},{8,12},{10,14},{12,8},{14,10},{16,20},{18,... | collective-permute-start | bytes 1769480 | tf_op jit(solution)/shard_map/ppermute | solution.py:339
  254.5 25.1 %collective-permute-start.35 = (bf16[256,1536]{1,0:T(8,128)(2,1)}, bf16[256,1536]{1,0:T(8,128)(2,1)}, u32[]{:S(2)}, u32[]{:S(2)}) collective-permute-start(bf16[256,1536]{1,0:T(8,128)(2,1)} %dynamic-slice_convert_fusion), channel_id=1, source_target_pairs={{0,1},{1,0},{2,3},{3,2},{4,5},{5,4},{6,7},{7,6},{8,9},{9,8},{10,11... | collective-permute-start | bytes 2359304 | tf_op jit(solution)/shard_map/ppermute | solution.py:610
  (42 other events, 354.5 us)
Sparse Core Ops, SparseCore 0:
  70.9 60.7 all-gather.2

commit v10 on v9

--- a/solution.py
+++ b/solution.py
@@ -339,10 +339,10 @@
         return lax.ppermute(x, "ctx", [(i, i ^ k) for i in range(n)])
 
     first = jnp.where(plane // 2 == core, tile_sum, from_half)
-    first, *packs = lax.optimization_barrier((first, *packs))
     second = swap(first, in_plane)
     beside, above = swap(first, 1), swap(first, 2)
-    second, beside, above, *packs = lax.optimization_barrier((second, beside, above, *along_z(packs)))
+    second, beside, above, *packs = lax.optimization_barrier((second, beside, above, *packs))
+    packs = along_z(packs)
     middle = tile_rows // 2
     sources = [first, beside, above, swap(beside[:middle], 2), swap(above[middle:], 1)]
     beside, above = swap(second, 1), swap(second, 2)
@@ -513,8 +513,6 @@
     travel = [attn] + [
         lax.ppermute(attn, "ctx", [(i, i ^ k) for i in range(n) if held[i]]) for k in range(1, in_plane)
     ]
-    *travel, attn = lax.optimization_barrier((*travel, attn))
-
     dq, *dkv = pl.pallas_call(
         functools.partial(backward_kernel, t, tile, count),
         grid_spec=pltpu.PrefetchScalarGridSpec(
@@ -537,6 +535,8 @@
         functools.partial(unjoin_kernel, n, t), "unjoin", where,
         [attn, dq, dkv[0]] + got_dkv, [shape(PLANES, 4, sub, HEAD)] * in_plane,
     )
+    tied = lax.optimization_barrier((*travel, *back))
+    travel, back = list(tied[:in_plane]), list(tied[in_plane:])
     packs = simple_call(
         functools.partial(to_planes_kernel, n), "to_planes", where, in_the_plane(back, from_held),
         [shape(heads_plane, 4, sub, HEAD)] * PLANES,

time: 291 us -> 303 us (1.041)
  waiting for transfers between devices: 106 us -> 125 us
  starting transfers between devices: 80.7 us -> 74.6 us
    ppermute x9, starting transfers between devices: 22.5 us -> 9.79 us  [along_z(): lax.ppermute(packs[k], 'ctx', [(i, i ^ k * in_plane) for i in range(n)])]
    ppermute x9, waiting for transfers between devices: 22.8 us -> 32.1 us  [in_the_plane(): lax.ppermute(packs[m], 'ctx', pairs(m))]
    ppermute x9, waiting for transfers between devices: 50.1 us -> 59.1 us  [along_z(): lax.ppermute(packs[k], 'ctx', [(i, i ^ k * in_plane) for i in range(n)])]
    ppermute x1, waiting for transfers between devices: 0.01 us -> 5.78 us  [gather_tiles_by_core(): from_half = lax.ppermute(tile_sum, ('ctx', 'tp'), across)]
    ppermute x9, starting transfers between devices: 10.8 us -> 15.8 us  [swap(): return lax.ppermute(x, 'ctx', [(i, i ^ k) for i in range(n)])]
    ppermute x3, waiting for transfers between devices: 17.8 us -> 13.4 us  [per_device(): lax.ppermute(attn, 'ctx', [(i, i ^ k) for i in range(n) if held[i]])]
  transfers between devices with their start and end apart: 43 -> 43, of which waited for: 24 -> 21; matrix products, arithmetic and copies ran while one was open for 6% -> 5% of each run, Pallas kernels for 19% -> 17%
where the time goes in v10:
time: 303 us; the launch traced here: 301 us
  waiting for transfers between devices  125 us (41%)
  starting transfers between devices  74.6 us (25%)
  Pallas kernels  59.8 us (20%)
  local copies, waits for them, and re-layouts  16.8 us (6%)
  between operations  14.6 us (5%)
  other arithmetic  5.6 us (2%)
  matrix products  5.2 us (2%)
    ppermute x9, waiting for transfers between devices, along_z(): lax.ppermute(packs[k], 'ctx', [(i, i ^ k * in_plane) for i in range(n)])  59.1 us
    ppermute x9, waiting for transfers between devices, in_the_plane(): lax.ppermute(packs[m], 'ctx', pairs(m))  32.1 us
    ppermute x9, starting transfers between devices, in_the_plane(): lax.ppermute(packs[m], 'ctx', pairs(m))  28.2 us
    pallas_call x1, Pallas kernels, per_device(): pl.pallas_call(functools.partial(backward_kernel, t, tile, count), grid_s...  20.1 us
    ppermute x9, starting transfers between devices, swap(): return lax.ppermute(x, 'ctx', [(i, i ^ k) for i in range(n)])  15.8 us
    pallas_call x1, Pallas kernels, per_device(): pl.pallas_call(functools.partial(forward_kernel, t, tile, count), grid_sp...  15.2 us
    ppermute x3, waiting for transfers between devices, per_device(): lax.ppermute(attn, 'ctx', [(i, i ^ k) for i in range(n) if held[i]])  13.4 us
    pallas_call x11, Pallas kernels, simple_call(): pl.pallas_call(kernel, grid_spec=pltpu.PrefetchScalarGridSpec(num_scalar_...  12.9 us
  transfers between devices with their start and end apart: 43, of which 21 were waited for; matrix products, arithmetic and copies ran while one was open for 5% of the time, Pallas kernels for 17%

profile of v10, /device:TPU:13, one launch (start us, length us, event | category | flops | bytes accessed | tf_op | source)
XLA Modules:
  0.0 301.5 jit_solution(7413520602045452568)
XLA Ops:
  21.7 4.6 %collective-permute-done.1.refs_1_ = bf16[3,3,128,128]{3,2,1,0:T(8,128)(2,1)S(1)} collective-permute-done((bf16[3,3,128,128]{3,2,1,0:T(8,128)(2,1)S(1)}, bf16[3,3,128,128]{3,2,1,0:T(8,128)(2,1)S(1)}, u32[]{:S(2)}, u32[]{:S(2)}) %collective-permute-start.1) | collective-permute-done | bytes 294944 | tf_op jit(solution)/shard_map/ppermute | solution.py:446
  26.6 8.4 %collective-permute-done.2.refs_2_ = bf16[3,3,128,128]{3,2,1,0:T(8,128)(2,1)S(1)} collective-permute-done((bf16[3,3,128,128]{3,2,1,0:T(8,128)(2,1)S(1)}, bf16[3,3,128,128]{3,2,1,0:T(8,128)(2,1)S(1)}, u32[]{:S(2)}, u32[]{:S(2)}) %collective-permute-start.2) | collective-permute-done | bytes 294944 | tf_op jit(solution)/shard_map/ppermute | solution.py:446
  36.2 6.2 %collective-permute-done.3.refs_3_ = bf16[3,3,128,128]{3,2,1,0:T(8,128)(2,1)S(1)} collective-permute-done((bf16[3,3,128,128]{3,2,1,0:T(8,128)(2,1)S(1)}, bf16[3,3,128,128]{3,2,1,0:T(8,128)(2,1)S(1)}, u32[]{:S(2)}, u32[]{:S(2)}) %collective-permute-start.3) | collective-permute-done | bytes 294944 | tf_op jit(solution)/shard_map/ppermute | solution.py:446
  47.2 4.9 %collective-permute-start.11 = (bf16[4,3,128,128]{3,2,1,0:T(8,128)(2,1)S(1)}, bf16[4,3,128,128]{3,2,1,0:T(8,128)(2,1)S(1)}, u32[]{:S(2)}, u32[]{:S(2)}) collective-permute-start(bf16[4,3,128,128]{3,2,1,0:T(8,128)(2,1)S(1)} %get-tuple-element.94), channel_id=1, source_target_pairs={{2,4},{4,2},{6,0},{8,14},{10,12},{12,10},{16,22},{18,20},{22,16},{... | collective-permute-start | bytes 1179656 | tf_op jit(solution)/shard_map/ppermute | solution.py:451
  60.3 5.4 %collective-permute-done.14.refs_3_ = bf16[3,1,128,128]{3,2,1,0:T(8,128)(2,1)S(1)} collective-permute-done((bf16[3,1,128,128]{3,2,1,0:T(8,128)(2,1)S(1)}, bf16[3,1,128,128]{3,2,1,0:T(8,128)(2,1)S(1)}, u32[]{:S(2)}, u32[]{:S(2)}) %collective-permute-start.14) | collective-permute-done | bytes 98336 | tf_op jit(solution)/shard_map/ppermute | solution.py:446
  71.3 3.8 %collective-permute-start.15 = (bf16[4,1,128,128]{3,2,1,0:T(8,128)(2,1)}, bf16[4,1,128,128]{3,2,1,0:T(8,128)(2,1)S(1)}, u32[]{:S(2)}, u32[]{:S(2)}) collective-permute-start(bf16[4,1,128,128]{3,2,1,0:T(8,128)(2,1)} %copy-done.18), channel_id=1, source_target_pairs={{0,2},{2,0},{6,4},{8,10},{12,14},{14,12},{18,16},{20,22},{22,20},{... | collective-permute-start | bytes 393224 | tf_op jit(solution)/shard_map/ppermute | solution.py:451
  76.5 3.7 %collective-permute-start.17 = (bf16[4,1,128,128]{3,2,1,0:T(8,128)(2,1)S(1)}, bf16[4,1,128,128]{3,2,1,0:T(8,128)(2,1)S(1)}, u32[]{:S(2)}, u32[]{:S(2)}) collective-permute-start(bf16[4,1,128,128]{3,2,1,0:T(8,128)(2,1)S(1)} %copy-done.15), channel_id=1, source_target_pairs={{2,4},{4,2},{6,0},{8,14},{10,12},{12,10},{16,22},{18,20},{22,16},{... | collective-permute-start | bytes 393224 | tf_op jit(solution)/shard_map/ppermute | solution.py:451
  84.8 15.2 %forward.1 = (bf16[2048,128]{1,0:T(8,128)(2,1)S(1)}, f32[2048,128]{1,0:T(8,128)S(1)}) custom-call(s32[16]{0:T(128)S(1)} %get-tuple-element.156.full_ref, s32[16]{0:T(128)S(1)} %get-tuple-element.152.kcnt_ref, s32[16,10]{1,0:T(8,128)S(1)} %copy.11.kidx_ref, bf16[2048,128]{1,0:T(8,128)(2,1)S(1)} %get-tuple-element.112.q_ref, ...), custom_call_target="tpu_custom_call" | custom-call | flops 16000000000 | bytes 5242880 | tf_op jit(solution)/shard_map/forward/pallas_call | solution.py:498
  100.0 20.1 %backward.1 = (bf16[2048,128]{1,0:T(8,128)(2,1)S(1)}, bf16[2,2048,128]{2,1,0:T(8,128)(2,1)S(1)}, bf16[2,2048,128]{2,1,0:T(8,128)(2,1)S(1)}) custom-call(s32[16]{0:T(128)S(1)} %get-tuple-element.156.full_ref, s32[16]{0:T(128)S(1)} %get-tuple-element.152.kcnt_ref, s32[16,10]{1,0:T(8,128)S(1)} %copy.11.kidx_ref, ...), custom_call_target="tpu_custom_call" | custom-call | flops 20000000000 | bytes 8388608 | tf_op jit(solution)/shard_map/backward/pallas_call | solution.py:516
  125.0 5.3 %collective-permute-start.21 = (bf16[2048,128]{1,0:T(8,128)(2,1)S(1)}, bf16[2048,128]{1,0:T(8,128)(2,1)S(1)}, u32[]{:S(2)}, u32[]{:S(2)}) collective-permute-start(bf16[2048,128]{1,0:T(8,128)(2,1)S(1)} %get-tuple-element.124.o_ref.attn_ref.refs_0_), channel_id=1, source_target_pairs={{0,6},{2,4},{4,2},{10,12},{12,10},{14,8},{16,22},{20,18},{22,16},{... | collective-permute-start | bytes 1572872 | tf_op jit(solution)/shard_map/ppermute | solution.py:514
  133.5 3.7 %collective-permute-done.19.refs_1_ = bf16[2048,128]{1,0:T(8,128)(2,1)S(1)} collective-permute-done((bf16[2048,128]{1,0:T(8,128)(2,1)S(1)}, bf16[2048,128]{1,0:T(8,128)(2,1)S(1)}, u32[]{:S(2)}, u32[]{:S(2)}) %collective-permute-start.19) | collective-permute-done | bytes 524320 | tf_op jit(solution)/shard_map/ppermute | solution.py:514
  138.0 9.6 %collective-permute-done.21.refs_3_ = bf16[2048,128]{1,0:T(8,128)(2,1)S(1)} collective-permute-done((bf16[2048,128]{1,0:T(8,128)(2,1)S(1)}, bf16[2048,128]{1,0:T(8,128)(2,1)S(1)}, u32[]{:S(2)}, u32[]{:S(2)}) %collective-permute-start.21) | collective-permute-done | bytes 524320 | tf_op jit(solution)/shard_map/ppermute | solution.py:514
  150.5 4.8 %tile.1 = (f32[384,768]{1,0:T(8,128)S(1)}, bf16[384,768]{1,0:T(8,128)(2,1)S(1)}) custom-call(s32[2]{0:T(128)S(1)} %pad_add_fusion.where_ref, bf16[2048,128]{1,0:T(8,128)(2,1)S(1)} %get-tuple-element.124.o_ref.attn_ref.refs_0_, bf16[2048,128]{1,0:T(8,128)(2,1)S(1)} %collective-permute-done.19.refs_1_, bf16[2048,128]{1,0:T(8,128)(2,1)S(1)} %copy-done.11, ...), custom_call_target="tpu_custom_call" | custom-call | flops 5000000000 | bytes 4194304 | tf_op jit(solution)/shard_map/tile/pallas_call | solution.py:549
  159.2 4.8 %collective-permute-start.28 = (bf16[4,4,128,128]{3,2,1,0:T(8,128)(2,1)}, bf16[4,4,128,128]{3,2,1,0:T(8,128)(2,1)S(1)}, u32[]{:S(2)}, u32[]{:S(2)}) collective-permute-start(bf16[4,4,128,128]{3,2,1,0:T(8,128)(2,1)} %get-tuple-element.132), channel_id=1, source_target_pairs={{0,2},{2,0},{4,6},{10,8},{12,14},{14,12},{16,18},{20,22},{22,20},{... | collective-permute-start | bytes 1572872 | tf_op jit(solution)/shard_map/ppermute | solution.py:451
  164.1 5.8 %collective-permute-done.24 = bf16[384,768]{1,0:T(8,128)(2,1)S(1)} collective-permute-done((bf16[384,768]{1,0:T(8,128)(2,1)S(1)}, bf16[384,768]{1,0:T(8,128)(2,1)S(1)}, u32[]{:S(2)}, u32[]{:S(2)}) %collective-permute-start.24) | collective-permute-done | bytes 589856 | tf_op jit(solution)/shard_map/ppermute | solution.py:336
  169.9 7.5 %collective-permute-start.25 = (bf16[384,768]{1,0:T(8,128)(2,1)S(1)}, bf16[384,768]{1,0:T(8,128)(2,1)S(1)}, u32[]{:S(2)}, u32[]{:S(2)}) collective-permute-start(bf16[384,768]{1,0:T(8,128)(2,1)S(1)} %broadcast_select_fusion.2.refs_0_), channel_id=1, source_target_pairs={{0,8},{2,10},{4,12},{6,14},{8,0},{10,2},{12,4},{14,6},{16,24},{18,... | collective-permute-start | bytes 1769480 | tf_op jit(solution)/shard_map/ppermute | solution.py:339
  181.8 3.9 %collective-permute-start.30 = (bf16[4,4,128,128]{3,2,1,0:T(8,128)(2,1)}, bf16[4,4,128,128]{3,2,1,0:T(8,128)(2,1)S(1)}, u32[]{:S(2)}, u32[]{:S(2)}) collective-permute-start(bf16[4,4,128,128]{3,2,1,0:T(8,128)(2,1)} %copy-done.8), channel_id=1, source_target_pairs={{0,6},{2,4},{4,2},{10,12},{12,10},{14,8},{16,22},{20,18},{22,16},{... | collective-permute-start | bytes 1572872 | tf_op jit(solution)/shard_map/ppermute | solution.py:451
  185.8 28.8 %collective-permute-done.29.refs_2_ = bf16[4,4,128,128]{3,2,1,0:T(8,128)(2,1)S(1)} collective-permute-done((bf16[4,4,128,128]{3,2,1,0:T(8,128)(2,1)}, bf16[4,4,128,128]{3,2,1,0:T(8,128)(2,1)S(1)}, u32[]{:S(2)}, u32[]{:S(2)}) %collective-permute-start.29) | collective-permute-done | bytes 524320 | tf_op jit(solution)/shard_map/ppermute | solution.py:451
  218.0 7.7 %collective-permute-done.31.refs_1_ = bf16[3,4,128,128]{3,2,1,0:T(8,128)(2,1)S(1)} collective-permute-done((bf16[3,4,128,128]{3,2,1,0:T(8,128)(2,1)S(1)}, bf16[3,4,128,128]{3,2,1,0:T(8,128)(2,1)S(1)}, u32[]{:S(2)}, u32[]{:S(2)}) %collective-permute-start.31) | collective-permute-done | bytes 393248 | tf_op jit(solution)/shard_map/ppermute | solution.py:446
  227.7 24.4 %collective-permute-done.33.refs_3_ = bf16[3,4,128,128]{3,2,1,0:T(8,128)(2,1)S(1)} collective-permute-done((bf16[3,4,128,128]{3,2,1,0:T(8,128)(2,1)S(1)}, bf16[3,4,128,128]{3,2,1,0:T(8,128)(2,1)S(1)}, u32[]{:S(2)}, u32[]{:S(2)}) %collective-permute-start.33) | collective-permute-done | bytes 393248 | tf_op jit(solution)/shard_map/ppermute | solution.py:446
  262.4 3.8 %fusion.8 = f32[256,3072]{1,0:T(8,128)S(1)} fusion(bf16[256,768]{1,0:T(8,128)(2,1)S(1)} %get-tuple-element.145, bf16[768,3072]{1,0:T(8,128)(2,1)} %param.11), kind=kOutput, calls=%fused_computation.56 | convolution fusion | flops 1207959552 | bytes 8257536 | tf_op jit(solution)/shard_map/dot_general | solution.py:27
  274.9 3.4 %collective-permute-done.36.refs_3_ = bf16[192,768]{1,0:T(8,128)(2,1)} collective-permute-done((bf16[192,768]{1,0:T(8,128)(2,1)}, bf16[192,768]{1,0:T(8,128)(2,1)}, u32[]{:S(2)}, u32[]{:S(2)}) %collective-permute-start.36) | collective-permute-done | bytes 294944 | tf_op jit(solution)/shard_map/ppermute | solution.py:339
  279.4 5.2 %collective-permute-done.40.refs_8_ = bf16[192,768]{1,0:T(8,128)(2,1)} collective-permute-done((bf16[192,768]{1,0:T(8,128)(2,1)}, bf16[192,768]{1,0:T(8,128)(2,1)}, u32[]{:S(2)}, u32[]{:S(2)}) %collective-permute-start.40) | collective-permute-done | bytes 294944 | tf_op jit(solution)/shard_map/ppermute | solution.py:339
  285.7 6.7 %place.1 = f32[768,3072]{1,0:T(8,128)} custom-call(s32[2]{0:T(128)S(1)} %pad_add_fusion.2.place_ref, bf16[384,768]{1,0:T(8,128)(2,1)S(1)} %broadcast_select_fusion.2.refs_0_, bf16[384,768]{1,0:T(8,128)(2,1)S(1)} %collective-permute-done.26.refs_1_, bf16[384,768]{1,0:T(8,128)(2,1)S(1)} %collective-permute-done.27.refs_2_, ...), custom_call_target="tpu_custom_call" | custom-call | bytes 16777216 | tf_op jit(solution)/shard_map/place/pallas_call | solution.py:351
  (155 shorter events, 89.1 us)
Async XLA Ops:
  7.2 141.2 %all-gather.3.cloned.1.call-start = ((), (), s32[]{:S(2)}) async-start(), calls=%async_computation | async-start | bytes 3932160 | tf_op jit(solution)/shard_map/all_gather | solution.py:477
  14.2 20.8 %collective-permute-start.2 = (bf16[3,3,128,128]{3,2,1,0:T(8,128)(2,1)S(1)}, bf16[3,3,128,128]{3,2,1,0:T(8,128)(2,1)S(1)}, u32[]{:S(2)}, u32[]{:S(2)}) collective-permute-start(bf16[3,3,128,128]{3,2,1,0:T(8,128)(2,1)S(1)} %get-tuple-element.81), channel_id=1, source_target_pairs={{0,16},{2,18},{4,20},{6,22},{8,24},{10,26},{12,28},{14,30},{16,0},... | collective-permute-start | bytes 884744 | tf_op jit(solution)/shard_map/ppermute | solution.py:446
  16.5 25.9 %collective-permute-start.3 = (bf16[3,3,128,128]{3,2,1,0:T(8,128)(2,1)S(1)}, bf16[3,3,128,128]{3,2,1,0:T(8,128)(2,1)S(1)}, u32[]{:S(2)}, u32[]{:S(2)}) collective-permute-start(bf16[3,3,128,128]{3,2,1,0:T(8,128)(2,1)S(1)} %get-tuple-element.82), channel_id=1, source_target_pairs={{0,24},{2,26},{4,28},{6,30},{8,16},{10,18},{12,20},{14,22},{16,8},... | collective-permute-start | bytes 884744 | tf_op jit(solution)/shard_map/ppermute | solution.py:446
  18.3 25.5 %collective-permute-start.8 = (bf16[1,128,768]{2,1,0:T(8,128)(2,1)S(1)}, bf16[1,128,768]{2,1,0:T(8,128)(2,1)S(1)}, u32[]{:S(2)}, u32[]{:S(2)}) collective-permute-start(bf16[1,128,768]{2,1,0:T(8,128)(2,1)S(1)} %dynamic-slice_bitcast_fusion), channel_id=1, source_target_pairs={{0,1},{1,0},{2,3},{3,2},{4,5},{5,4},{6,7},{7,6},{8,9},{9,8},{10,11... | collective-permute-start | bytes 589832 | tf_op jit(solution)/shard_map/ppermute | solution.py:418
  20.4 24.0 %collective-permute-start.5 = (bf16[128,768]{1,0:T(8,128)(2,1)S(1)}, bf16[128,768]{1,0:T(8,128)(2,1)S(1)}, u32[]{:S(2)}, u32[]{:S(2)}) collective-permute-start(bf16[128,768]{1,0:T(8,128)(2,1)S(1)} %get-tuple-element.160), channel_id=1, source_target_pairs={{0,2},{2,0},{4,6},{6,4},{8,10},{10,8},{12,14},{14,12},{16,18},{18,... | collective-permute-start | bytes 589832 | tf_op jit(solution)/shard_map/ppermute | solution.py:440
  26.3 18.1 %collective-permute-start.6 = (bf16[128,768]{1,0:T(8,128)(2,1)S(1)}, bf16[128,768]{1,0:T(8,128)(2,1)S(1)}, u32[]{:S(2)}, u32[]{:S(2)}) collective-permute-start(bf16[128,768]{1,0:T(8,128)(2,1)S(1)} %get-tuple-element.161), channel_id=1, source_target_pairs={{0,4},{2,6},{4,0},{6,2},{8,12},{10,14},{12,8},{14,10},{16,20},{18,... | collective-permute-start | bytes 589832 | tf_op jit(solution)/shard_map/ppermute | solution.py:440
  46.0 22.3 %collective-permute-start.10 = (bf16[4,3,128,128]{3,2,1,0:T(8,128)(2,1)}, bf16[4,3,128,128]{3,2,1,0:T(8,128)(2,1)S(1)}, u32[]{:S(2)}, u32[]{:S(2)}) collective-permute-start(bf16[4,3,128,128]{3,2,1,0:T(8,128)(2,1)} %get-tuple-element.93), channel_id=1, source_target_pairs={{0,4},{4,0},{6,2},{8,12},{10,14},{14,10},{16,20},{18,22},{20,16},{... | collective-permute-start | bytes 1179656 | tf_op jit(solution)/shard_map/ppermute | solution.py:451
  47.2 21.0 %collective-permute-start.11 = (bf16[4,3,128,128]{3,2,1,0:T(8,128)(2,1)S(1)}, bf16[4,3,128,128]{3,2,1,0:T(8,128)(2,1)S(1)}, u32[]{:S(2)}, u32[]{:S(2)}) collective-permute-start(bf16[4,3,128,128]{3,2,1,0:T(8,128)(2,1)S(1)} %get-tuple-element.94), channel_id=1, source_target_pairs={{2,4},{4,2},{6,0},{8,14},{10,12},{12,10},{16,22},{18,20},{22,16},{... | collective-permute-start | bytes 1179656 | tf_op jit(solution)/shard_map/ppermute | solution.py:451
  52.2 16.1 %collective-permute-start.9 = (bf16[4,3,128,128]{3,2,1,0:T(8,128)(2,1)S(1)}, bf16[4,3,128,128]{3,2,1,0:T(8,128)(2,1)S(1)}, u32[]{:S(2)}, u32[]{:S(2)}) collective-permute-start(bf16[4,3,128,128]{3,2,1,0:T(8,128)(2,1)S(1)} %get-tuple-element.92), channel_id=1, source_target_pairs={{0,2},{2,0},{6,4},{8,10},{12,14},{14,12},{18,16},{20,22},{22,20},{... | collective-permute-start | bytes 1179656 | tf_op jit(solution)/shard_map/ppermute | solution.py:451
  69.0 15.8 %collective-permute-start.18 = (bf16[2,2048,128]{2,1,0:T(8,128)(2,1)S(1)}, bf16[2,2048,128]{2,1,0:T(8,128)(2,1)}, u32[]{:S(2)}, u32[]{:S(2)}) collective-permute-start(bf16[2,2048,128]{2,1,0:T(8,128)(2,1)S(1)} %get-tuple-element.113.refs_0_.refs_1_), channel_id=1, source_target_pairs={{0,1},{1,0},{2,3},{3,2},{4,5},{5,4},{6,7},{7,6},{8,9},{9,8},{10,11... | collective-permute-start | bytes 3145736 | tf_op jit(solution)/shard_map/ppermute | solution.py:490
  121.8 15.4 %collective-permute-start.19 = (bf16[2048,128]{1,0:T(8,128)(2,1)S(1)}, bf16[2048,128]{1,0:T(8,128)(2,1)S(1)}, u32[]{:S(2)}, u32[]{:S(2)}) collective-permute-start(bf16[2048,128]{1,0:T(8,128)(2,1)S(1)} %get-tuple-element.124.o_ref.attn_ref.refs_0_), channel_id=1, source_target_pairs={{0,2},{2,0},{4,6},{10,8},{12,14},{14,12},{16,18},{20,22},{22,20},{... | collective-permute-start | bytes 1572872 | tf_op jit(solution)/shard_map/ppermute | solution.py:514
  123.7 13.5 %collective-permute-start.20 = (bf16[2048,128]{1,0:T(8,128)(2,1)S(1)}, bf16[2048,128]{1,0:T(8,128)(2,1)S(1)}, u32[]{:S(2)}, u32[]{:S(2)}) collective-permute-start(bf16[2048,128]{1,0:T(8,128)(2,1)S(1)} %get-tuple-element.124.o_ref.attn_ref.refs_0_), channel_id=1, source_target_pairs={{0,4},{2,6},{4,0},{10,14},{12,8},{14,10},{16,20},{20,16},{22,18},{... | collective-permute-start | bytes 1572872 | tf_op jit(solution)/shard_map/ppermute | solution.py:514
  125.0 22.6 %collective-permute-start.21 = (bf16[2048,128]{1,0:T(8,128)(2,1)S(1)}, bf16[2048,128]{1,0:T(8,128)(2,1)S(1)}, u32[]{:S(2)}, u32[]{:S(2)}) collective-permute-start(bf16[2048,128]{1,0:T(8,128)(2,1)S(1)} %get-tuple-element.124.o_ref.attn_ref.refs_0_), channel_id=1, source_target_pairs={{0,6},{2,4},{4,2},{10,12},{12,10},{14,8},{16,22},{20,18},{22,16},{... | collective-permute-start | bytes 1572872 | tf_op jit(solution)/shard_map/ppermute | solution.py:514
  159.2 22.6 %collective-permute-start.28 = (bf16[4,4,128,128]{3,2,1,0:T(8,128)(2,1)}, bf16[4,4,128,128]{3,2,1,0:T(8,128)(2,1)S(1)}, u32[]{:S(2)}, u32[]{:S(2)}) collective-permute-start(bf16[4,4,128,128]{3,2,1,0:T(8,128)(2,1)} %get-tuple-element.132), channel_id=1, source_target_pairs={{0,2},{2,0},{4,6},{10,8},{12,14},{14,12},{16,18},{20,22},{22,20},{... | collective-permute-start | bytes 1572872 | tf_op jit(solution)/shard_map/ppermute | solution.py:451
  169.9 45.4 %collective-permute-start.25 = (bf16[384,768]{1,0:T(8,128)(2,1)S(1)}, bf16[384,768]{1,0:T(8,128)(2,1)S(1)}, u32[]{:S(2)}, u32[]{:S(2)}) collective-permute-start(bf16[384,768]{1,0:T(8,128)(2,1)S(1)} %broadcast_select_fusion.2.refs_0_), channel_id=1, source_target_pairs={{0,8},{2,10},{4,12},{6,14},{8,0},{10,2},{12,4},{14,6},{16,24},{18,... | collective-permute-start | bytes 1769480 | tf_op jit(solution)/shard_map/ppermute | solution.py:339
  177.4 37.9 %collective-permute-start.26 = (bf16[384,768]{1,0:T(8,128)(2,1)S(1)}, bf16[384,768]{1,0:T(8,128)(2,1)S(1)}, u32[]{:S(2)}, u32[]{:S(2)}) collective-permute-start(bf16[384,768]{1,0:T(8,128)(2,1)S(1)} %broadcast_select_fusion.2.refs_0_), channel_id=1, source_target_pairs={{0,2},{2,0},{4,6},{6,4},{8,10},{10,8},{12,14},{14,12},{16,18},{18,... | collective-permute-start | bytes 1769480 | tf_op jit(solution)/shard_map/ppermute | solution.py:339
  178.4 36.9 %collective-permute-start.27 = (bf16[384,768]{1,0:T(8,128)(2,1)S(1)}, bf16[384,768]{1,0:T(8,128)(2,1)S(1)}, u32[]{:S(2)}, u32[]{:S(2)}) collective-permute-start(bf16[384,768]{1,0:T(8,128)(2,1)S(1)} %broadcast_select_fusion.2.refs_0_), channel_id=1, source_target_pairs={{0,4},{2,6},{4,0},{6,2},{8,12},{10,14},{12,8},{14,10},{16,20},{18,... | collective-permute-start | bytes 1769480 | tf_op jit(solution)/shard_map/ppermute | solution.py:339
  179.3 35.3 %collective-permute-start.29 = (bf16[4,4,128,128]{3,2,1,0:T(8,128)(2,1)}, bf16[4,4,128,128]{3,2,1,0:T(8,128)(2,1)S(1)}, u32[]{:S(2)}, u32[]{:S(2)}) collective-permute-start(bf16[4,4,128,128]{3,2,1,0:T(8,128)(2,1)} %copy-done.9), channel_id=1, source_target_pairs={{0,4},{2,6},{4,0},{10,14},{12,8},{14,10},{16,20},{20,16},{22,18},{... | collective-permute-start | bytes 1572872 | tf_op jit(solution)/shard_map/ppermute | solution.py:451
  181.8 32.8 %collective-permute-start.30 = (bf16[4,4,128,128]{3,2,1,0:T(8,128)(2,1)}, bf16[4,4,128,128]{3,2,1,0:T(8,128)(2,1)S(1)}, u32[]{:S(2)}, u32[]{:S(2)}) collective-permute-start(bf16[4,4,128,128]{3,2,1,0:T(8,128)(2,1)} %copy-done.8), channel_id=1, source_target_pairs={{0,6},{2,4},{4,2},{10,12},{12,10},{14,8},{16,22},{20,18},{22,16},{... | collective-permute-start | bytes 1572872 | tf_op jit(solution)/shard_map/ppermute | solution.py:451
  215.7 36.4 %collective-permute-start.33 = (bf16[3,4,128,128]{3,2,1,0:T(8,128)(2,1)S(1)}, bf16[3,4,128,128]{3,2,1,0:T(8,128)(2,1)S(1)}, u32[]{:S(2)}, u32[]{:S(2)}) collective-permute-start(bf16[3,4,128,128]{3,2,1,0:T(8,128)(2,1)S(1)} %get-tuple-element.142), channel_id=1, source_target_pairs={{0,24},{2,26},{4,28},{6,30},{8,16},{10,18},{12,20},{14,22},{16,8},... | collective-permute-start | bytes 1179656 | tf_op jit(solution)/shard_map/ppermute | solution.py:446
  255.9 15.5 %collective-permute-start.38 = (bf16[384,768]{1,0:T(8,128)(2,1)S(1)}, bf16[384,768]{1,0:T(8,128)(2,1)S(1)}, u32[]{:S(2)}, u32[]{:S(2)}) collective-permute-start(bf16[384,768]{1,0:T(8,128)(2,1)S(1)} %collective-permute-done.25.refs_5_), channel_id=1, source_target_pairs={{0,2},{2,0},{4,6},{6,4},{8,10},{10,8},{12,14},{14,12},{16,18},{18,... | collective-permute-start | bytes 1769480 | tf_op jit(solution)/shard_map/ppermute | solution.py:339
  256.6 17.1 %collective-permute-start.39 = (bf16[384,768]{1,0:T(8,128)(2,1)S(1)}, bf16[384,768]{1,0:T(8,128)(2,1)S(1)}, u32[]{:S(2)}, u32[]{:S(2)}) collective-permute-start(bf16[384,768]{1,0:T(8,128)(2,1)S(1)} %collective-permute-done.25.refs_5_), channel_id=1, source_target_pairs={{0,4},{2,6},{4,0},{6,2},{8,12},{10,14},{12,8},{14,10},{16,20},{18,... | collective-permute-start | bytes 1769480 | tf_op jit(solution)/shard_map/ppermute | solution.py:339
  267.3 25.1 %collective-permute-start.35 = (bf16[256,1536]{1,0:T(8,128)(2,1)}, bf16[256,1536]{1,0:T(8,128)(2,1)}, u32[]{:S(2)}, u32[]{:S(2)}) collective-permute-start(bf16[256,1536]{1,0:T(8,128)(2,1)} %dynamic-slice_convert_fusion), channel_id=1, source_target_pairs={{0,1},{1,0},{2,3},{3,2},{4,5},{5,4},{6,7},{7,6},{8,9},{9,8},{10,11... | collective-permute-start | bytes 2359304 | tf_op jit(solution)/shard_map/ppermute | solution.py:610
  272.2 12.5 %collective-permute-start.40 = (bf16[192,768]{1,0:T(8,128)(2,1)}, bf16[192,768]{1,0:T(8,128)(2,1)}, u32[]{:S(2)}, u32[]{:S(2)}) collective-permute-start(bf16[192,768]{1,0:T(8,128)(2,1)} %slice.20), channel_id=1, source_target_pairs={{0,4},{2,6},{4,0},{6,2},{8,12},{10,14},{12,8},{14,10},{16,20},{18,... | collective-permute-start | bytes 884744 | tf_op jit(solution)/shard_map/ppermute | solution.py:339
  (42 other events, 317.5 us)
Sparse Core Ops, SparseCore 0:
  71.4 60.6 all-gather.2

commit v11 on v7

--- a/solution.py
+++ b/solution.py
@@ -452,11 +452,6 @@
         name="forward",
     )(full, kcnt, kidx, q_rows, *part_arrays)
 
-    travel = [attn] + [
-        lax.ppermute(attn, "ctx", [(i, i ^ k) for i in range(n) if held[i]]) for k in range(1, in_plane)
-    ]
-    *travel, attn = lax.optimization_barrier((*travel, attn))
-
     dq, *dkv = pl.pallas_call(
         functools.partial(backward_kernel, t, tile, count),
         grid_spec=pltpu.PrefetchScalarGridSpec(
@@ -479,7 +474,11 @@
         functools.partial(unjoin_kernel, n, t), "unjoin", where,
         [attn, dq, dkv[0]] + got_dkv, [shape(n, 4, sub, HEAD)],
     )
+    sent, attn = lax.optimization_barrier((sent, attn))
     chunks = lax.all_to_all(sent, "ctx", 0, 0, tiled=True)
+    travel = [attn] + [
+        lax.ppermute(attn, "ctx", [(i, i ^ k) for i in range(n) if held[i]]) for k in range(1, in_plane)
+    ]
 
     tile_rows = heads_plane * HEAD
     by_core = in_plane == 4 and t == 2

time: 271 us -> 272 us (level)
  waiting for transfers between devices: 101 us -> 110 us
  starting transfers between devices: 60.5 us -> 51.7 us
    ppermute x1, waiting for transfers between devices: 32.8 us -> 18.9 us  [gather_tiles_by_core(): from_half = lax.ppermute(tile_sum, ('ctx', 'tp'), across)]
    ppermute x3, waiting for transfers between devices: 18.6 us -> 32.5 us  [per_device(): lax.ppermute(attn, 'ctx', [(i, i ^ k) for i in range(n) if held[i]])]
    ppermute x9, starting transfers between devices: 23.1 us -> 11 us  [swap(): return lax.ppermute(x, 'ctx', [(i, i ^ k) for i in range(n)])]
    all_to_all x1, waiting for transfers between devices: 0.01 us -> 7.29 us  [per_device(): lax.all_to_all(sent_g, 'ctx', 0, 0, tiled=True).reshape(n * sub, HEAD)]
    ppermute x1, starting transfers between devices: 1.4 us -> 5.08 us  [per_device(): lax.ppermute(dkv[s], 'tp', [(c, (c - s) % t) for c in range(t)])]
    all_to_all x1, starting transfers between devices: 7.15 us -> 4.39 us  [per_device(): chunks = lax.all_to_all(sent, 'ctx', 0, 0, tiled=True)]
    unnamed x46 -> x42, local copies, waits for them, and re-layouts: 11.6 us -> 12.8 us
  transfers between devices with their start and end apart: 28 -> 28, of which waited for: 15 -> 17; matrix products, arithmetic and copies ran while one was open for 7% -> 7% of each run, Pallas kernels for 20% -> 19%
where the time goes in v11:
time: 272 us; the launch traced here: 269 us
  waiting for transfers between devices  110 us (40%)
  Pallas kernels  55.4 us (20%)
  starting transfers between devices  51.7 us (19%)
  local copies, waits for them, and re-layouts  21.9 us (8%)
  between operations  14.4 us (5%)
  other arithmetic  7.67 us (3%)
  matrix products  7.5 us (3%)
    ppermute x3, waiting for transfers between devices, per_device(): lax.ppermute(attn, 'ctx', [(i, i ^ k) for i in range(n) if held[i]])  32.5 us
    ppermute x9, waiting for transfers between devices, swap(): return lax.ppermute(x, 'ctx', [(i, i ^ k) for i in range(n)])  24.6 us
    pallas_call x1, Pallas kernels, per_device(): pl.pallas_call(functools.partial(backward_kernel, t, tile, count), grid_s...  20.1 us
    ppermute x1, waiting for transfers between devices, gather_tiles_by_core(): from_half = lax.ppermute(tile_sum, ('ctx', 'tp'), across)  18.9 us
    pallas_call x1, Pallas kernels, per_device(): pl.pallas_call(functools.partial(forward_kernel, t, tile, count), grid_sp...  13.9 us
    ppermute x3, waiting for transfers between devices, per_device(): plane_got.append(lax.ppermute(there, 'ctx', [(i, i ^ k) for i in range(n)]))  13.1 us
    unnamed x42, local copies, waits for them, and re-layouts  12.8 us
    ppermute x9, starting transfers between devices, swap(): return lax.ppermute(x, 'ctx', [(i, i ^ k) for i in range(n)])  11 us
  transfers between devices with their start and end apart: 28, of which 17 were waited for; matrix products, arithmetic and copies ran while one was open for 7% of the time, Pallas kernels for 19%

profile of v11, /device:TPU:13, one launch (start us, length us, event | category | flops | bytes accessed | tf_op | source)
XLA Modules:
  0.0 269.1 jit_solution(18096103241497923932)
XLA Ops:
  13.8 6.7 %all-to-all-start = ((bf16[16,3,128,128]{3,2,1,0:T(8,128)(2,1)}), bf16[16,3,128,128]{3,2,1,0:T(8,128)(2,1)S(1)}, u32[]{:S(2)}, u32[]{:S(2)}) async-start(bf16[16,3,128,128]{3,2,1,0:T(8,128)(2,1)} %pack.2), calls=%async_computation | async-start | bytes 3145728 | tf_op jit(solution)/shard_map/all_to_all | solution.py:422
  24.9 3.8 %fusion.1.refs_0_ = bf16[256,768]{1,0:T(8,128)(2,1)S(1)} fusion(bf16[768,3072]{1,0:T(8,128)(2,1)} %param.11, bf16[256,1536]{1,0:T(8,128)(2,1)S(1)} %get-tuple-element.65, bf16[256,1536]{1,0:T(8,128)(2,1)S(1)} %get-tuple-element.64), kind=kOutput, calls=%fused_computation.14 | convolution fusion | flops 1211301888 | bytes 6684672 | tf_op jit(solution)/shard_map/dot_general | solution.py:27
  37.0 11.1 %collective-permute-done.5.refs_3_ = bf16[128,768]{1,0:T(8,128)(2,1)S(1)} collective-permute-done((bf16[128,768]{1,0:T(8,128)(2,1)}, bf16[128,768]{1,0:T(8,128)(2,1)S(1)}, u32[]{:S(2)}, u32[]{:S(2)}) %collective-permute-start.5) | collective-permute-done | bytes 196640 | tf_op jit(solution)/shard_map/ppermute | solution.py:408
  51.5 5.8 %all-to-all-done.chunks_ref = bf16[16,3,128,128]{3,2,1,0:T(8,128)(2,1)S(1)} async-done(((bf16[16,3,128,128]{3,2,1,0:T(8,128)(2,1)}), bf16[16,3,128,128]{3,2,1,0:T(8,128)(2,1)S(1)}, u32[]{:S(2)}, u32[]{:S(2)}) %all-to-all-start) | async-done | bytes 1572896 | tf_op jit(solution)/shard_map/all_to_all | solution.py:422
  60.6 4.8 %all-to-all-start.1 = ((bf16[16,1,128,128]{3,2,1,0:T(8,128)(2,1)}), bf16[16,1,128,128]{3,2,1,0:T(8,128)(2,1)S(1)}, u32[]{:S(2)}, u32[]{:S(2)}) async-start(bf16[16,1,128,128]{3,2,1,0:T(8,128)(2,1)} %pack.3), calls=%async_computation.1 | async-start | bytes 1048576 | tf_op jit(solution)/shard_map/all_to_all | solution.py:427
  67.1 13.9 %forward.1 = (bf16[2048,128]{1,0:T(8,128)(2,1)S(1)}, f32[2048,128]{1,0:T(8,128)S(1)}) custom-call(s32[16]{0:T(128)S(1)} %get-tuple-element.58.full_ref, s32[16]{0:T(128)S(1)} %get-tuple-element.54.kcnt_ref, s32[16,10]{1,0:T(8,128)S(1)} %copy.11.kidx_ref, bf16[2048,128]{1,0:T(8,128)(2,1)S(1)} %get-tuple-element.31.q_ref, bf16[2,2048,128]{2,1,0:T(8,128)(2,1)S(1)} %copy-done.8, ...), custom_call_target="tpu_custom_call" | custom-call | flops 16000000000 | bytes 5242880 | tf_op jit(solution)/shard_map/forward/pallas_call | solution.py:440
  82.0 7.3 %all-to-all-done.1 = bf16[16,1,128,128]{3,2,1,0:T(8,128)(2,1)S(1)} async-done(((bf16[16,1,128,128]{3,2,1,0:T(8,128)(2,1)}), bf16[16,1,128,128]{3,2,1,0:T(8,128)(2,1)S(1)}, u32[]{:S(2)}, u32[]{:S(2)}) %all-to-all-start.1) | async-done | bytes 524320 | tf_op jit(solution)/shard_map/all_to_all | solution.py:427
  90.5 20.1 %backward.1 = (bf16[2048,128]{1,0:T(8,128)(2,1)S(1)}, bf16[2,2048,128]{2,1,0:T(8,128)(2,1)S(1)}, bf16[2,2048,128]{2,1,0:T(8,128)(2,1)S(1)}) custom-call(s32[16]{0:T(128)S(1)} %get-tuple-element.58.full_ref, s32[16]{0:T(128)S(1)} %get-tuple-element.54.kcnt_ref, s32[16,10]{1,0:T(8,128)S(1)} %copy.11.kidx_ref, bf16[2048,128]{1,0:T(8,128)(2,1)S(1)} %get-tuple-element.31.q_ref, ...), custom_call_target="tpu_custom_call" | custom-call | flops 20000000000 | bytes 8388608 | tf_op jit(solution)/shard_map/backward/pallas_call | solution.py:455
  110.7 5.1 %collective-permute-start.7 = (bf16[2,2048,128]{2,1,0:T(8,128)(2,1)S(1)}, bf16[2,2048,128]{2,1,0:T(8,128)(2,1)S(1)}, u32[]{:S(2)}, u32[]{:S(2)}) collective-permute-start(bf16[2,2048,128]{2,1,0:T(8,128)(2,1)S(1)} %get-tuple-element.38), channel_id=1, source_target_pairs={{0,1},{1,0},{2,3},{3,2},{4,5},{5,4},{6,7},{7,6},{8,9},{9,8},{10,11... | collective-permute-start | bytes 3145736 | tf_op jit(solution)/shard_map/ppermute | solution.py:471
  115.8 2.3 collective-permute-done.7.refs_0_
  120.2 4.4 %all-to-all-start.2 = ((bf16[16,4,128,128]{3,2,1,0:T(8,128)(2,1)}), bf16[16,4,128,128]{3,2,1,0:T(8,128)(2,1)S(1)}, u32[]{:S(2)}, u32[]{:S(2)}) async-start(bf16[16,4,128,128]{3,2,1,0:T(8,128)(2,1)} %copy-done.1), calls=%async_computation.2 | async-start | bytes 4194304 | tf_op jit(solution)/shard_map/all_to_all | solution.py:478
  124.6 3.1 %collective-permute-start.10 = (bf16[2048,128]{1,0:T(8,128)(2,1)S(1)}, bf16[2048,128]{1,0:T(8,128)(2,1)S(1)}, u32[]{:S(2)}, u32[]{:S(2)}) collective-permute-start(bf16[2048,128]{1,0:T(8,128)(2,1)S(1)} %get-tuple-element.39.o_ref.attn_ref.refs_0_), channel_id=1, source_target_pairs={{0,6},{2,4},{4,2},{10,12},{12,10},{14,8},{16,22},{20,18},{22,16},{... | collective-permute-start | bytes 1572872 | tf_op jit(solution)/shard_map/ppermute | solution.py:480
  129.0 4.1 %collective-permute-start.8 = (bf16[2048,128]{1,0:T(8,128)(2,1)S(1)}, bf16[2048,128]{1,0:T(8,128)(2,1)S(1)}, u32[]{:S(2)}, u32[]{:S(2)}) collective-permute-start(bf16[2048,128]{1,0:T(8,128)(2,1)S(1)} %get-tuple-element.39.o_ref.attn_ref.refs_0_), channel_id=1, source_target_pairs={{0,2},{2,0},{4,6},{10,8},{12,14},{14,12},{16,18},{20,22},{22,20},{... | collective-permute-start | bytes 1572872 | tf_op jit(solution)/shard_map/ppermute | solution.py:480
  133.1 21.9 %collective-permute-done.10.refs_3_ = bf16[2048,128]{1,0:T(8,128)(2,1)S(1)} collective-permute-done((bf16[2048,128]{1,0:T(8,128)(2,1)S(1)}, bf16[2048,128]{1,0:T(8,128)(2,1)S(1)}, u32[]{:S(2)}, u32[]{:S(2)}) %collective-permute-start.10) | collective-permute-done | bytes 524320 | tf_op jit(solution)/shard_map/ppermute | solution.py:480
  155.8 10.6 %collective-permute-done.9.refs_2_ = bf16[2048,128]{1,0:T(8,128)(2,1)S(1)} collective-permute-done((bf16[2048,128]{1,0:T(8,128)(2,1)S(1)}, bf16[2048,128]{1,0:T(8,128)(2,1)S(1)}, u32[]{:S(2)}, u32[]{:S(2)}) %collective-permute-start.9) | collective-permute-done | bytes 524320 | tf_op jit(solution)/shard_map/ppermute | solution.py:480
  171.1 4.8 %tile.1 = (f32[384,768]{1,0:T(8,128)S(1)}, bf16[384,768]{1,0:T(8,128)(2,1)S(1)}) custom-call(s32[2]{0:T(128)S(1)} %pad_add_fusion.where_ref, bf16[2048,128]{1,0:T(8,128)(2,1)S(1)} %get-tuple-element.39.o_ref.attn_ref.refs_0_, bf16[2048,128]{1,0:T(8,128)(2,1)S(1)} %copy-done.15, bf16[2048,128]{1,0:T(8,128)(2,1)S(1)} %copy-done.13, ...), custom_call_target="tpu_custom_call" | custom-call | flops 5000000000 | bytes 4194304 | tf_op jit(solution)/shard_map/tile/pallas_call | solution.py:487
  180.5 18.9 %collective-permute-done.12 = bf16[384,768]{1,0:T(8,128)(2,1)} collective-permute-done((bf16[384,768]{1,0:T(8,128)(2,1)S(1)}, bf16[384,768]{1,0:T(8,128)(2,1)}, u32[]{:S(2)}, u32[]{:S(2)}) %collective-permute-start.12) | collective-permute-done | bytes 589856 | tf_op jit(solution)/shard_map/ppermute | solution.py:305
  200.7 6.7 %collective-permute-start.13 = (bf16[384,768]{1,0:T(8,128)(2,1)S(1)}, bf16[384,768]{1,0:T(8,128)(2,1)}, u32[]{:S(2)}, u32[]{:S(2)}) collective-permute-start(bf16[384,768]{1,0:T(8,128)(2,1)S(1)} %broadcast_select_fusion.2.refs_0_), channel_id=1, source_target_pairs={{0,8},{2,10},{4,12},{6,14},{8,0},{10,2},{12,4},{14,6},{16,24},{18,... | collective-permute-start | bytes 1769480 | tf_op jit(solution)/shard_map/ppermute | solution.py:308
  207.4 4.3 %collective-permute-done.15.refs_2_ = bf16[384,768]{1,0:T(8,128)(2,1)S(1)} collective-permute-done((bf16[384,768]{1,0:T(8,128)(2,1)S(1)}, bf16[384,768]{1,0:T(8,128)(2,1)S(1)}, u32[]{:S(2)}, u32[]{:S(2)}) %collective-permute-start.15) | collective-permute-done | bytes 589856 | tf_op jit(solution)/shard_map/ppermute | solution.py:308
  211.7 8.4 %collective-permute-done.13.refs_5_ = bf16[384,768]{1,0:T(8,128)(2,1)} collective-permute-done((bf16[384,768]{1,0:T(8,128)(2,1)S(1)}, bf16[384,768]{1,0:T(8,128)(2,1)}, u32[]{:S(2)}, u32[]{:S(2)}) %collective-permute-start.13) | collective-permute-done | bytes 589856 | tf_op jit(solution)/shard_map/ppermute | solution.py:308
  229.3 3.7 %fusion.8 = f32[256,3072]{1,0:T(8,128)S(1)} fusion(bf16[256,768]{1,0:T(8,128)(2,1)S(1)} %get-tuple-element.47, bf16[768,3072]{1,0:T(8,128)(2,1)} %param.11), kind=kOutput, calls=%fused_computation.56 | convolution fusion | flops 1207959552 | bytes 8257536 | tf_op jit(solution)/shard_map/dot_general | solution.py:27
  242.4 4.4 %collective-permute-done.19.refs_4_ = bf16[192,768]{1,0:T(8,128)(2,1)S(1)} collective-permute-done((bf16[192,768]{1,0:T(8,128)(2,1)}, bf16[192,768]{1,0:T(8,128)(2,1)S(1)}, u32[]{:S(2)}, u32[]{:S(2)}) %collective-permute-start.19) | collective-permute-done | bytes 294944 | tf_op jit(solution)/shard_map/ppermute | solution.py:308
  246.8 6.4 %collective-permute-done.23.refs_9_ = bf16[192,768]{1,0:T(8,128)(2,1)S(1)} collective-permute-done((bf16[192,768]{1,0:T(8,128)(2,1)}, bf16[192,768]{1,0:T(8,128)(2,1)S(1)}, u32[]{:S(2)}, u32[]{:S(2)}) %collective-permute-start.23) | collective-permute-done | bytes 294944 | tf_op jit(solution)/shard_map/ppermute | solution.py:308
  253.2 6.8 %place.1 = f32[768,3072]{1,0:T(8,128)} custom-call(s32[2]{0:T(128)S(1)} %pad_add_fusion.2.place_ref, bf16[384,768]{1,0:T(8,128)(2,1)S(1)} %broadcast_select_fusion.2.refs_0_, bf16[384,768]{1,0:T(8,128)(2,1)} %collective-permute-done.14.refs_1_, bf16[384,768]{1,0:T(8,128)(2,1)S(1)} %collective-permute-done.15.refs_2_, ...), custom_call_target="tpu_custom_call" | custom-call | bytes 16777216 | tf_op jit(solution)/shard_map/place/pallas_call | solution.py:319
  (117 shorter events, 65.2 us)
Async XLA Ops:
  13.8 43.6 %all-to-all-start = ((bf16[16,3,128,128]{3,2,1,0:T(8,128)(2,1)}), bf16[16,3,128,128]{3,2,1,0:T(8,128)(2,1)S(1)}, u32[]{:S(2)}, u32[]{:S(2)}) async-start(bf16[16,3,128,128]{3,2,1,0:T(8,128)(2,1)} %pack.2), calls=%async_computation | async-start | bytes 3145728 | tf_op jit(solution)/shard_map/all_to_all | solution.py:422
  20.5 147.4 %all-gather.3.cloned.1.call-start = ((), (), s32[]{:S(2)}) async-start(), calls=%async_computation.3 | async-start | bytes 3932160 | tf_op jit(solution)/shard_map/all_gather | solution.py:425
  29.3 6.2 %collective-permute-start.2 = (bf16[1,128,768]{2,1,0:T(8,128)(2,1)}, bf16[1,128,768]{2,1,0:T(8,128)(2,1)S(1)}, u32[]{:S(2)}, u32[]{:S(2)}) collective-permute-start(bf16[1,128,768]{2,1,0:T(8,128)(2,1)} %dynamic-slice_bitcast_fusion), channel_id=1, source_target_pairs={{0,1},{1,0},{2,3},{3,2},{4,5},{5,4},{6,7},{7,6},{8,9},{9,8},{10,11... | collective-permute-start | bytes 589832 | tf_op jit(solution)/shard_map/ppermute | solution.py:386
  31.5 16.6 %collective-permute-start.5 = (bf16[128,768]{1,0:T(8,128)(2,1)}, bf16[128,768]{1,0:T(8,128)(2,1)S(1)}, u32[]{:S(2)}, u32[]{:S(2)}) collective-permute-start(bf16[128,768]{1,0:T(8,128)(2,1)} %get-tuple-element.60), channel_id=1, source_target_pairs={{0,6},{2,4},{4,2},{6,0},{8,14},{10,12},{12,10},{14,8},{16,22},{18,... | collective-permute-start | bytes 589832 | tf_op jit(solution)/shard_map/ppermute | solution.py:408
  32.7 17.4 %collective-permute-start.3 = (bf16[128,768]{1,0:T(8,128)(2,1)}, bf16[128,768]{1,0:T(8,128)(2,1)S(1)}, u32[]{:S(2)}, u32[]{:S(2)}) collective-permute-start(bf16[128,768]{1,0:T(8,128)(2,1)} %get-tuple-element.62), channel_id=1, source_target_pairs={{0,2},{2,0},{4,6},{6,4},{8,10},{10,8},{12,14},{14,12},{16,18},{18,... | collective-permute-start | bytes 589832 | tf_op jit(solution)/shard_map/ppermute | solution.py:408
  33.0 17.1 %collective-permute-start.4 = (bf16[128,768]{1,0:T(8,128)(2,1)S(1)}, bf16[128,768]{1,0:T(8,128)(2,1)S(1)}, u32[]{:S(2)}, u32[]{:S(2)}) collective-permute-start(bf16[128,768]{1,0:T(8,128)(2,1)S(1)} %get-tuple-element.63), channel_id=1, source_target_pairs={{0,4},{2,6},{4,0},{6,2},{8,12},{10,14},{12,8},{14,10},{16,20},{18,... | collective-permute-start | bytes 589832 | tf_op jit(solution)/shard_map/ppermute | solution.py:408
  58.0 7.3 %collective-permute-start.6 = (bf16[2,2048,128]{2,1,0:T(8,128)(2,1)S(1)}, bf16[2,2048,128]{2,1,0:T(8,128)(2,1)S(1)}, u32[]{:S(2)}, u32[]{:S(2)}) collective-permute-start(bf16[2,2048,128]{2,1,0:T(8,128)(2,1)S(1)} %get-tuple-element.32.refs_0_.refs_1_), channel_id=1, source_target_pairs={{0,1},{1,0},{2,3},{3,2},{4,5},{5,4},{6,7},{7,6},{8,9},{9,8},{10,11... | collective-permute-start | bytes 3145736 | tf_op jit(solution)/shard_map/ppermute | solution.py:432
  60.6 28.7 %all-to-all-start.1 = ((bf16[16,1,128,128]{3,2,1,0:T(8,128)(2,1)}), bf16[16,1,128,128]{3,2,1,0:T(8,128)(2,1)S(1)}, u32[]{:S(2)}, u32[]{:S(2)}) async-start(bf16[16,1,128,128]{3,2,1,0:T(8,128)(2,1)} %pack.3), calls=%async_computation.1 | async-start | bytes 1048576 | tf_op jit(solution)/shard_map/all_to_all | solution.py:427
  110.7 7.4 %collective-permute-start.7 = (bf16[2,2048,128]{2,1,0:T(8,128)(2,1)S(1)}, bf16[2,2048,128]{2,1,0:T(8,128)(2,1)S(1)}, u32[]{:S(2)}, u32[]{:S(2)}) collective-permute-start(bf16[2,2048,128]{2,1,0:T(8,128)(2,1)S(1)} %get-tuple-element.38), channel_id=1, source_target_pairs={{0,1},{1,0},{2,3},{3,2},{4,5},{5,4},{6,7},{7,6},{8,9},{9,8},{10,11... | collective-permute-start | bytes 3145736 | tf_op jit(solution)/shard_map/ppermute | solution.py:471
  120.2 87.2 %all-to-all-start.2 = ((bf16[16,4,128,128]{3,2,1,0:T(8,128)(2,1)}), bf16[16,4,128,128]{3,2,1,0:T(8,128)(2,1)S(1)}, u32[]{:S(2)}, u32[]{:S(2)}) async-start(bf16[16,4,128,128]{3,2,1,0:T(8,128)(2,1)} %copy-done.1), calls=%async_computation.2 | async-start | bytes 4194304 | tf_op jit(solution)/shard_map/all_to_all | solution.py:478
  124.6 30.4 %collective-permute-start.10 = (bf16[2048,128]{1,0:T(8,128)(2,1)S(1)}, bf16[2048,128]{1,0:T(8,128)(2,1)S(1)}, u32[]{:S(2)}, u32[]{:S(2)}) collective-permute-start(bf16[2048,128]{1,0:T(8,128)(2,1)S(1)} %get-tuple-element.39.o_ref.attn_ref.refs_0_), channel_id=1, source_target_pairs={{0,6},{2,4},{4,2},{10,12},{12,10},{14,8},{16,22},{20,18},{22,16},{... | collective-permute-start | bytes 1572872 | tf_op jit(solution)/shard_map/ppermute | solution.py:480
  127.6 38.7 %collective-permute-start.9 = (bf16[2048,128]{1,0:T(8,128)(2,1)S(1)}, bf16[2048,128]{1,0:T(8,128)(2,1)S(1)}, u32[]{:S(2)}, u32[]{:S(2)}) collective-permute-start(bf16[2048,128]{1,0:T(8,128)(2,1)S(1)} %get-tuple-element.39.o_ref.attn_ref.refs_0_), channel_id=1, source_target_pairs={{0,4},{2,6},{4,0},{10,14},{12,8},{14,10},{16,20},{20,16},{22,18},{... | collective-permute-start | bytes 1572872 | tf_op jit(solution)/shard_map/ppermute | solution.py:480
  129.0 38.2 %collective-permute-start.8 = (bf16[2048,128]{1,0:T(8,128)(2,1)S(1)}, bf16[2048,128]{1,0:T(8,128)(2,1)S(1)}, u32[]{:S(2)}, u32[]{:S(2)}) collective-permute-start(bf16[2048,128]{1,0:T(8,128)(2,1)S(1)} %get-tuple-element.39.o_ref.attn_ref.refs_0_), channel_id=1, source_target_pairs={{0,2},{2,0},{4,6},{10,8},{12,14},{14,12},{16,18},{20,22},{22,20},{... | collective-permute-start | bytes 1572872 | tf_op jit(solution)/shard_map/ppermute | solution.py:480
  179.2 20.2 %collective-permute-start.12 = (bf16[384,768]{1,0:T(8,128)(2,1)S(1)}, bf16[384,768]{1,0:T(8,128)(2,1)}, u32[]{:S(2)}, u32[]{:S(2)}) collective-permute-start(bf16[384,768]{1,0:T(8,128)(2,1)S(1)} %add_convert_fusion.1), channel_id=1, source_target_pairs={{0,16},{2,18},{4,20},{6,22},{8,24},{10,26},{12,28},{14,30},{17,1},... | collective-permute-start | bytes 1769480 | tf_op jit(solution)/shard_map/ppermute | solution.py:305
  200.6 11.1 %collective-permute-start.15 = (bf16[384,768]{1,0:T(8,128)(2,1)S(1)}, bf16[384,768]{1,0:T(8,128)(2,1)S(1)}, u32[]{:S(2)}, u32[]{:S(2)}) collective-permute-start(bf16[384,768]{1,0:T(8,128)(2,1)S(1)} %broadcast_select_fusion.2.refs_0_), channel_id=1, source_target_pairs={{0,4},{2,6},{4,0},{6,2},{8,12},{10,14},{12,8},{14,10},{16,20},{18,... | collective-permute-start | bytes 1769480 | tf_op jit(solution)/shard_map/ppermute | solution.py:308
  200.6 11.1 %collective-permute-start.14 = (bf16[384,768]{1,0:T(8,128)(2,1)S(1)}, bf16[384,768]{1,0:T(8,128)(2,1)}, u32[]{:S(2)}, u32[]{:S(2)}) collective-permute-start(bf16[384,768]{1,0:T(8,128)(2,1)S(1)} %broadcast_select_fusion.2.refs_0_), channel_id=1, source_target_pairs={{0,2},{2,0},{4,6},{6,4},{8,10},{10,8},{12,14},{14,12},{16,18},{18,... | collective-permute-start | bytes 1769480 | tf_op jit(solution)/shard_map/ppermute | solution.py:308
  200.7 19.3 %collective-permute-start.13 = (bf16[384,768]{1,0:T(8,128)(2,1)S(1)}, bf16[384,768]{1,0:T(8,128)(2,1)}, u32[]{:S(2)}, u32[]{:S(2)}) collective-permute-start(bf16[384,768]{1,0:T(8,128)(2,1)S(1)} %broadcast_select_fusion.2.refs_0_), channel_id=1, source_target_pairs={{0,8},{2,10},{4,12},{6,14},{8,0},{10,2},{12,4},{14,6},{16,24},{18,... | collective-permute-start | bytes 1769480 | tf_op jit(solution)/shard_map/ppermute | solution.py:308
  224.3 15.2 %collective-permute-start.21 = (bf16[384,768]{1,0:T(8,128)(2,1)}, bf16[384,768]{1,0:T(8,128)(2,1)S(1)}, u32[]{:S(2)}, u32[]{:S(2)}) collective-permute-start(bf16[384,768]{1,0:T(8,128)(2,1)} %collective-permute-done.13.refs_5_), channel_id=1, source_target_pairs={{0,4},{2,6},{4,0},{6,2},{8,12},{10,14},{12,8},{14,10},{16,20},{18,... | collective-permute-start | bytes 1769480 | tf_op jit(solution)/shard_map/ppermute | solution.py:308
  225.6 14.9 %collective-permute-start.20 = (bf16[384,768]{1,0:T(8,128)(2,1)}, bf16[384,768]{1,0:T(8,128)(2,1)S(1)}, u32[]{:S(2)}, u32[]{:S(2)}) collective-permute-start(bf16[384,768]{1,0:T(8,128)(2,1)} %collective-permute-done.13.refs_5_), channel_id=1, source_target_pairs={{0,2},{2,0},{4,6},{6,4},{8,10},{10,8},{12,14},{14,12},{16,18},{18,... | collective-permute-start | bytes 1769480 | tf_op jit(solution)/shard_map/ppermute | solution.py:308
  234.1 25.9 %collective-permute-start.17 = (bf16[256,1536]{1,0:T(8,128)(2,1)}, bf16[256,1536]{1,0:T(8,128)(2,1)}, u32[]{:S(2)}, u32[]{:S(2)}) collective-permute-start(bf16[256,1536]{1,0:T(8,128)(2,1)} %dynamic-slice_convert_fusion), channel_id=1, source_target_pairs={{0,1},{1,0},{2,3},{3,2},{4,5},{5,4},{6,7},{7,6},{8,9},{9,8},{10,11... | collective-permute-start | bytes 2359304 | tf_op jit(solution)/shard_map/ppermute | solution.py:545
  236.9 9.9 %collective-permute-start.19 = (bf16[192,768]{1,0:T(8,128)(2,1)}, bf16[192,768]{1,0:T(8,128)(2,1)S(1)}, u32[]{:S(2)}, u32[]{:S(2)}) collective-permute-start(bf16[192,768]{1,0:T(8,128)(2,1)} %slice.13), channel_id=1, source_target_pairs={{0,2},{2,0},{4,6},{6,4},{8,10},{10,8},{12,14},{14,12},{16,18},{18,... | collective-permute-start | bytes 884744 | tf_op jit(solution)/shard_map/ppermute | solution.py:308
  237.9 9.0 %collective-permute-start.18 = (bf16[192,768]{1,0:T(8,128)(2,1)}, bf16[192,768]{1,0:T(8,128)(2,1)S(1)}, u32[]{:S(2)}, u32[]{:S(2)}) collective-permute-start(bf16[192,768]{1,0:T(8,128)(2,1)} %slice.12), channel_id=1, source_target_pairs={{0,4},{2,6},{4,0},{6,2},{8,12},{10,14},{12,8},{14,10},{16,20},{18,... | collective-permute-start | bytes 884744 | tf_op jit(solution)/shard_map/ppermute | solution.py:308
  240.2 13.1 %collective-permute-start.23 = (bf16[192,768]{1,0:T(8,128)(2,1)}, bf16[192,768]{1,0:T(8,128)(2,1)S(1)}, u32[]{:S(2)}, u32[]{:S(2)}) collective-permute-start(bf16[192,768]{1,0:T(8,128)(2,1)} %slice.21), channel_id=1, source_target_pairs={{0,2},{2,0},{4,6},{6,4},{8,10},{10,8},{12,14},{14,12},{16,18},{18,... | collective-permute-start | bytes 884744 | tf_op jit(solution)/shard_map/ppermute | solution.py:308
  241.3 12.0 %collective-permute-start.22 = (bf16[192,768]{1,0:T(8,128)(2,1)}, bf16[192,768]{1,0:T(8,128)(2,1)}, u32[]{:S(2)}, u32[]{:S(2)}) collective-permute-start(bf16[192,768]{1,0:T(8,128)(2,1)} %slice.20), channel_id=1, source_target_pairs={{0,4},{2,6},{4,0},{6,2},{8,12},{10,14},{12,8},{14,10},{16,20},{18,... | collective-permute-start | bytes 884744 | tf_op jit(solution)/shard_map/ppermute | solution.py:308
  (25 other events, 120.4 us)
Sparse Core Ops, SparseCore 0:
  60.7 81.4 all-gather.2

commit v12 on v7

--- a/solution.py
+++ b/solution.py
@@ -294,7 +294,7 @@
             out_ref[middle:] = lower[...].astype(F32)
 
 
-def gather_tiles_by_core(n, t, tile_sum, chip, core, beside_chunks):
+def gather_tiles_by_core(n, t, tile_sum, chip, core, sent):
     in_plane = n // PLANES
     plane, seat = chip // in_plane, chip % in_plane
     tile_rows, cols = tile_sum.shape
@@ -308,13 +308,15 @@
         return lax.ppermute(x, "ctx", [(i, i ^ k) for i in range(n)])
 
     first = jnp.where(plane // 2 == core, tile_sum, from_half)
+    _, sent = lax.optimization_barrier((first, sent))
     second = swap(first, in_plane)
     beside, above = swap(first, 1), swap(first, 2)
-    second, beside, above, beside_chunks = lax.optimization_barrier((second, beside, above, beside_chunks))
     middle = tile_rows // 2
     sources = [first, beside, above, swap(beside[:middle], 2), swap(above[middle:], 1)]
     beside, above = swap(second, 1), swap(second, 2)
     sources += [second, beside, above, swap(beside[:middle], 2), swap(above[middle:], 1)]
+    chunks = lax.all_to_all(sent, "ctx", 0, 0, tiled=True)
+    *_, chunks = lax.optimization_barrier((*sources, chunks))
     place = jnp.stack([plane % 2, seat]).astype(jnp.int32)
     return pl.pallas_call(
         place_xor_kernel,
@@ -330,7 +332,7 @@
         compiler_params=pltpu.CompilerParams(vmem_limit_bytes=48 * 2**20),
         cost_estimate=pl.CostEstimate(flops=0, bytes_accessed=2**24, transcendentals=0),
         name="place",
-    )(place, *sources), beside_chunks
+    )(place, *sources), chunks
 
 
 def per_device(n, t, queries, key_vectors, value_vectors, out_weight, out_grad, block_segment):
@@ -479,7 +481,7 @@
         functools.partial(unjoin_kernel, n, t), "unjoin", where,
         [attn, dq, dkv[0]] + got_dkv, [shape(n, 4, sub, HEAD)],
     )
-    chunks = lax.all_to_all(sent, "ctx", 0, 0, tiled=True)
+    *travel, dq = lax.optimization_barrier((*travel, dq))
 
     tile_rows = heads_plane * HEAD
     by_core = in_plane == 4 and t == 2
@@ -506,8 +508,9 @@
     for s in range(1, t):
         tile_sum = tile_sum + lax.ppermute(tile_sends[s - 1], "tp", shifts(t, s)).astype(F32)
     if by_core:
-        grad_weight, chunks = gather_tiles_by_core(n, t, tile_sum.astype(BF16), chip, core, chunks)
+        grad_weight, chunks = gather_tiles_by_core(n, t, tile_sum.astype(BF16), chip, core, sent)
     else:
+        chunks = lax.all_to_all(sent, "ctx", 0, 0, tiled=True)
         tiles = lax.all_gather(tile_sum.astype(BF16), "ctx")
         here = n // t
         tiles_core = [tiles] + [

time: 271 us -> 287 us (1.059)
  waiting for transfers between devices: 101 us -> 118 us
  starting transfers between devices: 60.5 us -> 48.2 us
  local copies, waits for them, and re-layouts: 19.7 us -> 28.4 us
    ppermute x9, waiting for transfers between devices: 22.7 us -> 64.8 us  [swap(): return lax.ppermute(x, 'ctx', [(i, i ^ k) for i in range(n)])]
    ppermute x1, waiting for transfers between devices: 32.8 us -> 9.09 us  [gather_tiles_by_core(): from_half = lax.ppermute(tile_sum, ('ctx', 'tp'), across)]
    ppermute x9, starting transfers between devices: 23.1 us -> 6.03 us  [swap(): return lax.ppermute(x, 'ctx', [(i, i ^ k) for i in range(n)])]
    unnamed x46 -> x78, local copies, waits for them, and re-layouts: 11.6 us -> 23.2 us
    all_to_all x1, starting transfers between devices: 7.15 us -> 10.5 us  [gather_tiles_by_core(): chunks = lax.all_to_all(sent, 'ctx', 0, 0, tiled=True)]
    ppermute x1, starting transfers between devices: 0.01 us -> 3.02 us  [per_device(): lax.ppermute(mine[s], 'tp', shifts(t, s))]
  transfers between devices with their start and end apart: 28 -> 28, of which waited for: 15 -> 15; matrix products, arithmetic and copies ran while one was open for 7% -> 4% of each run, Pallas kernels for 20% -> 16%
where the time goes in v12:
time: 287 us; the launch traced here: 281 us
  waiting for transfers between devices  118 us (41%)
  Pallas kernels  56.3 us (20%)
  starting transfers between devices  48.2 us (17%)
  local copies, waits for them, and re-layouts  28.4 us (10%)
  between operations  14.4 us (5%)
  other arithmetic  8.48 us (3%)
  matrix products  7.58 us (3%)
    ppermute x9, waiting for transfers between devices, swap(): return lax.ppermute(x, 'ctx', [(i, i ^ k) for i in range(n)])  64.8 us
    unnamed x78, local copies, waits for them, and re-layouts  23.2 us
    pallas_call x1, Pallas kernels, per_device(): pl.pallas_call(functools.partial(backward_kernel, t, tile, count), grid_s...  21.1 us
    ppermute x3, waiting for transfers between devices, per_device(): lax.ppermute(attn, 'ctx', [(i, i ^ k) for i in range(n) if held[i]])  17.5 us
    pallas_call x1, Pallas kernels, per_device(): pl.pallas_call(functools.partial(forward_kernel, t, tile, count), grid_sp...  13.8 us
    ppermute x3, waiting for transfers between devices, per_device(): plane_got.append(lax.ppermute(there, 'ctx', [(i, i ^ k) for i in range(n)]))  13.1 us
    pallas_call x7, Pallas kernels, simple_call(): pl.pallas_call(kernel, grid_spec=pltpu.PrefetchScalarGridSpec(num_scalar_...  11.1 us
    all_to_all x1, starting transfers between devices, gather_tiles_by_core(): chunks = lax.all_to_all(sent, 'ctx', 0, 0, tiled=True)  10.5 us
  transfers between devices with their start and end apart: 28, of which 15 were waited for; matrix products, arithmetic and copies ran while one was open for 4% of the time, Pallas kernels for 16%

profile of v12, /device:TPU:13, one launch (start us, length us, event | category | flops | bytes accessed | tf_op | source)
XLA Modules:
  0.0 281.0 jit_solution(14019769422028889175)
XLA Ops:
  13.8 6.7 %all-to-all-start = ((bf16[16,3,128,128]{3,2,1,0:T(8,128)(2,1)}), bf16[16,3,128,128]{3,2,1,0:T(8,128)(2,1)S(1)}, u32[]{:S(2)}, u32[]{:S(2)}) async-start(bf16[16,3,128,128]{3,2,1,0:T(8,128)(2,1)} %pack.2), calls=%async_computation | async-start | bytes 3145728 | tf_op jit(solution)/shard_map/all_to_all | solution.py:424
  24.9 3.8 %fusion.1.refs_0_ = bf16[256,768]{1,0:T(8,128)(2,1)S(1)} fusion(bf16[768,3072]{1,0:T(8,128)(2,1)} %param.11, bf16[256,1536]{1,0:T(8,128)(2,1)S(1)} %get-tuple-element.75, bf16[256,1536]{1,0:T(8,128)(2,1)S(1)} %get-tuple-element.74), kind=kOutput, calls=%fused_computation.14 | convolution fusion | flops 1211301888 | bytes 6684672 | tf_op jit(solution)/shard_map/dot_general | solution.py:27
  37.0 11.2 %collective-permute-done.5.refs_3_ = bf16[128,768]{1,0:T(8,128)(2,1)S(1)} collective-permute-done((bf16[128,768]{1,0:T(8,128)(2,1)}, bf16[128,768]{1,0:T(8,128)(2,1)S(1)}, u32[]{:S(2)}, u32[]{:S(2)}) %collective-permute-start.5) | collective-permute-done | bytes 196640 | tf_op jit(solution)/shard_map/ppermute | solution.py:410
  51.6 5.8 %all-to-all-done.chunks_ref = bf16[16,3,128,128]{3,2,1,0:T(8,128)(2,1)S(1)} async-done(((bf16[16,3,128,128]{3,2,1,0:T(8,128)(2,1)}), bf16[16,3,128,128]{3,2,1,0:T(8,128)(2,1)S(1)}, u32[]{:S(2)}, u32[]{:S(2)}) %all-to-all-start) | async-done | bytes 1572896 | tf_op jit(solution)/shard_map/all_to_all | solution.py:424
  60.6 4.8 %all-to-all-start.1 = ((bf16[16,1,128,128]{3,2,1,0:T(8,128)(2,1)}), bf16[16,1,128,128]{3,2,1,0:T(8,128)(2,1)S(1)}, u32[]{:S(2)}, u32[]{:S(2)}) async-start(bf16[16,1,128,128]{3,2,1,0:T(8,128)(2,1)} %pack.3), calls=%async_computation.1 | async-start | bytes 1048576 | tf_op jit(solution)/shard_map/all_to_all | solution.py:429
  69.0 13.8 %forward.1 = (bf16[2048,128]{1,0:T(8,128)(2,1)S(1)}, f32[2048,128]{1,0:T(8,128)S(1)}) custom-call(s32[16]{0:T(128)S(1)} %get-tuple-element.68.full_ref, s32[16]{0:T(128)S(1)} %get-tuple-element.64.kcnt_ref, s32[16,10]{1,0:T(8,128)S(1)} %copy.11.kidx_ref, bf16[2048,128]{1,0:T(8,128)(2,1)S(1)} %get-tuple-element.36.q_ref, ...), custom_call_target="tpu_custom_call" | custom-call | flops 16000000000 | bytes 5242880 | tf_op jit(solution)/shard_map/forward/pallas_call | solution.py:442
  83.9 3.1 %collective-permute-start.9 = (bf16[2048,128]{1,0:T(8,128)(2,1)S(1)}, bf16[2048,128]{1,0:T(8,128)(2,1)S(1)}, u32[]{:S(2)}, u32[]{:S(2)}) collective-permute-start(bf16[2048,128]{1,0:T(8,128)(2,1)S(1)} %get-tuple-element.47.o_ref.refs_0_.attn_ref), channel_id=1, source_target_pairs={{0,6},{2,4},{4,2},{10,12},{12,10},{14,8},{16,22},{20,18},{22,16},{... | collective-permute-start | bytes 1572872 | tf_op jit(solution)/shard_map/ppermute | solution.py:458
  88.3 4.0 %collective-permute-start.7 = (bf16[2048,128]{1,0:T(8,128)(2,1)S(1)}, bf16[2048,128]{1,0:T(8,128)(2,1)S(1)}, u32[]{:S(2)}, u32[]{:S(2)}) collective-permute-start(bf16[2048,128]{1,0:T(8,128)(2,1)S(1)} %get-tuple-element.47.o_ref.refs_0_.attn_ref), channel_id=1, source_target_pairs={{0,2},{2,0},{4,6},{10,8},{12,14},{14,12},{16,18},{20,22},{22,20},{... | collective-permute-start | bytes 1572872 | tf_op jit(solution)/shard_map/ppermute | solution.py:458
  92.3 8.8 %collective-permute-done.9.refs_3_ = bf16[2048,128]{1,0:T(8,128)(2,1)S(1)} collective-permute-done((bf16[2048,128]{1,0:T(8,128)(2,1)S(1)}, bf16[2048,128]{1,0:T(8,128)(2,1)S(1)}, u32[]{:S(2)}, u32[]{:S(2)}) %collective-permute-start.9) | collective-permute-done | bytes 524320 | tf_op jit(solution)/shard_map/ppermute | solution.py:458
  101.9 8.5 %collective-permute-done.8.refs_2_ = bf16[2048,128]{1,0:T(8,128)(2,1)S(1)} collective-permute-done((bf16[2048,128]{1,0:T(8,128)(2,1)S(1)}, bf16[2048,128]{1,0:T(8,128)(2,1)S(1)}, u32[]{:S(2)}, u32[]{:S(2)}) %collective-permute-start.8) | collective-permute-done | bytes 524320 | tf_op jit(solution)/shard_map/ppermute | solution.py:458
  114.5 21.1 %backward.1 = (bf16[2048,128]{1,0:T(8,128)(2,1)S(1)}, bf16[2,2048,128]{2,1,0:T(8,128)(2,1)S(1)}, bf16[2,2048,128]{2,1,0:T(8,128)(2,1)}) custom-call(s32[16]{0:T(128)S(1)} %get-tuple-element.68.full_ref, s32[16]{0:T(128)S(1)} %get-tuple-element.64.kcnt_ref, s32[16,10]{1,0:T(8,128)S(1)} %copy.11.kidx_ref, bf16[2048,128]{1,0:T(8,128)(2,1)S(1)} %copy-done.27, ...), custom_call_target="tpu_custom_call" | custom-call | flops 20000000000 | bytes 8388608 | tf_op jit(solution)/shard_map/backward/pallas_call | solution.py:462
  138.7 4.8 %tile.1 = (f32[384,768]{1,0:T(8,128)S(1)}, bf16[384,768]{1,0:T(8,128)(2,1)S(1)}) custom-call(s32[2]{0:T(128)S(1)} %pad_add_fusion.where_ref, bf16[2048,128]{1,0:T(8,128)(2,1)S(1)} %get-tuple-element.47.o_ref.refs_0_.attn_ref, bf16[2048,128]{1,0:T(8,128)(2,1)S(1)} %copy-done.33, bf16[2048,128]{1,0:T(8,128)(2,1)S(1)} %copy-done.31, ...), custom_call_target="tpu_custom_call" | custom-call | flops 5000000000 | bytes 4194304 | tf_op jit(solution)/shard_map/tile/pallas_call | solution.py:490
  148.1 2.1 unjoin.1
  150.2 9.1 %collective-permute-done.11 = bf16[384,768]{1,0:T(8,128)(2,1)} collective-permute-done((bf16[384,768]{1,0:T(8,128)(2,1)}, bf16[384,768]{1,0:T(8,128)(2,1)}, u32[]{:S(2)}, u32[]{:S(2)}) %collective-permute-start.11) | collective-permute-done | bytes 589856 | tf_op jit(solution)/shard_map/ppermute | solution.py:305
  160.5 10.5 %all-to-all-start.2 = ((bf16[16,4,128,128]{3,2,1,0:T(8,128)(2,1)}), bf16[16,4,128,128]{3,2,1,0:T(8,128)(2,1)S(1)}, u32[]{:S(2)}, u32[]{:S(2)}) async-start(bf16[16,4,128,128]{3,2,1,0:T(8,128)(2,1)} %unjoin.1), calls=%async_computation.2 | async-start | bytes 4194304 | tf_op jit(solution)/shard_map/all_to_all | solution.py:318
  172.7 45.3 %collective-permute-done.16.refs_5_ = bf16[384,768]{1,0:T(8,128)(2,1)S(1)} collective-permute-done((bf16[384,768]{1,0:T(8,128)(2,1)S(1)}, bf16[384,768]{1,0:T(8,128)(2,1)S(1)}, u32[]{:S(2)}, u32[]{:S(2)}) %collective-permute-start.16) | collective-permute-done | bytes 589856 | tf_op jit(solution)/shard_map/ppermute | solution.py:308
  221.1 10.2 %collective-permute-done.18.refs_7_ = bf16[384,768]{1,0:T(8,128)(2,1)S(1)} collective-permute-done((bf16[384,768]{1,0:T(8,128)(2,1)S(1)}, bf16[384,768]{1,0:T(8,128)(2,1)S(1)}, u32[]{:S(2)}, u32[]{:S(2)}) %collective-permute-start.18) | collective-permute-done | bytes 589856 | tf_op jit(solution)/shard_map/ppermute | solution.py:308
  232.6 4.4 %collective-permute-done.15.refs_4_ = bf16[192,768]{1,0:T(8,128)(2,1)S(1)} collective-permute-done((bf16[192,768]{1,0:T(8,128)(2,1)S(1)}, bf16[192,768]{1,0:T(8,128)(2,1)S(1)}, u32[]{:S(2)}, u32[]{:S(2)}) %collective-permute-start.15) | collective-permute-done | bytes 294944 | tf_op jit(solution)/shard_map/ppermute | solution.py:308
  238.5 4.9 %collective-permute-done.20.refs_9_ = bf16[192,768]{1,0:T(8,128)(2,1)S(1)} collective-permute-done((bf16[192,768]{1,0:T(8,128)(2,1)S(1)}, bf16[192,768]{1,0:T(8,128)(2,1)S(1)}, u32[]{:S(2)}, u32[]{:S(2)}) %collective-permute-start.20) | collective-permute-done | bytes 294944 | tf_op jit(solution)/shard_map/ppermute | solution.py:308
  247.4 3.0 %collective-permute-start.22 = (bf16[6,4,128,128]{3,2,1,0:T(8,128)(2,1)}, bf16[6,4,128,128]{3,2,1,0:T(8,128)(2,1)S(1)}, u32[]{:S(2)}, u32[]{:S(2)}) collective-permute-start(bf16[6,4,128,128]{3,2,1,0:T(8,128)(2,1)} %get-tuple-element.59), channel_id=1, source_target_pairs={{0,1},{1,0},{2,3},{3,2},{4,5},{5,4},{6,7},{7,6},{8,9},{9,8},{10,11... | collective-permute-start | bytes 2359304 | tf_op jit(solution)/shard_map/ppermute | solution.py:541
  250.4 2.1 collective-permute-done.22.refs_1_
  255.4 3.8 %fusion.8 = f32[256,3072]{1,0:T(8,128)S(1)} fusion(bf16[256,768]{1,0:T(8,128)(2,1)S(1)} %get-tuple-element.60, bf16[768,3072]{1,0:T(8,128)(2,1)} %param.11), kind=kOutput, calls=%fused_computation.56 | convolution fusion | flops 1207959552 | bytes 8257536 | tf_op jit(solution)/shard_map/dot_general | solution.py:27
  266.5 5.4 %place.1 = f32[768,3072]{1,0:T(8,128)} custom-call(s32[2]{0:T(128)S(1)} %pad_add_fusion.2.place_ref, bf16[384,768]{1,0:T(8,128)(2,1)S(1)} %broadcast_select_fusion.2.refs_0_, bf16[384,768]{1,0:T(8,128)(2,1)S(1)} %copy-done.2, bf16[384,768]{1,0:T(8,128)(2,1)S(1)} %collective-permute-done.13.refs_2_, bf16[192,768]{1,0:T(8,128)(2,1)S(1)} %copy-done.17, ...), custom_call_target="tpu_custom_call" | custom-call | bytes 16777216 | tf_op jit(solution)/shard_map/place/pallas_call | solution.py:321
  271.9 2.2 add_convert_fusion
  (153 shorter events, 67.0 us)
Async XLA Ops:
  13.8 43.6 %all-to-all-start = ((bf16[16,3,128,128]{3,2,1,0:T(8,128)(2,1)}), bf16[16,3,128,128]{3,2,1,0:T(8,128)(2,1)S(1)}, u32[]{:S(2)}, u32[]{:S(2)}) async-start(bf16[16,3,128,128]{3,2,1,0:T(8,128)(2,1)} %pack.2), calls=%async_computation | async-start | bytes 3145728 | tf_op jit(solution)/shard_map/all_to_all | solution.py:424
  20.5 115.1 %all-gather.3.cloned.1.call-start = ((), (), s32[]{:S(2)}) async-start(), calls=%async_computation.3 | async-start | bytes 3932160 | tf_op jit(solution)/shard_map/all_gather | solution.py:427
  29.4 6.2 %collective-permute-start.2 = (bf16[1,128,768]{2,1,0:T(8,128)(2,1)}, bf16[1,128,768]{2,1,0:T(8,128)(2,1)S(1)}, u32[]{:S(2)}, u32[]{:S(2)}) collective-permute-start(bf16[1,128,768]{2,1,0:T(8,128)(2,1)} %dynamic-slice_bitcast_fusion), channel_id=1, source_target_pairs={{0,1},{1,0},{2,3},{3,2},{4,5},{5,4},{6,7},{7,6},{8,9},{9,8},{10,11... | collective-permute-start | bytes 589832 | tf_op jit(solution)/shard_map/ppermute | solution.py:388
  31.5 16.6 %collective-permute-start.5 = (bf16[128,768]{1,0:T(8,128)(2,1)}, bf16[128,768]{1,0:T(8,128)(2,1)S(1)}, u32[]{:S(2)}, u32[]{:S(2)}) collective-permute-start(bf16[128,768]{1,0:T(8,128)(2,1)} %get-tuple-element.70), channel_id=1, source_target_pairs={{0,6},{2,4},{4,2},{6,0},{8,14},{10,12},{12,10},{14,8},{16,22},{18,... | collective-permute-start | bytes 589832 | tf_op jit(solution)/shard_map/ppermute | solution.py:410
  32.7 17.4 %collective-permute-start.3 = (bf16[128,768]{1,0:T(8,128)(2,1)}, bf16[128,768]{1,0:T(8,128)(2,1)S(1)}, u32[]{:S(2)}, u32[]{:S(2)}) collective-permute-start(bf16[128,768]{1,0:T(8,128)(2,1)} %get-tuple-element.72), channel_id=1, source_target_pairs={{0,2},{2,0},{4,6},{6,4},{8,10},{10,8},{12,14},{14,12},{16,18},{18,... | collective-permute-start | bytes 589832 | tf_op jit(solution)/shard_map/ppermute | solution.py:410
  33.0 17.1 %collective-permute-start.4 = (bf16[128,768]{1,0:T(8,128)(2,1)S(1)}, bf16[128,768]{1,0:T(8,128)(2,1)S(1)}, u32[]{:S(2)}, u32[]{:S(2)}) collective-permute-start(bf16[128,768]{1,0:T(8,128)(2,1)S(1)} %get-tuple-element.73), channel_id=1, source_target_pairs={{0,4},{2,6},{4,0},{6,2},{8,12},{10,14},{12,8},{14,10},{16,20},{18,... | collective-permute-start | bytes 589832 | tf_op jit(solution)/shard_map/ppermute | solution.py:410
  58.0 7.3 %collective-permute-start.6 = (bf16[2,2048,128]{2,1,0:T(8,128)(2,1)S(1)}, bf16[2,2048,128]{2,1,0:T(8,128)(2,1)S(1)}, u32[]{:S(2)}, u32[]{:S(2)}) collective-permute-start(bf16[2,2048,128]{2,1,0:T(8,128)(2,1)S(1)} %get-tuple-element.37.refs_0_.refs_1_), channel_id=1, source_target_pairs={{0,1},{1,0},{2,3},{3,2},{4,5},{5,4},{6,7},{7,6},{8,9},{9,8},{10,11... | collective-permute-start | bytes 3145736 | tf_op jit(solution)/shard_map/ppermute | solution.py:434
  60.6 51.7 %all-to-all-start.1 = ((bf16[16,1,128,128]{3,2,1,0:T(8,128)(2,1)}), bf16[16,1,128,128]{3,2,1,0:T(8,128)(2,1)S(1)}, u32[]{:S(2)}, u32[]{:S(2)}) async-start(bf16[16,1,128,128]{3,2,1,0:T(8,128)(2,1)} %pack.3), calls=%async_computation.1 | async-start | bytes 1048576 | tf_op jit(solution)/shard_map/all_to_all | solution.py:429
  83.9 17.2 %collective-permute-start.9 = (bf16[2048,128]{1,0:T(8,128)(2,1)S(1)}, bf16[2048,128]{1,0:T(8,128)(2,1)S(1)}, u32[]{:S(2)}, u32[]{:S(2)}) collective-permute-start(bf16[2048,128]{1,0:T(8,128)(2,1)S(1)} %get-tuple-element.47.o_ref.refs_0_.attn_ref), channel_id=1, source_target_pairs={{0,6},{2,4},{4,2},{10,12},{12,10},{14,8},{16,22},{20,18},{22,16},{... | collective-permute-start | bytes 1572872 | tf_op jit(solution)/shard_map/ppermute | solution.py:458
  87.0 23.4 %collective-permute-start.8 = (bf16[2048,128]{1,0:T(8,128)(2,1)S(1)}, bf16[2048,128]{1,0:T(8,128)(2,1)S(1)}, u32[]{:S(2)}, u32[]{:S(2)}) collective-permute-start(bf16[2048,128]{1,0:T(8,128)(2,1)S(1)} %get-tuple-element.47.o_ref.refs_0_.attn_ref), channel_id=1, source_target_pairs={{0,4},{2,6},{4,0},{10,14},{12,8},{14,10},{16,20},{20,16},{22,18},{... | collective-permute-start | bytes 1572872 | tf_op jit(solution)/shard_map/ppermute | solution.py:458
  88.3 23.1 %collective-permute-start.7 = (bf16[2048,128]{1,0:T(8,128)(2,1)S(1)}, bf16[2048,128]{1,0:T(8,128)(2,1)S(1)}, u32[]{:S(2)}, u32[]{:S(2)}) collective-permute-start(bf16[2048,128]{1,0:T(8,128)(2,1)S(1)} %get-tuple-element.47.o_ref.refs_0_.attn_ref), channel_id=1, source_target_pairs={{0,2},{2,0},{4,6},{10,8},{12,14},{14,12},{16,18},{20,22},{22,20},{... | collective-permute-start | bytes 1572872 | tf_op jit(solution)/shard_map/ppermute | solution.py:458
  146.6 12.7 %collective-permute-start.11 = (bf16[384,768]{1,0:T(8,128)(2,1)}, bf16[384,768]{1,0:T(8,128)(2,1)}, u32[]{:S(2)}, u32[]{:S(2)}) collective-permute-start(bf16[384,768]{1,0:T(8,128)(2,1)} %add_convert_fusion.1), channel_id=1, source_target_pairs={{0,16},{2,18},{4,20},{6,22},{8,24},{10,26},{12,28},{14,30},{17,1},... | collective-permute-start | bytes 1769480 | tf_op jit(solution)/shard_map/ppermute | solution.py:305
  160.5 84.4 %all-to-all-start.2 = ((bf16[16,4,128,128]{3,2,1,0:T(8,128)(2,1)}), bf16[16,4,128,128]{3,2,1,0:T(8,128)(2,1)S(1)}, u32[]{:S(2)}, u32[]{:S(2)}) async-start(bf16[16,4,128,128]{3,2,1,0:T(8,128)(2,1)} %unjoin.1), calls=%async_computation.2 | async-start | bytes 4194304 | tf_op jit(solution)/shard_map/all_to_all | solution.py:318
  171.0 47.0 %collective-permute-start.16 = (bf16[384,768]{1,0:T(8,128)(2,1)S(1)}, bf16[384,768]{1,0:T(8,128)(2,1)S(1)}, u32[]{:S(2)}, u32[]{:S(2)}) collective-permute-start(bf16[384,768]{1,0:T(8,128)(2,1)S(1)} %broadcast_select_fusion.2.refs_0_), channel_id=1, source_target_pairs={{0,8},{2,10},{4,12},{6,14},{8,0},{10,2},{12,4},{14,6},{16,24},{18,... | collective-permute-start | bytes 1769480 | tf_op jit(solution)/shard_map/ppermute | solution.py:308
  171.4 47.4 %collective-permute-start.13 = (bf16[384,768]{1,0:T(8,128)(2,1)S(1)}, bf16[384,768]{1,0:T(8,128)(2,1)S(1)}, u32[]{:S(2)}, u32[]{:S(2)}) collective-permute-start(bf16[384,768]{1,0:T(8,128)(2,1)S(1)} %broadcast_select_fusion.2.refs_0_), channel_id=1, source_target_pairs={{0,4},{2,6},{4,0},{6,2},{8,12},{10,14},{12,8},{14,10},{16,20},{18,... | collective-permute-start | bytes 1769480 | tf_op jit(solution)/shard_map/ppermute | solution.py:308
  171.4 48.2 %collective-permute-start.12 = (bf16[384,768]{1,0:T(8,128)(2,1)S(1)}, bf16[384,768]{1,0:T(8,128)(2,1)S(1)}, u32[]{:S(2)}, u32[]{:S(2)}) collective-permute-start(bf16[384,768]{1,0:T(8,128)(2,1)S(1)} %broadcast_select_fusion.2.refs_0_), channel_id=1, source_target_pairs={{0,2},{2,0},{4,6},{6,4},{8,10},{10,8},{12,14},{14,12},{16,18},{18,... | collective-permute-start | bytes 1769480 | tf_op jit(solution)/shard_map/ppermute | solution.py:308
  218.0 13.3 %collective-permute-start.18 = (bf16[384,768]{1,0:T(8,128)(2,1)S(1)}, bf16[384,768]{1,0:T(8,128)(2,1)S(1)}, u32[]{:S(2)}, u32[]{:S(2)}) collective-permute-start(bf16[384,768]{1,0:T(8,128)(2,1)S(1)} %collective-permute-done.16.refs_5_), channel_id=1, source_target_pairs={{0,4},{2,6},{4,0},{6,2},{8,12},{10,14},{12,8},{14,10},{16,20},{18,... | collective-permute-start | bytes 1769480 | tf_op jit(solution)/shard_map/ppermute | solution.py:308
  218.0 13.7 %collective-permute-start.17 = (bf16[384,768]{1,0:T(8,128)(2,1)S(1)}, bf16[384,768]{1,0:T(8,128)(2,1)S(1)}, u32[]{:S(2)}, u32[]{:S(2)}) collective-permute-start(bf16[384,768]{1,0:T(8,128)(2,1)S(1)} %collective-permute-done.16.refs_5_), channel_id=1, source_target_pairs={{0,2},{2,0},{4,6},{6,4},{8,10},{10,8},{12,14},{14,12},{16,18},{18,... | collective-permute-start | bytes 1769480 | tf_op jit(solution)/shard_map/ppermute | solution.py:308
  218.8 18.3 %collective-permute-start.15 = (bf16[192,768]{1,0:T(8,128)(2,1)S(1)}, bf16[192,768]{1,0:T(8,128)(2,1)S(1)}, u32[]{:S(2)}, u32[]{:S(2)}) collective-permute-start(bf16[192,768]{1,0:T(8,128)(2,1)S(1)} %slice.21), channel_id=1, source_target_pairs={{0,2},{2,0},{4,6},{6,4},{8,10},{10,8},{12,14},{14,12},{16,18},{18,... | collective-permute-start | bytes 884744 | tf_op jit(solution)/shard_map/ppermute | solution.py:308
  219.6 18.2 %collective-permute-start.14 = (bf16[192,768]{1,0:T(8,128)(2,1)S(1)}, bf16[192,768]{1,0:T(8,128)(2,1)S(1)}, u32[]{:S(2)}, u32[]{:S(2)}) collective-permute-start(bf16[192,768]{1,0:T(8,128)(2,1)S(1)} %slice.20), channel_id=1, source_target_pairs={{0,4},{2,6},{4,0},{6,2},{8,12},{10,14},{12,8},{14,10},{16,20},{18,... | collective-permute-start | bytes 884744 | tf_op jit(solution)/shard_map/ppermute | solution.py:308
  231.4 12.0 %collective-permute-start.20 = (bf16[192,768]{1,0:T(8,128)(2,1)S(1)}, bf16[192,768]{1,0:T(8,128)(2,1)S(1)}, u32[]{:S(2)}, u32[]{:S(2)}) collective-permute-start(bf16[192,768]{1,0:T(8,128)(2,1)S(1)} %slice.23), channel_id=1, source_target_pairs={{0,2},{2,0},{4,6},{6,4},{8,10},{10,8},{12,14},{14,12},{16,18},{18,... | collective-permute-start | bytes 884744 | tf_op jit(solution)/shard_map/ppermute | solution.py:308
  231.8 12.4 %collective-permute-start.19 = (bf16[192,768]{1,0:T(8,128)(2,1)S(1)}, bf16[192,768]{1,0:T(8,128)(2,1)S(1)}, u32[]{:S(2)}, u32[]{:S(2)}) collective-permute-start(bf16[192,768]{1,0:T(8,128)(2,1)S(1)} %slice.22), channel_id=1, source_target_pairs={{0,4},{2,6},{4,0},{6,2},{8,12},{10,14},{12,8},{14,10},{16,20},{18,... | collective-permute-start | bytes 884744 | tf_op jit(solution)/shard_map/ppermute | solution.py:308
  247.4 5.1 %collective-permute-start.22 = (bf16[6,4,128,128]{3,2,1,0:T(8,128)(2,1)}, bf16[6,4,128,128]{3,2,1,0:T(8,128)(2,1)S(1)}, u32[]{:S(2)}, u32[]{:S(2)}) collective-permute-start(bf16[6,4,128,128]{3,2,1,0:T(8,128)(2,1)} %get-tuple-element.59), channel_id=1, source_target_pairs={{0,1},{1,0},{2,3},{3,2},{4,5},{5,4},{6,7},{7,6},{8,9},{9,8},{10,11... | collective-permute-start | bytes 2359304 | tf_op jit(solution)/shard_map/ppermute | solution.py:541
  261.9 10.0 %collective-permute-start.23 = (bf16[256,1536]{1,0:T(8,128)(2,1)}, bf16[256,1536]{1,0:T(8,128)(2,1)}, u32[]{:S(2)}, u32[]{:S(2)}) collective-permute-start(bf16[256,1536]{1,0:T(8,128)(2,1)} %dynamic-slice_convert_fusion), channel_id=1, source_target_pairs={{0,1},{1,0},{2,3},{3,2},{4,5},{5,4},{6,7},{7,6},{8,9},{9,8},{10,11... | collective-permute-start | bytes 2359304 | tf_op jit(solution)/shard_map/ppermute | solution.py:549
  (43 other events, 205.6 us)
Sparse Core Ops, SparseCore 0:
  59.7 68.5 all-gather.2

commit v13 on v12

--- a/solution.py
+++ b/solution.py
@@ -308,8 +308,8 @@
         return lax.ppermute(x, "ctx", [(i, i ^ k) for i in range(n)])
 
     first = jnp.where(plane // 2 == core, tile_sum, from_half)
-    _, sent = lax.optimization_barrier((first, sent))
     second = swap(first, in_plane)
+    _, sent = lax.optimization_barrier((second, sent))
     beside, above = swap(first, 1), swap(first, 2)
     middle = tile_rows // 2
     sources = [first, beside, above, swap(beside[:middle], 2), swap(above[middle:], 1)]

time: 287 us -> 283 us (0.986)
  starting transfers between devices: 48.2 us -> 53.9 us
  local copies, waits for them, and re-layouts: 28.4 us -> 23.2 us
  waiting for transfers between devices: 118 us -> 115 us
    ppermute x9, starting transfers between devices: 6.03 us -> 14.1 us  [swap(): return lax.ppermute(x, 'ctx', [(i, i ^ k) for i in range(n)])]
    all_to_all x1, starting transfers between devices: 10.5 us -> 5.14 us  [gather_tiles_by_core(): chunks = lax.all_to_all(sent, 'ctx', 0, 0, tiled=True)]
    unnamed x78 -> x68, local copies, waits for them, and re-layouts: 23.2 us -> 18 us
    ppermute x1, starting transfers between devices: 0.5 us -> 4.59 us  [per_device(): lax.ppermute(dkv[s], 'tp', [(c, (c - s) % t) for c in range(t)])]
    ppermute x1, waiting for transfers between devices: 9.09 us -> 5.87 us  [gather_tiles_by_core(): from_half = lax.ppermute(tile_sum, ('ctx', 'tp'), across)]
  transfers between devices with their start and end apart: 28 -> 28, of which waited for: 15 -> 17; matrix products, arithmetic and copies ran while one was open for 4% -> 4% of each run, Pallas kernels for 16% -> 17%
where the time goes in v13:
time: 283 us; the launch traced here: 280 us
  waiting for transfers between devices  115 us (41%)
  Pallas kernels  57.6 us (20%)
  starting transfers between devices  53.9 us (19%)
  local copies, waits for them, and re-layouts  23.2 us (8%)
  between operations  14.4 us (5%)
  other arithmetic  8.48 us (3%)
  matrix products  7.59 us (3%)
    ppermute x9, waiting for transfers between devices, swap(): return lax.ppermute(x, 'ctx', [(i, i ^ k) for i in range(n)])  62.7 us
    pallas_call x1, Pallas kernels, per_device(): pl.pallas_call(functools.partial(backward_kernel, t, tile, count), grid_s...  21.1 us
    ppermute x3, waiting for transfers between devices, per_device(): lax.ppermute(attn, 'ctx', [(i, i ^ k) for i in range(n) if held[i]])  19.5 us
    unnamed x68, local copies, waits for them, and re-layouts  18 us
    ppermute x9, starting transfers between devices, swap(): return lax.ppermute(x, 'ctx', [(i, i ^ k) for i in range(n)])  14.1 us
    pallas_call x1, Pallas kernels, per_device(): pl.pallas_call(functools.partial(forward_kernel, t, tile, count), grid_sp...  13.8 us
    ppermute x3, waiting for transfers between devices, per_device(): plane_got.append(lax.ppermute(there, 'ctx', [(i, i ^ k) for i in range(n)]))  13.1 us
    pallas_call x7, Pallas kernels, simple_call(): pl.pallas_call(kernel, grid_spec=pltpu.PrefetchScalarGridSpec(num_scalar_...  11.1 us
  transfers between devices with their start and end apart: 28, of which 17 were waited for; matrix products, arithmetic and copies ran while one was open for 4% of the time, Pallas kernels for 17%

profile of v13, /device:TPU:13, one launch (start us, length us, event | category | flops | bytes accessed | tf_op | source)
XLA Modules:
  0.0 279.8 jit_solution(6538782093315190937)
XLA Ops:
  13.8 6.7 %all-to-all-start = ((bf16[16,3,128,128]{3,2,1,0:T(8,128)(2,1)}), bf16[16,3,128,128]{3,2,1,0:T(8,128)(2,1)S(1)}, u32[]{:S(2)}, u32[]{:S(2)}) async-start(bf16[16,3,128,128]{3,2,1,0:T(8,128)(2,1)} %pack.2), calls=%async_computation | async-start | bytes 3145728 | tf_op jit(solution)/shard_map/all_to_all | solution.py:424
  24.9 3.8 %fusion.1.refs_0_ = bf16[256,768]{1,0:T(8,128)(2,1)S(1)} fusion(bf16[768,3072]{1,0:T(8,128)(2,1)} %param.11, bf16[256,1536]{1,0:T(8,128)(2,1)S(1)} %get-tuple-element.75, bf16[256,1536]{1,0:T(8,128)(2,1)S(1)} %get-tuple-element.74), kind=kOutput, calls=%fused_computation.14 | convolution fusion | flops 1211301888 | bytes 6684672 | tf_op jit(solution)/shard_map/dot_general | solution.py:27
  37.0 11.1 %collective-permute-done.5.refs_3_ = bf16[128,768]{1,0:T(8,128)(2,1)S(1)} collective-permute-done((bf16[128,768]{1,0:T(8,128)(2,1)}, bf16[128,768]{1,0:T(8,128)(2,1)S(1)}, u32[]{:S(2)}, u32[]{:S(2)}) %collective-permute-start.5) | collective-permute-done | bytes 196640 | tf_op jit(solution)/shard_map/ppermute | solution.py:410
  51.6 5.8 %all-to-all-done.chunks_ref = bf16[16,3,128,128]{3,2,1,0:T(8,128)(2,1)S(1)} async-done(((bf16[16,3,128,128]{3,2,1,0:T(8,128)(2,1)}), bf16[16,3,128,128]{3,2,1,0:T(8,128)(2,1)S(1)}, u32[]{:S(2)}, u32[]{:S(2)}) %all-to-all-start) | async-done | bytes 1572896 | tf_op jit(solution)/shard_map/all_to_all | solution.py:424
  60.6 4.8 %all-to-all-start.1 = ((bf16[16,1,128,128]{3,2,1,0:T(8,128)(2,1)}), bf16[16,1,128,128]{3,2,1,0:T(8,128)(2,1)S(1)}, u32[]{:S(2)}, u32[]{:S(2)}) async-start(bf16[16,1,128,128]{3,2,1,0:T(8,128)(2,1)} %pack.3), calls=%async_computation.1 | async-start | bytes 1048576 | tf_op jit(solution)/shard_map/all_to_all | solution.py:429
  66.9 13.8 %forward.1 = (bf16[2048,128]{1,0:T(8,128)(2,1)S(1)}, f32[2048,128]{1,0:T(8,128)S(1)}) custom-call(s32[16]{0:T(128)S(1)} %get-tuple-element.68.full_ref, s32[16]{0:T(128)S(1)} %get-tuple-element.64.kcnt_ref, s32[16,10]{1,0:T(8,128)S(1)} %copy.11.kidx_ref, bf16[2048,128]{1,0:T(8,128)(2,1)S(1)} %copy-done.25, ...), custom_call_target="tpu_custom_call" | custom-call | flops 16000000000 | bytes 5242880 | tf_op jit(solution)/shard_map/forward/pallas_call | solution.py:442
  81.7 3.1 %collective-permute-start.9 = (bf16[2048,128]{1,0:T(8,128)(2,1)S(1)}, bf16[2048,128]{1,0:T(8,128)(2,1)S(1)}, u32[]{:S(2)}, u32[]{:S(2)}) collective-permute-start(bf16[2048,128]{1,0:T(8,128)(2,1)S(1)} %get-tuple-element.47.o_ref.refs_0_.attn_ref), channel_id=1, source_target_pairs={{0,6},{2,4},{4,2},{10,12},{12,10},{14,8},{16,22},{20,18},{22,16},{... | collective-permute-start | bytes 1572872 | tf_op jit(solution)/shard_map/ppermute | solution.py:458
  86.1 4.0 %collective-permute-start.7 = (bf16[2048,128]{1,0:T(8,128)(2,1)S(1)}, bf16[2048,128]{1,0:T(8,128)(2,1)S(1)}, u32[]{:S(2)}, u32[]{:S(2)}) collective-permute-start(bf16[2048,128]{1,0:T(8,128)(2,1)S(1)} %get-tuple-element.47.o_ref.refs_0_.attn_ref), channel_id=1, source_target_pairs={{0,2},{2,0},{4,6},{10,8},{12,14},{14,12},{16,18},{20,22},{22,20},{... | collective-permute-start | bytes 1572872 | tf_op jit(solution)/shard_map/ppermute | solution.py:458
  90.1 8.9 %collective-permute-done.9.refs_3_ = bf16[2048,128]{1,0:T(8,128)(2,1)S(1)} collective-permute-done((bf16[2048,128]{1,0:T(8,128)(2,1)S(1)}, bf16[2048,128]{1,0:T(8,128)(2,1)S(1)}, u32[]{:S(2)}, u32[]{:S(2)}) %collective-permute-start.9) | collective-permute-done | bytes 524320 | tf_op jit(solution)/shard_map/ppermute | solution.py:458
  99.0 9.2 %collective-permute-done.8.refs_2_ = bf16[2048,128]{1,0:T(8,128)(2,1)S(1)} collective-permute-done((bf16[2048,128]{1,0:T(8,128)(2,1)S(1)}, bf16[2048,128]{1,0:T(8,128)(2,1)S(1)}, u32[]{:S(2)}, u32[]{:S(2)}) %collective-permute-start.8) | collective-permute-done | bytes 524320 | tf_op jit(solution)/shard_map/ppermute | solution.py:458
  112.6 21.1 %backward.1 = (bf16[2048,128]{1,0:T(8,128)(2,1)S(1)}, bf16[2,2048,128]{2,1,0:T(8,128)(2,1)S(1)}, bf16[2,2048,128]{2,1,0:T(8,128)(2,1)}) custom-call(s32[16]{0:T(128)S(1)} %get-tuple-element.68.full_ref, s32[16]{0:T(128)S(1)} %get-tuple-element.64.kcnt_ref, s32[16,10]{1,0:T(8,128)S(1)} %copy.11.kidx_ref, bf16[2048,128]{1,0:T(8,128)(2,1)S(1)} %copy-done.26, ...), custom_call_target="tpu_custom_call" | custom-call | flops 20000000000 | bytes 8388608 | tf_op jit(solution)/shard_map/backward/pallas_call | solution.py:462
  135.5 4.8 %tile.1 = (f32[384,768]{1,0:T(8,128)S(1)}, bf16[384,768]{1,0:T(8,128)(2,1)S(1)}) custom-call(s32[2]{0:T(128)S(1)} %pad_add_fusion.where_ref, bf16[2048,128]{1,0:T(8,128)(2,1)S(1)} %get-tuple-element.47.o_ref.refs_0_.attn_ref, bf16[2048,128]{1,0:T(8,128)(2,1)S(1)} %copy-done.28, bf16[2048,128]{1,0:T(8,128)(2,1)S(1)} %collective-permute-done.8.refs_2_, ...), custom_call_target="tpu_custom_call" | custom-call | flops 5000000000 | bytes 4194304 | tf_op jit(solution)/shard_map/tile/pallas_call | solution.py:490
  144.8 4.6 %collective-permute-start.21 = (bf16[2,2048,128]{2,1,0:T(8,128)(2,1)}, bf16[2,2048,128]{2,1,0:T(8,128)(2,1)S(1)}, u32[]{:S(2)}, u32[]{:S(2)}) collective-permute-start(bf16[2,2048,128]{2,1,0:T(8,128)(2,1)} %get-tuple-element.55), channel_id=1, source_target_pairs={{0,1},{1,0},{2,3},{3,2},{4,5},{5,4},{6,7},{7,6},{8,9},{9,8},{10,11... | collective-permute-start | bytes 3145736 | tf_op jit(solution)/shard_map/ppermute | solution.py:478
  149.4 5.9 %collective-permute-done.11 = bf16[384,768]{1,0:T(8,128)(2,1)} collective-permute-done((bf16[384,768]{1,0:T(8,128)(2,1)}, bf16[384,768]{1,0:T(8,128)(2,1)}, u32[]{:S(2)}, u32[]{:S(2)}) %collective-permute-start.11) | collective-permute-done | bytes 589856 | tf_op jit(solution)/shard_map/ppermute | solution.py:305
  156.4 7.0 %collective-permute-start.16 = (bf16[384,768]{1,0:T(8,128)(2,1)S(1)}, bf16[384,768]{1,0:T(8,128)(2,1)}, u32[]{:S(2)}, u32[]{:S(2)}) collective-permute-start(bf16[384,768]{1,0:T(8,128)(2,1)S(1)} %broadcast_select_fusion.2.refs_0_), channel_id=1, source_target_pairs={{0,8},{2,10},{4,12},{6,14},{8,0},{10,2},{12,4},{14,6},{16,24},{18,... | collective-permute-start | bytes 1769480 | tf_op jit(solution)/shard_map/ppermute | solution.py:308
  166.6 9.8 %collective-permute-done.16.refs_5_ = bf16[384,768]{1,0:T(8,128)(2,1)} collective-permute-done((bf16[384,768]{1,0:T(8,128)(2,1)S(1)}, bf16[384,768]{1,0:T(8,128)(2,1)}, u32[]{:S(2)}, u32[]{:S(2)}) %collective-permute-start.16) | collective-permute-done | bytes 589856 | tf_op jit(solution)/shard_map/ppermute | solution.py:308
  176.4 5.1 %all-to-all-start.2 = ((bf16[16,4,128,128]{3,2,1,0:T(8,128)(2,1)}), bf16[16,4,128,128]{3,2,1,0:T(8,128)(2,1)S(1)}, u32[]{:S(2)}, u32[]{:S(2)}) async-start(bf16[16,4,128,128]{3,2,1,0:T(8,128)(2,1)} %unjoin.1), calls=%async_computation.2 | async-start | bytes 4194304 | tf_op jit(solution)/shard_map/all_to_all | solution.py:318
  184.4 24.4 %collective-permute-done.13.refs_2_ = bf16[384,768]{1,0:T(8,128)(2,1)S(1)} collective-permute-done((bf16[384,768]{1,0:T(8,128)(2,1)S(1)}, bf16[384,768]{1,0:T(8,128)(2,1)S(1)}, u32[]{:S(2)}, u32[]{:S(2)}) %collective-permute-start.13) | collective-permute-done | bytes 589856 | tf_op jit(solution)/shard_map/ppermute | solution.py:308
  211.3 17.7 %collective-permute-done.18.refs_7_ = bf16[384,768]{1,0:T(8,128)(2,1)S(1)} collective-permute-done((bf16[384,768]{1,0:T(8,128)(2,1)}, bf16[384,768]{1,0:T(8,128)(2,1)S(1)}, u32[]{:S(2)}, u32[]{:S(2)}) %collective-permute-start.18) | collective-permute-done | bytes 589856 | tf_op jit(solution)/shard_map/ppermute | solution.py:308
  232.0 4.7 %collective-permute-done.15.refs_4_ = bf16[192,768]{1,0:T(8,128)(2,1)S(1)} collective-permute-done((bf16[192,768]{1,0:T(8,128)(2,1)S(1)}, bf16[192,768]{1,0:T(8,128)(2,1)S(1)}, u32[]{:S(2)}, u32[]{:S(2)}) %collective-permute-start.15) | collective-permute-done | bytes 294944 | tf_op jit(solution)/shard_map/ppermute | solution.py:308
  238.1 4.9 %collective-permute-done.20.refs_9_ = bf16[192,768]{1,0:T(8,128)(2,1)S(1)} collective-permute-done((bf16[192,768]{1,0:T(8,128)(2,1)S(1)}, bf16[192,768]{1,0:T(8,128)(2,1)S(1)}, u32[]{:S(2)}, u32[]{:S(2)}) %collective-permute-start.20) | collective-permute-done | bytes 294944 | tf_op jit(solution)/shard_map/ppermute | solution.py:308
  254.0 3.8 %fusion.8 = f32[256,3072]{1,0:T(8,128)S(1)} fusion(bf16[256,768]{1,0:T(8,128)(2,1)S(1)} %get-tuple-element.60, bf16[768,3072]{1,0:T(8,128)(2,1)} %param.11), kind=kOutput, calls=%fused_computation.56 | convolution fusion | flops 1207959552 | bytes 8257536 | tf_op jit(solution)/shard_map/dot_general | solution.py:27
  263.9 6.8 %place.1 = f32[768,3072]{1,0:T(8,128)} custom-call(s32[2]{0:T(128)S(1)} %pad_add_fusion.2.place_ref, bf16[384,768]{1,0:T(8,128)(2,1)S(1)} %broadcast_select_fusion.2.refs_0_, bf16[384,768]{1,0:T(8,128)(2,1)S(1)} %copy-done.2, bf16[384,768]{1,0:T(8,128)(2,1)S(1)} %collective-permute-done.13.refs_2_, bf16[192,768]{1,0:T(8,128)(2,1)S(1)} %copy-done.17, ...), custom_call_target="tpu_custom_call" | custom-call | bytes 16777216 | tf_op jit(solution)/shard_map/place/pallas_call | solution.py:321
  270.7 2.2 add_convert_fusion
  (143 shorter events, 71.4 us)
Async XLA Ops:
  13.8 43.6 %all-to-all-start = ((bf16[16,3,128,128]{3,2,1,0:T(8,128)(2,1)}), bf16[16,3,128,128]{3,2,1,0:T(8,128)(2,1)S(1)}, u32[]{:S(2)}, u32[]{:S(2)}) async-start(bf16[16,3,128,128]{3,2,1,0:T(8,128)(2,1)} %pack.2), calls=%async_computation | async-start | bytes 3145728 | tf_op jit(solution)/shard_map/all_to_all | solution.py:424
  20.5 114.0 %all-gather.3.cloned.1.call-start = ((), (), s32[]{:S(2)}) async-start(), calls=%async_computation.3 | async-start | bytes 3932160 | tf_op jit(solution)/shard_map/all_gather | solution.py:427
  29.4 6.2 %collective-permute-start.2 = (bf16[1,128,768]{2,1,0:T(8,128)(2,1)}, bf16[1,128,768]{2,1,0:T(8,128)(2,1)S(1)}, u32[]{:S(2)}, u32[]{:S(2)}) collective-permute-start(bf16[1,128,768]{2,1,0:T(8,128)(2,1)} %dynamic-slice_bitcast_fusion), channel_id=1, source_target_pairs={{0,1},{1,0},{2,3},{3,2},{4,5},{5,4},{6,7},{7,6},{8,9},{9,8},{10,11... | collective-permute-start | bytes 589832 | tf_op jit(solution)/shard_map/ppermute | solution.py:388
  31.5 16.6 %collective-permute-start.5 = (bf16[128,768]{1,0:T(8,128)(2,1)}, bf16[128,768]{1,0:T(8,128)(2,1)S(1)}, u32[]{:S(2)}, u32[]{:S(2)}) collective-permute-start(bf16[128,768]{1,0:T(8,128)(2,1)} %get-tuple-element.70), channel_id=1, source_target_pairs={{0,6},{2,4},{4,2},{6,0},{8,14},{10,12},{12,10},{14,8},{16,22},{18,... | collective-permute-start | bytes 589832 | tf_op jit(solution)/shard_map/ppermute | solution.py:410
  32.7 17.4 %collective-permute-start.3 = (bf16[128,768]{1,0:T(8,128)(2,1)}, bf16[128,768]{1,0:T(8,128)(2,1)S(1)}, u32[]{:S(2)}, u32[]{:S(2)}) collective-permute-start(bf16[128,768]{1,0:T(8,128)(2,1)} %get-tuple-element.72), channel_id=1, source_target_pairs={{0,2},{2,0},{4,6},{6,4},{8,10},{10,8},{12,14},{14,12},{16,18},{18,... | collective-permute-start | bytes 589832 | tf_op jit(solution)/shard_map/ppermute | solution.py:410
  33.0 17.1 %collective-permute-start.4 = (bf16[128,768]{1,0:T(8,128)(2,1)S(1)}, bf16[128,768]{1,0:T(8,128)(2,1)S(1)}, u32[]{:S(2)}, u32[]{:S(2)}) collective-permute-start(bf16[128,768]{1,0:T(8,128)(2,1)S(1)} %get-tuple-element.73), channel_id=1, source_target_pairs={{0,4},{2,6},{4,0},{6,2},{8,12},{10,14},{12,8},{14,10},{16,20},{18,... | collective-permute-start | bytes 589832 | tf_op jit(solution)/shard_map/ppermute | solution.py:410
  58.0 7.3 %collective-permute-start.6 = (bf16[2,2048,128]{2,1,0:T(8,128)(2,1)S(1)}, bf16[2,2048,128]{2,1,0:T(8,128)(2,1)S(1)}, u32[]{:S(2)}, u32[]{:S(2)}) collective-permute-start(bf16[2,2048,128]{2,1,0:T(8,128)(2,1)S(1)} %get-tuple-element.37.refs_0_.refs_1_), channel_id=1, source_target_pairs={{0,1},{1,0},{2,3},{3,2},{4,5},{5,4},{6,7},{7,6},{8,9},{9,8},{10,11... | collective-permute-start | bytes 3145736 | tf_op jit(solution)/shard_map/ppermute | solution.py:434
  60.6 49.8 %all-to-all-start.1 = ((bf16[16,1,128,128]{3,2,1,0:T(8,128)(2,1)}), bf16[16,1,128,128]{3,2,1,0:T(8,128)(2,1)S(1)}, u32[]{:S(2)}, u32[]{:S(2)}) async-start(bf16[16,1,128,128]{3,2,1,0:T(8,128)(2,1)} %pack.3), calls=%async_computation.1 | async-start | bytes 1048576 | tf_op jit(solution)/shard_map/all_to_all | solution.py:429
  81.7 17.3 %collective-permute-start.9 = (bf16[2048,128]{1,0:T(8,128)(2,1)S(1)}, bf16[2048,128]{1,0:T(8,128)(2,1)S(1)}, u32[]{:S(2)}, u32[]{:S(2)}) collective-permute-start(bf16[2048,128]{1,0:T(8,128)(2,1)S(1)} %get-tuple-element.47.o_ref.refs_0_.attn_ref), channel_id=1, source_target_pairs={{0,6},{2,4},{4,2},{10,12},{12,10},{14,8},{16,22},{20,18},{22,16},{... | collective-permute-start | bytes 1572872 | tf_op jit(solution)/shard_map/ppermute | solution.py:458
  84.8 23.4 %collective-permute-start.8 = (bf16[2048,128]{1,0:T(8,128)(2,1)S(1)}, bf16[2048,128]{1,0:T(8,128)(2,1)S(1)}, u32[]{:S(2)}, u32[]{:S(2)}) collective-permute-start(bf16[2048,128]{1,0:T(8,128)(2,1)S(1)} %get-tuple-element.47.o_ref.refs_0_.attn_ref), channel_id=1, source_target_pairs={{0,4},{2,6},{4,0},{10,14},{12,8},{14,10},{16,20},{20,16},{22,18},{... | collective-permute-start | bytes 1572872 | tf_op jit(solution)/shard_map/ppermute | solution.py:458
  86.1 23.4 %collective-permute-start.7 = (bf16[2048,128]{1,0:T(8,128)(2,1)S(1)}, bf16[2048,128]{1,0:T(8,128)(2,1)S(1)}, u32[]{:S(2)}, u32[]{:S(2)}) collective-permute-start(bf16[2048,128]{1,0:T(8,128)(2,1)S(1)} %get-tuple-element.47.o_ref.refs_0_.attn_ref), channel_id=1, source_target_pairs={{0,2},{2,0},{4,6},{10,8},{12,14},{14,12},{16,18},{20,22},{22,20},{... | collective-permute-start | bytes 1572872 | tf_op jit(solution)/shard_map/ppermute | solution.py:458
  143.4 11.9 %collective-permute-start.11 = (bf16[384,768]{1,0:T(8,128)(2,1)}, bf16[384,768]{1,0:T(8,128)(2,1)}, u32[]{:S(2)}, u32[]{:S(2)}) collective-permute-start(bf16[384,768]{1,0:T(8,128)(2,1)} %add_convert_fusion.1), channel_id=1, source_target_pairs={{0,16},{2,18},{4,20},{6,22},{8,24},{10,26},{12,28},{14,30},{17,1},... | collective-permute-start | bytes 1769480 | tf_op jit(solution)/shard_map/ppermute | solution.py:305
  144.8 18.6 %collective-permute-start.21 = (bf16[2,2048,128]{2,1,0:T(8,128)(2,1)}, bf16[2,2048,128]{2,1,0:T(8,128)(2,1)S(1)}, u32[]{:S(2)}, u32[]{:S(2)}) collective-permute-start(bf16[2,2048,128]{2,1,0:T(8,128)(2,1)} %get-tuple-element.55), channel_id=1, source_target_pairs={{0,1},{1,0},{2,3},{3,2},{4,5},{5,4},{6,7},{7,6},{8,9},{9,8},{10,11... | collective-permute-start | bytes 3145736 | tf_op jit(solution)/shard_map/ppermute | solution.py:478
  156.4 20.0 %collective-permute-start.16 = (bf16[384,768]{1,0:T(8,128)(2,1)S(1)}, bf16[384,768]{1,0:T(8,128)(2,1)}, u32[]{:S(2)}, u32[]{:S(2)}) collective-permute-start(bf16[384,768]{1,0:T(8,128)(2,1)S(1)} %broadcast_select_fusion.2.refs_0_), channel_id=1, source_target_pairs={{0,8},{2,10},{4,12},{6,14},{8,0},{10,2},{12,4},{14,6},{16,24},{18,... | collective-permute-start | bytes 1769480 | tf_op jit(solution)/shard_map/ppermute | solution.py:308
  176.4 68.1 %all-to-all-start.2 = ((bf16[16,4,128,128]{3,2,1,0:T(8,128)(2,1)}), bf16[16,4,128,128]{3,2,1,0:T(8,128)(2,1)S(1)}, u32[]{:S(2)}, u32[]{:S(2)}) async-start(bf16[16,4,128,128]{3,2,1,0:T(8,128)(2,1)} %unjoin.1), calls=%async_computation.2 | async-start | bytes 4194304 | tf_op jit(solution)/shard_map/all_to_all | solution.py:318
  181.5 27.3 %collective-permute-start.13 = (bf16[384,768]{1,0:T(8,128)(2,1)S(1)}, bf16[384,768]{1,0:T(8,128)(2,1)S(1)}, u32[]{:S(2)}, u32[]{:S(2)}) collective-permute-start(bf16[384,768]{1,0:T(8,128)(2,1)S(1)} %broadcast_select_fusion.2.refs_0_), channel_id=1, source_target_pairs={{0,4},{2,6},{4,0},{6,2},{8,12},{10,14},{12,8},{14,10},{16,20},{18,... | collective-permute-start | bytes 1769480 | tf_op jit(solution)/shard_map/ppermute | solution.py:308
  181.8 29.1 %collective-permute-start.12 = (bf16[384,768]{1,0:T(8,128)(2,1)S(1)}, bf16[384,768]{1,0:T(8,128)(2,1)S(1)}, u32[]{:S(2)}, u32[]{:S(2)}) collective-permute-start(bf16[384,768]{1,0:T(8,128)(2,1)S(1)} %broadcast_select_fusion.2.refs_0_), channel_id=1, source_target_pairs={{0,2},{2,0},{4,6},{6,4},{8,10},{10,8},{12,14},{14,12},{16,18},{18,... | collective-permute-start | bytes 1769480 | tf_op jit(solution)/shard_map/ppermute | solution.py:308
  183.0 46.0 %collective-permute-start.18 = (bf16[384,768]{1,0:T(8,128)(2,1)}, bf16[384,768]{1,0:T(8,128)(2,1)S(1)}, u32[]{:S(2)}, u32[]{:S(2)}) collective-permute-start(bf16[384,768]{1,0:T(8,128)(2,1)} %collective-permute-done.16.refs_5_), channel_id=1, source_target_pairs={{0,4},{2,6},{4,0},{6,2},{8,12},{10,14},{12,8},{14,10},{16,20},{18,... | collective-permute-start | bytes 1769480 | tf_op jit(solution)/shard_map/ppermute | solution.py:308
  184.2 46.6 %collective-permute-start.17 = (bf16[384,768]{1,0:T(8,128)(2,1)}, bf16[384,768]{1,0:T(8,128)(2,1)S(1)}, u32[]{:S(2)}, u32[]{:S(2)}) collective-permute-start(bf16[384,768]{1,0:T(8,128)(2,1)} %collective-permute-done.16.refs_5_), channel_id=1, source_target_pairs={{0,2},{2,0},{4,6},{6,4},{8,10},{10,8},{12,14},{14,12},{16,18},{18,... | collective-permute-start | bytes 1769480 | tf_op jit(solution)/shard_map/ppermute | solution.py:308
  208.9 27.8 %collective-permute-start.15 = (bf16[192,768]{1,0:T(8,128)(2,1)S(1)}, bf16[192,768]{1,0:T(8,128)(2,1)S(1)}, u32[]{:S(2)}, u32[]{:S(2)}) collective-permute-start(bf16[192,768]{1,0:T(8,128)(2,1)S(1)} %slice.21), channel_id=1, source_target_pairs={{0,2},{2,0},{4,6},{6,4},{8,10},{10,8},{12,14},{14,12},{16,18},{18,... | collective-permute-start | bytes 884744 | tf_op jit(solution)/shard_map/ppermute | solution.py:308
  210.9 26.5 %collective-permute-start.14 = (bf16[192,768]{1,0:T(8,128)(2,1)S(1)}, bf16[192,768]{1,0:T(8,128)(2,1)S(1)}, u32[]{:S(2)}, u32[]{:S(2)}) collective-permute-start(bf16[192,768]{1,0:T(8,128)(2,1)S(1)} %slice.20), channel_id=1, source_target_pairs={{0,4},{2,6},{4,0},{6,2},{8,12},{10,14},{12,8},{14,10},{16,20},{18,... | collective-permute-start | bytes 884744 | tf_op jit(solution)/shard_map/ppermute | solution.py:308
  229.0 14.0 %collective-permute-start.20 = (bf16[192,768]{1,0:T(8,128)(2,1)S(1)}, bf16[192,768]{1,0:T(8,128)(2,1)S(1)}, u32[]{:S(2)}, u32[]{:S(2)}) collective-permute-start(bf16[192,768]{1,0:T(8,128)(2,1)S(1)} %slice.23), channel_id=1, source_target_pairs={{0,2},{2,0},{4,6},{6,4},{8,10},{10,8},{12,14},{14,12},{16,18},{18,... | collective-permute-start | bytes 884744 | tf_op jit(solution)/shard_map/ppermute | solution.py:308
  230.8 13.0 %collective-permute-start.19 = (bf16[192,768]{1,0:T(8,128)(2,1)S(1)}, bf16[192,768]{1,0:T(8,128)(2,1)S(1)}, u32[]{:S(2)}, u32[]{:S(2)}) collective-permute-start(bf16[192,768]{1,0:T(8,128)(2,1)S(1)} %slice.22), channel_id=1, source_target_pairs={{0,4},{2,6},{4,0},{6,2},{8,12},{10,14},{12,8},{14,10},{16,20},{18,... | collective-permute-start | bytes 884744 | tf_op jit(solution)/shard_map/ppermute | solution.py:308
  260.4 10.3 %collective-permute-start.23 = (bf16[256,1536]{1,0:T(8,128)(2,1)}, bf16[256,1536]{1,0:T(8,128)(2,1)}, u32[]{:S(2)}, u32[]{:S(2)}) collective-permute-start(bf16[256,1536]{1,0:T(8,128)(2,1)} %dynamic-slice_convert_fusion), channel_id=1, source_target_pairs={{0,1},{1,0},{2,3},{3,2},{4,5},{5,4},{6,7},{7,6},{8,9},{9,8},{10,11... | collective-permute-start | bytes 2359304 | tf_op jit(solution)/shard_map/ppermute | solution.py:549
  (38 other events, 198.9 us)
Sparse Core Ops, SparseCore 0:
  59.7 68.5 all-gather.2

commit v14 on v7

--- a/solution.py
+++ b/solution.py
@@ -310,7 +310,7 @@
     first = jnp.where(plane // 2 == core, tile_sum, from_half)
     second = swap(first, in_plane)
     beside, above = swap(first, 1), swap(first, 2)
-    second, beside, above, beside_chunks = lax.optimization_barrier((second, beside, above, beside_chunks))
+    *_, beside_chunks = lax.optimization_barrier((second, beside, above, beside_chunks))
     middle = tile_rows // 2
     sources = [first, beside, above, swap(beside[:middle], 2), swap(above[middle:], 1)]
     beside, above = swap(second, 1), swap(second, 2)

time: 271 us -> 271 us (level)
  transfers between devices with their start and end apart: 28 -> 28, of which waited for: 15 -> 17; matrix products, arithmetic and copies ran while one was open for 7% -> 7% of each run, Pallas kernels for 20% -> 20%
where the time goes in v14:
time: 271 us; the launch traced here: 268 us
  waiting for transfers between devices  101 us (37%)
  starting transfers between devices  60.6 us (22%)
  Pallas kernels  56.6 us (21%)
  local copies, waits for them, and re-layouts  19.5 us (7%)
  between operations  14.4 us (5%)
  other arithmetic  7.67 us (3%)
  matrix products  7.5 us (3%)
    ppermute x1, waiting for transfers between devices, gather_tiles_by_core(): from_half = lax.ppermute(tile_sum, ('ctx', 'tp'), across)  32.8 us
    ppermute x9, starting transfers between devices, swap(): return lax.ppermute(x, 'ctx', [(i, i ^ k) for i in range(n)])  23.2 us
    ppermute x9, waiting for transfers between devices, swap(): return lax.ppermute(x, 'ctx', [(i, i ^ k) for i in range(n)])  22.7 us
    pallas_call x1, Pallas kernels, per_device(): pl.pallas_call(functools.partial(backward_kernel, t, tile, count), grid_s...  20.1 us
    ppermute x3, waiting for transfers between devices, per_device(): lax.ppermute(attn, 'ctx', [(i, i ^ k) for i in range(n) if held[i]])  18.6 us
    pallas_call x1, Pallas kernels, per_device(): pl.pallas_call(functools.partial(forward_kernel, t, tile, count), grid_sp...  13.9 us
    ppermute x3, waiting for transfers between devices, per_device(): plane_got.append(lax.ppermute(there, 'ctx', [(i, i ^ k) for i in range(n)]))  13.1 us
    unnamed x46, local copies, waits for them, and re-layouts  11.4 us
  transfers between devices with their start and end apart: 28, of which 17 were waited for; matrix products, arithmetic and copies ran while one was open for 7% of the time, Pallas kernels for 20%

profile of v14, /device:TPU:13, one launch (start us, length us, event | category | flops | bytes accessed | tf_op | source)
XLA Modules:
  0.0 267.6 jit_solution(4906171530541539888)
XLA Ops:
  13.8 6.7 %all-to-all-start = ((bf16[16,3,128,128]{3,2,1,0:T(8,128)(2,1)}), bf16[16,3,128,128]{3,2,1,0:T(8,128)(2,1)S(1)}, u32[]{:S(2)}, u32[]{:S(2)}) async-start(bf16[16,3,128,128]{3,2,1,0:T(8,128)(2,1)} %pack.2), calls=%async_computation | async-start | bytes 3145728 | tf_op jit(solution)/shard_map/all_to_all | solution.py:422
  21.6 2.0 collective-permute-done.1
  24.9 3.8 %fusion.1.refs_0_ = bf16[256,768]{1,0:T(8,128)(2,1)S(1)} fusion(bf16[768,3072]{1,0:T(8,128)(2,1)} %param.11, bf16[256,1536]{1,0:T(8,128)(2,1)S(1)} %get-tuple-element.65, bf16[256,1536]{1,0:T(8,128)(2,1)S(1)} %get-tuple-element.64), kind=kOutput, calls=%fused_computation.14 | convolution fusion | flops 1211301888 | bytes 6684672 | tf_op jit(solution)/shard_map/dot_general | solution.py:27
  37.0 11.1 %collective-permute-done.5.refs_3_ = bf16[128,768]{1,0:T(8,128)(2,1)S(1)} collective-permute-done((bf16[128,768]{1,0:T(8,128)(2,1)}, bf16[128,768]{1,0:T(8,128)(2,1)S(1)}, u32[]{:S(2)}, u32[]{:S(2)}) %collective-permute-start.5) | collective-permute-done | bytes 196640 | tf_op jit(solution)/shard_map/ppermute | solution.py:408
  51.5 5.8 %all-to-all-done.chunks_ref = bf16[16,3,128,128]{3,2,1,0:T(8,128)(2,1)S(1)} async-done(((bf16[16,3,128,128]{3,2,1,0:T(8,128)(2,1)}), bf16[16,3,128,128]{3,2,1,0:T(8,128)(2,1)S(1)}, u32[]{:S(2)}, u32[]{:S(2)}) %all-to-all-start) | async-done | bytes 1572896 | tf_op jit(solution)/shard_map/all_to_all | solution.py:422
  60.5 4.8 %all-to-all-start.1 = ((bf16[16,1,128,128]{3,2,1,0:T(8,128)(2,1)}), bf16[16,1,128,128]{3,2,1,0:T(8,128)(2,1)S(1)}, u32[]{:S(2)}, u32[]{:S(2)}) async-start(bf16[16,1,128,128]{3,2,1,0:T(8,128)(2,1)} %pack.3), calls=%async_computation.1 | async-start | bytes 1048576 | tf_op jit(solution)/shard_map/all_to_all | solution.py:427
  67.1 13.9 %forward.1 = (bf16[2048,128]{1,0:T(8,128)(2,1)S(1)}, f32[2048,128]{1,0:T(8,128)S(1)}) custom-call(s32[16]{0:T(128)S(1)} %get-tuple-element.58.full_ref, s32[16]{0:T(128)S(1)} %get-tuple-element.54.kcnt_ref, s32[16,10]{1,0:T(8,128)S(1)} %copy.11.kidx_ref, bf16[2048,128]{1,0:T(8,128)(2,1)S(1)} %get-tuple-element.31.q_ref, ...), custom_call_target="tpu_custom_call" | custom-call | flops 16000000000 | bytes 5242880 | tf_op jit(solution)/shard_map/forward/pallas_call | solution.py:440
  82.0 3.1 %collective-permute-start.9 = (bf16[2048,128]{1,0:T(8,128)(2,1)S(1)}, bf16[2048,128]{1,0:T(8,128)(2,1)S(1)}, u32[]{:S(2)}, u32[]{:S(2)}) collective-permute-start(bf16[2048,128]{1,0:T(8,128)(2,1)S(1)} %get-tuple-element.41.refs_0_.o_ref.attn_ref), channel_id=1, source_target_pairs={{0,6},{2,4},{4,2},{10,12},{12,10},{14,8},{16,22},{20,18},{22,16},{... | collective-permute-start | bytes 1572872 | tf_op jit(solution)/shard_map/ppermute | solution.py:456
  86.4 4.0 %collective-permute-start.7 = (bf16[2048,128]{1,0:T(8,128)(2,1)S(1)}, bf16[2048,128]{1,0:T(8,128)(2,1)S(1)}, u32[]{:S(2)}, u32[]{:S(2)}) collective-permute-start(bf16[2048,128]{1,0:T(8,128)(2,1)S(1)} %get-tuple-element.41.refs_0_.o_ref.attn_ref), channel_id=1, source_target_pairs={{0,2},{2,0},{4,6},{10,8},{12,14},{14,12},{16,18},{20,22},{22,20},{... | collective-permute-start | bytes 1572872 | tf_op jit(solution)/shard_map/ppermute | solution.py:456
  90.4 8.1 %collective-permute-done.9.refs_3_ = bf16[2048,128]{1,0:T(8,128)(2,1)S(1)} collective-permute-done((bf16[2048,128]{1,0:T(8,128)(2,1)S(1)}, bf16[2048,128]{1,0:T(8,128)(2,1)S(1)}, u32[]{:S(2)}, u32[]{:S(2)}) %collective-permute-start.9) | collective-permute-done | bytes 524320 | tf_op jit(solution)/shard_map/ppermute | solution.py:456
  98.5 9.8 %collective-permute-done.8.refs_2_ = bf16[2048,128]{1,0:T(8,128)(2,1)S(1)} collective-permute-done((bf16[2048,128]{1,0:T(8,128)(2,1)S(1)}, bf16[2048,128]{1,0:T(8,128)(2,1)S(1)}, u32[]{:S(2)}, u32[]{:S(2)}) %collective-permute-start.8) | collective-permute-done | bytes 524320 | tf_op jit(solution)/shard_map/ppermute | solution.py:456
  110.4 20.1 %backward.1 = (bf16[2048,128]{1,0:T(8,128)(2,1)S(1)}, bf16[2,2048,128]{2,1,0:T(8,128)(2,1)S(1)}, bf16[2,2048,128]{2,1,0:T(8,128)(2,1)S(1)}) custom-call(s32[16]{0:T(128)S(1)} %get-tuple-element.58.full_ref, s32[16]{0:T(128)S(1)} %get-tuple-element.54.kcnt_ref, s32[16,10]{1,0:T(8,128)S(1)} %copy.11.kidx_ref, bf16[2048,128]{1,0:T(8,128)(2,1)S(1)} %get-tuple-element.31.q_ref, ...), custom_call_target="tpu_custom_call" | custom-call | flops 20000000000 | bytes 8388608 | tf_op jit(solution)/shard_map/backward/pallas_call | solution.py:460
  132.0 2.3 collective-permute-done.15.refs_0_
  136.4 7.1 %all-to-all-start.2 = ((bf16[16,4,128,128]{3,2,1,0:T(8,128)(2,1)}), bf16[16,4,128,128]{3,2,1,0:T(8,128)(2,1)S(1)}, u32[]{:S(2)}, u32[]{:S(2)}) async-start(bf16[16,4,128,128]{3,2,1,0:T(8,128)(2,1)} %copy-done.1), calls=%async_computation.2 | async-start | bytes 4194304 | tf_op jit(solution)/shard_map/all_to_all | solution.py:482
  146.7 4.8 %tile.1 = (f32[384,768]{1,0:T(8,128)S(1)}, bf16[384,768]{1,0:T(8,128)(2,1)S(1)}) custom-call(s32[2]{0:T(128)S(1)} %pad_add_fusion.where_ref, bf16[2048,128]{1,0:T(8,128)(2,1)S(1)} %get-tuple-element.41.refs_0_.o_ref.attn_ref, bf16[2048,128]{1,0:T(8,128)(2,1)S(1)} %copy-done.17, bf16[2048,128]{1,0:T(8,128)(2,1)S(1)} %copy-done.15, ...), custom_call_target="tpu_custom_call" | custom-call | flops 5000000000 | bytes 4194304 | tf_op jit(solution)/shard_map/tile/pallas_call | solution.py:488
  155.6 32.8 %collective-permute-done.11 = bf16[384,768]{1,0:T(8,128)(2,1)} collective-permute-done((bf16[384,768]{1,0:T(8,128)(2,1)S(1)}, bf16[384,768]{1,0:T(8,128)(2,1)}, u32[]{:S(2)}, u32[]{:S(2)}) %collective-permute-start.11) | collective-permute-done | bytes 589856 | tf_op jit(solution)/shard_map/ppermute | solution.py:305
  190.4 17.2 %collective-permute-start.12 = (bf16[384,768]{1,0:T(8,128)(2,1)S(1)}, bf16[384,768]{1,0:T(8,128)(2,1)}, u32[]{:S(2)}, u32[]{:S(2)}) collective-permute-start(bf16[384,768]{1,0:T(8,128)(2,1)S(1)} %broadcast_select_fusion.2.refs_0_), channel_id=1, source_target_pairs={{0,8},{2,10},{4,12},{6,14},{8,0},{10,2},{12,4},{14,6},{16,24},{18,... | collective-permute-start | bytes 1769480 | tf_op jit(solution)/shard_map/ppermute | solution.py:308
  208.4 11.7 %collective-permute-done.12.refs_5_ = bf16[384,768]{1,0:T(8,128)(2,1)} collective-permute-done((bf16[384,768]{1,0:T(8,128)(2,1)S(1)}, bf16[384,768]{1,0:T(8,128)(2,1)}, u32[]{:S(2)}, u32[]{:S(2)}) %collective-permute-start.12) | collective-permute-done | bytes 589856 | tf_op jit(solution)/shard_map/ppermute | solution.py:308
  226.4 2.9 %unpack.1 = (bf16[256,768]{1,0:T(8,128)(2,1)S(1)}, bf16[256,768]{1,0:T(8,128)(2,1)}, bf16[256,768]{1,0:T(8,128)(2,1)}, bf16[256,768]{1,0:T(8,128)(2,1)}) custom-call(s32[2]{0:T(128)S(1)} %pad_add_fusion.where_ref, bf16[6,4,128,128]{3,2,1,0:T(8,128)(2,1)S(1)} %copy-done.8, bf16[6,4,128,128]{3,2,1,0:T(8,128)(2,1)} %collective-permute-done.16.refs_1_), custom_call_target="tpu_custom_call" | custom-call | bytes 6291456 | tf_op jit(solution)/shard_map/unpack/pallas_call | solution.py:260
  229.3 3.7 %fusion.8 = f32[256,3072]{1,0:T(8,128)S(1)} fusion(bf16[256,768]{1,0:T(8,128)(2,1)S(1)} %get-tuple-element.50, bf16[768,3072]{1,0:T(8,128)(2,1)} %param.11), kind=kOutput, calls=%fused_computation.56 | convolution fusion | flops 1207959552 | bytes 8257536 | tf_op jit(solution)/shard_map/dot_general | solution.py:27
  240.7 4.3 %collective-permute-done.19.refs_4_ = bf16[192,768]{1,0:T(8,128)(2,1)S(1)} collective-permute-done((bf16[192,768]{1,0:T(8,128)(2,1)}, bf16[192,768]{1,0:T(8,128)(2,1)S(1)}, u32[]{:S(2)}, u32[]{:S(2)}) %collective-permute-start.19) | collective-permute-done | bytes 294944 | tf_op jit(solution)/shard_map/ppermute | solution.py:308
  245.4 5.9 %collective-permute-done.23.refs_9_ = bf16[192,768]{1,0:T(8,128)(2,1)} collective-permute-done((bf16[192,768]{1,0:T(8,128)(2,1)}, bf16[192,768]{1,0:T(8,128)(2,1)}, u32[]{:S(2)}, u32[]{:S(2)}) %collective-permute-start.23) | collective-permute-done | bytes 294944 | tf_op jit(solution)/shard_map/ppermute | solution.py:308
  251.8 6.8 %place.1 = f32[768,3072]{1,0:T(8,128)} custom-call(s32[2]{0:T(128)S(1)} %pad_add_fusion.2.place_ref, bf16[384,768]{1,0:T(8,128)(2,1)S(1)} %broadcast_select_fusion.2.refs_0_, bf16[384,768]{1,0:T(8,128)(2,1)S(1)} %copy-done.3, bf16[384,768]{1,0:T(8,128)(2,1)S(1)} %collective-permute-done.14.refs_2_, bf16[192,768]{1,0:T(8,128)(2,1)} %collective-permute-done.18.refs_3_, ...), custom_call_target="tpu_custom_call" | custom-call | bytes 16777216 | tf_op jit(solution)/shard_map/place/pallas_call | solution.py:319
  258.5 2.2 add_convert_fusion
  (121 shorter events, 58.1 us)
Async XLA Ops:
  13.8 43.6 %all-to-all-start = ((bf16[16,3,128,128]{3,2,1,0:T(8,128)(2,1)}), bf16[16,3,128,128]{3,2,1,0:T(8,128)(2,1)S(1)}, u32[]{:S(2)}, u32[]{:S(2)}) async-start(bf16[16,3,128,128]{3,2,1,0:T(8,128)(2,1)} %pack.2), calls=%async_computation | async-start | bytes 3145728 | tf_op jit(solution)/shard_map/all_to_all | solution.py:422
  20.5 123.0 %all-gather.3.cloned.1.call-start = ((), (), s32[]{:S(2)}) async-start(), calls=%async_computation.3 | async-start | bytes 3932160 | tf_op jit(solution)/shard_map/all_gather | solution.py:425
  29.3 6.2 %collective-permute-start.2 = (bf16[1,128,768]{2,1,0:T(8,128)(2,1)}, bf16[1,128,768]{2,1,0:T(8,128)(2,1)S(1)}, u32[]{:S(2)}, u32[]{:S(2)}) collective-permute-start(bf16[1,128,768]{2,1,0:T(8,128)(2,1)} %dynamic-slice_bitcast_fusion), channel_id=1, source_target_pairs={{0,1},{1,0},{2,3},{3,2},{4,5},{5,4},{6,7},{7,6},{8,9},{9,8},{10,11... | collective-permute-start | bytes 589832 | tf_op jit(solution)/shard_map/ppermute | solution.py:386
  31.5 16.6 %collective-permute-start.5 = (bf16[128,768]{1,0:T(8,128)(2,1)}, bf16[128,768]{1,0:T(8,128)(2,1)S(1)}, u32[]{:S(2)}, u32[]{:S(2)}) collective-permute-start(bf16[128,768]{1,0:T(8,128)(2,1)} %get-tuple-element.60), channel_id=1, source_target_pairs={{0,6},{2,4},{4,2},{6,0},{8,14},{10,12},{12,10},{14,8},{16,22},{18,... | collective-permute-start | bytes 589832 | tf_op jit(solution)/shard_map/ppermute | solution.py:408
  32.7 17.4 %collective-permute-start.3 = (bf16[128,768]{1,0:T(8,128)(2,1)}, bf16[128,768]{1,0:T(8,128)(2,1)S(1)}, u32[]{:S(2)}, u32[]{:S(2)}) collective-permute-start(bf16[128,768]{1,0:T(8,128)(2,1)} %get-tuple-element.62), channel_id=1, source_target_pairs={{0,2},{2,0},{4,6},{6,4},{8,10},{10,8},{12,14},{14,12},{16,18},{18,... | collective-permute-start | bytes 589832 | tf_op jit(solution)/shard_map/ppermute | solution.py:408
  33.0 17.1 %collective-permute-start.4 = (bf16[128,768]{1,0:T(8,128)(2,1)S(1)}, bf16[128,768]{1,0:T(8,128)(2,1)S(1)}, u32[]{:S(2)}, u32[]{:S(2)}) collective-permute-start(bf16[128,768]{1,0:T(8,128)(2,1)S(1)} %get-tuple-element.63), channel_id=1, source_target_pairs={{0,4},{2,6},{4,0},{6,2},{8,12},{10,14},{12,8},{14,10},{16,20},{18,... | collective-permute-start | bytes 589832 | tf_op jit(solution)/shard_map/ppermute | solution.py:408
  58.0 7.3 %collective-permute-start.6 = (bf16[2,2048,128]{2,1,0:T(8,128)(2,1)S(1)}, bf16[2,2048,128]{2,1,0:T(8,128)(2,1)S(1)}, u32[]{:S(2)}, u32[]{:S(2)}) collective-permute-start(bf16[2,2048,128]{2,1,0:T(8,128)(2,1)S(1)} %get-tuple-element.32.refs_0_.refs_1_), channel_id=1, source_target_pairs={{0,1},{1,0},{2,3},{3,2},{4,5},{5,4},{6,7},{7,6},{8,9},{9,8},{10,11... | collective-permute-start | bytes 3145736 | tf_op jit(solution)/shard_map/ppermute | solution.py:432
  60.5 48.5 %all-to-all-start.1 = ((bf16[16,1,128,128]{3,2,1,0:T(8,128)(2,1)}), bf16[16,1,128,128]{3,2,1,0:T(8,128)(2,1)S(1)}, u32[]{:S(2)}, u32[]{:S(2)}) async-start(bf16[16,1,128,128]{3,2,1,0:T(8,128)(2,1)} %pack.3), calls=%async_computation.1 | async-start | bytes 1048576 | tf_op jit(solution)/shard_map/all_to_all | solution.py:427
  82.0 16.5 %collective-permute-start.9 = (bf16[2048,128]{1,0:T(8,128)(2,1)S(1)}, bf16[2048,128]{1,0:T(8,128)(2,1)S(1)}, u32[]{:S(2)}, u32[]{:S(2)}) collective-permute-start(bf16[2048,128]{1,0:T(8,128)(2,1)S(1)} %get-tuple-element.41.refs_0_.o_ref.attn_ref), channel_id=1, source_target_pairs={{0,6},{2,4},{4,2},{10,12},{12,10},{14,8},{16,22},{20,18},{22,16},{... | collective-permute-start | bytes 1572872 | tf_op jit(solution)/shard_map/ppermute | solution.py:456
  85.1 23.3 %collective-permute-start.8 = (bf16[2048,128]{1,0:T(8,128)(2,1)S(1)}, bf16[2048,128]{1,0:T(8,128)(2,1)S(1)}, u32[]{:S(2)}, u32[]{:S(2)}) collective-permute-start(bf16[2048,128]{1,0:T(8,128)(2,1)S(1)} %get-tuple-element.41.refs_0_.o_ref.attn_ref), channel_id=1, source_target_pairs={{0,4},{2,6},{4,0},{10,14},{12,8},{14,10},{16,20},{20,16},{22,18},{... | collective-permute-start | bytes 1572872 | tf_op jit(solution)/shard_map/ppermute | solution.py:456
  86.4 22.6 %collective-permute-start.7 = (bf16[2048,128]{1,0:T(8,128)(2,1)S(1)}, bf16[2048,128]{1,0:T(8,128)(2,1)S(1)}, u32[]{:S(2)}, u32[]{:S(2)}) collective-permute-start(bf16[2048,128]{1,0:T(8,128)(2,1)S(1)} %get-tuple-element.41.refs_0_.o_ref.attn_ref), channel_id=1, source_target_pairs={{0,2},{2,0},{4,6},{10,8},{12,14},{14,12},{16,18},{20,22},{22,20},{... | collective-permute-start | bytes 1572872 | tf_op jit(solution)/shard_map/ppermute | solution.py:456
  130.6 3.7 %collective-permute-start.15 = (bf16[2,2048,128]{2,1,0:T(8,128)(2,1)S(1)}, bf16[2,2048,128]{2,1,0:T(8,128)(2,1)S(1)}, u32[]{:S(2)}, u32[]{:S(2)}) collective-permute-start(bf16[2,2048,128]{2,1,0:T(8,128)(2,1)S(1)} %get-tuple-element.46), channel_id=1, source_target_pairs={{0,1},{1,0},{2,3},{3,2},{4,5},{5,4},{6,7},{7,6},{8,9},{9,8},{10,11... | collective-permute-start | bytes 3145736 | tf_op jit(solution)/shard_map/ppermute | solution.py:476
  136.4 83.7 %all-to-all-start.2 = ((bf16[16,4,128,128]{3,2,1,0:T(8,128)(2,1)}), bf16[16,4,128,128]{3,2,1,0:T(8,128)(2,1)S(1)}, u32[]{:S(2)}, u32[]{:S(2)}) async-start(bf16[16,4,128,128]{3,2,1,0:T(8,128)(2,1)} %copy-done.1), calls=%async_computation.2 | async-start | bytes 4194304 | tf_op jit(solution)/shard_map/all_to_all | solution.py:482
  154.3 34.1 %collective-permute-start.11 = (bf16[384,768]{1,0:T(8,128)(2,1)S(1)}, bf16[384,768]{1,0:T(8,128)(2,1)}, u32[]{:S(2)}, u32[]{:S(2)}) collective-permute-start(bf16[384,768]{1,0:T(8,128)(2,1)S(1)} %add_convert_fusion.1), channel_id=1, source_target_pairs={{0,16},{2,18},{4,20},{6,22},{8,24},{10,26},{12,28},{14,30},{17,1},... | collective-permute-start | bytes 1769480 | tf_op jit(solution)/shard_map/ppermute | solution.py:305
  189.6 18.0 %collective-permute-start.14 = (bf16[384,768]{1,0:T(8,128)(2,1)S(1)}, bf16[384,768]{1,0:T(8,128)(2,1)S(1)}, u32[]{:S(2)}, u32[]{:S(2)}) collective-permute-start(bf16[384,768]{1,0:T(8,128)(2,1)S(1)} %broadcast_select_fusion.2.refs_0_), channel_id=1, source_target_pairs={{0,4},{2,6},{4,0},{6,2},{8,12},{10,14},{12,8},{14,10},{16,20},{18,... | collective-permute-start | bytes 1769480 | tf_op jit(solution)/shard_map/ppermute | solution.py:308
  189.6 17.9 %collective-permute-start.13 = (bf16[384,768]{1,0:T(8,128)(2,1)S(1)}, bf16[384,768]{1,0:T(8,128)(2,1)S(1)}, u32[]{:S(2)}, u32[]{:S(2)}) collective-permute-start(bf16[384,768]{1,0:T(8,128)(2,1)S(1)} %broadcast_select_fusion.2.refs_0_), channel_id=1, source_target_pairs={{0,2},{2,0},{4,6},{6,4},{8,10},{10,8},{12,14},{14,12},{16,18},{18,... | collective-permute-start | bytes 1769480 | tf_op jit(solution)/shard_map/ppermute | solution.py:308
  190.4 29.7 %collective-permute-start.12 = (bf16[384,768]{1,0:T(8,128)(2,1)S(1)}, bf16[384,768]{1,0:T(8,128)(2,1)}, u32[]{:S(2)}, u32[]{:S(2)}) collective-permute-start(bf16[384,768]{1,0:T(8,128)(2,1)S(1)} %broadcast_select_fusion.2.refs_0_), channel_id=1, source_target_pairs={{0,8},{2,10},{4,12},{6,14},{8,0},{10,2},{12,4},{14,6},{16,24},{18,... | collective-permute-start | bytes 1769480 | tf_op jit(solution)/shard_map/ppermute | solution.py:308
  222.6 15.1 %collective-permute-start.21 = (bf16[384,768]{1,0:T(8,128)(2,1)}, bf16[384,768]{1,0:T(8,128)(2,1)S(1)}, u32[]{:S(2)}, u32[]{:S(2)}) collective-permute-start(bf16[384,768]{1,0:T(8,128)(2,1)} %collective-permute-done.12.refs_5_), channel_id=1, source_target_pairs={{0,4},{2,6},{4,0},{6,2},{8,12},{10,14},{12,8},{14,10},{16,20},{18,... | collective-permute-start | bytes 1769480 | tf_op jit(solution)/shard_map/ppermute | solution.py:308
  224.3 15.4 %collective-permute-start.20 = (bf16[384,768]{1,0:T(8,128)(2,1)}, bf16[384,768]{1,0:T(8,128)(2,1)S(1)}, u32[]{:S(2)}, u32[]{:S(2)}) collective-permute-start(bf16[384,768]{1,0:T(8,128)(2,1)} %collective-permute-done.12.refs_5_), channel_id=1, source_target_pairs={{0,2},{2,0},{4,6},{6,4},{8,10},{10,8},{12,14},{14,12},{16,18},{18,... | collective-permute-start | bytes 1769480 | tf_op jit(solution)/shard_map/ppermute | solution.py:308
  234.1 24.4 %collective-permute-start.17 = (bf16[256,1536]{1,0:T(8,128)(2,1)}, bf16[256,1536]{1,0:T(8,128)(2,1)}, u32[]{:S(2)}, u32[]{:S(2)}) collective-permute-start(bf16[256,1536]{1,0:T(8,128)(2,1)} %dynamic-slice_convert_fusion), channel_id=1, source_target_pairs={{0,1},{1,0},{2,3},{3,2},{4,5},{5,4},{6,7},{7,6},{8,9},{9,8},{10,11... | collective-permute-start | bytes 2359304 | tf_op jit(solution)/shard_map/ppermute | solution.py:546
  235.2 9.8 %collective-permute-start.19 = (bf16[192,768]{1,0:T(8,128)(2,1)}, bf16[192,768]{1,0:T(8,128)(2,1)S(1)}, u32[]{:S(2)}, u32[]{:S(2)}) collective-permute-start(bf16[192,768]{1,0:T(8,128)(2,1)} %slice.21), channel_id=1, source_target_pairs={{0,2},{2,0},{4,6},{6,4},{8,10},{10,8},{12,14},{14,12},{16,18},{18,... | collective-permute-start | bytes 884744 | tf_op jit(solution)/shard_map/ppermute | solution.py:308
  237.1 8.3 %collective-permute-start.18 = (bf16[192,768]{1,0:T(8,128)(2,1)}, bf16[192,768]{1,0:T(8,128)(2,1)}, u32[]{:S(2)}, u32[]{:S(2)}) collective-permute-start(bf16[192,768]{1,0:T(8,128)(2,1)} %slice.20), channel_id=1, source_target_pairs={{0,4},{2,6},{4,0},{6,2},{8,12},{10,14},{12,8},{14,10},{16,20},{18,... | collective-permute-start | bytes 884744 | tf_op jit(solution)/shard_map/ppermute | solution.py:308
  238.5 12.8 %collective-permute-start.23 = (bf16[192,768]{1,0:T(8,128)(2,1)}, bf16[192,768]{1,0:T(8,128)(2,1)}, u32[]{:S(2)}, u32[]{:S(2)}) collective-permute-start(bf16[192,768]{1,0:T(8,128)(2,1)} %slice.23), channel_id=1, source_target_pairs={{0,2},{2,0},{4,6},{6,4},{8,10},{10,8},{12,14},{14,12},{16,18},{18,... | collective-permute-start | bytes 884744 | tf_op jit(solution)/shard_map/ppermute | solution.py:308
  240.4 11.3 %collective-permute-start.22 = (bf16[192,768]{1,0:T(8,128)(2,1)}, bf16[192,768]{1,0:T(8,128)(2,1)}, u32[]{:S(2)}, u32[]{:S(2)}) collective-permute-start(bf16[192,768]{1,0:T(8,128)(2,1)} %slice.22), channel_id=1, source_target_pairs={{0,4},{2,6},{4,0},{6,2},{8,12},{10,14},{12,8},{14,10},{16,20},{18,... | collective-permute-start | bytes 884744 | tf_op jit(solution)/shard_map/ppermute | solution.py:308
  (27 other events, 195.0 us)
Sparse Core Ops, SparseCore 0:
  60.7 67.5 all-gather.2
